TPU v7x, 32 devices: a whole 2x2x4 slice. The times are simulated.
32 devices in a mesh: feat: 16 (over z, x, core), dom: 2 (over y).
Axes of the slice: x: 2, y: 2, z: 4, core: 2. Of those that a mesh axis runs over, the one named last changes fastest.
Arguments:
- features: bfloat16 [16384, 1024], P('dom', 'feat'), may hold values from -6 to 6
- self_weight: bfloat16 [1024, 512], P('feat'), may hold values from -0.1875 to 0.1875
- neighbour_weight: bfloat16 [1024, 512], P('feat'), may hold values from -1.5 to 1.5
- cotangent: bfloat16 [16384, 512], P(('dom', 'feat')), may hold values from -0.1875 to 0.1875
- send_rows: int32 [2, 2, 256], replicated, may hold values from 0 to 8191
- send_count: int32 [2, 2], replicated, may hold values from 32 to 256, as said below
- tile_source: int32 [2, 64, 8], P('dom'), may hold values from 0 to 67
- tile_kind: int32 [2, 64, 8], P('dom'), may hold values from 0 to 63
- tile_patterns: bfloat16 [64, 128, 128], replicated, may hold values from 0.0099487305 to 1
Outputs:
- hidden: bfloat16 [16384, 512], P(('dom', 'feat'))
- grad_self: float32 [1024, 512], P('feat')
- grad_neighbour: float32 [1024, 512], P('feat')
Inputs may be any that keep to these rules, and one draw needn't show every extreme that they name: `send_count`: one destination has 256 live slots from every owner.
All inputs are finite; a program needn't handle non-finite values.
Results may differ from a plain program's by a relative error of at most 0.005.
Values may be sent and summed in bfloat16 or wider, within the bound.
No kernel may reach another device: no remote copies, remote signals or barrier semaphores. Data moves between devices by JAX's collectives and lax.ppermute only.
A program may use at most 128 MiB of HBM per device.

v0:
```python
import jax
import jax.numpy as jnp
from jax import lax
from jax.sharding import PartitionSpec as P

inv_root_two = 0.7071067811865476
inv_root_two_pi = 0.3989422804014327


def gelu_pair(linear):
    normal_cdf = 0.5 * (1.0 + jax.scipy.special.erf(linear * inv_root_two))
    density = jnp.exp(-0.5 * linear * linear) * inv_root_two_pi
    return (linear * normal_cdf, normal_cdf + linear * density)


def on_device(
    features,
    self_weight,
    neighbour_weight,
    cotangent,
    send_rows,
    send_count,
    tile_source,
    tile_kind,
    tile_patterns,
):
    my_part = lax.axis_index("dom")
    part_count = lax.axis_size("dom")
    row_count = features.shape[0]
    col_count = features.shape[1]
    slot_count = send_rows.shape[2]
    tile_rows = tile_patterns.shape[1]
    slot_ids = jnp.arange(slot_count, dtype=jnp.int32)
    outgoing = lax.dynamic_index_in_dim(send_rows, my_part, 0, keepdims=False)
    counts = lax.dynamic_index_in_dim(send_count, my_part, 0, keepdims=False)
    picked = features[outgoing.reshape(-1)].reshape(part_count, slot_count, col_count)
    live_mask = slot_ids[None, :] < counts[:, None]
    picked = jnp.where(live_mask[:, :, None], picked, jnp.zeros((), jnp.bfloat16))
    remote = lax.all_to_all(picked, "dom", split_axis=0, concat_axis=0, tiled=True)
    extended = jnp.concatenate([features, remote.reshape(-1, col_count)], 0).reshape(
        -1, tile_rows, col_count
    )
    kinds = tile_kind[0]
    tile_mats = tile_patterns[kinds]
    sources = extended[tile_source[0]]
    summed = jnp.einsum("tkab,tkbf->taf", tile_mats, sources, preferred_element_type=jnp.float32)
    pattern_sums = jnp.sum(tile_patterns, axis=2, dtype=jnp.float32)
    degree = jnp.sum(pattern_sums[kinds], axis=1)
    neighbour_mean = (
        (summed / degree[:, :, None]).reshape(row_count, col_count).astype(jnp.bfloat16)
    )
    own_features, own_mean = (
        lax.all_to_all(features, "feat", split_axis=0, concat_axis=1, tiled=True),
        lax.all_to_all(neighbour_mean, "feat", split_axis=0, concat_axis=1, tiled=True),
    )
    linear = jnp.dot(
        own_features,
        lax.all_gather(self_weight, "feat", axis=0, tiled=True),
        preferred_element_type=jnp.float32,
    ) + jnp.dot(
        own_mean,
        lax.all_gather(neighbour_weight, "feat", axis=0, tiled=True),
        preferred_element_type=jnp.float32,
    )
    gelu_value, gelu_slope = gelu_pair(linear)
    hidden = gelu_value.astype(jnp.bfloat16)
    grad_linear = (cotangent.astype(jnp.float32) * gelu_slope).astype(jnp.bfloat16)
    shard_rows = lax.all_gather(grad_linear, "feat", axis=0, tiled=True)
    self_part = jnp.einsum("rc,rh->ch", features, shard_rows, preferred_element_type=jnp.float32)
    neigh_part = jnp.einsum(
        "rc,rh->ch", neighbour_mean, shard_rows, preferred_element_type=jnp.float32
    )
    self_local, neigh_local = (self_part, neigh_part)
    grad_self, grad_neighbour = lax.psum((self_local, neigh_local), "dom")
    return (hidden, grad_self, grad_neighbour)


def solution(mesh):
    placed = (
        P("dom", "feat"),
        P("feat", None),
        P("feat", None),
        P(("dom", "feat"), None),
        P(),
        P(),
        P("dom", None, None),
        P("dom", None, None),
        P(),
    )
    return jax.shard_map(
        on_device,
        mesh=mesh,
        in_specs=placed,
        out_specs=(P(("dom", "feat"), None), P("feat", None), P("feat", None)),
        check_vma=False,
    )
```

profile of v0, /device:TPU:0, one launch (start us, length us, event | category | flops | bytes accessed | tf_op | source)
XLA Modules:
  0.0 229.3 jit_solution(2324046446978525975)
XLA Ops:
  7.2 0.0 copy-start
  7.2 0.0 copy-start.1
  7.2 0.0 all-gather.4.cloned.1.call-start
  7.2 0.7 all-gather.4.cloned.1.call-update
  8.0 2.7 %copy.43 = bf16[8192,64]{1,0:T(8,128)(2,1)} copy(bf16[8192,64]{0,1:T(8,128)(2,1)} %param.9) | data formatting | bytes 2097152 | tf_op args[0]
  10.7 2.9 %gather_fusion.1 = bf16[512,64]{1,0:T(8,128)(2,1)S(1)} fusion(bf16[8192,64]{1,0:T(8,128)(2,1)} %copy.43, s32[1024]{0:T(1024)S(1)} %pad_clamp_fusion.1), kind=kCustom, calls=%fused_computation.1 | custom fusion | bytes 133120 | tf_op jit(solution)/shard_map/gather | solution.py:36
  13.6 0.1 copy.44
  13.7 0.7 dynamic-slice_bitcast_fusion.1
  14.4 0.1 iota_compare_fusion
  14.5 0.6 broadcast_select_fusion
  15.2 4.2 %all-to-all-start.1 = ((bf16[2,256,64]{1,2,0:T(8,128)(2,1)}), bf16[2,256,64]{1,2,0:T(8,128)(2,1)S(1)}, u32[]{:S(2)}, u32[]{:S(2)}) async-start(bf16[2,256,64]{1,2,0:T(8,128)(2,1)} %broadcast_select_fusion), calls=%async_computation.1 | async-start | bytes 131072 | tf_op jit(solution)/shard_map/all_to_all | solution.py:39
  19.4 0.7 all-gather.6.cloned.1.call-update
  20.1 0.7 compare_select_fusion.1
  20.8 0.1 copy.46
  20.9 0.1 reshape.161
  21.0 0.7 compare_select_fusion.2
  21.7 0.1 copy.42
  21.8 0.1 reshape.145
  21.9 2.2 convert_reduce_fusion
  24.1 1.0 gather_fusion.3
  25.1 0.1 bitcast_reduce_fusion
  25.2 0.0 copy-start.3
  25.3 13.9 %gather_fusion = bf16[512,128,128]{2,1,0:T(8,128)(2,1)} fusion(bf16[64,128,128]{2,1,0:T(8,128)(2,1)S(1)} %copy-done.1, s32[1024]{0:T(1024)S(1)} %pad_clamp_fusion.2), kind=kCustom, calls=%fused_computation | custom fusion | bytes 33556480 | tf_op jit(solution)/shard_map/gather | solution.py:44
  39.2 1.1 copy.63
  40.3 6.5 %all-to-all-start = ((bf16[16,512,64]{1,2,0:T(8,128)(2,1)}), bf16[16,512,64]{1,2,0:T(8,128)(2,1)}, u32[]{:S(2)}, u32[]{:S(2)}) async-start(bf16[16,512,64]{1,2,0:T(8,128)(2,1)} %bitcast.61), calls=%async_computation | async-start | bytes 2097152 | tf_op jit(solution)/shard_map/all_to_all | solution.py:53
  46.8 0.3 copy_bitcast_fusion
  47.2 13.5 %gather_fusion.2 = bf16[512,128,64]{1,2,0:T(8,128)(2,1)} fusion(bf16[68,128,64]{1,2,0:T(8,128)(2,1)S(1)} %copy_bitcast_fusion, s32[1024]{0:T(1024)S(1)} %pad_clamp_fusion), kind=kCustom, calls=%fused_computation.2 | custom fusion | bytes 16779264 | tf_op jit(solution)/shard_map/gather | solution.py:45
  60.6 11.3 %fusion = bf16[64,128,64]{1,2,0:T(8,128)(2,1)S(1)} fusion(bf16[64,8,128,128]{3,2,1,0:T(8,128)(2,1)} %bitcast.64, bf16[64,8,128,64]{2,3,1,0:T(8,128)(2,1)} %bitcast.62, f32[64,128]{1,0:T(8,128)S(1)} %bitcast_reduce_fusion), kind=kOutput, calls=%fused_computation.6 | convolution fusion | flops 1074790400 | bytes 26247168 | tf_op jit(solution)/shard_map/tkab,tkbf->taf/dot_general | solution.py:46
  72.0 1.7 copy.48
  73.6 1.7 convert_element_type.24
  75.3 1.6 copy.49
  76.9 6.0 %all-to-all-start.2 = ((bf16[16,512,64]{1,2,0:T(8,128)(2,1)}), bf16[16,512,64]{1,2,0:T(8,128)(2,1)S(1)}, u32[]{:S(2)}, u32[]{:S(2)}) async-start(bf16[16,512,64]{1,2,0:T(8,128)(2,1)} %copy.49), calls=%async_computation.2 | async-start | bytes 2097152 | tf_op jit(solution)/shard_map/all_to_all | solution.py:54
  82.9 0.0 all-gather.8.cloned.1.call-start
  82.9 0.0 all-gather.4.cloned.1.call-done
  82.9 3.3 %fusion.10 = f32[512,512]{1,0:T(8,128)} fusion(bf16[512,1024]{0,1:T(8,128)(2,1)} %bitcast.1, bf16[1024,512]{1,0:T(8,128)(2,1)} %all-gather.4.cloned.1.call-done), kind=kOutput, calls=%fused_computation.35 | convolution fusion | flops 536870912 | bytes 3145728 | tf_op jit(solution)/shard_map/dot_general | solution.py:56
  86.2 12.1 %all-gather.6.cloned.1.call-done = bf16[1024,512]{1,0:T(8,128)(2,1)} async-done(((bf16[64,512]{1,0:T(8,128)(2,1)}), bf16[1024,512]{1,0:T(8,128)(2,1)}) %all-gather.6.cloned.1.call-update) | async-done | bytes 1048592 | tf_op jit(solution)/shard_map/all_gather | solution.py:62
  98.3 10.1 %all-to-all-done.2 = bf16[16,512,64]{1,2,0:T(8,128)(2,1)S(1)} async-done(((bf16[16,512,64]{1,2,0:T(8,128)(2,1)}), bf16[16,512,64]{1,2,0:T(8,128)(2,1)S(1)}, u32[]{:S(2)}, u32[]{:S(2)}) %all-to-all-start.2) | async-done | bytes 1048608 | tf_op jit(solution)/shard_map/all_to_all | solution.py:54
  108.4 3.9 %fusion.6 = (bf16[512,512]{1,0:T(8,128)(2,1)}, bf16[512,512]{1,0:T(8,128)(2,1)}) fusion(bf16[512,512]{1,0:T(8,128)(2,1)} %param.12, f32[512,512]{1,0:T(8,128)} %fusion.10, bf16[512,1024]{0,1:T(8,128)(2,1)S(1)} %bitcast.65, bf16[1024,512]{1,0:T(8,128)(2,1)} %all-gather.6.cloned.1.call-done), kind=kOutput, calls=%fused_computation.17 | convolution fusion | flops 540540928 | bytes 4718592 | tf_op jit(solution)/shard_map/dot_general | solution.py:60
  112.3 0.0 all-gather.8.cloned.1.call-update
  112.3 0.0 all-reduce.3.cloned.1.call-start
  112.3 77.6 %all-gather.8.cloned.1.call-done = bf16[8192,512]{1,0:T(8,128)(2,1)} async-done(((bf16[512,512]{1,0:T(8,128)(2,1)}), bf16[8192,512]{1,0:T(8,128)(2,1)}) %all-gather.8.cloned.1.call-update) | async-done | bytes 8388624 | tf_op jit(solution)/shard_map/all_gather | solution.py:68
  189.9 5.7 %fusion.7 = f32[64,512]{1,0:T(8,128)} fusion(bf16[8192,512]{1,0:T(8,128)(2,1)} %all-gather.8.cloned.1.call-done, bf16[64,128,64]{1,2,0:T(8,128)(2,1)S(1)} %fusion), kind=kOutput, calls=%fused_computation.18 | convolution fusion | flops 536870912 | bytes 9568256 | tf_op jit(solution)/shard_map/rc,rh->ch/dot_general | solution.py:70
  195.7 0.0 copy-done.2
  195.7 2.2 convolution_bitcast_fusion
  197.9 0.0 all-reduce.3.cloned.1.call-update
  197.9 21.8 %all-reduce.3.cloned.1.call-done = (f32[64,512]{1,0:T(8,128)}, f32[64,512]{1,0:T(8,128)}) async-done(((f32[64,512]{1,0:T(8,128)}, f32[64,512]{1,0:T(8,128)}), (f32[64,512]{1,0:T(8,128)}, f32[64,512]{1,0:T(8,128)})) %all-reduce.3.cloned.1.call-update) | async-done | bytes 262160 | tf_op jit(solution)/shard_map/psum | solution.py:74
  219.7 1.6 copy.66
  221.2 1.6 copy.67
  (14 shorter events, 0.1 us)
Async XLA Ops:
  7.2 0.8 copy-start
  7.2 18.1 %copy-start.1 = (bf16[64,128,128]{2,1,0:T(8,128)(2,1)S(1)}, bf16[64,128,128]{2,1,0:T(8,128)(2,1)}, u32[]{:S(2)}) copy-start(bf16[64,128,128]{2,1,0:T(8,128)(2,1)} %param.17) | copy-start | bytes 6291460
  7.2 75.7 %all-gather.4.cloned.1.call-start = ((), (), s32[]{:S(2)}) async-start(), calls=%async_computation.3 | async-start | bytes 1114112 | tf_op jit(solution)/shard_map/all_gather | solution.py:58
  15.2 25.1 %all-to-all-start.1 = ((bf16[2,256,64]{1,2,0:T(8,128)(2,1)}), bf16[2,256,64]{1,2,0:T(8,128)(2,1)S(1)}, u32[]{:S(2)}, u32[]{:S(2)}) async-start(bf16[2,256,64]{1,2,0:T(8,128)(2,1)} %broadcast_select_fusion), calls=%async_computation.1 | async-start | bytes 131072 | tf_op jit(solution)/shard_map/all_to_all | solution.py:39
  19.4 78.9 %all-gather.6.cloned.1.call-start = ((), (), s32[]{:S(2)}) async-start(), calls=%async_computation.4 | async-start | bytes 1114112 | tf_op jit(solution)/shard_map/all_gather | solution.py:62
  25.2 13.9 %copy-start.3 = (bf16[8192,64]{0,1:T(8,128)(2,1)S(1)}, bf16[8192,64]{0,1:T(8,128)(2,1)}, u32[]{:S(2)}) copy-start(bf16[8192,64]{0,1:T(8,128)(2,1)} %param.9) | copy-start | bytes 3145732
  40.3 36.6 %all-to-all-start = ((bf16[16,512,64]{1,2,0:T(8,128)(2,1)}), bf16[16,512,64]{1,2,0:T(8,128)(2,1)}, u32[]{:S(2)}, u32[]{:S(2)}) async-start(bf16[16,512,64]{1,2,0:T(8,128)(2,1)} %bitcast.61), calls=%async_computation | async-start | bytes 2097152 | tf_op jit(solution)/shard_map/all_to_all | solution.py:53
  76.9 31.5 %all-to-all-start.2 = ((bf16[16,512,64]{1,2,0:T(8,128)(2,1)}), bf16[16,512,64]{1,2,0:T(8,128)(2,1)S(1)}, u32[]{:S(2)}, u32[]{:S(2)}) async-start(bf16[16,512,64]{1,2,0:T(8,128)(2,1)} %copy.49), calls=%async_computation.2 | async-start | bytes 2097152 | tf_op jit(solution)/shard_map/all_to_all | solution.py:54
  82.9 107.0 %all-gather.8.cloned.1.call-start = ((), (), s32[]{:S(2)}) async-start(), calls=%async_computation.5 | async-start | bytes 8912896 | tf_op jit(solution)/shard_map/all_gather | solution.py:68
  112.3 107.4 %all-reduce.3.cloned.1.call-start = ((), (), s32[]{:S(2)}) async-start(), calls=%async_computation.6 | async-start | bytes 524288 | tf_op jit(solution)/shard_map/psum | solution.py:74
  189.9 5.8 %copy-start.2 = (bf16[8192,512]{1,0:T(8,128)(2,1)S(1)}, bf16[8192,512]{1,0:T(8,128)(2,1)}, u32[]{:S(2)}) copy-start(bf16[8192,512]{1,0:T(8,128)(2,1)} %all-gather.8.cloned.1.call-done) | copy-start | bytes 25165828
Sparse Core Ops, SparseCore 0:
  10.2 40.6 all-gather.3
  53.0 45.2 all-gather.5
  112.4 77.4 all-gather.7
  198.0 21.5 all-reduce.2
where the time goes:
time: 230 us; the launch traced here: 229 us
  waiting for transfers between devices  123 us (53%)
  local copies, waits for them, and re-layouts  44.5 us (19%)
  matrix products  26.4 us (11%)
  starting transfers between devices  16.8 us (7%)
  between operations  13.9 us (6%)
  other arithmetic  4.71 us (2%)
    all_gather x1, waiting for transfers between devices, on_device(): shard_rows = lax.all_gather(grad_linear, 'feat', axis=0, tiled=True)  77.6 us
    psum x1, waiting for transfers between devices, on_device(): grad_self, grad_neighbour = lax.psum((self_local, neigh_local), 'dom')  21.8 us
    gather x1, local copies, waits for them, and re-layouts, on_device(): tile_mats = tile_patterns[kinds]  13.9 us
    gather x1, local copies, waits for them, and re-layouts, on_device(): sources = extended[tile_source[0]]  13.5 us
    all_gather x1, waiting for transfers between devices, on_device(): lax.all_gather(neighbour_weight, 'feat', axis=0, tiled=True)  12.1 us
    dot_general x1, matrix products, on_device(): jnp.einsum('tkab,tkbf->taf', tile_mats, sources, preferred_element_type=j...  11.3 us
    all_to_all x1, waiting for transfers between devices, on_device(): lax.all_to_all(neighbour_mean, 'feat', split_axis=0, concat_axis=1, tiled...  10.1 us
    all_to_all x1, starting transfers between devices, on_device(): lax.all_to_all(features, 'feat', split_axis=0, concat_axis=1, tiled=True)  6.52 us
  transfers between devices with their start and end apart: 7, of which 4 were waited for; matrix products, arithmetic and copies ran while one was open for 26% of the time, Pallas kernels for 0%

commit v1 on v0

v1 whole, which is shorter than its diff:
```python
import functools

import jax
import jax.numpy as jnp
from jax import lax
from jax.experimental import pallas as pl
from jax.experimental.pallas import tpu as pltpu
from jax.sharding import PartitionSpec as P

inv_root_two = 0.7071067811865476
inv_root_two_pi = 0.3989422804014327
bf16 = jnp.bfloat16
f32 = jnp.float32
vmem_bytes = 48 * 2**20
whole_vmem = pl.BlockSpec(memory_space=pltpu.VMEM)
whole_smem = pl.BlockSpec(memory_space=pltpu.SMEM)
last_with_last = (((1,), (1,)), ((), ()))
first_with_first = (((0,), (0,)), ((), ()))


def gelu_pair(linear):
    normal_cdf = 0.5 * (1.0 + lax.erf(linear * inv_root_two))
    density = jnp.exp(-0.5 * linear * linear) * inv_root_two_pi
    return (linear * normal_cdf, normal_cdf + linear * density)


def flip(axis, bit):
    size = lax.axis_size(axis)
    return functools.partial(
        lax.ppermute, axis_name=axis, perm=[(i, i ^ bit) for i in range(size)]
    )


def bits_of(size):
    return [1 << i for i in range(size.bit_length() - 1)]


def pick_kernel(step, columns_ref, rows_ref, picked_ref):
    total = jnp.zeros(picked_ref.shape, f32)
    for at in range(0, columns_ref.shape[1], step):
        ids = lax.broadcasted_iota(jnp.int32, (step, rows_ref.shape[1]), 0) + at
        one_hot = jnp.where(ids == rows_ref[...], 1.0, 0.0).astype(bf16)
        total = total + jnp.dot(
            columns_ref[:, at : at + step], one_hot, preferred_element_type=f32
        )
    picked_ref[...] = total.astype(bf16)


def pick_rows(columns, rows):
    depth, width = columns.shape[0], rows.shape[1]
    return pl.pallas_call(
        functools.partial(pick_kernel, min(256, columns.shape[1])),
        out_shape=jax.ShapeDtypeStruct((depth, width), bf16),
        in_specs=[whole_vmem, whole_vmem],
        out_specs=whole_vmem,
        cost_estimate=pl.CostEstimate(
            flops=2 * columns.size * width, bytes_accessed=2 * columns.size, transcendentals=0
        ),
        compiler_params=pltpu.CompilerParams(vmem_limit_bytes=vmem_bytes),
        name="pick_rows",
    )(columns, rows)


def mean_kernel(unroll, source_ref, kind_ref, local_ref, halo_ref, pattern_ref, mean_ref, tiles):
    depth = local_ref.shape[0]
    side = pattern_ref.shape[1]
    local_tiles, halo_tiles = local_ref.shape[1] // side, halo_ref.shape[1] // side
    for i in range(local_tiles):
        tiles[i, 0:depth, :] = local_ref[:, i * side : (i + 1) * side]
    for i in range(halo_tiles):
        tiles[local_tiles + i, 0:depth, :] = halo_ref[:, i * side : (i + 1) * side]
    tiles[:, depth:, :] = jnp.ones((tiles.shape[0], tiles.shape[1] - depth, side), bf16)
    per_block = mean_ref.shape[2] // side

    def one(t):
        rows = [tiles[source_ref[k, t]] for k in range(source_ref.shape[0])]
        weights = [pattern_ref[kind_ref[k, t]] for k in range(source_ref.shape[0])]
        summed = lax.dot_general(
            jnp.concatenate(rows, 1),
            jnp.concatenate(weights, 1),
            last_with_last,
            preferred_element_type=f32,
        )
        mean = (summed[0:depth] / summed[depth : depth + 1]).astype(bf16)
        at = lax.rem(t, per_block) * side
        mean_ref[lax.div(t, per_block), :, pl.ds(pl.multiple_of(at, side), side)] = mean

    @pl.loop(0, source_ref.shape[1] // unroll)
    def _(step):
        for u in range(unroll):
            one(step * unroll + u)


def neighbour_means(source, kind, local, halo, patterns, blocks):
    depth, count = local.shape
    side = patterns.shape[1]
    tile_count = (count + halo.shape[1]) // side
    dest = source.shape[1]
    flops = 2 * source.size * side * side * depth
    return pl.pallas_call(
        functools.partial(mean_kernel, 4 if dest % 4 == 0 else 1),
        out_shape=jax.ShapeDtypeStruct((blocks, depth, count // blocks), bf16),
        in_specs=[whole_smem, whole_smem, whole_vmem, whole_vmem, whole_vmem],
        out_specs=whole_vmem,
        scratch_shapes=[pltpu.VMEM((tile_count, depth + 16, side), bf16)],
        cost_estimate=pl.CostEstimate(
            flops=8 * flops, bytes_accessed=2 * (patterns.size + 2 * local.size), transcendentals=0
        ),
        compiler_params=pltpu.CompilerParams(vmem_limit_bytes=vmem_bytes),
        name="neighbour_means",
    )(source, kind, local, halo, patterns)


def gather_weights(weights):
    size = lax.axis_size("feat")
    me = lax.axis_index("feat")
    held = weights
    for place, bit in enumerate(reversed(bits_of(size))):
        other = flip("feat", bit)(held)
        upper = (me & bit) != 0
        held = jnp.stack(
            [jnp.where(upper, other, held), jnp.where(upper, held, other)], axis=place
        )
    return held.reshape((size,) + weights.shape)


def halve(parts, axis_name, bit, axis):
    mine = (lax.axis_index(axis_name) & bit) // bit
    sent = lax.dynamic_index_in_dim(parts, 1 - mine, axis, keepdims=False)
    kept = lax.dynamic_index_in_dim(parts, mine, axis, keepdims=False)
    return kept.astype(f32) + flip(axis_name, bit)(sent.astype(bf16)).astype(f32)


def reduce_gradients(parts):
    feat, dom = lax.axis_size("feat"), lax.axis_size("dom")
    rows, cols = parts.shape[2:]
    cores, rest = 2, feat // 2
    near = min(4, rest)
    far = rest // near
    parts = halve(parts.reshape(rest, cores, dom, rows, cols), "feat", 1, 1)
    parts = parts.astype(bf16).reshape(far, near, dom, rows, cols)
    blocks = jnp.transpose(parts, (2, 1, 0, 3, 4)).reshape(dom * near, far, rows, cols)
    groups = [
        [d * feat + (h * near + n) * cores + c for d in range(dom) for n in range(near)]
        for h in range(far)
        for c in range(cores)
    ]
    blocks = lax.all_to_all(
        blocks, ("dom", "feat"), 0, 0, axis_index_groups=groups, tiled=True
    )
    total = jnp.sum(blocks.astype(f32), axis=0)
    for place, bit in enumerate(reversed(bits_of(far))):
        total = halve(
            total.reshape((2, -1) + total.shape[1:]), "feat", bit * near * cores, 0
        )
    total = total.reshape(rows, cols)
    me = lax.axis_index("dom")
    if dom == 2:
        other = flip("dom", 1)(total)
        return jnp.stack([jnp.where(me == 0, total, other), jnp.where(me == 0, other, total)])
    return lax.all_gather(total, "dom", axis=0)


def on_device(
    features,
    self_weight,
    neighbour_weight,
    cotangent,
    send_rows,
    send_count,
    tile_source,
    tile_kind,
    tile_patterns,
):
    feat, dom = lax.axis_size("feat"), lax.axis_size("dom")
    my_part = lax.axis_index("dom")
    count, depth = features.shape
    rows = count // feat
    hid = self_weight.shape[1]
    slots = send_rows.shape[2]
    columns = features.T
    own_features = lax.all_to_all(
        jnp.transpose(columns.reshape(depth, feat, rows), (1, 0, 2)), "feat", 0, 0, tiled=True
    )
    outgoing = lax.dynamic_index_in_dim(send_rows, my_part, 0, keepdims=False)
    live = lax.dynamic_index_in_dim(send_count, my_part, 0, keepdims=False)
    slot_ids = jnp.arange(slots, dtype=jnp.int32)
    outgoing = jnp.where(slot_ids[None, :] < live[:, None], outgoing, -1)
    picked = pick_rows(columns, outgoing.reshape(1, dom * slots))
    if dom == 2:
        to_me = lax.dynamic_slice_in_dim(picked, my_part * slots, slots, 1)
        to_other = lax.dynamic_slice_in_dim(picked, (1 - my_part) * slots, slots, 1)
        got = flip("dom", 1)(to_other)
        first = my_part == 0
        halo = jnp.concatenate(
            [jnp.where(first, to_me, got), jnp.where(first, got, to_me)], axis=1
        )
    else:
        halo = lax.all_to_all(picked, "dom", 1, 1, tiled=True)
    own_mean = lax.all_to_all(
        neighbour_means(tile_source[0].T, tile_kind[0].T, columns, halo, tile_patterns, feat),
        "feat",
        0,
        0,
        tiled=True,
    )
    weights = gather_weights(jnp.stack([self_weight, neighbour_weight]))
    own_features = own_features.reshape(feat * depth, rows)
    own_mean = own_mean.reshape(feat * depth, rows)
    linear = lax.dot_general(
        own_features,
        weights[:, 0].reshape(feat * depth, hid),
        first_with_first,
        preferred_element_type=f32,
    ) + lax.dot_general(
        own_mean,
        weights[:, 1].reshape(feat * depth, hid),
        first_with_first,
        preferred_element_type=f32,
    )
    gelu_value, gelu_slope = gelu_pair(linear)
    hidden = gelu_value.astype(bf16)
    grad_linear = (cotangent.astype(f32) * gelu_slope).astype(bf16)
    self_part = jnp.dot(own_features, grad_linear, preferred_element_type=f32)
    neigh_part = jnp.dot(own_mean, grad_linear, preferred_element_type=f32)
    both = jnp.stack(
        [self_part.reshape(feat, depth, hid), neigh_part.reshape(feat, depth, hid)], axis=1
    )
    split = dom // 2 if dom > 2 else 1
    both = both.reshape(feat, 2 * split, depth // split, hid)
    grads = reduce_gradients(both).reshape(2, depth, hid)
    return (hidden, grads[0], grads[1])


def solution(mesh):
    placed = (
        P("dom", "feat"),
        P("feat", None),
        P("feat", None),
        P(("dom", "feat"), None),
        P(),
        P(),
        P("dom", None, None),
        P("dom", None, None),
        P(),
    )
    return jax.shard_map(
        on_device,
        mesh=mesh,
        in_specs=placed,
        out_specs=(P(("dom", "feat"), None), P("feat", None), P("feat", None)),
        check_vma=False,
    )
```

time: 230 us -> 145 us (0.63)
  waiting for transfers between devices: 123 us -> 75.5 us
  local copies, waits for them, and re-layouts: 44.5 us -> 9.9 us
  matrix products: 26.4 us -> 9.33 us
  between operations: 13.9 us -> 0.91 us
  starting transfers between devices: 16.8 us -> 28.7 us
  Pallas kernels: 0 us -> 11.3 us
  other arithmetic: 4.71 us -> 8.95 us
    all_gather x3 -> x0, waiting for transfers between devices: 89.7 us -> none  [the longest x1 77.6 us: on_device(): shard_rows = lax.all_gather(grad_linear, 'feat', axis=0, tiled=True)]
    ppermute x0 -> x8, waiting for transfers between devices: none -> 40.9 us  [the longest x4 29.8 us: gather_weights(): other = flip('feat', bit)(held)]
    gather x4 -> x0, local copies, waits for them, and re-layouts: 31.4 us -> none  [the longest x1 13.9 us: on_device(): tile_mats = tile_patterns[kinds]]
    all_to_all x3, waiting for transfers between devices: 10.1 us -> 34.6 us  [the longest x1 17.3 us: reduce_gradients(): lax.all_to_all(blocks, ('dom', 'feat'), 0, 0, axis_index_groups=groups, t...]
    psum x1 -> x0, waiting for transfers between devices: 21.8 us -> none  [on_device(): grad_self, grad_neighbour = lax.psum((self_local, neigh_local), 'dom')]
    dot_general x5 -> x4, matrix products: 26.4 us -> 9.33 us  [the longest x1 3.73 us: on_device(): lax.dot_general(own_mean, weights[:, 1].reshape(feat * depth, hid), first...]
    ppermute x0 -> x8, starting transfers between devices: none -> 13.1 us  [the longest x4 7.64 us: gather_weights(): other = flip('feat', bit)(held)]
    pallas_call x0 -> x2, Pallas kernels: none -> 11.3 us  [the longest x1 9.73 us: neighbour_means(): pl.pallas_call(functools.partial(mean_kernel, 4 if dest % 4 == 0 else 1),...]
  transfers between devices with their start and end apart: 7 -> 11, of which waited for: 4 -> 8; matrix products, arithmetic and copies ran while one was open for 26% -> 8% of each run, Pallas kernels for 0% -> 8%
where the time goes in v1:
time: 145 us
  waiting for transfers between devices  75.5 us (52%)
  starting transfers between devices  28.7 us (20%)
  Pallas kernels  11.3 us (8%)
  local copies, waits for them, and re-layouts  9.9 us (7%)
  matrix products  9.33 us (6%)
  other arithmetic  8.95 us (6%)
    ppermute x4, waiting for transfers between devices, gather_weights(): other = flip('feat', bit)(held)  29.8 us
    all_to_all x1, waiting for transfers between devices, reduce_gradients(): lax.all_to_all(blocks, ('dom', 'feat'), 0, 0, axis_index_groups=groups, t...  17.3 us
    all_to_all x1, waiting for transfers between devices, on_device(): lax.all_to_all(neighbour_means(tile_source[0].T, tile_kind[0].T, columns,...  17.3 us
    pallas_call x1, Pallas kernels, neighbour_means(): pl.pallas_call(functools.partial(mean_kernel, 4 if dest % 4 == 0 else 1),...  9.73 us
    ppermute x4, starting transfers between devices, gather_weights(): other = flip('feat', bit)(held)  7.64 us
    all_to_all x1, starting transfers between devices, reduce_gradients(): lax.all_to_all(blocks, ('dom', 'feat'), 0, 0, axis_index_groups=groups, t...  6.78 us
    ppermute x2, waiting for transfers between devices, halve(): flip(axis_name, bit)(sent.astype(bf16)).astype(f32)  5.8 us
    all_to_all x1, starting transfers between devices, on_device(): lax.all_to_all(neighbour_means(tile_source[0].T, tile_kind[0].T, columns,...  4.91 us
  transfers between devices with their start and end apart: 11, of which 8 were waited for; matrix products, arithmetic and copies ran while one was open for 8% of the time, Pallas kernels for 8%

profile of v1, /device:TPU:0, one launch (start us, length us, event | category | flops | bytes accessed | tf_op | source)
XLA Modules:
  0.0 144.6 jit_solution(12945614421969243183)
XLA Ops:
  0.6 0.0 copy-start
  0.6 0.9 pad_maximum_fusion.4
  1.5 4.1 %collective-permute-start = (bf16[2,64,512]{2,1,0:T(8,128)(2,1)S(1)}, bf16[2,64,512]{2,1,0:T(8,128)(2,1)S(1)}, u32[]{:S(2)}, u32[]{:S(2)}) collective-permute-start(bf16[2,64,512]{2,1,0:T(8,128)(2,1)S(1)} %pad_maximum_fusion.4), channel_id=1, source_target_pairs={{0,16},{2,18},{4,20},{6,22},{8,24},{10,26},{12,28},{14,30},{16,0},... | collective-permute-start | bytes 393224 | tf_op jit(solution)/shard_map/ppermute | solution.py:119
  5.6 2.3 %copy.49 = bf16[8,16,8,512]{3,2,0,1:T(8,128)(2,1)} copy(bf16[8,16,8,512]{3,2,1,0:T(8,128)(2,1)} %bitcast.80) | data formatting | bytes 2097152 | tf_op jit(solution)/shard_map/reshape | solution.py:183
  8.0 3.9 %all-to-all-start = ((bf16[16,64,512]{2,1,0:T(8,128)(2,1)}), bf16[16,64,512]{2,1,0:T(8,128)(2,1)S(1)}, u32[]{:S(2)}, u32[]{:S(2)}) async-start(bf16[16,64,512]{2,1,0:T(8,128)(2,1)} %bitcast.79), calls=%async_computation | async-start | bytes 2097152 | tf_op jit(solution)/shard_map/all_to_all | solution.py:182
  11.9 0.0 copy-start.1
  11.9 0.1 compare_bitcast_fusion
  12.1 2.0 %collective-permute-start.1 = (bf16[2,2,64,512]{3,2,1,0:T(8,128)(2,1)S(1)}, bf16[2,2,64,512]{3,2,1,0:T(8,128)(2,1)S(1)}, u32[]{:S(2)}, u32[]{:S(2)}) collective-permute-start(bf16[2,2,64,512]{3,2,1,0:T(8,128)(2,1)S(1)} %pad_maximum_fusion.3), channel_id=1, source_target_pairs={{0,8},{2,10},{4,12},{6,14},{8,0},{10,2},{12,4},{14,6},{16,24},{18,... | collective-permute-start | bytes 786440 | tf_op jit(solution)/shard_map/ppermute | solution.py:119
  14.1 23.4 %collective-permute-done.1 = bf16[2,2,64,512]{3,2,1,0:T(8,128)(2,1)S(1)} collective-permute-done((bf16[2,2,64,512]{3,2,1,0:T(8,128)(2,1)S(1)}, bf16[2,2,64,512]{3,2,1,0:T(8,128)(2,1)S(1)}, u32[]{:S(2)}, u32[]{:S(2)}) %collective-permute-start.1) | collective-permute-done | bytes 262176 | tf_op jit(solution)/shard_map/ppermute | solution.py:119
  37.5 0.0 copy-start.8
  37.5 0.1 pad_maximum_fusion.2
  37.6 1.5 %collective-permute-start.2 = (bf16[2,2,2,64,512]{4,3,2,1,0:T(8,128)(2,1)S(1)}, bf16[2,2,2,64,512]{4,3,2,1,0:T(8,128)(2,1)}, u32[]{:S(2)}, u32[]{:S(2)}) collective-permute-start(bf16[2,2,2,64,512]{4,3,2,1,0:T(8,128)(2,1)S(1)} %pad_maximum_fusion.2), channel_id=1, source_target_pairs={{0,4},{2,6},{4,0},{6,2},{8,12},{10,14},{12,8},{14,10},{16,20},{18,... | collective-permute-start | bytes 1572872 | tf_op jit(solution)/shard_map/ppermute | solution.py:119
  39.2 1.6 %pick_rows.1 = bf16[64,512]{1,0:T(8,128)(2,1)S(1)} custom-call(bf16[64,8192]{1,0:T(8,128)(2,1)S(1)} %bitcast.81, s32[1,512]{1,0:T(1,128)S(1)} %broadcast_select_fusion.4.rows_ref), custom_call_target="tpu_custom_call" | custom-call | flops 536870912 | bytes 1048576 | tf_op jit(solution)/shard_map/pick_rows/pallas_call | solution.py:51
  40.8 1.6 %collective-permute-start.4 = (bf16[64,256]{1,0:T(8,128)(2,1)S(1)}, bf16[64,256]{1,0:T(8,128)(2,1)S(1)}, u32[]{:S(2)}, u32[]{:S(2)}) collective-permute-start(bf16[64,256]{1,0:T(8,128)(2,1)S(1)} %constant_dynamic-slice_fusion), channel_id=1, source_target_pairs={{0,1},{1,0},{2,3},{3,2},{4,5},{5,4},{6,7},{7,6},{8,9},{9,8},{10,11... | collective-permute-start | bytes 98312 | tf_op jit(solution)/shard_map/ppermute | solution.py:193
  42.3 2.4 %collective-permute-done.4 = bf16[64,256]{1,0:T(8,128)(2,1)S(1)} collective-permute-done((bf16[64,256]{1,0:T(8,128)(2,1)S(1)}, bf16[64,256]{1,0:T(8,128)(2,1)S(1)}, u32[]{:S(2)}, u32[]{:S(2)}) %collective-permute-start.4) | collective-permute-done | bytes 32800 | tf_op jit(solution)/shard_map/ppermute | solution.py:193
  44.8 0.0 copy-start.2
  44.8 0.0 copy-start.3
  44.8 6.4 %collective-permute-done.2 = bf16[2,2,2,64,512]{4,3,2,1,0:T(8,128)(2,1)} collective-permute-done((bf16[2,2,2,64,512]{4,3,2,1,0:T(8,128)(2,1)S(1)}, bf16[2,2,2,64,512]{4,3,2,1,0:T(8,128)(2,1)}, u32[]{:S(2)}, u32[]{:S(2)}) %collective-permute-start.2) | collective-permute-done | bytes 524320 | tf_op jit(solution)/shard_map/ppermute | solution.py:119
  51.2 1.2 select_bitcast_fusion.3
  52.5 1.1 pad_maximum_fusion.1
  53.6 9.7 %neighbour_means.1 = bf16[16,64,512]{2,1,0:T(8,128)(2,1)} custom-call(s32[8,64]{1,0:T(8,128)S(1)} %bitcast.83, s32[8,64]{1,0:T(8,128)S(1)} %bitcast.84, bf16[64,8192]{1,0:T(8,128)(2,1)S(1)} %bitcast.82, bf16[64,512]{1,0:T(8,128)(2,1)S(1)} %pad_maximum_fusion.5.halo_ref, bf16[64,128,128]{2,1,0:T(8,128)(2,1)S(1)} %copy-done.2), custom_call_target="tpu_custom_call" | custom-call | flops 8589934592 | bytes 4194304 | tf_op jit(solution)/shard_map/neighbour_means/pallas_call | solution.py:100
  63.3 4.9 %all-to-all-start.1 = ((bf16[16,64,512]{2,1,0:T(8,128)(2,1)}), bf16[16,64,512]{2,1,0:T(8,128)(2,1)S(1)}, u32[]{:S(2)}, u32[]{:S(2)}) async-start(bf16[16,64,512]{2,1,0:T(8,128)(2,1)} %neighbour_means.1), calls=%async_computation.1 | async-start | bytes 2097152 | tf_op jit(solution)/shard_map/all_to_all | solution.py:200
  68.2 2.0 %copy.33 = bf16[512,512]{0,1:T(8,128)(2,1)} copy(bf16[512,512]{1,0:T(8,128)(2,1)} %param.12) | data formatting | bytes 1048576 | tf_op args[3]
  70.3 1.5 %select_bitcast_fusion.1 = (bf16[2,2,2,1,2,64,512]{6,5,4,3,2,1,0:T(8,128)(2,1)S(1)}, bf16[2,2,2,1,2,64,512]{6,5,4,3,2,1,0:T(8,128)(2,1)S(1)}) fusion(bf16[2,2,2,2,64,512]{5,4,3,2,1,0:T(8,128)(2,1)} %collective-permute-done.3, pred[]{:T(512)S(6)} %ne.22, bf16[2,2,1,2,64,512]{5,4,3,2,1,0:T(8,128)(2,1)S(1)} %get-tuple-element.19, ...), kind=kLoop, calls=%fused_computation.27 | loop fusion | flops 1572864 | bytes 4194305 | tf_op jit(solution)/shard_map/stack | solution.py:121
  71.8 0.2 pad_maximum_fusion
  72.0 0.2 fusion.14
  72.2 1.7 %convolution_bitcast_fusion.1 = f32[512,512]{0,1:T(8,128)} fusion(bf16[1024,512]{1,0:T(8,128)(2,1)S(1)} %bitcast.95, bf16[1024,512]{1,0:T(8,128)(2,1)S(1)} %bitcast.90), kind=kOutput, calls=%fused_computation.14 | convolution fusion | flops 536870912 | bytes 3145728 | tf_op jit(solution)/shard_map/dot_general | solution.py:210
  73.9 17.3 %all-to-all-done.1 = bf16[16,64,512]{2,1,0:T(8,128)(2,1)S(1)} async-done(((bf16[16,64,512]{2,1,0:T(8,128)(2,1)}), bf16[16,64,512]{2,1,0:T(8,128)(2,1)S(1)}, u32[]{:S(2)}, u32[]{:S(2)}) %all-to-all-start.1) | async-done | bytes 1048608 | tf_op jit(solution)/shard_map/all_to_all | solution.py:200
  91.2 3.7 %fusion.9 = (bf16[512,512]{0,1:T(8,128)(2,1)S(1)}, bf16[512,512]{0,1:T(8,128)(2,1)}) fusion(bf16[512,512]{0,1:T(8,128)(2,1)} %copy.33, f32[512,512]{0,1:T(8,128)} %convolution_bitcast_fusion.1, bf16[1024,512]{1,0:T(8,128)(2,1)S(1)} %bitcast.92, bf16[1024,512]{1,0:T(8,128)(2,1)S(1)} %bitcast.94), kind=kOutput, calls=%fused_computation.20 | convolution fusion | flops 540540928 | bytes 4718592 | tf_op jit(solution)/shard_map/dot_general | solution.py:215
  94.9 0.8 copy-done.9
  95.7 2.1 %convolution_bitcast_fusion = f32[1024,512]{0,1:T(8,128)} fusion(bf16[512,512]{0,1:T(8,128)(2,1)S(1)} %get-tuple-element.16, bf16[1024,512]{1,0:T(8,128)(2,1)S(1)} %bitcast.91), kind=kOutput, calls=%fused_computation.11 | convolution fusion | flops 536870912 | bytes 3670016 | tf_op jit(solution)/shard_map/dot_general | solution.py:224
  97.8 2.0 %copy.34 = f32[1024,512]{1,0:T(8,128)S(1)} copy(f32[1024,512]{0,1:T(8,128)} %convolution_bitcast_fusion) | data formatting | bytes 4194304 | tf_op jit(solution)/shard_map/dot_general | solution.py:224
  99.8 1.8 %fusion.10 = f32[16,64,512]{2,1,0:T(8,128)S(1)} fusion(bf16[16,64,512]{2,1,0:T(8,128)(2,1)S(1)} %copy-done.7, bf16[512,512]{0,1:T(8,128)(2,1)} %copy-done.9), kind=kOutput, calls=%fused_computation.29 | convolution fusion | flops 536870912 | bytes 3670016 | tf_op jit(solution)/shard_map/dot_general | solution.py:225
  101.6 1.3 copy_bitcast_fusion
  102.9 0.3 copy-done.5
  103.2 0.6 collective-permute-start.5
  103.9 2.5 %collective-permute-done.5 = bf16[8,2,64,512]{3,2,1,0:T(8,128)(2,1)S(1)} collective-permute-done((bf16[8,2,64,512]{3,2,1,0:T(8,128)(2,1)}, bf16[8,2,64,512]{3,2,1,0:T(8,128)(2,1)S(1)}, u32[]{:S(2)}, u32[]{:S(2)}) %collective-permute-start.5) | collective-permute-done | bytes 1048608 | tf_op jit(solution)/shard_map/ppermute | solution.py:131
  106.3 1.6 %fusion.3 = bf16[8,2,64,512]{3,2,1,0:T(8,128)(2,1)S(1)} fusion(bf16[8,2,64,512]{3,2,1,0:T(8,128)(2,1)S(1)} %collective-permute-done.5, s32[]{:T(128)S(6)} %select_n.135, f32[8,2,1,64,512]{4,3,1,0,2:T(8,128)S(1)} %bitcast.86, f32[8,2,1,64,512]{4,3,1,0,2:T(8,128)} %bitcast.88), kind=kLoop, calls=%fused_computation.9 | loop fusion | flops 2097152 | bytes 6291460 | tf_op jit(solution)/shard_map/convert_element_type | solution.py:141
  108.0 1.1 copy.38
  109.1 6.8 %all-to-all-start.2 = ((bf16[8,2,64,512]{3,2,1,0:T(8,128)(2,1)}), bf16[8,2,64,512]{3,2,1,0:T(8,128)(2,1)S(1)}, u32[]{:S(2)}, u32[]{:S(2)}) async-start(bf16[8,2,64,512]{3,2,1,0:T(8,128)(2,1)} %bitcast.34), calls=%async_computation.2 | async-start | bytes 2097152 | tf_op jit(solution)/shard_map/all_to_all | solution.py:148
  115.8 17.3 %all-to-all-done.2 = bf16[8,2,64,512]{3,2,1,0:T(8,128)(2,1)S(1)} async-done(((bf16[8,2,64,512]{3,2,1,0:T(8,128)(2,1)}), bf16[8,2,64,512]{3,2,1,0:T(8,128)(2,1)S(1)}, u32[]{:S(2)}, u32[]{:S(2)}) %all-to-all-start.2) | async-done | bytes 1048608 | tf_op jit(solution)/shard_map/all_to_all | solution.py:148
  133.2 0.2 convert_reduce_fusion
  133.3 2.1 %collective-permute-start.6 = (bf16[1,64,512]{2,1,0:T(8,128)(2,1)S(1)}, bf16[1,64,512]{2,1,0:T(8,128)(2,1)S(1)}, u32[]{:S(2)}, u32[]{:S(2)}) collective-permute-start(bf16[1,64,512]{2,1,0:T(8,128)(2,1)S(1)} %dynamic-slice_convert_fusion), channel_id=1, source_target_pairs={{0,16},{2,18},{4,20},{6,22},{8,24},{10,26},{12,28},{14,30},{16,0},... | collective-permute-start | bytes 196616 | tf_op jit(solution)/shard_map/ppermute | solution.py:131
  135.5 3.3 %collective-permute-done.6 = bf16[1,64,512]{2,1,0:T(8,128)(2,1)S(1)} collective-permute-done((bf16[1,64,512]{2,1,0:T(8,128)(2,1)S(1)}, bf16[1,64,512]{2,1,0:T(8,128)(2,1)S(1)}, u32[]{:S(2)}, u32[]{:S(2)}) %collective-permute-start.6) | collective-permute-done | bytes 65568 | tf_op jit(solution)/shard_map/ppermute | solution.py:131
  138.8 1.1 collective-permute-start.7
  139.9 1.0 copy.39
  140.9 2.9 %collective-permute-done.7 = f32[64,512]{1,0:T(8,128)S(1)} collective-permute-done((f32[64,512]{1,0:T(8,128)S(1)}, f32[64,512]{1,0:T(8,128)S(1)}, u32[]{:S(2)}, u32[]{:S(2)}) %collective-permute-start.7) | collective-permute-done | bytes 131104 | tf_op jit(solution)/shard_map/ppermute | solution.py:159
  143.8 0.7 broadcast_select_fusion
  (38 shorter events, 0.2 us)
Async XLA Ops:
  0.6 13.4 %copy-start = (s32[2,2,256]{2,1,0:T(2,128)S(1)}, s32[2,2,256]{2,1,0:T(2,128)}, u32[]{:S(2)}) copy-start(s32[2,2,256]{2,1,0:T(2,128)} %param.13) | copy-start | bytes 12292
  1.5 10.5 %collective-permute-start = (bf16[2,64,512]{2,1,0:T(8,128)(2,1)S(1)}, bf16[2,64,512]{2,1,0:T(8,128)(2,1)S(1)}, u32[]{:S(2)}, u32[]{:S(2)}) collective-permute-start(bf16[2,64,512]{2,1,0:T(8,128)(2,1)S(1)} %pad_maximum_fusion.4), channel_id=1, source_target_pairs={{0,16},{2,18},{4,20},{6,22},{8,24},{10,26},{12,28},{14,30},{16,0},... | collective-permute-start | bytes 393224 | tf_op jit(solution)/shard_map/ppermute | solution.py:119
  5.6 6.3 %copy-start.13 = (s32[2,2]{1,0:T(2,128)S(1)}, s32[2,2]{1,0:T(2,128)}, u32[]{:S(2)}) copy-start(s32[2,2]{1,0:T(2,128)} %param.14) | copy-start | bytes 52
  5.6 6.4 %copy-start.11 = (bf16[64,512]{1,0:T(8,128)(2,1)S(1)}, bf16[64,512]{1,0:T(8,128)(2,1)}, u32[]{:S(2)}) copy-start(bf16[64,512]{1,0:T(8,128)(2,1)} %param.11) | copy-start | bytes 196612
  5.6 6.4 %copy-start.12 = (bf16[64,512]{1,0:T(8,128)(2,1)S(1)}, bf16[64,512]{1,0:T(8,128)(2,1)}, u32[]{:S(2)}) copy-start(bf16[64,512]{1,0:T(8,128)(2,1)} %param.10) | copy-start | bytes 196612
  8.0 55.3 %all-to-all-start = ((bf16[16,64,512]{2,1,0:T(8,128)(2,1)}), bf16[16,64,512]{2,1,0:T(8,128)(2,1)S(1)}, u32[]{:S(2)}, u32[]{:S(2)}) async-start(bf16[16,64,512]{2,1,0:T(8,128)(2,1)} %bitcast.79), calls=%async_computation | async-start | bytes 2097152 | tf_op jit(solution)/shard_map/all_to_all | solution.py:182
  11.9 27.3 %copy-start.1 = (bf16[8192,64]{0,1:T(8,128)(2,1)S(1)}, bf16[8192,64]{0,1:T(8,128)(2,1)}, u32[]{:S(2)}) copy-start(bf16[8192,64]{0,1:T(8,128)(2,1)} %param.9) | copy-start | bytes 3145732
  12.1 25.4 %collective-permute-start.1 = (bf16[2,2,64,512]{3,2,1,0:T(8,128)(2,1)S(1)}, bf16[2,2,64,512]{3,2,1,0:T(8,128)(2,1)S(1)}, u32[]{:S(2)}, u32[]{:S(2)}) collective-permute-start(bf16[2,2,64,512]{3,2,1,0:T(8,128)(2,1)S(1)} %pad_maximum_fusion.3), channel_id=1, source_target_pairs={{0,8},{2,10},{4,12},{6,14},{8,0},{10,2},{12,4},{14,6},{16,24},{18,... | collective-permute-start | bytes 786440 | tf_op jit(solution)/shard_map/ppermute | solution.py:119
  37.5 3.2 %copy-start.8 = (bf16[2,1,2,64,512]{4,3,2,1,0:T(8,128)(2,1)}, bf16[2,1,2,64,512]{4,3,2,1,0:T(8,128)(2,1)S(1)}, u32[]{:S(2)}) copy-start(bf16[2,1,2,64,512]{4,3,2,1,0:T(8,128)(2,1)S(1)} %get-tuple-element.21) | copy-start | bytes 786436
  37.6 13.6 %collective-permute-start.2 = (bf16[2,2,2,64,512]{4,3,2,1,0:T(8,128)(2,1)S(1)}, bf16[2,2,2,64,512]{4,3,2,1,0:T(8,128)(2,1)}, u32[]{:S(2)}, u32[]{:S(2)}) collective-permute-start(bf16[2,2,2,64,512]{4,3,2,1,0:T(8,128)(2,1)S(1)} %pad_maximum_fusion.2), channel_id=1, source_target_pairs={{0,4},{2,6},{4,0},{6,2},{8,12},{10,14},{12,8},{14,10},{16,20},{18,... | collective-permute-start | bytes 1572872 | tf_op jit(solution)/shard_map/ppermute | solution.py:119
  40.8 4.0 %collective-permute-start.4 = (bf16[64,256]{1,0:T(8,128)(2,1)S(1)}, bf16[64,256]{1,0:T(8,128)(2,1)S(1)}, u32[]{:S(2)}, u32[]{:S(2)}) collective-permute-start(bf16[64,256]{1,0:T(8,128)(2,1)S(1)} %constant_dynamic-slice_fusion), channel_id=1, source_target_pairs={{0,1},{1,0},{2,3},{3,2},{4,5},{5,4},{6,7},{7,6},{8,9},{9,8},{10,11... | collective-permute-start | bytes 98312 | tf_op jit(solution)/shard_map/ppermute | solution.py:193
  44.8 8.8 %copy-start.2 = (bf16[64,128,128]{2,1,0:T(8,128)(2,1)S(1)}, bf16[64,128,128]{2,1,0:T(8,128)(2,1)}, u32[]{:S(2)}) copy-start(bf16[64,128,128]{2,1,0:T(8,128)(2,1)} %pattern_ref.1) | copy-start | bytes 6291460
  44.8 8.8 %copy-start.3 = (s32[1,64,8]{1,2,0:T(8,128)S(1)}, s32[1,64,8]{1,2,0:T(8,128)}, u32[]{:S(2)}) copy-start(s32[1,64,8]{1,2,0:T(8,128)} %param.15) | copy-start | bytes 6148
  44.8 8.7 %copy-start.4 = (s32[1,64,8]{1,2,0:T(8,128)S(1)}, s32[1,64,8]{1,2,0:T(8,128)}, u32[]{:S(2)}) copy-start(s32[1,64,8]{1,2,0:T(8,128)} %param.16) | copy-start | bytes 6148
  53.5 16.7 %collective-permute-start.3 = (bf16[2,2,2,2,64,512]{5,4,3,2,1,0:T(8,128)(2,1)}, bf16[2,2,2,2,64,512]{5,4,3,2,1,0:T(8,128)(2,1)}, u32[]{:S(2)}, u32[]{:S(2)}) collective-permute-start(bf16[2,2,2,2,64,512]{5,4,3,2,1,0:T(8,128)(2,1)} %pad_maximum_fusion.1), channel_id=1, source_target_pairs={{0,2},{2,0},{4,6},{6,4},{8,10},{10,8},{12,14},{14,12},{16,18},{18,... | collective-permute-start | bytes 3145736 | tf_op jit(solution)/shard_map/ppermute | solution.py:119
  63.3 27.9 %all-to-all-start.1 = ((bf16[16,64,512]{2,1,0:T(8,128)(2,1)}), bf16[16,64,512]{2,1,0:T(8,128)(2,1)S(1)}, u32[]{:S(2)}, u32[]{:S(2)}) async-start(bf16[16,64,512]{2,1,0:T(8,128)(2,1)} %neighbour_means.1), calls=%async_computation.1 | async-start | bytes 2097152 | tf_op jit(solution)/shard_map/all_to_all | solution.py:200
  91.2 3.7 %copy-start.6 = (bf16[16,64,512]{2,1,0:T(8,128)(2,1)}, bf16[16,64,512]{2,1,0:T(8,128)(2,1)S(1)}, u32[]{:S(2)}) copy-start(bf16[16,64,512]{2,1,0:T(8,128)(2,1)S(1)} %all-to-all-done.1) | copy-start | bytes 3145732
  94.9 0.8 copy-start.9
  97.8 2.0 %copy-start.7 = (bf16[16,64,512]{2,1,0:T(8,128)(2,1)S(1)}, bf16[16,64,512]{2,1,0:T(8,128)(2,1)}, u32[]{:S(2)}) copy-start(bf16[16,64,512]{2,1,0:T(8,128)(2,1)} %copy-done.6) | copy-start | bytes 3145732
  101.6 1.6 %copy-start.5 = (f32[16,64,512]{2,1,0:T(8,128)}, f32[16,64,512]{2,1,0:T(8,128)S(1)}, u32[]{:S(2)}) copy-start(f32[16,64,512]{2,1,0:T(8,128)S(1)} %fusion.10) | copy-start | bytes 6291460
  103.2 3.1 %collective-permute-start.5 = (bf16[8,2,64,512]{3,2,1,0:T(8,128)(2,1)}, bf16[8,2,64,512]{3,2,1,0:T(8,128)(2,1)S(1)}, u32[]{:S(2)}, u32[]{:S(2)}) collective-permute-start(bf16[8,2,64,512]{3,2,1,0:T(8,128)(2,1)} %copy_bitcast_fusion), channel_id=1, source_target_pairs={{0,2},{2,0},{4,6},{6,4},{8,10},{10,8},{12,14},{14,12},{16,18},{18,... | collective-permute-start | bytes 3145736 | tf_op jit(solution)/shard_map/ppermute | solution.py:131
  109.1 30.9 %copy-start.10 = (bf16[512,512]{0,1:T(8,128)(2,1)S(1)}, bf16[512,512]{0,1:T(8,128)(2,1)}, u32[]{:S(2)}) copy-start(bf16[512,512]{0,1:T(8,128)(2,1)} %get-tuple-element.17) | copy-start | bytes 1572868
  109.1 24.1 %all-to-all-start.2 = ((bf16[8,2,64,512]{3,2,1,0:T(8,128)(2,1)}), bf16[8,2,64,512]{3,2,1,0:T(8,128)(2,1)S(1)}, u32[]{:S(2)}, u32[]{:S(2)}) async-start(bf16[8,2,64,512]{3,2,1,0:T(8,128)(2,1)} %bitcast.34), calls=%async_computation.2 | async-start | bytes 2097152 | tf_op jit(solution)/shard_map/all_to_all | solution.py:148
  133.3 5.4 %collective-permute-start.6 = (bf16[1,64,512]{2,1,0:T(8,128)(2,1)S(1)}, bf16[1,64,512]{2,1,0:T(8,128)(2,1)S(1)}, u32[]{:S(2)}, u32[]{:S(2)}) collective-permute-start(bf16[1,64,512]{2,1,0:T(8,128)(2,1)S(1)} %dynamic-slice_convert_fusion), channel_id=1, source_target_pairs={{0,16},{2,18},{4,20},{6,22},{8,24},{10,26},{12,28},{14,30},{16,0},... | collective-permute-start | bytes 196616 | tf_op jit(solution)/shard_map/ppermute | solution.py:131
  138.8 5.0 %collective-permute-start.7 = (f32[64,512]{1,0:T(8,128)S(1)}, f32[64,512]{1,0:T(8,128)S(1)}, u32[]{:S(2)}, u32[]{:S(2)}) collective-permute-start(f32[64,512]{1,0:T(8,128)S(1)} %add_bitcast_fusion), channel_id=1, source_target_pairs={{0,1},{1,0},{2,3},{3,2},{4,5},{5,4},{6,7},{7,6},{8,9},{9,8},{10,11... | collective-permute-start | bytes 393224 | tf_op jit(solution)/shard_map/ppermute | solution.py:159

commit v2 on v1

v2 whole, which is shorter than its diff:
```python
import functools

import jax
import jax.numpy as jnp
from jax import lax
from jax.experimental import pallas as pl
from jax.experimental.pallas import tpu as pltpu
from jax.sharding import PartitionSpec as P

inv_root_two = 0.7071067811865476
inv_root_two_pi = 0.3989422804014327
bf16 = jnp.bfloat16
f32 = jnp.float32
vmem_bytes = 48 * 2**20
whole_vmem = pl.BlockSpec(memory_space=pltpu.VMEM)
whole_smem = pl.BlockSpec(memory_space=pltpu.SMEM)
last_with_last = (((1,), (1,)), ((), ()))
first_with_first = (((0,), (0,)), ((), ()))


def gelu_pair(linear):
    normal_cdf = 0.5 * (1.0 + lax.erf(linear * inv_root_two))
    density = jnp.exp(-0.5 * linear * linear) * inv_root_two_pi
    return (linear * normal_cdf, normal_cdf + linear * density)


def flip(axis, bit):
    size = lax.axis_size(axis)
    return functools.partial(
        lax.ppermute, axis_name=axis, perm=[(i, i ^ bit) for i in range(size)]
    )


def bits_of(size):
    return [1 << i for i in range(size.bit_length() - 1)]


def local_call(kernel, name, outs, operands, scalars=0, scratch=(), flops=0):
    moved = sum(2 * x.size for x in operands)
    return pl.pallas_call(
        kernel,
        out_shape=outs,
        in_specs=[whole_smem] * scalars + [whole_vmem] * (len(operands) - scalars),
        out_specs=[whole_vmem] * len(outs),
        scratch_shapes=list(scratch),
        cost_estimate=pl.CostEstimate(flops=flops, bytes_accessed=moved, transcendentals=0),
        compiler_params=pltpu.CompilerParams(vmem_limit_bytes=vmem_bytes),
        name=name,
    )(*operands)


def pick_kernel(step, me_ref, columns_ref, rows_ref, picked_ref, *cut_refs):
    total = jnp.zeros(picked_ref.shape, f32)
    for at in range(0, columns_ref.shape[1], step):
        ids = lax.broadcasted_iota(jnp.int32, (step, rows_ref.shape[1]), 0) + at
        one_hot = jnp.where(ids == rows_ref[...], 1.0, 0.0).astype(bf16)
        total = total + jnp.dot(
            columns_ref[:, at : at + step], one_hot, preferred_element_type=f32
        )
    picked_ref[...] = total.astype(bf16)
    for i, cut_ref in enumerate(cut_refs):
        width = cut_ref.shape[2]
        at = pl.multiple_of((me_ref[0] ^ (i + 1)) * width, width)
        cut_ref[0] = columns_ref[:, pl.ds(at, width)]


def pick_rows(quarter, columns, rows, quarters):
    depth, width = columns.shape[0], rows.shape[1]
    cut = jax.ShapeDtypeStruct((1, depth, columns.shape[1] // quarters), bf16)
    return local_call(
        functools.partial(pick_kernel, min(256, columns.shape[1])),
        "pick_rows",
        [jax.ShapeDtypeStruct((depth, width), bf16)] + [cut] * (quarters - 1),
        (quarter, columns, rows),
        scalars=1,
    )


def mean_kernel(unroll, source_ref, kind_ref, local_ref, halo_ref, pattern_ref, mean_ref, tiles):
    depth = local_ref.shape[0]
    side = pattern_ref.shape[1]
    local_tiles, halo_tiles = local_ref.shape[1] // side, halo_ref.shape[1] // side
    for i in range(local_tiles):
        tiles[i, 0:depth, :] = local_ref[:, i * side : (i + 1) * side]
    for i in range(halo_tiles):
        tiles[local_tiles + i, 0:depth, :] = halo_ref[:, i * side : (i + 1) * side]
    tiles[:, depth:, :] = jnp.ones((tiles.shape[0], tiles.shape[1] - depth, side), bf16)
    per_block = mean_ref.shape[2] // side

    def one(t):
        rows = [tiles[source_ref[k, t]] for k in range(source_ref.shape[0])]
        weights = [pattern_ref[kind_ref[k, t]] for k in range(source_ref.shape[0])]
        summed = lax.dot_general(
            jnp.concatenate(rows, 1),
            jnp.concatenate(weights, 1),
            last_with_last,
            preferred_element_type=f32,
        )
        mean = (summed[0:depth] / summed[depth : depth + 1]).astype(bf16)
        at = lax.rem(t, per_block) * side
        mean_ref[lax.div(t, per_block), :, pl.ds(pl.multiple_of(at, side), side)] = mean

    @pl.loop(0, source_ref.shape[1] // unroll)
    def _(step):
        for u in range(unroll):
            one(step * unroll + u)


def neighbour_means(source, kind, local, halo, patterns, blocks):
    depth, count = local.shape
    side = patterns.shape[1]
    tile_count = (count + halo.shape[1]) // side
    return local_call(
        functools.partial(mean_kernel, 4 if source.shape[1] % 4 == 0 else 1),
        "neighbour_means",
        [jax.ShapeDtypeStruct((blocks, depth, count // blocks), bf16)],
        (source, kind, local, halo, patterns),
        scalars=2,
        scratch=[pltpu.VMEM((tile_count, depth + 16, side), bf16)],
        flops=2 * source.size * side * side * depth,
    )[0]


def cut_kernel(bit_ref, *refs):
    sent_ref, kept_ref = refs[-2:]
    half = sent_ref.shape[2]
    mine = pl.multiple_of(bit_ref[0] * half, half)
    theirs = pl.multiple_of((1 - bit_ref[0]) * half, half)
    at = 0
    for ref in refs[:-2]:
        for i in range(ref.shape[0]):
            sent_ref[at] = ref[i, :, pl.ds(theirs, half)]
            kept_ref[at] = ref[i, :, pl.ds(mine, half)]
            at += 1


def cut_rows(bit, parts):
    count = sum(p.shape[0] for p in parts)
    out = jax.ShapeDtypeStruct((count, parts[0].shape[1], parts[0].shape[2] // 2), bf16)
    return local_call(cut_kernel, "cut_rows", [out, out], (bit, *parts), scalars=1)


def masks_of(first, later):
    masks = list(first)
    for bit in later:
        masks = masks + [m ^ bit for m in masks]
    return masks


def own_linear_kernel(row_masks, weight_masks, me_ref, *refs):
    kept_ref, got_ref, held_ref, came_ref, features_ref, weights_ref, linear_ref, own_ref = refs
    half = kept_ref.shape[0]
    for i, mask in enumerate(row_masks):
        part = kept_ref[i] if i < half else got_ref[i - half]
        features_ref[me_ref[0] ^ mask] = part
    half = held_ref.shape[0]
    for i, mask in enumerate(weight_masks):
        part = held_ref if i < half else came_ref
        own_ref[me_ref[0] ^ mask] = part[i % half, 0]
        weights_ref[me_ref[0] ^ mask] = part[i % half, 1]
    linear_ref[...] = lax.dot_general(
        features_ref[...].reshape(-1, features_ref.shape[2]),
        own_ref[...].reshape(-1, own_ref.shape[2]),
        first_with_first,
        preferred_element_type=f32,
    )


def forward_kernel(
    core_ref, linear_ref, weight_ref, mean_ref, features_ref, cot_ref, hidden_ref, grad_ref, sent_ref
):
    rows, hid = linear_ref.shape
    step = min(256, rows)
    weight = weight_ref[...].reshape(-1, hid)
    for at in range(0, rows, step):
        mean = mean_ref[:, :, :, at : at + step].reshape(-1, step)
        linear = linear_ref[at : at + step] + lax.dot_general(
            mean, weight, first_with_first, preferred_element_type=f32
        )
        value, slope = gelu_pair(linear)
        hidden_ref[at : at + step] = value.astype(bf16)
        grad_ref[at : at + step] = (cot_ref[at : at + step].astype(f32) * slope).astype(bf16)
    partial_gradients(1 - core_ref[0], features_ref, mean_ref, grad_ref, sent_ref)


def partial_gradients(core, features_ref, mean_ref, grad_ref, out_ref):
    for i, ref in enumerate((features_ref, mean_ref)):
        part = jnp.dot(
            ref[:, core].reshape(-1, ref.shape[3]), grad_ref[...], preferred_element_type=f32
        )
        out_ref[:, i] = part.astype(out_ref.dtype).reshape(out_ref[:, i].shape)


def kept_kernel(core_ref, features_ref, mean_ref, grad_ref, kept_ref):
    partial_gradients(core_ref[0], features_ref, mean_ref, grad_ref, kept_ref)


def first_kernel(bits_ref, kept_ref, got_ref, own_ref, own_sent_ref, neigh_ref, neigh_sent_ref):
    for far in range(kept_ref.shape[0] // 4):
        for a in range(2):
            for b in range(2):
                at = far * 4 + (bits_ref[1] ^ a) * 2 + (bits_ref[0] ^ b)
                own = kept_ref[at, 0] + got_ref[at, 0].astype(f32)
                neigh = kept_ref[at, 1] + got_ref[at, 1].astype(f32)
                if b == 0:
                    own_ref[far, a] = own
                else:
                    own_sent_ref[far, a] = own.astype(bf16)
                if a == 0:
                    neigh_ref[far, b] = neigh
                else:
                    neigh_sent_ref[far, b] = neigh.astype(bf16)


def second_kernel(kept_ref, got_ref, out_ref, sent_ref):
    for far in range(kept_ref.shape[0]):
        total = kept_ref[far] + got_ref[far].astype(f32)
        out_ref[far] = total[0]
        sent_ref[far] = total[1].astype(bf16)


def third_kernel(bit_ref, own_ref, own_got_ref, neigh_ref, neigh_got_ref, out_ref, sent_ref):
    half = out_ref.shape[0]
    for i in range(half):
        for side, ref in ((bit_ref[0], out_ref), (1 - bit_ref[0], sent_ref)):
            at = side * half + i
            ref[i, 0] = (own_ref[at] + own_got_ref[at].astype(f32)).astype(ref.dtype)
            ref[i, 1] = (neigh_ref[at] + neigh_got_ref[at].astype(f32)).astype(ref.dtype)


def halving_kernel(bit_ref, kept_ref, got_ref, out_ref, sent_ref):
    half = out_ref.shape[0]
    for i in range(half):
        for side, ref in ((bit_ref[0], out_ref), (1 - bit_ref[0], sent_ref)):
            at = side * half + i
            ref[i] = (kept_ref[at] + got_ref[at].astype(f32)).astype(ref.dtype)


def round_sum_kernel(kept_ref, got_ref, out_ref):
    out_ref[...] = (kept_ref[...].astype(f32) + got_ref[...].astype(f32)).astype(out_ref.dtype)


def last_sum_kernel(kept_ref, got_ref, own_ref, neigh_ref):
    total = kept_ref[...].astype(f32) + got_ref[...].astype(f32)
    own_ref[...] = total[0, 0]
    neigh_ref[...] = total[0, 1]


def bit_of(axis, bit):
    return ((lax.axis_index(axis) // bit) % 2).astype(jnp.int32).reshape(1)


def sum_gradients(kept, got):
    feat, dom = lax.axis_size("feat"), lax.axis_size("dom")
    depth, hid = kept.shape[2:]
    far = feat // 8

    def pair(*lead):
        shape = (*lead, depth, hid)
        return [jax.ShapeDtypeStruct(shape, f32), jax.ShapeDtypeStruct(shape, bf16)]

    bits = jnp.concatenate([bit_of("feat", 2), bit_of("feat", 4)])
    own, own_sent, neigh, neigh_sent = local_call(
        first_kernel, "first_sum", pair(far, 2) + pair(far, 2), (bits, kept, got), scalars=1
    )
    own_got, neigh_got = flip("feat", 2)(own_sent), flip("feat", 4)(neigh_sent)
    own, own_sent = local_call(second_kernel, "own_sum", pair(far), (own, own_got))
    own_got = flip("feat", 4)(own_sent)
    neigh, neigh_sent = local_call(second_kernel, "neigh_sum", pair(far), (neigh, neigh_got))
    neigh_got = flip("feat", 2)(neigh_sent)
    half = far // 2
    kept, sent = local_call(
        third_kernel,
        "third_sum",
        pair(half, 2),
        (bit_of("feat", half * 8), own, own_got, neigh, neigh_got),
        scalars=1,
    )
    got = flip("feat", half * 8)(sent)
    while half > 1:
        half //= 2
        kept, sent = local_call(
            halving_kernel, "halving", pair(half, 2), (bit_of("feat", half * 8), kept, got), scalars=1
        )
        got = flip("feat", half * 8)(sent)
    rounded = jax.ShapeDtypeStruct(kept.shape, bf16)
    for bit in bits_of(dom):
        (kept,) = local_call(round_sum_kernel, "rounded_sum", [rounded], (kept, got))
        got = flip("dom", bit)(kept)
    out = jax.ShapeDtypeStruct((depth, hid), f32)
    return local_call(last_sum_kernel, "last_sum", [out, out], (kept, got))


def on_device(
    features,
    self_weight,
    neighbour_weight,
    cotangent,
    send_rows,
    send_count,
    tile_source,
    tile_kind,
    tile_patterns,
):
    feat, dom = lax.axis_size("feat"), lax.axis_size("dom")
    my_part = lax.axis_index("dom")
    me = lax.axis_index("feat").astype(jnp.int32).reshape(1)
    count, depth = features.shape
    rows = count // feat
    hid = self_weight.shape[1]
    slots = send_rows.shape[2]
    columns = features.T
    quarters, below = 4, feat // 4
    outgoing = lax.dynamic_index_in_dim(send_rows, my_part, 0, keepdims=False)
    live = lax.dynamic_index_in_dim(send_count, my_part, 0, keepdims=False)
    slot_ids = jnp.arange(slots, dtype=jnp.int32)
    outgoing = jnp.where(slot_ids[None, :] < live[:, None], outgoing, -1)
    picked, *cuts = pick_rows(
        me // below, columns, outgoing.reshape(1, dom * slots), quarters
    )
    if dom == 2:
        to_me = lax.dynamic_slice_in_dim(picked, my_part * slots, slots, 1)
        to_other = lax.dynamic_slice_in_dim(picked, (1 - my_part) * slots, slots, 1)
        got = flip("dom", 1)(to_other)
        first = my_part == 0
        halo = jnp.concatenate(
            [jnp.where(first, to_me, got), jnp.where(first, got, to_me)], axis=1
        )
    else:
        halo = lax.all_to_all(picked, "dom", 1, 1, tiled=True)
    own_cut = lax.dynamic_slice_in_dim(columns, me[0] // below * (count // quarters), count // quarters, 1)
    parts = [own_cut[None]] + [flip("feat", i * below)(cuts[i - 1]) for i in range(1, quarters)]
    weights = jnp.stack([self_weight, neighbour_weight])[None]
    weights_got = flip("feat", feat // 2)(weights)
    means = neighbour_means(
        tile_source[0].T, tile_kind[0].T, columns, halo, tile_patterns, feat
    )
    own_mean = lax.all_to_all(means, "feat", 0, 0, tiled=True)
    *parts, weights_got, _ = lax.optimization_barrier((*parts, weights_got, means))
    row_bits = list(reversed(bits_of(below)))
    for bit in row_bits:
        sent, kept = cut_rows(bit_of("feat", bit), parts)
        parts = [kept, flip("feat", bit)(sent)]
    weight_bits = [feat // 2] + [b for b in bits_of(feat)[1:-2]] + [feat // 4, 1]
    for bit in weight_bits[1:]:
        weights = jnp.concatenate([weights, weights_got])
        weights_got = flip("feat", bit)(weights)
    row_masks = masks_of([i * below for i in range(quarters)], row_bits)
    block = jax.ShapeDtypeStruct((feat, depth, rows), bf16)
    weight_block = jax.ShapeDtypeStruct((feat, depth, hid), bf16)
    own_features, neighbour_weights, linear = local_call(
        functools.partial(own_linear_kernel, row_masks, masks_of([0], weight_bits)),
        "own_linear",
        [block, weight_block, jax.ShapeDtypeStruct((rows, hid), f32)],
        (me, *parts, weights, weights_got),
        scalars=1,
        scratch=[pltpu.VMEM((feat, depth, hid), bf16)],
    )
    own_features = own_features.reshape(feat // 2, 2, depth, rows)
    own_mean = own_mean.reshape(feat // 2, 2, depth, rows)
    core = bit_of("feat", 1)
    sums = (feat // 2, 2, depth, hid)
    hidden, grad_linear, sent = local_call(
        forward_kernel,
        "forward",
        [
            jax.ShapeDtypeStruct((rows, hid), bf16),
            jax.ShapeDtypeStruct((rows, hid), bf16),
            jax.ShapeDtypeStruct(sums, bf16),
        ],
        (core, linear, neighbour_weights, own_mean, own_features, cotangent),
        scalars=1,
    )
    got = flip("feat", 1)(sent)
    (kept,) = local_call(
        kept_kernel,
        "kept_gradients",
        [jax.ShapeDtypeStruct(sums, f32)],
        (core, own_features, own_mean, grad_linear),
        scalars=1,
    )
    grad_self, grad_neighbour = sum_gradients(kept, got)
    return (hidden, grad_self, grad_neighbour)


def solution(mesh):
    placed = (
        P("dom", "feat"),
        P("feat", None),
        P("feat", None),
        P(("dom", "feat"), None),
        P(),
        P(),
        P("dom", None, None),
        P("dom", None, None),
        P(),
    )
    return jax.shard_map(
        on_device,
        mesh=mesh,
        in_specs=placed,
        out_specs=(P(("dom", "feat"), None), P("feat", None), P("feat", None)),
        check_vma=False,
    )
```

time: 145 us -> 120 us (0.83)
  waiting for transfers between devices: 75.5 us -> 53.6 us
  Pallas kernels: 11.3 us -> 20.8 us
  matrix products: 9.33 us -> 0 us
  other arithmetic: 8.95 us -> 3.22 us
  starting transfers between devices: 28.7 us -> 30.7 us
    all_to_all x3 -> x1, waiting for transfers between devices: 34.6 us -> 0.01 us  [on_device(): own_mean = lax.all_to_all(means, 'feat', 0, 0, tiled=True)]
    ppermute x7 -> x16, waiting for transfers between devices: 38.5 us -> 53.6 us  [the longest x3 24.3 us: on_device(): weights_got = flip('feat', bit)(weights)]
    ppermute x7 -> x16, starting transfers between devices: 11.5 us -> 23.3 us  [the longest x3 5.35 us: on_device(): weights_got = flip('feat', bit)(weights)]
    all_to_all x3 -> x1, starting transfers between devices: 15.6 us -> 5.84 us  [on_device(): own_mean = lax.all_to_all(means, 'feat', 0, 0, tiled=True)]
    pallas_call x2 -> x13, Pallas kernels: 11.3 us -> 20.8 us  [local_call(): pl.pallas_call(kernel, out_shape=outs, in_specs=[whole_smem] * scalars +...]
    dot_general x4 -> x0, matrix products: 9.33 us -> none  [the longest x1 3.73 us: on_device(): lax.dot_general(own_mean, weights[:, 1].reshape(feat * depth, hid), first...]
    another operation x9 -> x0, other arithmetic: 5.02 us -> none  [the longest x8 4.12 us: gather_weights(): jnp.stack([jnp.where(upper, other, held), jnp.where(upper, held, other)],...]
    unnamed x33 -> x31, local copies, waits for them, and re-layouts: 4.24 us -> 8.93 us
  transfers between devices with their start and end apart: 11 -> 18, of which waited for: 8 -> 10; matrix products, arithmetic and copies ran while one was open for 8% -> 3% of each run, Pallas kernels for 8% -> 13%
where the time goes in v2:
time: 120 us
  waiting for transfers between devices  53.6 us (45%)
  starting transfers between devices  30.7 us (26%)
  Pallas kernels  20.8 us (17%)
  local copies, waits for them, and re-layouts  10.6 us (9%)
  other arithmetic  3.22 us (3%)
    ppermute x3, waiting for transfers between devices, on_device(): weights_got = flip('feat', bit)(weights)  24.3 us
    pallas_call x13, Pallas kernels, local_call(): pl.pallas_call(kernel, out_shape=outs, in_specs=[whole_smem] * scalars +...  20.8 us
    unnamed x31, local copies, waits for them, and re-layouts  8.93 us
    ppermute x1, waiting for transfers between devices, sum_gradients(): flip('feat', 2)(own_sent)  6.24 us
    ppermute x3, waiting for transfers between devices, on_device(): flip('feat', i * below)(cuts[i - 1])  5.86 us
    all_to_all x1, starting transfers between devices, on_device(): own_mean = lax.all_to_all(means, 'feat', 0, 0, tiled=True)  5.84 us
    ppermute x3, starting transfers between devices, on_device(): weights_got = flip('feat', bit)(weights)  5.35 us
    ppermute x1, waiting for transfers between devices, sum_gradients(): got = flip('feat', half * 8)(sent)  4.77 us
  transfers between devices with their start and end apart: 18, of which 10 were waited for; matrix products, arithmetic and copies ran while one was open for 3% of the time, Pallas kernels for 13%

profile of v2, /device:TPU:0, one launch (start us, length us, event | category | flops | bytes accessed | tf_op | source)
XLA Modules:
  0.0 119.8 jit_solution(1551146763426864395)
XLA Ops:
  0.7 0.9 maximum_bitcast_fusion
  1.6 4.1 %collective-permute-start.3 = (bf16[1,2,64,512]{3,2,1,0:T(8,128)(2,1)S(1)}, bf16[1,2,64,512]{3,2,1,0:T(8,128)(2,1)S(1)}, u32[]{:S(2)}, u32[]{:S(2)}) collective-permute-start(bf16[1,2,64,512]{3,2,1,0:T(8,128)(2,1)S(1)} %maximum_bitcast_fusion), channel_id=1, source_target_pairs={{0,16},{2,18},{4,20},{6,22},{8,24},{10,26},{12,28},{14,30},{16,0},... | collective-permute-start | bytes 393224 | tf_op jit(solution)/shard_map/ppermute | solution.py:334
  5.7 0.7 fusion
  6.5 1.2 %copy-done.1 = bf16[8192,64]{0,1:T(8,128)(2,1)S(1)} copy-done((bf16[8192,64]{0,1:T(8,128)(2,1)S(1)}, bf16[8192,64]{0,1:T(8,128)(2,1)}, u32[]{:S(2)}) %copy-start.1) | copy-done | bytes 1048600
  7.7 1.6 %pick_rows.1 = (bf16[64,512]{1,0:T(8,128)(2,1)S(1)}, bf16[1,64,2048]{2,1,0:T(8,128)(2,1)S(1)}, bf16[1,64,2048]{2,1,0:T(8,128)(2,1)S(1)}, bf16[1,64,2048]{2,1,0:T(8,128)(2,1)S(1)}) custom-call(s32[1]{0:T(128)S(6)} %select_n.85.me_ref, bf16[64,8192]{1,0:T(8,128)(2,1)S(1)} %bitcast.33, s32[1,512]{1,0:T(1,128)S(1)} %broadcast_select_fusion.2.rows_ref), custom_call_target="tpu_custom_call" | custom-call | bytes 1049602 | tf_op jit(solution)/shard_map/pick_rows/pallas_call | solution.py:40
  9.3 1.6 %collective-permute-start.4 = (bf16[64,256]{1,0:T(8,128)(2,1)S(1)}, bf16[64,256]{1,0:T(8,128)(2,1)S(1)}, u32[]{:S(2)}, u32[]{:S(2)}) collective-permute-start(bf16[64,256]{1,0:T(8,128)(2,1)S(1)} %constant_dynamic-slice_fusion), channel_id=1, source_target_pairs={{0,1},{1,0},{2,3},{3,2},{4,5},{5,4},{6,7},{7,6},{8,9},{9,8},{10,11... | collective-permute-start | bytes 98312 | tf_op jit(solution)/shard_map/ppermute | solution.py:324
  10.9 1.6 %collective-permute-start = (bf16[1,64,2048]{2,1,0:T(8,128)(2,1)S(1)}, bf16[1,64,2048]{2,1,0:T(8,128)(2,1)S(1)}, u32[]{:S(2)}, u32[]{:S(2)}) collective-permute-start(bf16[1,64,2048]{2,1,0:T(8,128)(2,1)S(1)} %get-tuple-element.34), channel_id=1, source_target_pairs={{0,8},{2,10},{4,12},{6,14},{8,0},{10,2},{12,4},{14,6},{16,24},{18,... | collective-permute-start | bytes 786440 | tf_op jit(solution)/shard_map/ppermute | solution.py:332
  12.5 0.3 collective-permute-start.1
  12.8 2.5 %collective-permute-start.2 = (bf16[1,64,2048]{2,1,0:T(8,128)(2,1)S(1)}, bf16[1,64,2048]{2,1,0:T(8,128)(2,1)S(1)}, u32[]{:S(2)}, u32[]{:S(2)}) collective-permute-start(bf16[1,64,2048]{2,1,0:T(8,128)(2,1)S(1)} %get-tuple-element.36), channel_id=1, source_target_pairs={{0,24},{2,26},{4,28},{6,30},{8,16},{10,18},{12,20},{14,22},{16,8},... | collective-permute-start | bytes 786440 | tf_op jit(solution)/shard_map/ppermute | solution.py:332
  15.3 1.0 dynamic-slice_bitcast_fusion.refs_0_
  16.4 1.6 %copy-done.5 = bf16[64,128,128]{2,1,0:T(8,128)(2,1)S(1)} copy-done((bf16[64,128,128]{2,1,0:T(8,128)(2,1)S(1)}, bf16[64,128,128]{2,1,0:T(8,128)(2,1)}, u32[]{:S(2)}) %copy-start.5) | copy-done | bytes 2097176
  18.0 9.8 %neighbour_means.1 = bf16[16,64,512]{2,1,0:T(8,128)(2,1)} custom-call(s32[8,64]{1,0:T(8,128)S(1)} %bitcast.37, s32[8,64]{1,0:T(8,128)S(1)} %bitcast.38, bf16[64,8192]{1,0:T(8,128)(2,1)S(1)} %bitcast.34, bf16[64,512]{1,0:T(8,128)(2,1)S(1)} %pad_maximum_fusion.3.halo_ref, bf16[64,128,128]{2,1,0:T(8,128)(2,1)S(1)} %copy-done.5), custom_call_target="tpu_custom_call" | custom-call | flops 1073741824 | bytes 3213312 | tf_op jit(solution)/shard_map/neighbour_means/pallas_call | solution.py:40
  27.7 5.9 %collective-permute-done.1.refs_2_ = bf16[1,64,2048]{2,1,0:T(8,128)(2,1)S(1)} collective-permute-done((bf16[1,64,2048]{2,1,0:T(8,128)(2,1)S(1)}, bf16[1,64,2048]{2,1,0:T(8,128)(2,1)S(1)}, u32[]{:S(2)}, u32[]{:S(2)}) %collective-permute-start.1) | collective-permute-done | bytes 262176 | tf_op jit(solution)/shard_map/ppermute | solution.py:332
  33.6 1.6 %collective-permute-start.7 = (bf16[2,2,64,512]{3,2,1,0:T(8,128)(2,1)S(1)}, bf16[2,2,64,512]{3,2,1,0:T(8,128)(2,1)S(1)}, u32[]{:S(2)}, u32[]{:S(2)}) collective-permute-start(bf16[2,2,64,512]{3,2,1,0:T(8,128)(2,1)S(1)} %pad_maximum_fusion.2), channel_id=1, source_target_pairs={{0,4},{2,6},{4,0},{6,2},{8,12},{10,14},{12,8},{14,10},{16,20},{18,... | collective-permute-start | bytes 786440 | tf_op jit(solution)/shard_map/ppermute | solution.py:347
  35.2 5.8 %all-to-all-start = ((bf16[16,64,512]{2,1,0:T(8,128)(2,1)}), bf16[16,64,512]{2,1,0:T(8,128)(2,1)S(1)}, u32[]{:S(2)}, u32[]{:S(2)}) async-start(bf16[16,64,512]{2,1,0:T(8,128)(2,1)} %neighbour_means.1), calls=%async_computation | async-start | bytes 2097152 | tf_op jit(solution)/shard_map/all_to_all | solution.py:338
  41.1 0.9 pad_maximum_fusion.1
  42.0 3.7 %collective-permute-start.8 = (bf16[4,2,64,512]{3,2,1,0:T(8,128)(2,1)}, bf16[4,2,64,512]{3,2,1,0:T(8,128)(2,1)}, u32[]{:S(2)}, u32[]{:S(2)}) collective-permute-start(bf16[4,2,64,512]{3,2,1,0:T(8,128)(2,1)} %pad_maximum_fusion.1), channel_id=1, source_target_pairs={{0,8},{2,10},{4,12},{6,14},{8,0},{10,2},{12,4},{14,6},{16,24},{18,... | collective-permute-start | bytes 1572872 | tf_op jit(solution)/shard_map/ppermute | solution.py:347
  45.7 0.9 cut_rows.2
  46.5 1.5 %collective-permute-start.5 = (bf16[4,64,1024]{2,1,0:T(8,128)(2,1)}, bf16[4,64,1024]{2,1,0:T(8,128)(2,1)S(1)}, u32[]{:S(2)}, u32[]{:S(2)}) collective-permute-start(bf16[4,64,1024]{2,1,0:T(8,128)(2,1)} %get-tuple-element.43), channel_id=1, source_target_pairs={{0,4},{2,6},{4,0},{6,2},{8,12},{10,14},{12,8},{14,10},{16,20},{18,... | collective-permute-start | bytes 1572872 | tf_op jit(solution)/shard_map/ppermute | solution.py:343
  48.0 24.3 %collective-permute-done.8 = bf16[4,2,64,512]{3,2,1,0:T(8,128)(2,1)} collective-permute-done((bf16[4,2,64,512]{3,2,1,0:T(8,128)(2,1)}, bf16[4,2,64,512]{3,2,1,0:T(8,128)(2,1)}, u32[]{:S(2)}, u32[]{:S(2)}) %collective-permute-start.8) | collective-permute-done | bytes 524320 | tf_op jit(solution)/shard_map/ppermute | solution.py:347
  72.4 1.2 %pad_maximum_fusion.refs_2_ = bf16[8,2,64,512]{3,2,1,0:T(8,128)(2,1)S(1)} fusion(bf16[4,2,64,512]{3,2,1,0:T(8,128)(2,1)} %collective-permute-done.8, bf16[2,2,64,512]{3,2,1,0:T(8,128)(2,1)} %copy-done.13, bf16[1,2,64,512]{3,2,1,0:T(8,128)(2,1)S(1)} %collective-permute-done.3, bf16[1,2,64,512]{3,2,1,0:T(8,128)(2,1)S(1)} %maximum_bitcast_fusion), kind=kLoop, calls=%fused_computation | loop fusion | flops 1572864 | bytes 2097152 | tf_op jit(solution)/shard_map/concatenate | solution.py:346
  73.8 0.5 collective-permute-start.6
  74.3 2.8 %collective-permute-done.6.refs_1_ = bf16[8,64,512]{2,1,0:T(8,128)(2,1)S(1)} collective-permute-done((bf16[8,64,512]{2,1,0:T(8,128)(2,1)S(1)}, bf16[8,64,512]{2,1,0:T(8,128)(2,1)S(1)}, u32[]{:S(2)}, u32[]{:S(2)}) %collective-permute-start.6) | collective-permute-done | bytes 524320 | tf_op jit(solution)/shard_map/ppermute | solution.py:343
  77.1 2.2 %own_linear.1 = (bf16[16,64,512]{2,1,0:T(8,128)(2,1)S(1)}, bf16[16,64,512]{2,1,0:T(8,128)(2,1)S(1)}, f32[512,512]{1,0:T(8,128)S(1)}) custom-call(s32[1]{0:T(128)} %bitcast.1.me_ref, bf16[8,64,512]{2,1,0:T(8,128)(2,1)S(1)} %get-tuple-element.44.refs_0_, bf16[8,64,512]{2,1,0:T(8,128)(2,1)S(1)} %collective-permute-done.6.refs_1_, ...), custom_call_target="tpu_custom_call" | custom-call | bytes 3145730 | tf_op jit(solution)/shard_map/own_linear/pallas_call | solution.py:40
  79.3 1.0 copy-done.3
  80.2 1.0 copy-done.6
  81.2 1.2 %copy-done.7 = f32[512,512]{1,0:T(8,128)S(1)} copy-done((f32[512,512]{1,0:T(8,128)S(1)}, f32[512,512]{1,0:T(8,128)}, u32[]{:S(2)}) %copy-start.7) | copy-done | bytes 1048600
  82.5 1.0 copy-done.8
  83.5 4.0 %forward.1 = (bf16[512,512]{1,0:T(8,128)(2,1)}, bf16[512,512]{1,0:T(8,128)(2,1)S(1)}, bf16[8,2,64,512]{3,2,1,0:T(8,128)(2,1)}) custom-call(s32[1]{0:T(128)} %bitcast.bit_ref.core_ref, f32[512,512]{1,0:T(8,128)S(1)} %copy-done.7, bf16[16,64,512]{2,1,0:T(8,128)(2,1)S(1)} %get-tuple-element.48.weight_ref, bf16[8,2,64,512]{3,2,1,0:T(8,128)(2,1)S(1)} %bitcast.31, ...), custom_call_target="tpu_custom_call" | custom-call | bytes 4194306 | tf_op jit(solution)/shard_map/forward/pallas_call | solution.py:40
  87.5 0.8 copy-done.9
  88.3 0.1 collective-permute-start.10
  88.5 1.0 copy-done.10
  89.6 0.7 kept_gradients.1.kept_ref
  90.3 0.9 collective-permute-done.10.got_ref
  91.2 0.7 first_sum.1
  91.9 1.5 %collective-permute-start.11 = (bf16[2,2,64,512]{3,2,1,0:T(8,128)(2,1)S(1)}, bf16[2,2,64,512]{3,2,1,0:T(8,128)(2,1)S(1)}, u32[]{:S(2)}, u32[]{:S(2)}) collective-permute-start(bf16[2,2,64,512]{3,2,1,0:T(8,128)(2,1)S(1)} %get-tuple-element.54), channel_id=1, source_target_pairs={{0,4},{2,6},{4,0},{6,2},{8,12},{10,14},{12,8},{14,10},{16,20},{18,... | collective-permute-start | bytes 786440 | tf_op jit(solution)/shard_map/ppermute | solution.py:266
  93.5 0.6 collective-permute-start.13
  94.1 6.2 %collective-permute-done.11.got_ref = bf16[2,2,64,512]{3,2,1,0:T(8,128)(2,1)S(1)} collective-permute-done((bf16[2,2,64,512]{3,2,1,0:T(8,128)(2,1)S(1)}, bf16[2,2,64,512]{3,2,1,0:T(8,128)(2,1)S(1)}, u32[]{:S(2)}, u32[]{:S(2)}) %collective-permute-start.11) | collective-permute-done | bytes 262176 | tf_op jit(solution)/shard_map/ppermute | solution.py:266
  100.4 0.8 collective-permute-start.12
  101.2 0.4 collective-permute-done.13.got_ref
  101.6 1.1 collective-permute-start.14
  102.7 2.7 %collective-permute-done.12.own_got_ref = bf16[2,64,512]{2,1,0:T(8,128)(2,1)S(1)} collective-permute-done((bf16[2,64,512]{2,1,0:T(8,128)(2,1)S(1)}, bf16[2,64,512]{2,1,0:T(8,128)(2,1)S(1)}, u32[]{:S(2)}, u32[]{:S(2)}) %collective-permute-start.12) | collective-permute-done | bytes 131104 | tf_op jit(solution)/shard_map/ppermute | solution.py:268
  105.4 1.2 %collective-permute-done.14.neigh_got_ref = bf16[2,64,512]{2,1,0:T(8,128)(2,1)S(1)} collective-permute-done((bf16[2,64,512]{2,1,0:T(8,128)(2,1)S(1)}, bf16[2,64,512]{2,1,0:T(8,128)(2,1)S(1)}, u32[]{:S(2)}, u32[]{:S(2)}) %collective-permute-start.14) | collective-permute-done | bytes 131104 | tf_op jit(solution)/shard_map/ppermute | solution.py:270
  106.7 2.6 %collective-permute-start.15 = (bf16[1,2,64,512]{3,2,1,0:T(8,128)(2,1)S(1)}, bf16[1,2,64,512]{3,2,1,0:T(8,128)(2,1)S(1)}, u32[]{:S(2)}, u32[]{:S(2)}) collective-permute-start(bf16[1,2,64,512]{3,2,1,0:T(8,128)(2,1)S(1)} %get-tuple-element.62), channel_id=1, source_target_pairs={{0,16},{2,18},{4,20},{6,22},{8,24},{10,26},{12,28},{14,30},{16,0},... | collective-permute-start | bytes 393224 | tf_op jit(solution)/shard_map/ppermute | solution.py:279
  109.2 4.8 %collective-permute-done.15.got_ref = bf16[1,2,64,512]{3,2,1,0:T(8,128)(2,1)S(1)} collective-permute-done((bf16[1,2,64,512]{3,2,1,0:T(8,128)(2,1)S(1)}, bf16[1,2,64,512]{3,2,1,0:T(8,128)(2,1)S(1)}, u32[]{:S(2)}, u32[]{:S(2)}) %collective-permute-start.15) | collective-permute-done | bytes 131104 | tf_op jit(solution)/shard_map/ppermute | solution.py:279
  114.0 0.7 collective-permute-start.16
  114.7 4.4 %collective-permute-done.16.got_ref = bf16[1,2,64,512]{3,2,1,0:T(8,128)(2,1)S(1)} collective-permute-done((bf16[1,2,64,512]{3,2,1,0:T(8,128)(2,1)S(1)}, bf16[1,2,64,512]{3,2,1,0:T(8,128)(2,1)S(1)}, u32[]{:S(2)}, u32[]{:S(2)}) %collective-permute-start.16) | collective-permute-done | bytes 131104 | tf_op jit(solution)/shard_map/ppermute | solution.py:289
  119.1 0.7 last_sum.1
  (44 shorter events, 0.6 us)
Async XLA Ops:
  0.6 5.8 %copy-start = (s32[2,2,256]{2,1,0:T(2,128)S(1)}, s32[2,2,256]{2,1,0:T(2,128)}, u32[]{:S(2)}) copy-start(s32[2,2,256]{2,1,0:T(2,128)} %param.13) | copy-start | bytes 12292
  0.6 15.7 %copy-start.12 = (s32[1,64,8]{1,2,0:T(8,128)S(1)}, s32[1,64,8]{1,2,0:T(8,128)}, u32[]{:S(2)}) copy-start(s32[1,64,8]{1,2,0:T(8,128)} %param.16) | copy-start | bytes 6148
  0.7 15.7 %copy-start.11 = (s32[1,64,8]{1,2,0:T(8,128)S(1)}, s32[1,64,8]{1,2,0:T(8,128)}, u32[]{:S(2)}) copy-start(s32[1,64,8]{1,2,0:T(8,128)} %param.15) | copy-start | bytes 6148
  1.6 26.2 %collective-permute-start.3 = (bf16[1,2,64,512]{3,2,1,0:T(8,128)(2,1)S(1)}, bf16[1,2,64,512]{3,2,1,0:T(8,128)(2,1)S(1)}, u32[]{:S(2)}, u32[]{:S(2)}) collective-permute-start(bf16[1,2,64,512]{3,2,1,0:T(8,128)(2,1)S(1)} %maximum_bitcast_fusion), channel_id=1, source_target_pairs={{0,16},{2,18},{4,20},{6,22},{8,24},{10,26},{12,28},{14,30},{16,0},... | collective-permute-start | bytes 393224 | tf_op jit(solution)/shard_map/ppermute | solution.py:334
  6.5 1.2 %copy-start.1 = (bf16[8192,64]{0,1:T(8,128)(2,1)S(1)}, bf16[8192,64]{0,1:T(8,128)(2,1)}, u32[]{:S(2)}) copy-start(bf16[8192,64]{0,1:T(8,128)(2,1)} %param.9) | copy-start | bytes 3145732
  7.7 8.6 %copy-start.2 = (bf16[8192,64]{0,1:T(8,128)(2,1)S(1)}, bf16[8192,64]{0,1:T(8,128)(2,1)}, u32[]{:S(2)}) copy-start(bf16[8192,64]{0,1:T(8,128)(2,1)} %param.9) | copy-start | bytes 3145732
  9.3 7.0 %collective-permute-start.4 = (bf16[64,256]{1,0:T(8,128)(2,1)S(1)}, bf16[64,256]{1,0:T(8,128)(2,1)S(1)}, u32[]{:S(2)}, u32[]{:S(2)}) collective-permute-start(bf16[64,256]{1,0:T(8,128)(2,1)S(1)} %constant_dynamic-slice_fusion), channel_id=1, source_target_pairs={{0,1},{1,0},{2,3},{3,2},{4,5},{5,4},{6,7},{7,6},{8,9},{9,8},{10,11... | collective-permute-start | bytes 98312 | tf_op jit(solution)/shard_map/ppermute | solution.py:324
  10.9 16.8 %collective-permute-start = (bf16[1,64,2048]{2,1,0:T(8,128)(2,1)S(1)}, bf16[1,64,2048]{2,1,0:T(8,128)(2,1)S(1)}, u32[]{:S(2)}, u32[]{:S(2)}) collective-permute-start(bf16[1,64,2048]{2,1,0:T(8,128)(2,1)S(1)} %get-tuple-element.34), channel_id=1, source_target_pairs={{0,8},{2,10},{4,12},{6,14},{8,0},{10,2},{12,4},{14,6},{16,24},{18,... | collective-permute-start | bytes 786440 | tf_op jit(solution)/shard_map/ppermute | solution.py:332
  12.5 21.1 %collective-permute-start.1 = (bf16[1,64,2048]{2,1,0:T(8,128)(2,1)S(1)}, bf16[1,64,2048]{2,1,0:T(8,128)(2,1)S(1)}, u32[]{:S(2)}, u32[]{:S(2)}) collective-permute-start(bf16[1,64,2048]{2,1,0:T(8,128)(2,1)S(1)} %get-tuple-element.35), channel_id=1, source_target_pairs={{0,16},{2,18},{4,20},{6,22},{8,24},{10,26},{12,28},{14,30},{16,0},... | collective-permute-start | bytes 786440 | tf_op jit(solution)/shard_map/ppermute | solution.py:332
  12.8 20.8 %collective-permute-start.2 = (bf16[1,64,2048]{2,1,0:T(8,128)(2,1)S(1)}, bf16[1,64,2048]{2,1,0:T(8,128)(2,1)S(1)}, u32[]{:S(2)}, u32[]{:S(2)}) collective-permute-start(bf16[1,64,2048]{2,1,0:T(8,128)(2,1)S(1)} %get-tuple-element.36), channel_id=1, source_target_pairs={{0,24},{2,26},{4,28},{6,30},{8,16},{10,18},{12,20},{14,22},{16,8},... | collective-permute-start | bytes 786440 | tf_op jit(solution)/shard_map/ppermute | solution.py:332
  16.4 1.6 %copy-start.5 = (bf16[64,128,128]{2,1,0:T(8,128)(2,1)S(1)}, bf16[64,128,128]{2,1,0:T(8,128)(2,1)}, u32[]{:S(2)}) copy-start(bf16[64,128,128]{2,1,0:T(8,128)(2,1)} %pattern_ref.1) | copy-start | bytes 6291460
  33.6 7.4 %collective-permute-start.7 = (bf16[2,2,64,512]{3,2,1,0:T(8,128)(2,1)S(1)}, bf16[2,2,64,512]{3,2,1,0:T(8,128)(2,1)S(1)}, u32[]{:S(2)}, u32[]{:S(2)}) collective-permute-start(bf16[2,2,64,512]{3,2,1,0:T(8,128)(2,1)S(1)} %pad_maximum_fusion.2), channel_id=1, source_target_pairs={{0,4},{2,6},{4,0},{6,2},{8,12},{10,14},{12,8},{14,10},{16,20},{18,... | collective-permute-start | bytes 786440 | tf_op jit(solution)/shard_map/ppermute | solution.py:347
  35.2 46.0 %all-to-all-start = ((bf16[16,64,512]{2,1,0:T(8,128)(2,1)}), bf16[16,64,512]{2,1,0:T(8,128)(2,1)S(1)}, u32[]{:S(2)}, u32[]{:S(2)}) async-start(bf16[16,64,512]{2,1,0:T(8,128)(2,1)} %neighbour_means.1), calls=%async_computation | async-start | bytes 2097152 | tf_op jit(solution)/shard_map/all_to_all | solution.py:338
  41.0 4.6 %copy-start.13 = (bf16[2,2,64,512]{3,2,1,0:T(8,128)(2,1)}, bf16[2,2,64,512]{3,2,1,0:T(8,128)(2,1)S(1)}, u32[]{:S(2)}) copy-start(bf16[2,2,64,512]{3,2,1,0:T(8,128)(2,1)S(1)} %collective-permute-done.7) | copy-start | bytes 786436
  42.0 30.4 %collective-permute-start.8 = (bf16[4,2,64,512]{3,2,1,0:T(8,128)(2,1)}, bf16[4,2,64,512]{3,2,1,0:T(8,128)(2,1)}, u32[]{:S(2)}, u32[]{:S(2)}) collective-permute-start(bf16[4,2,64,512]{3,2,1,0:T(8,128)(2,1)} %pad_maximum_fusion.1), channel_id=1, source_target_pairs={{0,8},{2,10},{4,12},{6,14},{8,0},{10,2},{12,4},{14,6},{16,24},{18,... | collective-permute-start | bytes 1572872 | tf_op jit(solution)/shard_map/ppermute | solution.py:347
  46.5 27.1 %collective-permute-start.5 = (bf16[4,64,1024]{2,1,0:T(8,128)(2,1)}, bf16[4,64,1024]{2,1,0:T(8,128)(2,1)S(1)}, u32[]{:S(2)}, u32[]{:S(2)}) collective-permute-start(bf16[4,64,1024]{2,1,0:T(8,128)(2,1)} %get-tuple-element.43), channel_id=1, source_target_pairs={{0,4},{2,6},{4,0},{6,2},{8,12},{10,14},{12,8},{14,10},{16,20},{18,... | collective-permute-start | bytes 1572872 | tf_op jit(solution)/shard_map/ppermute | solution.py:343
  73.6 3.5 %collective-permute-start.9 = (bf16[8,2,64,512]{3,2,1,0:T(8,128)(2,1)S(1)}, bf16[8,2,64,512]{3,2,1,0:T(8,128)(2,1)}, u32[]{:S(2)}, u32[]{:S(2)}) collective-permute-start(bf16[8,2,64,512]{3,2,1,0:T(8,128)(2,1)S(1)} %pad_maximum_fusion.refs_2_), channel_id=1, source_target_pairs={{0,2},{2,0},{4,6},{6,4},{8,10},{10,8},{12,14},{14,12},{16,18},{18,... | collective-permute-start | bytes 3145736 | tf_op jit(solution)/shard_map/ppermute | solution.py:347
  73.8 3.3 %collective-permute-start.6 = (bf16[8,64,512]{2,1,0:T(8,128)(2,1)S(1)}, bf16[8,64,512]{2,1,0:T(8,128)(2,1)S(1)}, u32[]{:S(2)}, u32[]{:S(2)}) collective-permute-start(bf16[8,64,512]{2,1,0:T(8,128)(2,1)S(1)} %get-tuple-element.45), channel_id=1, source_target_pairs={{0,2},{2,0},{4,6},{6,4},{8,10},{10,8},{12,14},{14,12},{16,18},{18,... | collective-permute-start | bytes 1572872 | tf_op jit(solution)/shard_map/ppermute | solution.py:343
  79.2 1.0 copy-start.3
  80.2 1.0 copy-start.6
  81.2 1.2 %copy-start.7 = (f32[512,512]{1,0:T(8,128)S(1)}, f32[512,512]{1,0:T(8,128)}, u32[]{:S(2)}) copy-start(f32[512,512]{1,0:T(8,128)} %copy-done.6) | copy-start | bytes 3145732
  82.4 1.0 copy-start.8
  83.5 5.0 %copy-start.4 = (bf16[16,64,512]{2,1,0:T(8,128)(2,1)S(1)}, bf16[16,64,512]{2,1,0:T(8,128)(2,1)}, u32[]{:S(2)}) copy-start(bf16[16,64,512]{2,1,0:T(8,128)(2,1)} %copy-done.3) | copy-start | bytes 3145732
  87.5 0.8 copy-start.9
  88.3 2.9 %collective-permute-start.10 = (bf16[8,2,64,512]{3,2,1,0:T(8,128)(2,1)}, bf16[8,2,64,512]{3,2,1,0:T(8,128)(2,1)S(1)}, u32[]{:S(2)}, u32[]{:S(2)}) collective-permute-start(bf16[8,2,64,512]{3,2,1,0:T(8,128)(2,1)} %get-tuple-element.52), channel_id=1, source_target_pairs={{0,2},{2,0},{4,6},{6,4},{8,10},{10,8},{12,14},{14,12},{16,18},{18,... | collective-permute-start | bytes 3145736 | tf_op jit(solution)/shard_map/ppermute | solution.py:374
  88.5 1.0 copy-start.10
  91.9 8.4 %collective-permute-start.11 = (bf16[2,2,64,512]{3,2,1,0:T(8,128)(2,1)S(1)}, bf16[2,2,64,512]{3,2,1,0:T(8,128)(2,1)S(1)}, u32[]{:S(2)}, u32[]{:S(2)}) collective-permute-start(bf16[2,2,64,512]{3,2,1,0:T(8,128)(2,1)S(1)} %get-tuple-element.54), channel_id=1, source_target_pairs={{0,4},{2,6},{4,0},{6,2},{8,12},{10,14},{12,8},{14,10},{16,20},{18,... | collective-permute-start | bytes 786440 | tf_op jit(solution)/shard_map/ppermute | solution.py:266
  93.5 8.1 %collective-permute-start.13 = (bf16[2,2,64,512]{3,2,1,0:T(8,128)(2,1)S(1)}, bf16[2,2,64,512]{3,2,1,0:T(8,128)(2,1)S(1)}, u32[]{:S(2)}, u32[]{:S(2)}) collective-permute-start(bf16[2,2,64,512]{3,2,1,0:T(8,128)(2,1)S(1)} %get-tuple-element.58), channel_id=1, source_target_pairs={{0,8},{2,10},{4,12},{6,14},{8,0},{10,2},{12,4},{14,6},{16,24},{18,... | collective-permute-start | bytes 786440 | tf_op jit(solution)/shard_map/ppermute | solution.py:266
  100.4 5.0 %collective-permute-start.12 = (bf16[2,64,512]{2,1,0:T(8,128)(2,1)S(1)}, bf16[2,64,512]{2,1,0:T(8,128)(2,1)S(1)}, u32[]{:S(2)}, u32[]{:S(2)}) collective-permute-start(bf16[2,64,512]{2,1,0:T(8,128)(2,1)S(1)} %get-tuple-element.56), channel_id=1, source_target_pairs={{0,8},{2,10},{4,12},{6,14},{8,0},{10,2},{12,4},{14,6},{16,24},{18,... | collective-permute-start | bytes 393224 | tf_op jit(solution)/shard_map/ppermute | solution.py:268
  101.6 5.0 %collective-permute-start.14 = (bf16[2,64,512]{2,1,0:T(8,128)(2,1)S(1)}, bf16[2,64,512]{2,1,0:T(8,128)(2,1)S(1)}, u32[]{:S(2)}, u32[]{:S(2)}) collective-permute-start(bf16[2,64,512]{2,1,0:T(8,128)(2,1)S(1)} %get-tuple-element.60), channel_id=1, source_target_pairs={{0,4},{2,6},{4,0},{6,2},{8,12},{10,14},{12,8},{14,10},{16,20},{18,... | collective-permute-start | bytes 393224 | tf_op jit(solution)/shard_map/ppermute | solution.py:270
  106.7 7.3 %collective-permute-start.15 = (bf16[1,2,64,512]{3,2,1,0:T(8,128)(2,1)S(1)}, bf16[1,2,64,512]{3,2,1,0:T(8,128)(2,1)S(1)}, u32[]{:S(2)}, u32[]{:S(2)}) collective-permute-start(bf16[1,2,64,512]{3,2,1,0:T(8,128)(2,1)S(1)} %get-tuple-element.62), channel_id=1, source_target_pairs={{0,16},{2,18},{4,20},{6,22},{8,24},{10,26},{12,28},{14,30},{16,0},... | collective-permute-start | bytes 393224 | tf_op jit(solution)/shard_map/ppermute | solution.py:279
  114.0 5.0 %collective-permute-start.16 = (bf16[1,2,64,512]{3,2,1,0:T(8,128)(2,1)S(1)}, bf16[1,2,64,512]{3,2,1,0:T(8,128)(2,1)S(1)}, u32[]{:S(2)}, u32[]{:S(2)}) collective-permute-start(bf16[1,2,64,512]{3,2,1,0:T(8,128)(2,1)S(1)} %rounded_sum.1.kept_ref), channel_id=1, source_target_pairs={{0,1},{1,0},{2,3},{3,2},{4,5},{5,4},{6,7},{7,6},{8,9},{9,8},{10,11... | collective-permute-start | bytes 393224 | tf_op jit(solution)/shard_map/ppermute | solution.py:289

commit v3 on v2

v3 whole, which is shorter than its diff:
```python
import functools

import jax
import jax.numpy as jnp
from jax import lax
from jax.experimental import pallas as pl
from jax.experimental.pallas import tpu as pltpu
from jax.sharding import PartitionSpec as P

inv_root_two = 0.7071067811865476
inv_root_two_pi = 0.3989422804014327
bf16 = jnp.bfloat16
f32 = jnp.float32
vmem_bytes = 16 * 2**20
most_vmem = 60 * 2**20
whole_vmem = pl.BlockSpec(memory_space=pltpu.VMEM)
whole_smem = pl.BlockSpec(memory_space=pltpu.SMEM)
anywhere = pl.BlockSpec(memory_space=pl.ANY)
last_with_last = (((1,), (1,)), ((), ()))
first_with_first = (((0,), (0,)), ((), ()))


def gelu_pair(linear):
    normal_cdf = 0.5 * (1.0 + lax.erf(linear * inv_root_two))
    density = jnp.exp(-0.5 * linear * linear) * inv_root_two_pi
    return (linear * normal_cdf, normal_cdf + linear * density)


def flip(axis, bit):
    size = lax.axis_size(axis)
    return functools.partial(
        lax.ppermute, axis_name=axis, perm=[(i, i ^ bit) for i in range(size)]
    )


def bits_of(size):
    return [1 << i for i in range(size.bit_length() - 1)]


def with_copies(kernel, lazy, operands, outs, *refs):
    given, refs = refs[:operands], refs[operands:]
    made, refs = refs[:outs], refs[outs:]
    held, done, rest = refs[:operands], refs[operands], refs[operands + 1 :]
    copies = [pltpu.make_async_copy(g, h, done.at[i]) for i, (g, h) in enumerate(zip(given, held))]
    for copy in copies:
        copy.start()
    if lazy:

        def ready(*operands):
            for i in operands:
                copies[i].wait()

        kernel(ready, *held, *made, *rest)
        return
    for copy in copies:
        copy.wait()
    kernel(*held, *made, *rest)


def local_call(kernel, name, outs, operands, scalars=0, scratch=(), fetch=False, lazy=False):
    in_specs = [whole_smem] * scalars + [whole_vmem] * (len(operands) - scalars)
    if fetch or lazy:
        in_specs = [anywhere] * len(operands)
        held = [
            (pltpu.SMEM if i < scalars else pltpu.VMEM)(x.shape, x.dtype)
            for i, x in enumerate(operands)
        ]
        scratch = [*held, pltpu.SemaphoreType.DMA((len(operands),)), *scratch]
        kernel = functools.partial(with_copies, kernel, lazy, len(operands), len(outs))
    return pl.pallas_call(
        kernel,
        out_shape=outs,
        in_specs=in_specs,
        out_specs=[whole_vmem] * len(outs),
        scratch_shapes=list(scratch),
        cost_estimate=pl.CostEstimate(flops=0, bytes_accessed=0, transcendentals=0),
        compiler_params=pltpu.CompilerParams(vmem_limit_bytes=most_vmem if fetch or lazy else vmem_bytes),
        name=name,
    )(*operands)


def pick(columns_ref, asked):
    count = columns_ref.shape[1]
    step = min(256, count)
    total = jnp.zeros((columns_ref.shape[0], asked.shape[1]), f32)
    for at in range(0, count, step):
        ids = lax.broadcasted_iota(jnp.int32, (step, asked.shape[1]), 0) + at
        one_hot = jnp.where(ids == asked, 1.0, 0.0).astype(bf16)
        total = total + jnp.dot(
            columns_ref[:, at : at + step], one_hot, preferred_element_type=f32
        )
    return total.astype(bf16)


def asked_rows(ask_ref, count_ref, part, to):
    slot = lax.broadcasted_iota(jnp.int32, (1, ask_ref.shape[2]), 1)
    return jnp.where(slot < count_ref[part, to], ask_ref[part, pl.ds(to, 1), :], -1)


def open_kernel(
    quarters, count_ref, columns_ref, self_ref, neighbour_ref, ask_ref, picked_ref, weight_ref, across_ref, *cut_refs
):
    me, part = lax.axis_index("feat"), lax.axis_index("dom")
    below = lax.axis_size("feat") // quarters
    quarter, half = me // below, me % below // (below // 2)
    weight_ref[0] = jnp.where(part % 2 == 0, self_ref[...], neighbour_ref[...])
    width = across_ref.shape[2]
    for i, cut_ref in enumerate(cut_refs):
        at = (quarter ^ i) * 2 + half
        cut_ref[0] = columns_ref[:, pl.ds(pl.multiple_of(at * width, width), width)]
        at = (quarter ^ i) * 2 + 1 - half
        across_ref[i] = columns_ref[:, pl.ds(pl.multiple_of(at * width, width), width)]
    parts = ask_ref.shape[1]
    if parts == 2:
        asked = asked_rows(ask_ref, count_ref, part, 1 - part)
    else:
        asked = jnp.concatenate(
            [asked_rows(ask_ref, count_ref, part, to) for to in range(parts)], axis=1
        )
    picked_ref[...] = pick(columns_ref, asked)


def open_exchange(counts, columns, self_weight, neighbour_weight, asks, quarters):
    depth, count = columns.shape
    width = count // quarters // 2
    parts, slots = asks.shape[1:]
    asked = slots if parts == 2 else parts * slots
    return local_call(
        functools.partial(open_kernel, quarters),
        "open_exchange",
        [
            jax.ShapeDtypeStruct((depth, asked), bf16),
            jax.ShapeDtypeStruct((1, *self_weight.shape), bf16),
            jax.ShapeDtypeStruct((quarters, depth, width), bf16),
        ]
        + [jax.ShapeDtypeStruct((1, depth, width), bf16)] * quarters,
        (counts, columns, self_weight, neighbour_weight, asks),
        scalars=1,
        fetch=True,
    )


def mean_kernel(
    unroll, ready, source_ref, kind_ref, count_ref, local_ref, halo_ref, ask_ref, pattern_ref, mean_ref, tiles
):
    depth = local_ref.shape[0]
    side = pattern_ref.shape[1]
    local_tiles, halo_tiles = local_ref.shape[1] // side, halo_ref.shape[1] // side
    ready(2, 3, 5)
    for i in range(local_tiles):
        tiles[i, 0:depth, :] = local_ref[:, i * side : (i + 1) * side]
    first = local_tiles
    if ask_ref.shape[1] == 2:
        part = lax.axis_index("dom")
        own = pick(local_ref, asked_rows(ask_ref, count_ref, part, part))
        for i in range(halo_tiles):
            tiles[local_tiles + part * halo_tiles + i, 0:depth, :] = own[:, i * side : (i + 1) * side]
        first = local_tiles + (1 - part) * halo_tiles
    ready(4)
    for i in range(halo_tiles):
        tiles[first + i, 0:depth, :] = halo_ref[:, i * side : (i + 1) * side]
    tiles[:, depth:, :] = jnp.ones((tiles.shape[0], tiles.shape[1] - depth, side), bf16)
    per_block = mean_ref.shape[2] // side
    ready(0, 1, 6)

    def one(t):
        rows = [tiles[source_ref[k, t]] for k in range(source_ref.shape[0])]
        weights = [pattern_ref[kind_ref[k, t]] for k in range(source_ref.shape[0])]
        summed = lax.dot_general(
            jnp.concatenate(rows, 1),
            jnp.concatenate(weights, 1),
            last_with_last,
            preferred_element_type=f32,
        )
        mean = (summed[0:depth] / summed[depth : depth + 1]).astype(bf16)
        at = lax.rem(t, per_block) * side
        mean_ref[lax.div(t, per_block), :, pl.ds(pl.multiple_of(at, side), side)] = mean

    @pl.loop(0, source_ref.shape[1] // unroll)
    def _(step):
        for u in range(unroll):
            one(step * unroll + u)


def neighbour_means(source, kind, counts, local, halo, asks, patterns, blocks):
    depth, count = local.shape
    side = patterns.shape[1]
    tile_count = (count + asks.shape[1] * asks.shape[2]) // side
    return local_call(
        functools.partial(mean_kernel, 8 if source.shape[1] % 8 == 0 else 1),
        "neighbour_means",
        [jax.ShapeDtypeStruct((blocks, depth, count // blocks), bf16)],
        (source, kind, counts, local, halo, asks, patterns),
        scalars=3,
        scratch=[pltpu.VMEM((tile_count, depth + 16, side), bf16)],
        lazy=True,
    )[0]


def cut_kernel(bit, *refs):
    *held_refs, sent_ref, kept_ref = refs
    half = sent_ref.shape[2]
    bit = lax.axis_index("feat") // bit % 2
    mine = pl.multiple_of(bit * half, half)
    theirs = pl.multiple_of((1 - bit) * half, half)
    at = 0
    for ref in held_refs:
        for i in range(ref.shape[0]):
            sent_ref[at] = ref[i, :, pl.ds(theirs, half)]
            kept_ref[at] = ref[i, :, pl.ds(mine, half)]
            at += 1


def cut_rows(bit, parts, width):
    count = sum(p.shape[0] for p in parts)
    out = jax.ShapeDtypeStruct((count, parts[0].shape[1], width // 2), bf16)
    return local_call(
        functools.partial(cut_kernel, bit), "cut_rows", [out, out], parts, fetch=True
    )


def gathered(parts):
    shape = (sum(p.shape[0] for p in parts), *parts[0].shape[1:])
    return local_call(gather_kernel, "gathered", [jax.ShapeDtypeStruct(shape, bf16)], parts)[0]


def gather_kernel(*refs):
    *held_refs, out_ref = refs
    at = 0
    for ref in held_refs:
        out_ref[at : at + ref.shape[0]] = ref[...]
        at += ref.shape[0]


def flipped(masks, bit):
    return [m ^ bit for m in masks]


def features_in_order(row_masks, kept_ref, got_ref):
    half = kept_ref.shape[0]
    place = {mask: i for i, mask in enumerate(row_masks)}

    def features(mask, at=0, size=None):
        i = place[mask]
        ref = kept_ref if i < half else got_ref
        return ref[i % half, :, at : at + (size or ref.shape[2])]

    return features


def means_in_order(mean_ref):
    me = lax.axis_index("feat")

    def means(mask, at=0, size=None):
        return mean_ref[me ^ mask, :, at : at + (size or mean_ref.shape[2])]

    return means


def forward_kernel(row_masks, weight_masks, ready, *refs):
    pieces = len(weight_masks)
    kept_ref, got_ref, mean_ref, cot_ref = refs[:4]
    mine_refs, other_refs = refs[4 : 4 + pieces], refs[4 + pieces : 4 + 2 * pieces]
    hidden_ref, grad_ref, sums_ref, linear_ref = refs[4 + 2 * pieces :]
    side = lax.axis_index("dom") % 2
    features, means = features_in_order(row_masks, kept_ref, got_ref), means_in_order(mean_ref)
    rows, hid = linear_ref.shape

    def fill_linear(source, weight_refs, more):
        step = min(256, rows)
        for at in range(0, rows, step):
            total = linear_ref[at : at + step] if more else jnp.zeros((step, hid), f32)
            for masks, weight_ref in zip(weight_masks, weight_refs):
                part = jnp.concatenate([source(mask, at, step) for mask in masks], axis=0)
                total = total + lax.dot_general(
                    part,
                    weight_ref[...].reshape(-1, hid),
                    first_with_first,
                    preferred_element_type=f32,
                )
            linear_ref[at : at + step] = total

    ready(0, 1, *range(4, 4 + 2 * pieces))

    @pl.when(side == 0)
    def _():
        fill_linear(features, mine_refs, False)

    @pl.when(side != 0)
    def _():
        fill_linear(features, other_refs, False)

    ready(2)

    @pl.when(side == 0)
    def _():
        fill_linear(means, other_refs, True)

    @pl.when(side != 0)
    def _():
        fill_linear(means, mine_refs, True)

    ready(3)
    step = min(128, rows)
    for at in range(0, rows, step):
        value, slope = gelu_pair(linear_ref[at : at + step])
        hidden_ref[at : at + step] = value.astype(bf16)
        grad_ref[at : at + step] = (cot_ref[at : at + step].astype(f32) * slope).astype(bf16)
    fill_sums(1, features, means, grad_ref, sums_ref)


def fill_sums(core, features, means, grad_ref, sums_ref):
    for i, source in enumerate((features, means)):
        part = jnp.concatenate(
            [source(mask) for mask in range(core, 2 * sums_ref.shape[0], 2)], axis=0
        )
        sums = jnp.dot(part, grad_ref[...], preferred_element_type=f32)
        sums_ref[:, i] = sums.astype(sums_ref.dtype).reshape(sums_ref[:, i].shape)


def kept_kernel(row_masks, kept_ref, got_ref, mean_ref, grad_ref, sums_ref):
    features, means = features_in_order(row_masks, kept_ref, got_ref), means_in_order(mean_ref)
    fill_sums(0, features, means, grad_ref, sums_ref)


def first_kernel(kept_ref, got_ref, own_ref, own_sent_ref, neigh_ref, neigh_sent_ref):
    for at in range(kept_ref.shape[0]):
        far, a, b = at // 4, at // 2 % 2, at % 2
        own = kept_ref[at, 0] + got_ref[at, 0].astype(f32)
        neigh = kept_ref[at, 1] + got_ref[at, 1].astype(f32)
        if b == 0:
            own_ref[far, a] = own
        else:
            own_sent_ref[far, a] = own.astype(bf16)
        if a == 0:
            neigh_ref[far, b] = neigh
        else:
            neigh_sent_ref[far, b] = neigh.astype(bf16)


def second_kernel(kept_ref, got_ref, out_ref, sent_ref):
    for far in range(kept_ref.shape[0]):
        total = kept_ref[far] + got_ref[far].astype(f32)
        out_ref[far] = total[0]
        sent_ref[far] = total[1].astype(bf16)


def third_kernel(own_ref, own_got_ref, neigh_ref, neigh_got_ref, out_ref, sent_ref):
    half = out_ref.shape[0]
    for i in range(half):
        for at, ref in ((i, out_ref), (half + i, sent_ref)):
            ref[i, 0] = (own_ref[at] + own_got_ref[at].astype(f32)).astype(ref.dtype)
            ref[i, 1] = (neigh_ref[at] + neigh_got_ref[at].astype(f32)).astype(ref.dtype)


def halving_kernel(kept_ref, got_ref, out_ref, sent_ref):
    half = out_ref.shape[0]
    for i in range(half):
        for at, ref in ((i, out_ref), (half + i, sent_ref)):
            ref[i] = (kept_ref[at] + got_ref[at].astype(f32)).astype(ref.dtype)


def round_sum_kernel(kept_ref, got_ref, out_ref):
    out_ref[...] = (kept_ref[...].astype(f32) + got_ref[...].astype(f32)).astype(out_ref.dtype)


def last_sum_kernel(kept_ref, got_ref, own_ref, neigh_ref):
    total = kept_ref[...].astype(f32) + got_ref[...].astype(f32)
    own_ref[...] = total[0, 0]
    neigh_ref[...] = total[0, 1]


def sum_gradients(kept, got):
    feat, dom = lax.axis_size("feat"), lax.axis_size("dom")
    depth, hid = kept.shape[2:]
    far = feat // 8

    def pair(*lead):
        shape = (*lead, depth, hid)
        return [jax.ShapeDtypeStruct(shape, f32), jax.ShapeDtypeStruct(shape, bf16)]

    own, own_sent, neigh, neigh_sent = local_call(
        first_kernel, "first_sum", pair(far, 2) + pair(far, 2), (kept, got)
    )
    own_got, neigh_got = flip("feat", 2)(own_sent), flip("feat", 4)(neigh_sent)
    own, own_sent = local_call(second_kernel, "own_sum", pair(far), (own, own_got))
    own_got = flip("feat", 4)(own_sent)
    neigh, neigh_sent = local_call(second_kernel, "neigh_sum", pair(far), (neigh, neigh_got))
    neigh_got = flip("feat", 2)(neigh_sent)
    half = far // 2
    kept, sent = local_call(
        third_kernel, "third_sum", pair(half, 2), (own, own_got, neigh, neigh_got)
    )
    got = flip("feat", half * 8)(sent)
    while half > 1:
        half //= 2
        kept, sent = local_call(halving_kernel, "halving", pair(half, 2), (kept, got))
        got = flip("feat", half * 8)(sent)
    rounded = jax.ShapeDtypeStruct(kept.shape, bf16)
    for bit in bits_of(dom):
        (kept,) = local_call(round_sum_kernel, "rounded_sum", [rounded], (kept, got))
        got = flip("dom", bit)(kept)
    out = jax.ShapeDtypeStruct((depth, hid), f32)
    return local_call(last_sum_kernel, "last_sum", [out, out], (kept, got))


def on_device(
    features,
    self_weight,
    neighbour_weight,
    cotangent,
    send_rows,
    send_count,
    tile_source,
    tile_kind,
    tile_patterns,
):
    feat, dom = lax.axis_size("feat"), lax.axis_size("dom")
    count, depth = features.shape
    rows = count // feat
    hid = self_weight.shape[1]
    columns = features.T
    quarters, below = 4, feat // 4
    row_bits = list(reversed(bits_of(below)))
    picked, weight, across, *cuts = open_exchange(
        send_count, columns, self_weight, neighbour_weight, send_rows, quarters
    )
    came = flip("feat", row_bits[0])(across)
    weight = gathered([weight] + [flip("feat", i * below)(weight) for i in range(1, quarters)])
    near = [cuts[0]] + [flip("feat", i * below)(cuts[i]) for i in range(1, quarters)]
    far = [came[0:1]] + [flip("feat", i * below)(came[i : i + 1]) for i in range(1, quarters)]
    row_masks = [i * below for i in range(quarters)]
    pieces, weight_masks = [weight], [list(row_masks)]
    row_masks = row_masks + flipped(row_masks, row_bits[0])
    for bit in row_bits[:-1]:
        pieces = pieces + [flip("feat", bit)(p) for p in pieces]
        weight_masks = weight_masks + [flipped(m, bit) for m in weight_masks]
    if dom == 2:
        halo = flip("dom", 1)(picked)
    else:
        halo = lax.all_to_all(picked, "dom", 1, 1, tiled=True)
    halo, _, _ = lax.optimization_barrier((halo, came, pieces))
    means = neighbour_means(
        tile_source[0].T, tile_kind[0].T, send_count, columns, halo, send_rows, tile_patterns, feat
    )
    held = lax.optimization_barrier((means, near, far, pieces))
    means, near, far, pieces = held
    own_mean = lax.all_to_all(means, "feat", 0, 0, tiled=True)
    others = [flip("dom", 1)(p) for p in pieces]
    parts, width = [*near, *far], came.shape[2]
    for bit in row_bits[1:]:
        sent, kept = cut_rows(bit, parts, width)
        parts, width = [kept, flip("feat", bit)(sent)], width // 2
        row_masks = row_masks + flipped(row_masks, bit)
    pieces = pieces + [flip("feat", 1)(p) for p in pieces]
    others = others + [flip("feat", 1)(p) for p in others]
    weight_masks = weight_masks + [flipped(m, 1) for m in weight_masks]
    sums = (feat // 2, 2, depth, hid)
    square = jax.ShapeDtypeStruct((rows, hid), bf16)
    hidden, grad_linear, sent = local_call(
        functools.partial(forward_kernel, row_masks, weight_masks),
        "forward",
        [square, square, jax.ShapeDtypeStruct(sums, bf16)],
        (*parts, own_mean, cotangent, *pieces, *others),
        scratch=[pltpu.VMEM((rows, hid), f32)],
        lazy=True,
    )
    got = flip("feat", 1)(sent)
    (kept,) = local_call(
        functools.partial(kept_kernel, row_masks),
        "kept_gradients",
        [jax.ShapeDtypeStruct(sums, f32)],
        (*parts, own_mean, grad_linear),
    )
    grad_self, grad_neighbour = sum_gradients(kept, got)
    return (hidden, grad_self, grad_neighbour)


def solution(mesh):
    placed = (
        P("dom", "feat"),
        P("feat", None),
        P("feat", None),
        P(("dom", "feat"), None),
        P(),
        P(),
        P("dom", None, None),
        P("dom", None, None),
        P(),
    )
    return jax.shard_map(
        on_device,
        mesh=mesh,
        in_specs=placed,
        out_specs=(P(("dom", "feat"), None), P("feat", None), P("feat", None)),
        check_vma=False,
    )
```

time: 120 us -> 113 us (0.942)
  waiting for transfers between devices: 53.6 us -> 43.9 us
  starting transfers between devices: 30.7 us -> 39 us
  local copies, waits for them, and re-layouts: 10.6 us -> 5.82 us
  other arithmetic: 3.22 us -> 0 us
  Pallas kernels: 20.8 us -> 23.4 us
    ppermute x10 -> x19, waiting for transfers between devices: 33 us -> 20 us  [the longest x2 9.06 us: on_device(): others = [flip('dom', 1)(p) for p in pieces]]
    all_to_all x1, waiting for transfers between devices: 0.01 us -> 7.03 us  [on_device(): own_mean = lax.all_to_all(means, 'feat', 0, 0, tiled=True)]
    ppermute x10 -> x19, starting transfers between devices: 17.4 us -> 21.9 us  [the longest x3 4.88 us: on_device(): flip('feat', i * below)(cuts[i])]
    unnamed x31 -> x42, local copies, waits for them, and re-layouts: 8.93 us -> 5.14 us
    ppermute x1, waiting for transfers between devices: 6.24 us -> 3.6 us  [sum_gradients(): flip('feat', 2)(own_sent)]
    pallas_call x13 -> x12, Pallas kernels: 20.8 us -> 23.4 us  [local_call(): pl.pallas_call(kernel, out_shape=outs, in_specs=in_specs, out_specs=[whol...]
    ppermute x1, starting transfers between devices: 0.8 us -> 3.2 us  [sum_gradients(): own_got = flip('feat', 4)(own_sent)]
    ppermute x1, starting transfers between devices: 0.63 us -> 2.89 us  [sum_gradients(): flip('feat', 4)(neigh_sent)]
  transfers between devices with their start and end apart: 18 -> 27, of which waited for: 10 -> 13; matrix products, arithmetic and copies ran while one was open for 3% -> 1% of each run, Pallas kernels for 13% -> 12%
where the time goes in v3:
time: 113 us
  waiting for transfers between devices  43.9 us (39%)
  starting transfers between devices  39 us (35%)
  Pallas kernels  23.4 us (21%)
  local copies, waits for them, and re-layouts  5.82 us (5%)
    pallas_call x12, Pallas kernels, local_call(): pl.pallas_call(kernel, out_shape=outs, in_specs=in_specs, out_specs=[whol...  23.4 us
    ppermute x2, waiting for transfers between devices, on_device(): others = [flip('dom', 1)(p) for p in pieces]  9.06 us
    all_to_all x1, waiting for transfers between devices, on_device(): own_mean = lax.all_to_all(means, 'feat', 0, 0, tiled=True)  7.03 us
    ppermute x1, waiting for transfers between devices, sum_gradients(): got = flip('feat', half * 8)(sent)  5.51 us
    unnamed x42, local copies, waits for them, and re-layouts  5.14 us
    ppermute x3, starting transfers between devices, on_device(): flip('feat', i * below)(cuts[i])  4.88 us
    ppermute x3, waiting for transfers between devices, on_device(): flip('feat', i * below)(weight)  4.86 us
    ppermute x3, starting transfers between devices, on_device(): flip('feat', i * below)(came[i:i + 1])  4.72 us
  transfers between devices with their start and end apart: 27, of which 13 were waited for; matrix products, arithmetic and copies ran while one was open for 1% of the time, Pallas kernels for 12%

profile of v3, /device:TPU:0, one launch (start us, length us, event | category | flops | bytes accessed | tf_op | source)
XLA Modules:
  0.0 113.0 jit_solution(5824643859680769241)
XLA Ops:
  0.6 3.0 %open_exchange.1 = (bf16[64,256]{1,0:T(8,128)(2,1)}, bf16[1,64,512]{2,1,0:T(8,128)(2,1)}, bf16[4,64,1024]{2,1,0:T(8,128)(2,1)}, bf16[1,64,1024]{2,1,0:T(8,128)(2...) custom-call(s32[2,2]{1,0:T(2,128)} %refs_2_.3, ...), custom_call_target="tpu_custom_call" | custom-call | tf_op jit(solution)/shard_map/open_exchange/pallas_call | solution.py:70
  3.6 3.0 %collective-permute-start.1 = (bf16[4,64,1024]{2,1,0:T(8,128)(2,1)}, bf16[4,64,1024]{2,1,0:T(8,128)(2,1)S(1)}, u32[]{:S(2)}, u32[]{:S(2)}) collective-permute-start(bf16[4,64,1024]{2,1,0:T(8,128)(2,1)} %get-tuple-element.40), channel_id=1, source_target_pairs={{0,4},{2,6},{4,0},{6,2},{8,12},{10,14},{12,8},{14,10},{16,20},{18,... | collective-permute-start | bytes 1572872 | tf_op jit(solution)/shard_map/ppermute | solution.py:428
  6.6 3.6 %collective-permute-start.4 = (bf16[1,64,512]{2,1,0:T(8,128)(2,1)}, bf16[1,64,512]{2,1,0:T(8,128)(2,1)S(1)}, u32[]{:S(2)}, u32[]{:S(2)}) collective-permute-start(bf16[1,64,512]{2,1,0:T(8,128)(2,1)} %get-tuple-element.41.refs_0_), channel_id=1, source_target_pairs={{0,24},{2,26},{4,28},{6,30},{8,16},{10,18},{12,20},{14,22},{16,8},... | collective-permute-start | bytes 196616 | tf_op jit(solution)/shard_map/ppermute | solution.py:429
  10.2 0.8 collective-permute-start.2
  11.0 2.7 %collective-permute-done.4.refs_3_ = bf16[1,64,512]{2,1,0:T(8,128)(2,1)S(1)} collective-permute-done((bf16[1,64,512]{2,1,0:T(8,128)(2,1)}, bf16[1,64,512]{2,1,0:T(8,128)(2,1)S(1)}, u32[]{:S(2)}, u32[]{:S(2)}) %collective-permute-start.4) | collective-permute-done | bytes 65568 | tf_op jit(solution)/shard_map/ppermute | solution.py:429
  13.7 2.1 %collective-permute-done.3.refs_2_ = bf16[1,64,512]{2,1,0:T(8,128)(2,1)S(1)} collective-permute-done((bf16[1,64,512]{2,1,0:T(8,128)(2,1)}, bf16[1,64,512]{2,1,0:T(8,128)(2,1)S(1)}, u32[]{:S(2)}, u32[]{:S(2)}) %collective-permute-start.3) | collective-permute-done | bytes 65568 | tf_op jit(solution)/shard_map/ppermute | solution.py:429
  15.9 0.8 copy-done.7
  16.8 0.5 collective-permute-start.5
  17.3 1.6 %collective-permute-start = (bf16[64,256]{1,0:T(8,128)(2,1)}, bf16[64,256]{1,0:T(8,128)(2,1)S(1)}, u32[]{:S(2)}, u32[]{:S(2)}) collective-permute-start(bf16[64,256]{1,0:T(8,128)(2,1)} %get-tuple-element.39), channel_id=1, source_target_pairs={{0,1},{1,0},{2,3},{3,2},{4,5},{5,4},{6,7},{7,6},{8,9},{9,8},{10,11... | collective-permute-start | bytes 98312 | tf_op jit(solution)/shard_map/ppermute | solution.py:439
  18.9 1.0 collective-permute-start.6
  19.8 2.1 %collective-permute-start.7 = (bf16[1,64,1024]{2,1,0:T(8,128)(2,1)}, bf16[1,64,1024]{2,1,0:T(8,128)(2,1)S(1)}, u32[]{:S(2)}, u32[]{:S(2)}) collective-permute-start(bf16[1,64,1024]{2,1,0:T(8,128)(2,1)} %get-tuple-element.45), channel_id=1, source_target_pairs={{0,16},{2,18},{4,20},{6,22},{8,24},{10,26},{12,28},{14,30},{16,0},... | collective-permute-start | bytes 393224 | tf_op jit(solution)/shard_map/ppermute | solution.py:430
  22.0 1.8 %collective-permute-start.8 = (bf16[1,64,1024]{2,1,0:T(8,128)(2,1)}, bf16[1,64,1024]{2,1,0:T(8,128)(2,1)S(1)}, u32[]{:S(2)}, u32[]{:S(2)}) collective-permute-start(bf16[1,64,1024]{2,1,0:T(8,128)(2,1)} %get-tuple-element.46), channel_id=1, source_target_pairs={{0,24},{2,26},{4,28},{6,30},{8,16},{10,18},{12,20},{14,22},{16,8},... | collective-permute-start | bytes 393224 | tf_op jit(solution)/shard_map/ppermute | solution.py:430
  23.8 0.7 fusion
  24.4 2.0 %collective-permute-start.11 = (bf16[1,64,1024]{2,1,0:T(8,128)(2,1)S(1)}, bf16[1,64,1024]{2,1,0:T(8,128)(2,1)S(1)}, u32[]{:S(2)}, u32[]{:S(2)}) collective-permute-start(bf16[1,64,1024]{2,1,0:T(8,128)(2,1)S(1)} %get-tuple-element.75), channel_id=1, source_target_pairs={{0,24},{2,26},{4,28},{6,30},{8,16},{10,18},{12,20},{14,22},{16,8},... | collective-permute-start | bytes 393224 | tf_op jit(solution)/shard_map/ppermute | solution.py:431
  26.5 0.8 collective-permute-start.10
  27.3 1.9 %collective-permute-start.9 = (bf16[1,64,1024]{2,1,0:T(8,128)(2,1)S(1)}, bf16[1,64,1024]{2,1,0:T(8,128)(2,1)S(1)}, u32[]{:S(2)}, u32[]{:S(2)}) collective-permute-start(bf16[1,64,1024]{2,1,0:T(8,128)(2,1)S(1)} %get-tuple-element.77), channel_id=1, source_target_pairs={{0,8},{2,10},{4,12},{6,14},{8,0},{10,2},{12,4},{14,6},{16,24},{18,... | collective-permute-start | bytes 393224 | tf_op jit(solution)/shard_map/ppermute | solution.py:431
  29.2 10.2 %neighbour_means.1 = bf16[16,64,512]{2,1,0:T(8,128)(2,1)} custom-call(s32[8,64]{1,0:T(8,128)} %bitcast.9, s32[8,64]{1,0:T(8,128)} %bitcast.10, s32[2,2]{1,0:T(2,128)} %refs_2_.3, bf16[64,8192]{1,0:T(8,128)(2,1)} %bitcast.8, bf16[64,256]{1,0:T(8,128)(2,1)} %copy-done.20, s32[2,2,256]{2,1,0:T(2,128)} %refs_5_.1, bf16[64,128,128]{2,1,0:T(8,128)(2,1)} %refs_6_.1), custom_call_target="tpu_custom_call" | custom-call | tf_op jit(solution)/shard_map/neighbour_means/pallas_call | solution.py:70
  39.5 4.5 %collective-permute-done.10.refs_6_ = bf16[1,64,1024]{2,1,0:T(8,128)(2,1)S(1)} collective-permute-done((bf16[1,64,1024]{2,1,0:T(8,128)(2,1)S(1)}, bf16[1,64,1024]{2,1,0:T(8,128)(2,1)S(1)}, u32[]{:S(2)}, u32[]{:S(2)}) %collective-permute-start.10) | collective-permute-done | bytes 131104 | tf_op jit(solution)/shard_map/ppermute | solution.py:431
  43.9 4.2 %all-to-all-start = ((bf16[16,64,512]{2,1,0:T(8,128)(2,1)}), bf16[16,64,512]{2,1,0:T(8,128)(2,1)S(1)}, u32[]{:S(2)}, u32[]{:S(2)}) async-start(bf16[16,64,512]{2,1,0:T(8,128)(2,1)} %neighbour_means.1), calls=%async_computation | async-start | bytes 2097152 | tf_op jit(solution)/shard_map/all_to_all | solution.py:448
  48.1 0.6 collective-permute-start.15
  48.7 2.4 %cut_rows.1 = (bf16[8,64,512]{2,1,0:T(8,128)(2,1)}, bf16[8,64,512]{2,1,0:T(8,128)(2,1)}) custom-call(bf16[1,64,1024]{2,1,0:T(8,128)(2,1)} %get-tuple-element.47.refs_0_, bf16[1,64,1024]{2,1,0:T(8,128)(2,1)} %copy-done.14, bf16[1,64,1024]{2,1,0:T(8,128)(2,1)} %copy-done.15, bf16[1,64,1024]{2,1,0:T(8,128)(2,1)} %copy-done.16, ...), custom_call_target="tpu_custom_call" | custom-call | tf_op jit(solution)/shard_map/cut_rows/pallas_call | solution.py:70
  51.2 1.5 %collective-permute-start.16 = (bf16[4,64,512]{2,1,0:T(8,128)(2,1)S(1)}, bf16[4,64,512]{2,1,0:T(8,128)(2,1)S(1)}, u32[]{:S(2)}, u32[]{:S(2)}) collective-permute-start(bf16[4,64,512]{2,1,0:T(8,128)(2,1)S(1)} %collective-permute-done.5.refs_5_), channel_id=1, source_target_pairs={{0,1},{1,0},{2,3},{3,2},{4,5},{5,4},{6,7},{7,6},{8,9},{9,8},{10,11... | collective-permute-start | bytes 786440 | tf_op jit(solution)/shard_map/ppermute | solution.py:449
  52.8 0.2 collective-permute-start.13
  52.9 0.3 collective-permute-start.14
  53.3 4.0 %collective-permute-done.15.refs_8_ = bf16[4,64,512]{2,1,0:T(8,128)(2,1)S(1)} collective-permute-done((bf16[4,64,512]{2,1,0:T(8,128)(2,1)S(1)}, bf16[4,64,512]{2,1,0:T(8,128)(2,1)S(1)}, u32[]{:S(2)}, u32[]{:S(2)}) %collective-permute-start.15) | collective-permute-done | bytes 262176 | tf_op jit(solution)/shard_map/ppermute | solution.py:449
  57.3 5.0 %collective-permute-done.16.refs_9_ = bf16[4,64,512]{2,1,0:T(8,128)(2,1)S(1)} collective-permute-done((bf16[4,64,512]{2,1,0:T(8,128)(2,1)S(1)}, bf16[4,64,512]{2,1,0:T(8,128)(2,1)S(1)}, u32[]{:S(2)}, u32[]{:S(2)}) %collective-permute-start.16) | collective-permute-done | bytes 262176 | tf_op jit(solution)/shard_map/ppermute | solution.py:449
  62.4 1.6 %collective-permute-done.18.refs_11_ = bf16[4,64,512]{2,1,0:T(8,128)(2,1)} collective-permute-done((bf16[4,64,512]{2,1,0:T(8,128)(2,1)S(1)}, bf16[4,64,512]{2,1,0:T(8,128)(2,1)}, u32[]{:S(2)}, u32[]{:S(2)}) %collective-permute-start.18) | collective-permute-done | bytes 262176 | tf_op jit(solution)/shard_map/ppermute | solution.py:456
  64.0 7.0 %all-to-all-done.refs_2_.mean_ref = bf16[16,64,512]{2,1,0:T(8,128)(2,1)S(1)} async-done(((bf16[16,64,512]{2,1,0:T(8,128)(2,1)}), bf16[16,64,512]{2,1,0:T(8,128)(2,1)S(1)}, u32[]{:S(2)}, u32[]{:S(2)}) %all-to-all-start) | async-done | bytes 1048608 | tf_op jit(solution)/shard_map/all_to_all | solution.py:448
  71.1 0.9 copy-done
  72.0 6.0 %forward.1 = (bf16[512,512]{1,0:T(8,128)(2,1)}, bf16[512,512]{1,0:T(8,128)(2,1)}, bf16[8,2,64,512]{3,2,1,0:T(8,128)(2,1)}) custom-call(bf16[8,64,512]{2,1,0:T(8,128)(2,1)} %get-tuple-element.55.refs_0_.kept_ref, bf16[8,64,512]{2,1,0:T(8,128)(2,1)} %copy-done.3, bf16[16,64,512]{2,1,0:T(8,128)(2,1)} %copy-done, bf16[512,512]{1,0:T(8,128)(2,1)} %refs_3_.3, ...), custom_call_target="tpu_custom_call" | custom-call | tf_op jit(solution)/shard_map/forward/pallas_call | solution.py:70
  78.1 0.7 collective-permute-start.19
  78.7 1.2 %copy-done.1 = bf16[16,64,512]{2,1,0:T(8,128)(2,1)S(1)} copy-done((bf16[16,64,512]{2,1,0:T(8,128)(2,1)S(1)}, bf16[16,64,512]{2,1,0:T(8,128)(2,1)}, u32[]{:S(2)}) %copy-start.1) | copy-done | bytes 1048600
  80.0 1.0 copy-done.4
  81.0 1.0 copy-done.6
  82.1 0.7 kept_gradients.1.kept_ref
  82.8 0.2 first_sum.1
  82.9 2.0 %collective-permute-start.20 = (bf16[2,2,64,512]{3,2,1,0:T(8,128)(2,1)S(1)}, bf16[2,2,64,512]{3,2,1,0:T(8,128)(2,1)S(1)}, u32[]{:S(2)}, u32[]{:S(2)}) collective-permute-start(bf16[2,2,64,512]{3,2,1,0:T(8,128)(2,1)S(1)} %get-tuple-element.64), channel_id=1, source_target_pairs={{0,4},{2,6},{4,0},{6,2},{8,12},{10,14},{12,8},{14,10},{16,20},{18,... | collective-permute-start | bytes 786440 | tf_op jit(solution)/shard_map/ppermute | solution.py:385
  85.0 2.9 %collective-permute-start.22 = (bf16[2,2,64,512]{3,2,1,0:T(8,128)(2,1)S(1)}, bf16[2,2,64,512]{3,2,1,0:T(8,128)(2,1)S(1)}, u32[]{:S(2)}, u32[]{:S(2)}) collective-permute-start(bf16[2,2,64,512]{3,2,1,0:T(8,128)(2,1)S(1)} %get-tuple-element.68), channel_id=1, source_target_pairs={{0,8},{2,10},{4,12},{6,14},{8,0},{10,2},{12,4},{14,6},{16,24},{18,... | collective-permute-start | bytes 786440 | tf_op jit(solution)/shard_map/ppermute | solution.py:385
  87.9 3.6 %collective-permute-done.20.got_ref = bf16[2,2,64,512]{3,2,1,0:T(8,128)(2,1)S(1)} collective-permute-done((bf16[2,2,64,512]{3,2,1,0:T(8,128)(2,1)S(1)}, bf16[2,2,64,512]{3,2,1,0:T(8,128)(2,1)S(1)}, u32[]{:S(2)}, u32[]{:S(2)}) %collective-permute-start.20) | collective-permute-done | bytes 262176 | tf_op jit(solution)/shard_map/ppermute | solution.py:385
  91.5 3.2 %collective-permute-start.21 = (bf16[2,64,512]{2,1,0:T(8,128)(2,1)S(1)}, bf16[2,64,512]{2,1,0:T(8,128)(2,1)S(1)}, u32[]{:S(2)}, u32[]{:S(2)}) collective-permute-start(bf16[2,64,512]{2,1,0:T(8,128)(2,1)S(1)} %get-tuple-element.66), channel_id=1, source_target_pairs={{0,8},{2,10},{4,12},{6,14},{8,0},{10,2},{12,4},{14,6},{16,24},{18,... | collective-permute-start | bytes 393224 | tf_op jit(solution)/shard_map/ppermute | solution.py:387
  94.8 1.8 %collective-permute-start.23 = (bf16[2,64,512]{2,1,0:T(8,128)(2,1)S(1)}, bf16[2,64,512]{2,1,0:T(8,128)(2,1)S(1)}, u32[]{:S(2)}, u32[]{:S(2)}) collective-permute-start(bf16[2,64,512]{2,1,0:T(8,128)(2,1)S(1)} %get-tuple-element.70), channel_id=1, source_target_pairs={{0,4},{2,6},{4,0},{6,2},{8,12},{10,14},{12,8},{14,10},{16,20},{18,... | collective-permute-start | bytes 393224 | tf_op jit(solution)/shard_map/ppermute | solution.py:389
  96.5 1.1 collective-permute-done.21.own_got_ref
  97.7 2.1 %collective-permute-done.23.neigh_got_ref = bf16[2,64,512]{2,1,0:T(8,128)(2,1)S(1)} collective-permute-done((bf16[2,64,512]{2,1,0:T(8,128)(2,1)S(1)}, bf16[2,64,512]{2,1,0:T(8,128)(2,1)S(1)}, u32[]{:S(2)}, u32[]{:S(2)}) %collective-permute-start.23) | collective-permute-done | bytes 131104 | tf_op jit(solution)/shard_map/ppermute | solution.py:389
  99.9 1.8 %collective-permute-start.24 = (bf16[1,2,64,512]{3,2,1,0:T(8,128)(2,1)S(1)}, bf16[1,2,64,512]{3,2,1,0:T(8,128)(2,1)S(1)}, u32[]{:S(2)}, u32[]{:S(2)}) collective-permute-start(bf16[1,2,64,512]{3,2,1,0:T(8,128)(2,1)S(1)} %get-tuple-element.72), channel_id=1, source_target_pairs={{0,16},{2,18},{4,20},{6,22},{8,24},{10,26},{12,28},{14,30},{16,0},... | collective-permute-start | bytes 393224 | tf_op jit(solution)/shard_map/ppermute | solution.py:394
  101.7 5.5 %collective-permute-done.24.got_ref = bf16[1,2,64,512]{3,2,1,0:T(8,128)(2,1)S(1)} collective-permute-done((bf16[1,2,64,512]{3,2,1,0:T(8,128)(2,1)S(1)}, bf16[1,2,64,512]{3,2,1,0:T(8,128)(2,1)S(1)}, u32[]{:S(2)}, u32[]{:S(2)}) %collective-permute-start.24) | collective-permute-done | bytes 131104 | tf_op jit(solution)/shard_map/ppermute | solution.py:394
  107.2 0.6 collective-permute-start.25
  107.8 4.5 %collective-permute-done.25.got_ref = bf16[1,2,64,512]{3,2,1,0:T(8,128)(2,1)S(1)} collective-permute-done((bf16[1,2,64,512]{3,2,1,0:T(8,128)(2,1)S(1)}, bf16[1,2,64,512]{3,2,1,0:T(8,128)(2,1)S(1)}, u32[]{:S(2)}, u32[]{:S(2)}) %collective-permute-start.25) | collective-permute-done | bytes 131104 | tf_op jit(solution)/shard_map/ppermute | solution.py:402
  112.3 0.7 last_sum.1
  (61 shorter events, 0.5 us)
Async XLA Ops:
  3.6 18.3 %collective-permute-start.1 = (bf16[4,64,1024]{2,1,0:T(8,128)(2,1)}, bf16[4,64,1024]{2,1,0:T(8,128)(2,1)S(1)}, u32[]{:S(2)}, u32[]{:S(2)}) collective-permute-start(bf16[4,64,1024]{2,1,0:T(8,128)(2,1)} %get-tuple-element.40), channel_id=1, source_target_pairs={{0,4},{2,6},{4,0},{6,2},{8,12},{10,14},{12,8},{14,10},{16,20},{18,... | collective-permute-start | bytes 1572872 | tf_op jit(solution)/shard_map/ppermute | solution.py:428
  6.6 7.1 %collective-permute-start.4 = (bf16[1,64,512]{2,1,0:T(8,128)(2,1)}, bf16[1,64,512]{2,1,0:T(8,128)(2,1)S(1)}, u32[]{:S(2)}, u32[]{:S(2)}) collective-permute-start(bf16[1,64,512]{2,1,0:T(8,128)(2,1)} %get-tuple-element.41.refs_0_), channel_id=1, source_target_pairs={{0,24},{2,26},{4,28},{6,30},{8,16},{10,18},{12,20},{14,22},{16,8},... | collective-permute-start | bytes 196616 | tf_op jit(solution)/shard_map/ppermute | solution.py:429
  10.2 5.6 %collective-permute-start.3 = (bf16[1,64,512]{2,1,0:T(8,128)(2,1)}, bf16[1,64,512]{2,1,0:T(8,128)(2,1)S(1)}, u32[]{:S(2)}, u32[]{:S(2)}) collective-permute-start(bf16[1,64,512]{2,1,0:T(8,128)(2,1)} %get-tuple-element.41.refs_0_), channel_id=1, source_target_pairs={{0,16},{2,18},{4,20},{6,22},{8,24},{10,26},{12,28},{14,30},{16,0},... | collective-permute-start | bytes 196616 | tf_op jit(solution)/shard_map/ppermute | solution.py:429
  10.2 5.6 %collective-permute-start.2 = (bf16[1,64,512]{2,1,0:T(8,128)(2,1)}, bf16[1,64,512]{2,1,0:T(8,128)(2,1)S(1)}, u32[]{:S(2)}, u32[]{:S(2)}) collective-permute-start(bf16[1,64,512]{2,1,0:T(8,128)(2,1)} %get-tuple-element.41.refs_0_), channel_id=1, source_target_pairs={{0,8},{2,10},{4,12},{6,14},{8,0},{10,2},{12,4},{14,6},{16,24},{18,... | collective-permute-start | bytes 196616 | tf_op jit(solution)/shard_map/ppermute | solution.py:429
  15.9 0.8 copy-start.7
  16.7 36.0 %copy-start.5 = (bf16[4,64,512]{2,1,0:T(8,128)(2,1)}, bf16[4,64,512]{2,1,0:T(8,128)(2,1)S(1)}, u32[]{:S(2)}) copy-start(bf16[4,64,512]{2,1,0:T(8,128)(2,1)S(1)} %gathered.1.refs_4_) | copy-start | bytes 786436
  16.8 10.5 %collective-permute-start.5 = (bf16[4,64,512]{2,1,0:T(8,128)(2,1)S(1)}, bf16[4,64,512]{2,1,0:T(8,128)(2,1)S(1)}, u32[]{:S(2)}, u32[]{:S(2)}) collective-permute-start(bf16[4,64,512]{2,1,0:T(8,128)(2,1)S(1)} %gathered.1.refs_4_), channel_id=1, source_target_pairs={{0,4},{2,6},{4,0},{6,2},{8,12},{10,14},{12,8},{14,10},{16,20},{18,... | collective-permute-start | bytes 786440 | tf_op jit(solution)/shard_map/ppermute | solution.py:436
  17.3 7.2 %collective-permute-start = (bf16[64,256]{1,0:T(8,128)(2,1)}, bf16[64,256]{1,0:T(8,128)(2,1)S(1)}, u32[]{:S(2)}, u32[]{:S(2)}) collective-permute-start(bf16[64,256]{1,0:T(8,128)(2,1)} %get-tuple-element.39), channel_id=1, source_target_pairs={{0,1},{1,0},{2,3},{3,2},{4,5},{5,4},{6,7},{7,6},{8,9},{9,8},{10,11... | collective-permute-start | bytes 98312 | tf_op jit(solution)/shard_map/ppermute | solution.py:439
  18.9 7.6 %collective-permute-start.6 = (bf16[1,64,1024]{2,1,0:T(8,128)(2,1)}, bf16[1,64,1024]{2,1,0:T(8,128)(2,1)S(1)}, u32[]{:S(2)}, u32[]{:S(2)}) collective-permute-start(bf16[1,64,1024]{2,1,0:T(8,128)(2,1)} %get-tuple-element.44), channel_id=1, source_target_pairs={{0,8},{2,10},{4,12},{6,14},{8,0},{10,2},{12,4},{14,6},{16,24},{18,... | collective-permute-start | bytes 393224 | tf_op jit(solution)/shard_map/ppermute | solution.py:430
  19.8 19.6 %collective-permute-start.7 = (bf16[1,64,1024]{2,1,0:T(8,128)(2,1)}, bf16[1,64,1024]{2,1,0:T(8,128)(2,1)S(1)}, u32[]{:S(2)}, u32[]{:S(2)}) collective-permute-start(bf16[1,64,1024]{2,1,0:T(8,128)(2,1)} %get-tuple-element.45), channel_id=1, source_target_pairs={{0,16},{2,18},{4,20},{6,22},{8,24},{10,26},{12,28},{14,30},{16,0},... | collective-permute-start | bytes 393224 | tf_op jit(solution)/shard_map/ppermute | solution.py:430
  22.0 17.5 %collective-permute-start.8 = (bf16[1,64,1024]{2,1,0:T(8,128)(2,1)}, bf16[1,64,1024]{2,1,0:T(8,128)(2,1)S(1)}, u32[]{:S(2)}, u32[]{:S(2)}) collective-permute-start(bf16[1,64,1024]{2,1,0:T(8,128)(2,1)} %get-tuple-element.46), channel_id=1, source_target_pairs={{0,24},{2,26},{4,28},{6,30},{8,16},{10,18},{12,20},{14,22},{16,8},... | collective-permute-start | bytes 393224 | tf_op jit(solution)/shard_map/ppermute | solution.py:430
  24.4 4.7 %copy-start.20 = (bf16[64,256]{1,0:T(8,128)(2,1)}, bf16[64,256]{1,0:T(8,128)(2,1)S(1)}, u32[]{:S(2)}) copy-start(bf16[64,256]{1,0:T(8,128)(2,1)S(1)} %collective-permute-done.refs_4_) | copy-start | bytes 98308
  24.4 15.0 %collective-permute-start.11 = (bf16[1,64,1024]{2,1,0:T(8,128)(2,1)S(1)}, bf16[1,64,1024]{2,1,0:T(8,128)(2,1)S(1)}, u32[]{:S(2)}, u32[]{:S(2)}) collective-permute-start(bf16[1,64,1024]{2,1,0:T(8,128)(2,1)S(1)} %get-tuple-element.75), channel_id=1, source_target_pairs={{0,24},{2,26},{4,28},{6,30},{8,16},{10,18},{12,20},{14,22},{16,8},... | collective-permute-start | bytes 393224 | tf_op jit(solution)/shard_map/ppermute | solution.py:431
  26.5 12.9 %copy-start.14 = (bf16[1,64,1024]{2,1,0:T(8,128)(2,1)}, bf16[1,64,1024]{2,1,0:T(8,128)(2,1)S(1)}, u32[]{:S(2)}) copy-start(bf16[1,64,1024]{2,1,0:T(8,128)(2,1)S(1)} %collective-permute-done.6.refs_1_) | copy-start | bytes 393220
  26.5 17.4 %collective-permute-start.10 = (bf16[1,64,1024]{2,1,0:T(8,128)(2,1)S(1)}, bf16[1,64,1024]{2,1,0:T(8,128)(2,1)S(1)}, u32[]{:S(2)}, u32[]{:S(2)}) collective-permute-start(bf16[1,64,1024]{2,1,0:T(8,128)(2,1)S(1)} %get-tuple-element.76), channel_id=1, source_target_pairs={{0,16},{2,18},{4,20},{6,22},{8,24},{10,26},{12,28},{14,30},{16,0},... | collective-permute-start | bytes 393224 | tf_op jit(solution)/shard_map/ppermute | solution.py:431
  27.2 25.7 %copy-start.8 = (bf16[4,64,512]{2,1,0:T(8,128)(2,1)}, bf16[4,64,512]{2,1,0:T(8,128)(2,1)S(1)}, u32[]{:S(2)}) copy-start(bf16[4,64,512]{2,1,0:T(8,128)(2,1)S(1)} %collective-permute-done.5.refs_5_) | copy-start | bytes 786436
  27.3 16.7 %collective-permute-start.9 = (bf16[1,64,1024]{2,1,0:T(8,128)(2,1)S(1)}, bf16[1,64,1024]{2,1,0:T(8,128)(2,1)S(1)}, u32[]{:S(2)}, u32[]{:S(2)}) collective-permute-start(bf16[1,64,1024]{2,1,0:T(8,128)(2,1)S(1)} %get-tuple-element.77), channel_id=1, source_target_pairs={{0,8},{2,10},{4,12},{6,14},{8,0},{10,2},{12,4},{14,6},{16,24},{18,... | collective-permute-start | bytes 393224 | tf_op jit(solution)/shard_map/ppermute | solution.py:431
  39.4 9.2 %copy-start.15 = (bf16[1,64,1024]{2,1,0:T(8,128)(2,1)}, bf16[1,64,1024]{2,1,0:T(8,128)(2,1)S(1)}, u32[]{:S(2)}) copy-start(bf16[1,64,1024]{2,1,0:T(8,128)(2,1)S(1)} %collective-permute-done.7.refs_2_) | copy-start | bytes 393220
  39.4 9.2 %copy-start.16 = (bf16[1,64,1024]{2,1,0:T(8,128)(2,1)}, bf16[1,64,1024]{2,1,0:T(8,128)(2,1)S(1)}, u32[]{:S(2)}) copy-start(bf16[1,64,1024]{2,1,0:T(8,128)(2,1)S(1)} %collective-permute-done.8.refs_3_) | copy-start | bytes 393220
  39.5 9.2 %copy-start.17 = (bf16[1,64,1024]{2,1,0:T(8,128)(2,1)}, bf16[1,64,1024]{2,1,0:T(8,128)(2,1)S(1)}, u32[]{:S(2)}) copy-start(bf16[1,64,1024]{2,1,0:T(8,128)(2,1)S(1)} %collective-permute-done.11.refs_7_) | copy-start | bytes 393220
  43.9 4.8 %copy-start.18 = (bf16[1,64,1024]{2,1,0:T(8,128)(2,1)}, bf16[1,64,1024]{2,1,0:T(8,128)(2,1)S(1)}, u32[]{:S(2)}) copy-start(bf16[1,64,1024]{2,1,0:T(8,128)(2,1)S(1)} %collective-permute-done.10.refs_6_) | copy-start | bytes 393220
  43.9 4.8 %copy-start.19 = (bf16[1,64,1024]{2,1,0:T(8,128)(2,1)}, bf16[1,64,1024]{2,1,0:T(8,128)(2,1)S(1)}, u32[]{:S(2)}) copy-start(bf16[1,64,1024]{2,1,0:T(8,128)(2,1)S(1)} %collective-permute-done.9.refs_5_) | copy-start | bytes 393220
  43.9 27.1 %all-to-all-start = ((bf16[16,64,512]{2,1,0:T(8,128)(2,1)}), bf16[16,64,512]{2,1,0:T(8,128)(2,1)S(1)}, u32[]{:S(2)}, u32[]{:S(2)}) async-start(bf16[16,64,512]{2,1,0:T(8,128)(2,1)} %neighbour_means.1), calls=%async_computation | async-start | bytes 2097152 | tf_op jit(solution)/shard_map/all_to_all | solution.py:448
  48.1 9.2 %collective-permute-start.15 = (bf16[4,64,512]{2,1,0:T(8,128)(2,1)S(1)}, bf16[4,64,512]{2,1,0:T(8,128)(2,1)S(1)}, u32[]{:S(2)}, u32[]{:S(2)}) collective-permute-start(bf16[4,64,512]{2,1,0:T(8,128)(2,1)S(1)} %gathered.1.refs_4_), channel_id=1, source_target_pairs={{0,1},{1,0},{2,3},{3,2},{4,5},{5,4},{6,7},{7,6},{8,9},{9,8},{10,11... | collective-permute-start | bytes 786440 | tf_op jit(solution)/shard_map/ppermute | solution.py:449
  51.1 11.3 %collective-permute-start.12 = (bf16[8,64,512]{2,1,0:T(8,128)(2,1)}, bf16[8,64,512]{2,1,0:T(8,128)(2,1)S(1)}, u32[]{:S(2)}, u32[]{:S(2)}) collective-permute-start(bf16[8,64,512]{2,1,0:T(8,128)(2,1)} %get-tuple-element.56), channel_id=1, source_target_pairs={{0,2},{2,0},{4,6},{6,4},{8,10},{10,8},{12,14},{14,12},{16,18},{18,... | collective-permute-start | bytes 1572872 | tf_op jit(solution)/shard_map/ppermute | solution.py:453
  51.2 11.1 %collective-permute-start.16 = (bf16[4,64,512]{2,1,0:T(8,128)(2,1)S(1)}, bf16[4,64,512]{2,1,0:T(8,128)(2,1)S(1)}, u32[]{:S(2)}, u32[]{:S(2)}) collective-permute-start(bf16[4,64,512]{2,1,0:T(8,128)(2,1)S(1)} %collective-permute-done.5.refs_5_), channel_id=1, source_target_pairs={{0,1},{1,0},{2,3},{3,2},{4,5},{5,4},{6,7},{7,6},{8,9},{9,8},{10,11... | collective-permute-start | bytes 786440 | tf_op jit(solution)/shard_map/ppermute | solution.py:449
  52.8 9.6 %collective-permute-start.13 = (bf16[4,64,512]{2,1,0:T(8,128)(2,1)S(1)}, bf16[4,64,512]{2,1,0:T(8,128)(2,1)S(1)}, u32[]{:S(2)}, u32[]{:S(2)}) collective-permute-start(bf16[4,64,512]{2,1,0:T(8,128)(2,1)S(1)} %gathered.1.refs_4_), channel_id=1, source_target_pairs={{0,2},{2,0},{4,6},{6,4},{8,10},{10,8},{12,14},{14,12},{16,18},{18,... | collective-permute-start | bytes 786440 | tf_op jit(solution)/shard_map/ppermute | solution.py:455
  52.9 9.4 %collective-permute-start.14 = (bf16[4,64,512]{2,1,0:T(8,128)(2,1)S(1)}, bf16[4,64,512]{2,1,0:T(8,128)(2,1)S(1)}, u32[]{:S(2)}, u32[]{:S(2)}) collective-permute-start(bf16[4,64,512]{2,1,0:T(8,128)(2,1)S(1)} %collective-permute-done.5.refs_5_), channel_id=1, source_target_pairs={{0,2},{2,0},{4,6},{6,4},{8,10},{10,8},{12,14},{14,12},{16,18},{18,... | collective-permute-start | bytes 786440 | tf_op jit(solution)/shard_map/ppermute | solution.py:455
  57.3 13.8 %copy-start.9 = (bf16[4,64,512]{2,1,0:T(8,128)(2,1)}, bf16[4,64,512]{2,1,0:T(8,128)(2,1)S(1)}, u32[]{:S(2)}) copy-start(bf16[4,64,512]{2,1,0:T(8,128)(2,1)S(1)} %collective-permute-done.15.refs_8_) | copy-start | bytes 786436
  57.3 5.1 %collective-permute-start.17 = (bf16[4,64,512]{2,1,0:T(8,128)(2,1)S(1)}, bf16[4,64,512]{2,1,0:T(8,128)(2,1)S(1)}, u32[]{:S(2)}, u32[]{:S(2)}) collective-permute-start(bf16[4,64,512]{2,1,0:T(8,128)(2,1)S(1)} %collective-permute-done.15.refs_8_), channel_id=1, source_target_pairs={{0,2},{2,0},{4,6},{6,4},{8,10},{10,8},{12,14},{14,12},{16,18},{18,... | collective-permute-start | bytes 786440 | tf_op jit(solution)/shard_map/ppermute | solution.py:456
  62.3 8.7 %copy-start.10 = (bf16[4,64,512]{2,1,0:T(8,128)(2,1)}, bf16[4,64,512]{2,1,0:T(8,128)(2,1)S(1)}, u32[]{:S(2)}) copy-start(bf16[4,64,512]{2,1,0:T(8,128)(2,1)S(1)} %collective-permute-done.16.refs_9_) | copy-start | bytes 786436
  62.3 1.7 %collective-permute-start.18 = (bf16[4,64,512]{2,1,0:T(8,128)(2,1)S(1)}, bf16[4,64,512]{2,1,0:T(8,128)(2,1)}, u32[]{:S(2)}, u32[]{:S(2)}) collective-permute-start(bf16[4,64,512]{2,1,0:T(8,128)(2,1)S(1)} %collective-permute-done.16.refs_9_), channel_id=1, source_target_pairs={{0,2},{2,0},{4,6},{6,4},{8,10},{10,8},{12,14},{14,12},{16,18},{18,... | collective-permute-start | bytes 786440 | tf_op jit(solution)/shard_map/ppermute | solution.py:456
  62.4 8.7 %copy-start.11 = (bf16[4,64,512]{2,1,0:T(8,128)(2,1)}, bf16[4,64,512]{2,1,0:T(8,128)(2,1)S(1)}, u32[]{:S(2)}) copy-start(bf16[4,64,512]{2,1,0:T(8,128)(2,1)S(1)} %collective-permute-done.13.refs_6_) | copy-start | bytes 786436
  62.4 8.7 %copy-start.12 = (bf16[4,64,512]{2,1,0:T(8,128)(2,1)}, bf16[4,64,512]{2,1,0:T(8,128)(2,1)S(1)}, u32[]{:S(2)}) copy-start(bf16[4,64,512]{2,1,0:T(8,128)(2,1)S(1)} %collective-permute-done.14.refs_7_) | copy-start | bytes 786436
  62.4 8.7 %copy-start.3 = (bf16[8,64,512]{2,1,0:T(8,128)(2,1)}, bf16[8,64,512]{2,1,0:T(8,128)(2,1)S(1)}, u32[]{:S(2)}) copy-start(bf16[8,64,512]{2,1,0:T(8,128)(2,1)S(1)} %collective-permute-done.12.refs_1_.got_ref) | copy-start | bytes 1572868
  62.4 8.7 %copy-start.13 = (bf16[4,64,512]{2,1,0:T(8,128)(2,1)}, bf16[4,64,512]{2,1,0:T(8,128)(2,1)S(1)}, u32[]{:S(2)}) copy-start(bf16[4,64,512]{2,1,0:T(8,128)(2,1)S(1)} %collective-permute-done.17.refs_10_) | copy-start | bytes 786436
  71.0 1.0 copy-start
  72.0 6.7 %copy-start.2 = (bf16[8,64,512]{2,1,0:T(8,128)(2,1)S(1)}, bf16[8,64,512]{2,1,0:T(8,128)(2,1)}, u32[]{:S(2)}) copy-start(bf16[8,64,512]{2,1,0:T(8,128)(2,1)} %get-tuple-element.55.refs_0_.kept_ref) | copy-start | bytes 1572868
  78.1 4.7 %collective-permute-start.19 = (bf16[8,2,64,512]{3,2,1,0:T(8,128)(2,1)}, bf16[8,2,64,512]{3,2,1,0:T(8,128)(2,1)S(1)}, u32[]{:S(2)}, u32[]{:S(2)}) collective-permute-start(bf16[8,2,64,512]{3,2,1,0:T(8,128)(2,1)} %get-tuple-element.62), channel_id=1, source_target_pairs={{0,2},{2,0},{4,6},{6,4},{8,10},{10,8},{12,14},{14,12},{16,18},{18,... | collective-permute-start | bytes 3145736 | tf_op jit(solution)/shard_map/ppermute | solution.py:468
  78.7 1.2 %copy-start.1 = (bf16[16,64,512]{2,1,0:T(8,128)(2,1)S(1)}, bf16[16,64,512]{2,1,0:T(8,128)(2,1)}, u32[]{:S(2)}) copy-start(bf16[16,64,512]{2,1,0:T(8,128)(2,1)} %copy-done) | copy-start | bytes 3145732
  80.0 1.0 copy-start.4
  81.0 1.0 copy-start.6
  82.9 8.5 %collective-permute-start.20 = (bf16[2,2,64,512]{3,2,1,0:T(8,128)(2,1)S(1)}, bf16[2,2,64,512]{3,2,1,0:T(8,128)(2,1)S(1)}, u32[]{:S(2)}, u32[]{:S(2)}) collective-permute-start(bf16[2,2,64,512]{3,2,1,0:T(8,128)(2,1)S(1)} %get-tuple-element.64), channel_id=1, source_target_pairs={{0,4},{2,6},{4,0},{6,2},{8,12},{10,14},{12,8},{14,10},{16,20},{18,... | collective-permute-start | bytes 786440 | tf_op jit(solution)/shard_map/ppermute | solution.py:385
  85.0 9.7 %collective-permute-start.22 = (bf16[2,2,64,512]{3,2,1,0:T(8,128)(2,1)S(1)}, bf16[2,2,64,512]{3,2,1,0:T(8,128)(2,1)S(1)}, u32[]{:S(2)}, u32[]{:S(2)}) collective-permute-start(bf16[2,2,64,512]{3,2,1,0:T(8,128)(2,1)S(1)} %get-tuple-element.68), channel_id=1, source_target_pairs={{0,8},{2,10},{4,12},{6,14},{8,0},{10,2},{12,4},{14,6},{16,24},{18,... | collective-permute-start | bytes 786440 | tf_op jit(solution)/shard_map/ppermute | solution.py:385
  91.5 6.1 %collective-permute-start.21 = (bf16[2,64,512]{2,1,0:T(8,128)(2,1)S(1)}, bf16[2,64,512]{2,1,0:T(8,128)(2,1)S(1)}, u32[]{:S(2)}, u32[]{:S(2)}) collective-permute-start(bf16[2,64,512]{2,1,0:T(8,128)(2,1)S(1)} %get-tuple-element.66), channel_id=1, source_target_pairs={{0,8},{2,10},{4,12},{6,14},{8,0},{10,2},{12,4},{14,6},{16,24},{18,... | collective-permute-start | bytes 393224 | tf_op jit(solution)/shard_map/ppermute | solution.py:387
  94.8 5.0 %collective-permute-start.23 = (bf16[2,64,512]{2,1,0:T(8,128)(2,1)S(1)}, bf16[2,64,512]{2,1,0:T(8,128)(2,1)S(1)}, u32[]{:S(2)}, u32[]{:S(2)}) collective-permute-start(bf16[2,64,512]{2,1,0:T(8,128)(2,1)S(1)} %get-tuple-element.70), channel_id=1, source_target_pairs={{0,4},{2,6},{4,0},{6,2},{8,12},{10,14},{12,8},{14,10},{16,20},{18,... | collective-permute-start | bytes 393224 | tf_op jit(solution)/shard_map/ppermute | solution.py:389
  99.9 7.3 %collective-permute-start.24 = (bf16[1,2,64,512]{3,2,1,0:T(8,128)(2,1)S(1)}, bf16[1,2,64,512]{3,2,1,0:T(8,128)(2,1)S(1)}, u32[]{:S(2)}, u32[]{:S(2)}) collective-permute-start(bf16[1,2,64,512]{3,2,1,0:T(8,128)(2,1)S(1)} %get-tuple-element.72), channel_id=1, source_target_pairs={{0,16},{2,18},{4,20},{6,22},{8,24},{10,26},{12,28},{14,30},{16,0},... | collective-permute-start | bytes 393224 | tf_op jit(solution)/shard_map/ppermute | solution.py:394
  107.2 5.0 %collective-permute-start.25 = (bf16[1,2,64,512]{3,2,1,0:T(8,128)(2,1)S(1)}, bf16[1,2,64,512]{3,2,1,0:T(8,128)(2,1)S(1)}, u32[]{:S(2)}, u32[]{:S(2)}) collective-permute-start(bf16[1,2,64,512]{3,2,1,0:T(8,128)(2,1)S(1)} %rounded_sum.1.kept_ref), channel_id=1, source_target_pairs={{0,1},{1,0},{2,3},{3,2},{4,5},{5,4},{6,7},{7,6},{8,9},{9,8},{10,11... | collective-permute-start | bytes 393224 | tf_op jit(solution)/shard_map/ppermute | solution.py:402

commit v4 on v3

--- a/solution.py
+++ b/solution.py
@@ -16,6 +16,7 @@
 whole_vmem = pl.BlockSpec(memory_space=pltpu.VMEM)
 whole_smem = pl.BlockSpec(memory_space=pltpu.SMEM)
 anywhere = pl.BlockSpec(memory_space=pl.ANY)
+whole_hbm = pl.BlockSpec(memory_space=pltpu.HBM)
 last_with_last = (((1,), (1,)), ((), ()))
 first_with_first = (((0,), (0,)), ((), ()))
 
@@ -37,36 +38,44 @@
     return [1 << i for i in range(size.bit_length() - 1)]
 
 
-def with_copies(kernel, lazy, operands, outs, *refs):
+def with_copies(kernel, lazy, still, operands, outs, *refs):
     given, refs = refs[:operands], refs[operands:]
     made, refs = refs[:outs], refs[outs:]
-    held, done, rest = refs[:operands], refs[operands], refs[operands + 1 :]
-    copies = [pltpu.make_async_copy(g, h, done.at[i]) for i, (g, h) in enumerate(zip(given, held))]
-    for copy in copies:
-        copy.start()
+    moved = [i for i in range(operands) if i not in still]
+    places, done, rest = refs[: len(moved)], refs[len(moved)], refs[len(moved) + 1 :]
+    held = list(given)
+    copies = {}
+    for n, i in enumerate(moved):
+        held[i] = places[n]
+        copies[i] = pltpu.make_async_copy(given[i], places[n], done.at[n])
+        copies[i].start()
+
+    def ready(*which):
+        for i in which:
+            copies[i].wait()
+
     if lazy:
-
-        def ready(*operands):
-            for i in operands:
-                copies[i].wait()
-
         kernel(ready, *held, *made, *rest)
-        return
-    for copy in copies:
-        copy.wait()
-    kernel(*held, *made, *rest)
-
-
-def local_call(kernel, name, outs, operands, scalars=0, scratch=(), fetch=False, lazy=False):
+    else:
+        ready(*moved)
+        kernel(*held, *made, *rest)
+
+
+def local_call(
+    kernel, name, outs, operands, scalars=0, scratch=(), fetch=False, lazy=False, still=(), limit=None
+):
     in_specs = [whole_smem] * scalars + [whole_vmem] * (len(operands) - scalars)
     if fetch or lazy:
-        in_specs = [anywhere] * len(operands)
+        limit = limit or most_vmem
+        space = anywhere if limit == most_vmem else whole_hbm
+        in_specs = [whole_vmem if i in still else space for i in range(len(operands))]
         held = [
             (pltpu.SMEM if i < scalars else pltpu.VMEM)(x.shape, x.dtype)
             for i, x in enumerate(operands)
+            if i not in still
         ]
-        scratch = [*held, pltpu.SemaphoreType.DMA((len(operands),)), *scratch]
-        kernel = functools.partial(with_copies, kernel, lazy, len(operands), len(outs))
+        scratch = [*held, pltpu.SemaphoreType.DMA((len(held),)), *scratch]
+        kernel = functools.partial(with_copies, kernel, lazy, still, len(operands), len(outs))
     return pl.pallas_call(
         kernel,
         out_shape=outs,
@@ -74,7 +83,7 @@
         out_specs=[whole_vmem] * len(outs),
         scratch_shapes=list(scratch),
         cost_estimate=pl.CostEstimate(flops=0, bytes_accessed=0, transcendentals=0),
-        compiler_params=pltpu.CompilerParams(vmem_limit_bytes=most_vmem if fetch or lazy else vmem_bytes),
+        compiler_params=pltpu.CompilerParams(vmem_limit_bytes=limit or vmem_bytes),
         name=name,
     )(*operands)
 
@@ -98,16 +107,17 @@
 
 
 def open_kernel(
-    quarters, count_ref, columns_ref, self_ref, neighbour_ref, ask_ref, picked_ref, weight_ref, across_ref, *cut_refs
+    quarters, count_ref, columns_ref, self_ref, neighbour_ref, ask_ref, picked_ref, across_ref, *cut_refs
 ):
     me, part = lax.axis_index("feat"), lax.axis_index("dom")
     below = lax.axis_size("feat") // quarters
     quarter, half = me // below, me % below // (below // 2)
-    weight_ref[0] = jnp.where(part % 2 == 0, self_ref[...], neighbour_ref[...])
+    weight = jnp.where(part % 2 == 0, self_ref[...], neighbour_ref[...])
     width = across_ref.shape[2]
     for i, cut_ref in enumerate(cut_refs):
         at = (quarter ^ i) * 2 + half
-        cut_ref[0] = columns_ref[:, pl.ds(pl.multiple_of(at * width, width), width)]
+        cut_ref[0, :, 0:width] = columns_ref[:, pl.ds(pl.multiple_of(at * width, width), width)]
+        cut_ref[0, :, width:] = weight
         at = (quarter ^ i) * 2 + 1 - half
         across_ref[i] = columns_ref[:, pl.ds(pl.multiple_of(at * width, width), width)]
     parts = ask_ref.shape[1]
@@ -130,10 +140,9 @@
         "open_exchange",
         [
             jax.ShapeDtypeStruct((depth, asked), bf16),
-            jax.ShapeDtypeStruct((1, *self_weight.shape), bf16),
             jax.ShapeDtypeStruct((quarters, depth, width), bf16),
         ]
-        + [jax.ShapeDtypeStruct((1, depth, width), bf16)] * quarters,
+        + [jax.ShapeDtypeStruct((1, depth, width + self_weight.shape[1]), bf16)] * quarters,
         (counts, columns, self_weight, neighbour_weight, asks),
         scalars=1,
         fetch=True,
@@ -215,21 +224,19 @@
     count = sum(p.shape[0] for p in parts)
     out = jax.ShapeDtypeStruct((count, parts[0].shape[1], width // 2), bf16)
     return local_call(
-        functools.partial(cut_kernel, bit), "cut_rows", [out, out], parts, fetch=True
-    )
-
-
-def gathered(parts):
-    shape = (sum(p.shape[0] for p in parts), *parts[0].shape[1:])
-    return local_call(gather_kernel, "gathered", [jax.ShapeDtypeStruct(shape, bf16)], parts)[0]
-
-
-def gather_kernel(*refs):
+        functools.partial(cut_kernel, bit), "cut_rows", [out, out], parts
+    )
+
+
+def weight_kernel(*refs):
     *held_refs, out_ref = refs
-    at = 0
-    for ref in held_refs:
-        out_ref[at : at + ref.shape[0]] = ref[...]
-        at += ref.shape[0]
+    for i, ref in enumerate(held_refs):
+        out_ref[i] = ref[0, :, ref.shape[2] - out_ref.shape[2] :]
+
+
+def weight_pieces(parts, hid):
+    out = jax.ShapeDtypeStruct((len(parts), parts[0].shape[1], hid), bf16)
+    return local_call(weight_kernel, "weight_pieces", [out], parts)[0]
 
 
 def flipped(masks, bit):
@@ -257,56 +264,61 @@
     return means
 
 
-def forward_kernel(row_masks, weight_masks, ready, *refs):
+def own_linear_kernel(row_masks, weight_masks, *refs):
     pieces = len(weight_masks)
-    kept_ref, got_ref, mean_ref, cot_ref = refs[:4]
-    mine_refs, other_refs = refs[4 : 4 + pieces], refs[4 + pieces : 4 + 2 * pieces]
-    hidden_ref, grad_ref, sums_ref, linear_ref = refs[4 + 2 * pieces :]
+    kept_ref, got_ref = refs[:2]
+    mine_refs, other_refs = refs[2 : 2 + pieces], refs[2 + pieces : 2 + 2 * pieces]
+    linear_ref, weight_ref = refs[2 + 2 * pieces :]
+    features = features_in_order(row_masks, kept_ref, got_ref)
     side = lax.axis_index("dom") % 2
-    features, means = features_in_order(row_masks, kept_ref, got_ref), means_in_order(mean_ref)
-    rows, hid = linear_ref.shape
-
-    def fill_linear(source, weight_refs, more):
-        step = min(256, rows)
-        for at in range(0, rows, step):
-            total = linear_ref[at : at + step] if more else jnp.zeros((step, hid), f32)
-            for masks, weight_ref in zip(weight_masks, weight_refs):
-                part = jnp.concatenate([source(mask, at, step) for mask in masks], axis=0)
-                total = total + lax.dot_general(
-                    part,
-                    weight_ref[...].reshape(-1, hid),
-                    first_with_first,
-                    preferred_element_type=f32,
-                )
-            linear_ref[at : at + step] = total
-
-    ready(0, 1, *range(4, 4 + 2 * pieces))
+
+    def fill(self_refs, neighbour_refs):
+        at = 0
+        for ref in neighbour_refs:
+            weight_ref[at : at + ref.shape[0]] = ref[...]
+            at += ref.shape[0]
+        fill_linear(features, weight_masks, self_refs, linear_ref, linear_ref, False)
 
     @pl.when(side == 0)
     def _():
-        fill_linear(features, mine_refs, False)
+        fill(mine_refs, other_refs)
 
     @pl.when(side != 0)
     def _():
-        fill_linear(features, other_refs, False)
-
-    ready(2)
-
-    @pl.when(side == 0)
-    def _():
-        fill_linear(means, other_refs, True)
-
-    @pl.when(side != 0)
-    def _():
-        fill_linear(means, mine_refs, True)
-
+        fill(other_refs, mine_refs)
+
+
+def fill_linear(source, weight_masks, weight_refs, base_ref, linear_ref, more):
+    rows, hid = linear_ref.shape
+    step = min(256, rows)
+    for at in range(0, rows, step):
+        total = base_ref[at : at + step] if more else jnp.zeros((step, hid), f32)
+        for masks, weight_ref in zip(weight_masks, weight_refs):
+            part = jnp.concatenate([source(mask, at, step) for mask in masks], axis=0)
+            total = total + lax.dot_general(
+                part,
+                weight_ref[...].reshape(-1, hid),
+                first_with_first,
+                preferred_element_type=f32,
+            )
+        linear_ref[at : at + step] = total
+
+
+def forward_kernel(row_masks, masks, ready, *refs):
+    mean_ref, weight_ref, base_ref, cot_ref, kept_ref, got_ref = refs[:6]
+    hidden_ref, other_sums_ref, my_sums_ref, linear_ref, grad_ref = refs[6:]
+    features, means = features_in_order(row_masks, kept_ref, got_ref), means_in_order(mean_ref)
+    ready(1, 2)
+    fill_linear(means, [masks], [weight_ref], base_ref, linear_ref, True)
     ready(3)
-    step = min(128, rows)
-    for at in range(0, rows, step):
+    step = min(128, linear_ref.shape[0])
+    for at in range(0, linear_ref.shape[0], step):
         value, slope = gelu_pair(linear_ref[at : at + step])
         hidden_ref[at : at + step] = value.astype(bf16)
         grad_ref[at : at + step] = (cot_ref[at : at + step].astype(f32) * slope).astype(bf16)
-    fill_sums(1, features, means, grad_ref, sums_ref)
+    ready(4, 5)
+    fill_sums(1, features, means, grad_ref, other_sums_ref)
+    fill_sums(0, features, means, grad_ref, my_sums_ref)
 
 
 def fill_sums(core, features, means, grad_ref, sums_ref):
@@ -316,11 +328,6 @@
         )
         sums = jnp.dot(part, grad_ref[...], preferred_element_type=f32)
         sums_ref[:, i] = sums.astype(sums_ref.dtype).reshape(sums_ref[:, i].shape)
-
-
-def kept_kernel(row_masks, kept_ref, got_ref, mean_ref, grad_ref, sums_ref):
-    features, means = features_in_order(row_masks, kept_ref, got_ref), means_in_order(mean_ref)
-    fill_sums(0, features, means, grad_ref, sums_ref)
 
 
 def first_kernel(kept_ref, got_ref, own_ref, own_sent_ref, neigh_ref, neigh_sent_ref):
@@ -422,29 +429,27 @@
     columns = features.T
     quarters, below = 4, feat // 4
     row_bits = list(reversed(bits_of(below)))
-    picked, weight, across, *cuts = open_exchange(
+    picked, across, *cuts = open_exchange(
         send_count, columns, self_weight, neighbour_weight, send_rows, quarters
     )
     came = flip("feat", row_bits[0])(across)
-    weight = gathered([weight] + [flip("feat", i * below)(weight) for i in range(1, quarters)])
     near = [cuts[0]] + [flip("feat", i * below)(cuts[i]) for i in range(1, quarters)]
+    if dom == 2:
+        halo = flip("dom", 1)(picked)
+    else:
+        halo = lax.all_to_all(picked, "dom", 1, 1, tiled=True)
+    means = neighbour_means(
+        tile_source[0].T, tile_kind[0].T, send_count, columns, halo, send_rows, tile_patterns, feat
+    )
+    came, means = lax.optimization_barrier((came, means))
     far = [came[0:1]] + [flip("feat", i * below)(came[i : i + 1]) for i in range(1, quarters)]
     row_masks = [i * below for i in range(quarters)]
-    pieces, weight_masks = [weight], [list(row_masks)]
+    pieces, weight_masks = [weight_pieces(near, hid)], [list(row_masks)]
     row_masks = row_masks + flipped(row_masks, row_bits[0])
     for bit in row_bits[:-1]:
         pieces = pieces + [flip("feat", bit)(p) for p in pieces]
         weight_masks = weight_masks + [flipped(m, bit) for m in weight_masks]
-    if dom == 2:
-        halo = flip("dom", 1)(picked)
-    else:
-        halo = lax.all_to_all(picked, "dom", 1, 1, tiled=True)
-    halo, _, _ = lax.optimization_barrier((halo, came, pieces))
-    means = neighbour_means(
-        tile_source[0].T, tile_kind[0].T, send_count, columns, halo, send_rows, tile_patterns, feat
-    )
-    held = lax.optimization_barrier((means, near, far, pieces))
-    means, near, far, pieces = held
+    means, near, far, pieces = lax.optimization_barrier((means, near, far, pieces))
     own_mean = lax.all_to_all(means, "feat", 0, 0, tiled=True)
     others = [flip("dom", 1)(p) for p in pieces]
     parts, width = [*near, *far], came.shape[2]
@@ -456,22 +461,31 @@
     others = others + [flip("feat", 1)(p) for p in others]
     weight_masks = weight_masks + [flipped(m, 1) for m in weight_masks]
     sums = (feat // 2, 2, depth, hid)
-    square = jax.ShapeDtypeStruct((rows, hid), bf16)
-    hidden, grad_linear, sent = local_call(
-        functools.partial(forward_kernel, row_masks, weight_masks),
+    linear, weights = local_call(
+        functools.partial(own_linear_kernel, row_masks, weight_masks),
+        "own_linear",
+        [
+            jax.ShapeDtypeStruct((rows, hid), f32),
+            jax.ShapeDtypeStruct((feat, depth, hid), bf16),
+        ],
+        (*parts, *pieces, *others),
+
+    )
+    hidden, sent, kept = local_call(
+        functools.partial(forward_kernel, row_masks, sum(weight_masks, [])),
         "forward",
-        [square, square, jax.ShapeDtypeStruct(sums, bf16)],
-        (*parts, own_mean, cotangent, *pieces, *others),
-        scratch=[pltpu.VMEM((rows, hid), f32)],
+        [
+            jax.ShapeDtypeStruct((rows, hid), bf16),
+            jax.ShapeDtypeStruct(sums, bf16),
+            jax.ShapeDtypeStruct(sums, f32),
+        ],
+        (own_mean, weights, linear, cotangent, *parts),
+        scratch=[pltpu.VMEM((rows, hid), f32), pltpu.VMEM((rows, hid), bf16)],
         lazy=True,
+        still=(0,),
+        limit=24 * 2**20,
     )
     got = flip("feat", 1)(sent)
-    (kept,) = local_call(
-        functools.partial(kept_kernel, row_masks),
-        "kept_gradients",
-        [jax.ShapeDtypeStruct(sums, f32)],
-        (*parts, own_mean, grad_linear),
-    )
     grad_self, grad_neighbour = sum_gradients(kept, got)
     return (hidden, grad_self, grad_neighbour)
 

time: 113 us -> 108 us (0.956)
  Pallas kernels: 23.4 us -> 18.5 us
  waiting for transfers between devices: 43.9 us -> 48.2 us
  starting transfers between devices: 39 us -> 35.5 us
    pallas_call x12, Pallas kernels: 23.4 us -> 18.5 us  [local_call(): pl.pallas_call(kernel, out_shape=outs, in_specs=in_specs, out_specs=[whol...]
    ppermute x3 -> x0, waiting for transfers between devices: 4.86 us -> none  [on_device(): flip('feat', i * below)(weight)]
    ppermute x3 -> x0, starting transfers between devices: 4.39 us -> none  [on_device(): flip('feat', i * below)(weight)]
    ppermute x3, waiting for transfers between devices: 4.46 us -> 7.54 us  [on_device(): flip('feat', i * below)(came[i:i + 1])]
    ppermute x1, waiting for transfers between devices: 0.01 us -> 2.61 us  [on_device(): halo = flip('dom', 1)(picked)]
    all_to_all x1, waiting for transfers between devices: 7.03 us -> 4.46 us  [on_device(): own_mean = lax.all_to_all(means, 'feat', 0, 0, tiled=True)]
    ppermute x2, waiting for transfers between devices: 9.06 us -> 11.4 us  [on_device(): others = [flip('dom', 1)(p) for p in pieces]]
    ppermute x1, waiting for transfers between devices: 0.01 us -> 2.29 us  [on_device(): got = flip('feat', 1)(sent)]
  transfers between devices with their start and end apart: 27 -> 24, of which waited for: 13 -> 14; matrix products, arithmetic and copies ran while one was open for 1% -> 0% of each run, Pallas kernels for 12% -> 10%
where the time goes in v4:
time: 108 us
  waiting for transfers between devices  48.2 us (45%)
  starting transfers between devices  35.5 us (33%)
  Pallas kernels  18.5 us (17%)
  local copies, waits for them, and re-layouts  4.83 us (4%)
    pallas_call x12, Pallas kernels, local_call(): pl.pallas_call(kernel, out_shape=outs, in_specs=in_specs, out_specs=[whol...  18.5 us
    ppermute x2, waiting for transfers between devices, on_device(): others = [flip('dom', 1)(p) for p in pieces]  11.4 us
    ppermute x3, waiting for transfers between devices, on_device(): flip('feat', i * below)(came[i:i + 1])  7.54 us
    ppermute x1, waiting for transfers between devices, sum_gradients(): got = flip('feat', half * 8)(sent)  6.11 us
    all_to_all x1, starting transfers between devices, on_device(): own_mean = lax.all_to_all(means, 'feat', 0, 0, tiled=True)  5.63 us
    unnamed x14, local copies, waits for them, and re-layouts  4.8 us
    ppermute x3, starting transfers between devices, on_device(): flip('feat', i * below)(came[i:i + 1])  4.53 us
    all_to_all x1, waiting for transfers between devices, on_device(): own_mean = lax.all_to_all(means, 'feat', 0, 0, tiled=True)  4.46 us
  transfers between devices with their start and end apart: 24, of which 14 were waited for; matrix products, arithmetic and copies ran while one was open for 0% of the time, Pallas kernels for 10%

profile of v4, /device:TPU:0, one launch (start us, length us, event | category | flops | bytes accessed | tf_op | source)
XLA Modules:
  0.0 107.9 jit_solution(9881791305565704560)
XLA Ops:
  0.6 3.1 %open_exchange.1 = (bf16[64,256]{1,0:T(8,128)(2,1)}, bf16[4,64,1024]{2,1,0:T(8,128)(2,1)}, bf16[1,64,1536]{2,1,0:T(8,128)(2,1)}, bf16[1,64,1536]{2,1,0:T(8,128)(...) custom-call(s32[2,2]{1,0:T(2,128)} %refs_2_.3, bf16[64,8192]{1,0:T(8,128)(2,1)} %bitcast.7, ...), custom_call_target="tpu_custom_call" | custom-call | tf_op jit(solution)/shard_map/open_exchange/pallas_call | solution.py:79
  3.7 3.0 %collective-permute-start = (bf16[4,64,1024]{2,1,0:T(8,128)(2,1)}, bf16[4,64,1024]{2,1,0:T(8,128)(2,1)S(1)}, u32[]{:S(2)}, u32[]{:S(2)}) collective-permute-start(bf16[4,64,1024]{2,1,0:T(8,128)(2,1)} %get-tuple-element.41), channel_id=1, source_target_pairs={{0,4},{2,6},{4,0},{6,2},{8,12},{10,14},{12,8},{14,10},{16,20},{18,... | collective-permute-start | bytes 1572872 | tf_op jit(solution)/shard_map/ppermute | solution.py:435
  6.7 1.6 %collective-permute-start.2 = (bf16[1,64,1536]{2,1,0:T(8,128)(2,1)}, bf16[1,64,1536]{2,1,0:T(8,128)(2,1)S(1)}, u32[]{:S(2)}, u32[]{:S(2)}) collective-permute-start(bf16[1,64,1536]{2,1,0:T(8,128)(2,1)} %get-tuple-element.45), channel_id=1, source_target_pairs={{0,8},{2,10},{4,12},{6,14},{8,0},{10,2},{12,4},{14,6},{16,24},{18,... | collective-permute-start | bytes 589832 | tf_op jit(solution)/shard_map/ppermute | solution.py:436
  8.3 2.6 %collective-permute-start.3 = (bf16[1,64,1536]{2,1,0:T(8,128)(2,1)}, bf16[1,64,1536]{2,1,0:T(8,128)(2,1)S(1)}, u32[]{:S(2)}, u32[]{:S(2)}) collective-permute-start(bf16[1,64,1536]{2,1,0:T(8,128)(2,1)} %get-tuple-element.46), channel_id=1, source_target_pairs={{0,16},{2,18},{4,20},{6,22},{8,24},{10,26},{12,28},{14,30},{16,0},... | collective-permute-start | bytes 589832 | tf_op jit(solution)/shard_map/ppermute | solution.py:436
  10.9 0.2 collective-permute-start.4
  11.1 1.5 %collective-permute-start.1 = (bf16[64,256]{1,0:T(8,128)(2,1)}, bf16[64,256]{1,0:T(8,128)(2,1)S(1)}, u32[]{:S(2)}, u32[]{:S(2)}) collective-permute-start(bf16[64,256]{1,0:T(8,128)(2,1)} %get-tuple-element.42), channel_id=1, source_target_pairs={{0,1},{1,0},{2,3},{3,2},{4,5},{5,4},{6,7},{7,6},{8,9},{9,8},{10,11... | collective-permute-start | bytes 98312 | tf_op jit(solution)/shard_map/ppermute | solution.py:438
  12.6 2.6 %collective-permute-done.1.refs_4_ = bf16[64,256]{1,0:T(8,128)(2,1)S(1)} collective-permute-done((bf16[64,256]{1,0:T(8,128)(2,1)}, bf16[64,256]{1,0:T(8,128)(2,1)S(1)}, u32[]{:S(2)}, u32[]{:S(2)}) %collective-permute-start.1) | collective-permute-done | bytes 32800 | tf_op jit(solution)/shard_map/ppermute | solution.py:438
  15.3 0.6 copy-done.6
  15.9 10.2 %neighbour_means.1 = bf16[16,64,512]{2,1,0:T(8,128)(2,1)} custom-call(s32[8,64]{1,0:T(8,128)} %bitcast.9, s32[8,64]{1,0:T(8,128)} %bitcast.10, s32[2,2]{1,0:T(2,128)} %refs_2_.3, bf16[64,8192]{1,0:T(8,128)(2,1)} %bitcast.8, bf16[64,256]{1,0:T(8,128)(2,1)} %copy-done.6, s32[2,2,256]{2,1,0:T(2,128)} %refs_5_.1, bf16[64,128,128]{2,1,0:T(8,128)(2,1)} %refs_6_.1), custom_call_target="tpu_custom_call" | custom-call | tf_op jit(solution)/shard_map/neighbour_means/pallas_call | solution.py:79
  26.2 0.4 collective-permute-start.8
  26.6 3.9 %collective-permute-start.7 = (bf16[1,64,1024]{2,1,0:T(8,128)(2,1)S(1)}, bf16[1,64,1024]{2,1,0:T(8,128)(2,1)S(1)}, u32[]{:S(2)}, u32[]{:S(2)}) collective-permute-start(bf16[1,64,1024]{2,1,0:T(8,128)(2,1)S(1)} %get-tuple-element.79), channel_id=1, source_target_pairs={{0,24},{2,26},{4,28},{6,30},{8,16},{10,18},{12,20},{14,22},{16,8},... | collective-permute-start | bytes 393224 | tf_op jit(solution)/shard_map/ppermute | solution.py:445
  30.5 0.5 collective-permute-start.6
  30.9 0.2 collective-permute-start.5
  31.1 1.5 %collective-permute-done.8.refs_3_ = bf16[4,64,512]{2,1,0:T(8,128)(2,1)S(1)} collective-permute-done((bf16[4,64,512]{2,1,0:T(8,128)(2,1)S(1)}, bf16[4,64,512]{2,1,0:T(8,128)(2,1)S(1)}, u32[]{:S(2)}, u32[]{:S(2)}) %collective-permute-start.8) | collective-permute-done | bytes 262176 | tf_op jit(solution)/shard_map/ppermute | solution.py:450
  32.6 2.3 %collective-permute-done.7.refs_7_ = bf16[1,64,1024]{2,1,0:T(8,128)(2,1)S(1)} collective-permute-done((bf16[1,64,1024]{2,1,0:T(8,128)(2,1)S(1)}, bf16[1,64,1024]{2,1,0:T(8,128)(2,1)S(1)}, u32[]{:S(2)}, u32[]{:S(2)}) %collective-permute-start.7) | collective-permute-done | bytes 131104 | tf_op jit(solution)/shard_map/ppermute | solution.py:445
  34.9 5.3 %collective-permute-done.6.refs_6_ = bf16[1,64,1024]{2,1,0:T(8,128)(2,1)S(1)} collective-permute-done((bf16[1,64,1024]{2,1,0:T(8,128)(2,1)S(1)}, bf16[1,64,1024]{2,1,0:T(8,128)(2,1)S(1)}, u32[]{:S(2)}, u32[]{:S(2)}) %collective-permute-start.6) | collective-permute-done | bytes 131104 | tf_op jit(solution)/shard_map/ppermute | solution.py:445
  40.1 5.6 %all-to-all-start = ((bf16[16,64,512]{2,1,0:T(8,128)(2,1)}), bf16[16,64,512]{2,1,0:T(8,128)(2,1)S(1)}, u32[]{:S(2)}, u32[]{:S(2)}) async-start(bf16[16,64,512]{2,1,0:T(8,128)(2,1)} %neighbour_means.1), calls=%async_computation | async-start | bytes 2097152 | tf_op jit(solution)/shard_map/all_to_all | solution.py:453
  45.8 1.6 %collective-permute-start.12 = (bf16[4,64,512]{2,1,0:T(8,128)(2,1)S(1)}, bf16[4,64,512]{2,1,0:T(8,128)(2,1)S(1)}, u32[]{:S(2)}, u32[]{:S(2)}) collective-permute-start(bf16[4,64,512]{2,1,0:T(8,128)(2,1)S(1)} %weight_pieces.1.refs_2_), channel_id=1, source_target_pairs={{0,1},{1,0},{2,3},{3,2},{4,5},{5,4},{6,7},{7,6},{8,9},{9,8},{10,11... | collective-permute-start | bytes 786440 | tf_op jit(solution)/shard_map/ppermute | solution.py:454
  47.4 0.1 cut_rows.1
  47.4 0.1 collective-permute-start.9
  47.6 0.5 collective-permute-start.13
  48.1 0.2 collective-permute-start.10
  48.3 0.3 collective-permute-start.11
  48.6 6.4 %collective-permute-done.12.refs_6_ = bf16[4,64,512]{2,1,0:T(8,128)(2,1)S(1)} collective-permute-done((bf16[4,64,512]{2,1,0:T(8,128)(2,1)S(1)}, bf16[4,64,512]{2,1,0:T(8,128)(2,1)S(1)}, u32[]{:S(2)}, u32[]{:S(2)}) %collective-permute-start.12) | collective-permute-done | bytes 262176 | tf_op jit(solution)/shard_map/ppermute | solution.py:454
  55.0 5.0 %collective-permute-done.13.refs_7_ = bf16[4,64,512]{2,1,0:T(8,128)(2,1)S(1)} collective-permute-done((bf16[4,64,512]{2,1,0:T(8,128)(2,1)S(1)}, bf16[4,64,512]{2,1,0:T(8,128)(2,1)S(1)}, u32[]{:S(2)}, u32[]{:S(2)}) %collective-permute-start.13) | collective-permute-done | bytes 262176 | tf_op jit(solution)/shard_map/ppermute | solution.py:454
  60.1 1.5 %collective-permute-done.15.refs_9_ = bf16[4,64,512]{2,1,0:T(8,128)(2,1)S(1)} collective-permute-done((bf16[4,64,512]{2,1,0:T(8,128)(2,1)S(1)}, bf16[4,64,512]{2,1,0:T(8,128)(2,1)S(1)}, u32[]{:S(2)}, u32[]{:S(2)}) %collective-permute-start.15) | collective-permute-done | bytes 262176 | tf_op jit(solution)/shard_map/ppermute | solution.py:461
  61.6 0.9 copy-done.5
  62.5 0.8 own_linear.1
  63.3 1.0 copy-done
  64.3 4.5 %all-to-all-done.refs_0_ = bf16[16,64,512]{2,1,0:T(8,128)(2,1)S(1)} async-done(((bf16[16,64,512]{2,1,0:T(8,128)(2,1)}), bf16[16,64,512]{2,1,0:T(8,128)(2,1)S(1)}, u32[]{:S(2)}, u32[]{:S(2)}) %all-to-all-start) | async-done | bytes 1048608 | tf_op jit(solution)/shard_map/all_to_all | solution.py:453
  68.7 1.2 %copy-done.1 = bf16[16,64,512]{2,1,0:T(8,128)(2,1)S(1)} copy-done((bf16[16,64,512]{2,1,0:T(8,128)(2,1)S(1)}, bf16[16,64,512]{2,1,0:T(8,128)(2,1)}, u32[]{:S(2)}) %copy-start.1) | copy-done | bytes 1048600
  70.0 1.0 copy-done.3
  71.0 3.3 %forward.1 = (bf16[512,512]{1,0:T(8,128)(2,1)}, bf16[8,2,64,512]{3,2,1,0:T(8,128)(2,1)S(1)}, f32[8,2,64,512]{3,2,1,0:T(8,128)S(1)}) custom-call(bf16[16,64,512]{2,1,0:T(8,128)(2,1)S(1)} %all-to-all-done.refs_0_, bf16[16,64,512]{2,1,0:T(8,128)(2,1)S(1)} %copy-done.1, f32[512,512]{1,0:T(8,128)S(1)} %get-tuple-element.63.refs_2_, ...), custom_call_target="tpu_custom_call" | custom-call | tf_op jit(solution)/shard_map/forward/pallas_call | solution.py:79
  74.3 0.7 collective-permute-start.16
  75.0 2.3 %collective-permute-done.16.got_ref = bf16[8,2,64,512]{3,2,1,0:T(8,128)(2,1)S(1)} collective-permute-done((bf16[8,2,64,512]{3,2,1,0:T(8,128)(2,1)S(1)}, bf16[8,2,64,512]{3,2,1,0:T(8,128)(2,1)S(1)}, u32[]{:S(2)}, u32[]{:S(2)}) %collective-permute-start.16) | collective-permute-done | bytes 1048608 | tf_op jit(solution)/shard_map/ppermute | solution.py:488
  77.3 0.2 first_sum.1
  77.5 2.0 %collective-permute-start.17 = (bf16[2,2,64,512]{3,2,1,0:T(8,128)(2,1)S(1)}, bf16[2,2,64,512]{3,2,1,0:T(8,128)(2,1)S(1)}, u32[]{:S(2)}, u32[]{:S(2)}) collective-permute-start(bf16[2,2,64,512]{3,2,1,0:T(8,128)(2,1)S(1)} %get-tuple-element.68), channel_id=1, source_target_pairs={{0,4},{2,6},{4,0},{6,2},{8,12},{10,14},{12,8},{14,10},{16,20},{18,... | collective-permute-start | bytes 786440 | tf_op jit(solution)/shard_map/ppermute | solution.py:392
  79.5 3.0 %collective-permute-start.19 = (bf16[2,2,64,512]{3,2,1,0:T(8,128)(2,1)S(1)}, bf16[2,2,64,512]{3,2,1,0:T(8,128)(2,1)S(1)}, u32[]{:S(2)}, u32[]{:S(2)}) collective-permute-start(bf16[2,2,64,512]{3,2,1,0:T(8,128)(2,1)S(1)} %get-tuple-element.72), channel_id=1, source_target_pairs={{0,8},{2,10},{4,12},{6,14},{8,0},{10,2},{12,4},{14,6},{16,24},{18,... | collective-permute-start | bytes 786440 | tf_op jit(solution)/shard_map/ppermute | solution.py:392
  82.5 3.9 %collective-permute-done.17.got_ref = bf16[2,2,64,512]{3,2,1,0:T(8,128)(2,1)S(1)} collective-permute-done((bf16[2,2,64,512]{3,2,1,0:T(8,128)(2,1)S(1)}, bf16[2,2,64,512]{3,2,1,0:T(8,128)(2,1)S(1)}, u32[]{:S(2)}, u32[]{:S(2)}) %collective-permute-start.17) | collective-permute-done | bytes 262176 | tf_op jit(solution)/shard_map/ppermute | solution.py:392
  86.4 3.2 %collective-permute-start.18 = (bf16[2,64,512]{2,1,0:T(8,128)(2,1)S(1)}, bf16[2,64,512]{2,1,0:T(8,128)(2,1)S(1)}, u32[]{:S(2)}, u32[]{:S(2)}) collective-permute-start(bf16[2,64,512]{2,1,0:T(8,128)(2,1)S(1)} %get-tuple-element.70), channel_id=1, source_target_pairs={{0,8},{2,10},{4,12},{6,14},{8,0},{10,2},{12,4},{14,6},{16,24},{18,... | collective-permute-start | bytes 393224 | tf_op jit(solution)/shard_map/ppermute | solution.py:394
  89.6 1.6 %collective-permute-start.20 = (bf16[2,64,512]{2,1,0:T(8,128)(2,1)S(1)}, bf16[2,64,512]{2,1,0:T(8,128)(2,1)S(1)}, u32[]{:S(2)}, u32[]{:S(2)}) collective-permute-start(bf16[2,64,512]{2,1,0:T(8,128)(2,1)S(1)} %get-tuple-element.74), channel_id=1, source_target_pairs={{0,4},{2,6},{4,0},{6,2},{8,12},{10,14},{12,8},{14,10},{16,20},{18,... | collective-permute-start | bytes 393224 | tf_op jit(solution)/shard_map/ppermute | solution.py:396
  91.2 1.6 %collective-permute-done.18.own_got_ref = bf16[2,64,512]{2,1,0:T(8,128)(2,1)S(1)} collective-permute-done((bf16[2,64,512]{2,1,0:T(8,128)(2,1)S(1)}, bf16[2,64,512]{2,1,0:T(8,128)(2,1)S(1)}, u32[]{:S(2)}, u32[]{:S(2)}) %collective-permute-start.18) | collective-permute-done | bytes 131104 | tf_op jit(solution)/shard_map/ppermute | solution.py:394
  92.8 1.9 %collective-permute-done.20.neigh_got_ref = bf16[2,64,512]{2,1,0:T(8,128)(2,1)S(1)} collective-permute-done((bf16[2,64,512]{2,1,0:T(8,128)(2,1)S(1)}, bf16[2,64,512]{2,1,0:T(8,128)(2,1)S(1)}, u32[]{:S(2)}, u32[]{:S(2)}) %collective-permute-start.20) | collective-permute-done | bytes 131104 | tf_op jit(solution)/shard_map/ppermute | solution.py:396
  94.7 1.3 %collective-permute-start.21 = (bf16[1,2,64,512]{3,2,1,0:T(8,128)(2,1)S(1)}, bf16[1,2,64,512]{3,2,1,0:T(8,128)(2,1)S(1)}, u32[]{:S(2)}, u32[]{:S(2)}) collective-permute-start(bf16[1,2,64,512]{3,2,1,0:T(8,128)(2,1)S(1)} %get-tuple-element.76), channel_id=1, source_target_pairs={{0,16},{2,18},{4,20},{6,22},{8,24},{10,26},{12,28},{14,30},{16,0},... | collective-permute-start | bytes 393224 | tf_op jit(solution)/shard_map/ppermute | solution.py:401
  96.0 6.1 %collective-permute-done.21.got_ref = bf16[1,2,64,512]{3,2,1,0:T(8,128)(2,1)S(1)} collective-permute-done((bf16[1,2,64,512]{3,2,1,0:T(8,128)(2,1)S(1)}, bf16[1,2,64,512]{3,2,1,0:T(8,128)(2,1)S(1)}, u32[]{:S(2)}, u32[]{:S(2)}) %collective-permute-start.21) | collective-permute-done | bytes 131104 | tf_op jit(solution)/shard_map/ppermute | solution.py:401
  102.2 1.6 %collective-permute-start.22 = (bf16[1,2,64,512]{3,2,1,0:T(8,128)(2,1)S(1)}, bf16[1,2,64,512]{3,2,1,0:T(8,128)(2,1)S(1)}, u32[]{:S(2)}, u32[]{:S(2)}) collective-permute-start(bf16[1,2,64,512]{3,2,1,0:T(8,128)(2,1)S(1)} %rounded_sum.1.kept_ref), channel_id=1, source_target_pairs={{0,1},{1,0},{2,3},{3,2},{4,5},{5,4},{6,7},{7,6},{8,9},{9,8},{10,11... | collective-permute-start | bytes 393224 | tf_op jit(solution)/shard_map/ppermute | solution.py:409
  103.8 3.5 %collective-permute-done.22.got_ref = bf16[1,2,64,512]{3,2,1,0:T(8,128)(2,1)S(1)} collective-permute-done((bf16[1,2,64,512]{3,2,1,0:T(8,128)(2,1)S(1)}, bf16[1,2,64,512]{3,2,1,0:T(8,128)(2,1)S(1)}, u32[]{:S(2)}, u32[]{:S(2)}) %collective-permute-start.22) | collective-permute-done | bytes 131104 | tf_op jit(solution)/shard_map/ppermute | solution.py:409
  107.2 0.7 last_sum.1
  (27 shorter events, 0.3 us)
Async XLA Ops:
  3.7 22.8 %collective-permute-start = (bf16[4,64,1024]{2,1,0:T(8,128)(2,1)}, bf16[4,64,1024]{2,1,0:T(8,128)(2,1)S(1)}, u32[]{:S(2)}, u32[]{:S(2)}) collective-permute-start(bf16[4,64,1024]{2,1,0:T(8,128)(2,1)} %get-tuple-element.41), channel_id=1, source_target_pairs={{0,4},{2,6},{4,0},{6,2},{8,12},{10,14},{12,8},{14,10},{16,20},{18,... | collective-permute-start | bytes 1572872 | tf_op jit(solution)/shard_map/ppermute | solution.py:435
  6.7 19.4 %collective-permute-start.2 = (bf16[1,64,1536]{2,1,0:T(8,128)(2,1)}, bf16[1,64,1536]{2,1,0:T(8,128)(2,1)S(1)}, u32[]{:S(2)}, u32[]{:S(2)}) collective-permute-start(bf16[1,64,1536]{2,1,0:T(8,128)(2,1)} %get-tuple-element.45), channel_id=1, source_target_pairs={{0,8},{2,10},{4,12},{6,14},{8,0},{10,2},{12,4},{14,6},{16,24},{18,... | collective-permute-start | bytes 589832 | tf_op jit(solution)/shard_map/ppermute | solution.py:436
  8.3 17.8 %collective-permute-start.3 = (bf16[1,64,1536]{2,1,0:T(8,128)(2,1)}, bf16[1,64,1536]{2,1,0:T(8,128)(2,1)S(1)}, u32[]{:S(2)}, u32[]{:S(2)}) collective-permute-start(bf16[1,64,1536]{2,1,0:T(8,128)(2,1)} %get-tuple-element.46), channel_id=1, source_target_pairs={{0,16},{2,18},{4,20},{6,22},{8,24},{10,26},{12,28},{14,30},{16,0},... | collective-permute-start | bytes 589832 | tf_op jit(solution)/shard_map/ppermute | solution.py:436
  10.9 15.2 %collective-permute-start.4 = (bf16[1,64,1536]{2,1,0:T(8,128)(2,1)}, bf16[1,64,1536]{2,1,0:T(8,128)(2,1)S(1)}, u32[]{:S(2)}, u32[]{:S(2)}) collective-permute-start(bf16[1,64,1536]{2,1,0:T(8,128)(2,1)} %get-tuple-element.47), channel_id=1, source_target_pairs={{0,24},{2,26},{4,28},{6,30},{8,16},{10,18},{12,20},{14,22},{16,8},... | collective-permute-start | bytes 589832 | tf_op jit(solution)/shard_map/ppermute | solution.py:436
  11.1 4.1 %collective-permute-start.1 = (bf16[64,256]{1,0:T(8,128)(2,1)}, bf16[64,256]{1,0:T(8,128)(2,1)S(1)}, u32[]{:S(2)}, u32[]{:S(2)}) collective-permute-start(bf16[64,256]{1,0:T(8,128)(2,1)} %get-tuple-element.42), channel_id=1, source_target_pairs={{0,1},{1,0},{2,3},{3,2},{4,5},{5,4},{6,7},{7,6},{8,9},{9,8},{10,11... | collective-permute-start | bytes 98312 | tf_op jit(solution)/shard_map/ppermute | solution.py:438
  15.2 0.6 copy-start.6
  15.9 10.3 %copy-start.2 = (bf16[1,64,1536]{2,1,0:T(8,128)(2,1)S(1)}, bf16[1,64,1536]{2,1,0:T(8,128)(2,1)}, u32[]{:S(2)}) copy-start(bf16[1,64,1536]{2,1,0:T(8,128)(2,1)} %get-tuple-element.50.refs_0_) | copy-start | bytes 589828
  26.2 6.4 %collective-permute-start.8 = (bf16[4,64,512]{2,1,0:T(8,128)(2,1)S(1)}, bf16[4,64,512]{2,1,0:T(8,128)(2,1)S(1)}, u32[]{:S(2)}, u32[]{:S(2)}) collective-permute-start(bf16[4,64,512]{2,1,0:T(8,128)(2,1)S(1)} %weight_pieces.1.refs_2_), channel_id=1, source_target_pairs={{0,4},{2,6},{4,0},{6,2},{8,12},{10,14},{12,8},{14,10},{16,20},{18,... | collective-permute-start | bytes 786440 | tf_op jit(solution)/shard_map/ppermute | solution.py:450
  26.6 8.3 %collective-permute-start.7 = (bf16[1,64,1024]{2,1,0:T(8,128)(2,1)S(1)}, bf16[1,64,1024]{2,1,0:T(8,128)(2,1)S(1)}, u32[]{:S(2)}, u32[]{:S(2)}) collective-permute-start(bf16[1,64,1024]{2,1,0:T(8,128)(2,1)S(1)} %get-tuple-element.79), channel_id=1, source_target_pairs={{0,24},{2,26},{4,28},{6,30},{8,16},{10,18},{12,20},{14,22},{16,8},... | collective-permute-start | bytes 393224 | tf_op jit(solution)/shard_map/ppermute | solution.py:445
  30.5 9.7 %collective-permute-start.6 = (bf16[1,64,1024]{2,1,0:T(8,128)(2,1)S(1)}, bf16[1,64,1024]{2,1,0:T(8,128)(2,1)S(1)}, u32[]{:S(2)}, u32[]{:S(2)}) collective-permute-start(bf16[1,64,1024]{2,1,0:T(8,128)(2,1)S(1)} %get-tuple-element.80), channel_id=1, source_target_pairs={{0,16},{2,18},{4,20},{6,22},{8,24},{10,26},{12,28},{14,30},{16,0},... | collective-permute-start | bytes 393224 | tf_op jit(solution)/shard_map/ppermute | solution.py:445
  30.9 9.2 %collective-permute-start.5 = (bf16[1,64,1024]{2,1,0:T(8,128)(2,1)S(1)}, bf16[1,64,1024]{2,1,0:T(8,128)(2,1)S(1)}, u32[]{:S(2)}, u32[]{:S(2)}) collective-permute-start(bf16[1,64,1024]{2,1,0:T(8,128)(2,1)S(1)} %get-tuple-element.81), channel_id=1, source_target_pairs={{0,8},{2,10},{4,12},{6,14},{8,0},{10,2},{12,4},{14,6},{16,24},{18,... | collective-permute-start | bytes 393224 | tf_op jit(solution)/shard_map/ppermute | solution.py:445
  32.6 29.0 %copy-start.4 = (bf16[4,64,512]{2,1,0:T(8,128)(2,1)}, bf16[4,64,512]{2,1,0:T(8,128)(2,1)S(1)}, u32[]{:S(2)}) copy-start(bf16[4,64,512]{2,1,0:T(8,128)(2,1)S(1)} %collective-permute-done.8.refs_3_) | copy-start | bytes 786436
  40.1 28.6 %all-to-all-start = ((bf16[16,64,512]{2,1,0:T(8,128)(2,1)}), bf16[16,64,512]{2,1,0:T(8,128)(2,1)S(1)}, u32[]{:S(2)}, u32[]{:S(2)}) async-start(bf16[16,64,512]{2,1,0:T(8,128)(2,1)} %neighbour_means.1), calls=%async_computation | async-start | bytes 2097152 | tf_op jit(solution)/shard_map/all_to_all | solution.py:453
  45.8 9.2 %collective-permute-start.12 = (bf16[4,64,512]{2,1,0:T(8,128)(2,1)S(1)}, bf16[4,64,512]{2,1,0:T(8,128)(2,1)S(1)}, u32[]{:S(2)}, u32[]{:S(2)}) collective-permute-start(bf16[4,64,512]{2,1,0:T(8,128)(2,1)S(1)} %weight_pieces.1.refs_2_), channel_id=1, source_target_pairs={{0,1},{1,0},{2,3},{3,2},{4,5},{5,4},{6,7},{7,6},{8,9},{9,8},{10,11... | collective-permute-start | bytes 786440 | tf_op jit(solution)/shard_map/ppermute | solution.py:454
  47.4 12.6 %collective-permute-start.9 = (bf16[8,64,512]{2,1,0:T(8,128)(2,1)S(1)}, bf16[8,64,512]{2,1,0:T(8,128)(2,1)S(1)}, u32[]{:S(2)}, u32[]{:S(2)}) collective-permute-start(bf16[8,64,512]{2,1,0:T(8,128)(2,1)S(1)} %get-tuple-element.59), channel_id=1, source_target_pairs={{0,2},{2,0},{4,6},{6,4},{8,10},{10,8},{12,14},{14,12},{16,18},{18,... | collective-permute-start | bytes 1572872 | tf_op jit(solution)/shard_map/ppermute | solution.py:458
  47.6 12.5 %collective-permute-start.13 = (bf16[4,64,512]{2,1,0:T(8,128)(2,1)S(1)}, bf16[4,64,512]{2,1,0:T(8,128)(2,1)S(1)}, u32[]{:S(2)}, u32[]{:S(2)}) collective-permute-start(bf16[4,64,512]{2,1,0:T(8,128)(2,1)S(1)} %collective-permute-done.8.refs_3_), channel_id=1, source_target_pairs={{0,1},{1,0},{2,3},{3,2},{4,5},{5,4},{6,7},{7,6},{8,9},{9,8},{10,11... | collective-permute-start | bytes 786440 | tf_op jit(solution)/shard_map/ppermute | solution.py:454
  48.1 11.9 %collective-permute-start.10 = (bf16[4,64,512]{2,1,0:T(8,128)(2,1)S(1)}, bf16[4,64,512]{2,1,0:T(8,128)(2,1)S(1)}, u32[]{:S(2)}, u32[]{:S(2)}) collective-permute-start(bf16[4,64,512]{2,1,0:T(8,128)(2,1)S(1)} %weight_pieces.1.refs_2_), channel_id=1, source_target_pairs={{0,2},{2,0},{4,6},{6,4},{8,10},{10,8},{12,14},{14,12},{16,18},{18,... | collective-permute-start | bytes 786440 | tf_op jit(solution)/shard_map/ppermute | solution.py:460
  48.3 11.8 %collective-permute-start.11 = (bf16[4,64,512]{2,1,0:T(8,128)(2,1)S(1)}, bf16[4,64,512]{2,1,0:T(8,128)(2,1)S(1)}, u32[]{:S(2)}, u32[]{:S(2)}) collective-permute-start(bf16[4,64,512]{2,1,0:T(8,128)(2,1)S(1)} %collective-permute-done.8.refs_3_), channel_id=1, source_target_pairs={{0,2},{2,0},{4,6},{6,4},{8,10},{10,8},{12,14},{14,12},{16,18},{18,... | collective-permute-start | bytes 786440 | tf_op jit(solution)/shard_map/ppermute | solution.py:460
  55.0 5.1 %collective-permute-start.14 = (bf16[4,64,512]{2,1,0:T(8,128)(2,1)S(1)}, bf16[4,64,512]{2,1,0:T(8,128)(2,1)S(1)}, u32[]{:S(2)}, u32[]{:S(2)}) collective-permute-start(bf16[4,64,512]{2,1,0:T(8,128)(2,1)S(1)} %collective-permute-done.12.refs_6_), channel_id=1, source_target_pairs={{0,2},{2,0},{4,6},{6,4},{8,10},{10,8},{12,14},{14,12},{16,18},{18,... | collective-permute-start | bytes 786440 | tf_op jit(solution)/shard_map/ppermute | solution.py:461
  60.0 1.5 %collective-permute-start.15 = (bf16[4,64,512]{2,1,0:T(8,128)(2,1)S(1)}, bf16[4,64,512]{2,1,0:T(8,128)(2,1)S(1)}, u32[]{:S(2)}, u32[]{:S(2)}) collective-permute-start(bf16[4,64,512]{2,1,0:T(8,128)(2,1)S(1)} %collective-permute-done.13.refs_7_), channel_id=1, source_target_pairs={{0,2},{2,0},{4,6},{6,4},{8,10},{10,8},{12,14},{14,12},{16,18},{18,... | collective-permute-start | bytes 786440 | tf_op jit(solution)/shard_map/ppermute | solution.py:461
  61.6 1.0 copy-start.5
  63.3 1.0 copy-start
  68.7 1.2 %copy-start.1 = (bf16[16,64,512]{2,1,0:T(8,128)(2,1)S(1)}, bf16[16,64,512]{2,1,0:T(8,128)(2,1)}, u32[]{:S(2)}) copy-start(bf16[16,64,512]{2,1,0:T(8,128)(2,1)} %copy-done) | copy-start | bytes 3145732
  70.0 1.0 copy-start.3
  74.3 3.0 %collective-permute-start.16 = (bf16[8,2,64,512]{3,2,1,0:T(8,128)(2,1)S(1)}, bf16[8,2,64,512]{3,2,1,0:T(8,128)(2,1)S(1)}, u32[]{:S(2)}, u32[]{:S(2)}) collective-permute-start(bf16[8,2,64,512]{3,2,1,0:T(8,128)(2,1)S(1)} %get-tuple-element.66), channel_id=1, source_target_pairs={{0,2},{2,0},{4,6},{6,4},{8,10},{10,8},{12,14},{14,12},{16,18},{18,... | collective-permute-start | bytes 3145736 | tf_op jit(solution)/shard_map/ppermute | solution.py:488
  77.5 8.9 %collective-permute-start.17 = (bf16[2,2,64,512]{3,2,1,0:T(8,128)(2,1)S(1)}, bf16[2,2,64,512]{3,2,1,0:T(8,128)(2,1)S(1)}, u32[]{:S(2)}, u32[]{:S(2)}) collective-permute-start(bf16[2,2,64,512]{3,2,1,0:T(8,128)(2,1)S(1)} %get-tuple-element.68), channel_id=1, source_target_pairs={{0,4},{2,6},{4,0},{6,2},{8,12},{10,14},{12,8},{14,10},{16,20},{18,... | collective-permute-start | bytes 786440 | tf_op jit(solution)/shard_map/ppermute | solution.py:392
  79.5 10.1 %collective-permute-start.19 = (bf16[2,2,64,512]{3,2,1,0:T(8,128)(2,1)S(1)}, bf16[2,2,64,512]{3,2,1,0:T(8,128)(2,1)S(1)}, u32[]{:S(2)}, u32[]{:S(2)}) collective-permute-start(bf16[2,2,64,512]{3,2,1,0:T(8,128)(2,1)S(1)} %get-tuple-element.72), channel_id=1, source_target_pairs={{0,8},{2,10},{4,12},{6,14},{8,0},{10,2},{12,4},{14,6},{16,24},{18,... | collective-permute-start | bytes 786440 | tf_op jit(solution)/shard_map/ppermute | solution.py:392
  86.4 6.4 %collective-permute-start.18 = (bf16[2,64,512]{2,1,0:T(8,128)(2,1)S(1)}, bf16[2,64,512]{2,1,0:T(8,128)(2,1)S(1)}, u32[]{:S(2)}, u32[]{:S(2)}) collective-permute-start(bf16[2,64,512]{2,1,0:T(8,128)(2,1)S(1)} %get-tuple-element.70), channel_id=1, source_target_pairs={{0,8},{2,10},{4,12},{6,14},{8,0},{10,2},{12,4},{14,6},{16,24},{18,... | collective-permute-start | bytes 393224 | tf_op jit(solution)/shard_map/ppermute | solution.py:394
  89.6 5.0 %collective-permute-start.20 = (bf16[2,64,512]{2,1,0:T(8,128)(2,1)S(1)}, bf16[2,64,512]{2,1,0:T(8,128)(2,1)S(1)}, u32[]{:S(2)}, u32[]{:S(2)}) collective-permute-start(bf16[2,64,512]{2,1,0:T(8,128)(2,1)S(1)} %get-tuple-element.74), channel_id=1, source_target_pairs={{0,4},{2,6},{4,0},{6,2},{8,12},{10,14},{12,8},{14,10},{16,20},{18,... | collective-permute-start | bytes 393224 | tf_op jit(solution)/shard_map/ppermute | solution.py:396
  94.7 7.4 %collective-permute-start.21 = (bf16[1,2,64,512]{3,2,1,0:T(8,128)(2,1)S(1)}, bf16[1,2,64,512]{3,2,1,0:T(8,128)(2,1)S(1)}, u32[]{:S(2)}, u32[]{:S(2)}) collective-permute-start(bf16[1,2,64,512]{3,2,1,0:T(8,128)(2,1)S(1)} %get-tuple-element.76), channel_id=1, source_target_pairs={{0,16},{2,18},{4,20},{6,22},{8,24},{10,26},{12,28},{14,30},{16,0},... | collective-permute-start | bytes 393224 | tf_op jit(solution)/shard_map/ppermute | solution.py:401
  102.2 5.0 %collective-permute-start.22 = (bf16[1,2,64,512]{3,2,1,0:T(8,128)(2,1)S(1)}, bf16[1,2,64,512]{3,2,1,0:T(8,128)(2,1)S(1)}, u32[]{:S(2)}, u32[]{:S(2)}) collective-permute-start(bf16[1,2,64,512]{3,2,1,0:T(8,128)(2,1)S(1)} %rounded_sum.1.kept_ref), channel_id=1, source_target_pairs={{0,1},{1,0},{2,3},{3,2},{4,5},{5,4},{6,7},{7,6},{8,9},{9,8},{10,11... | collective-permute-start | bytes 393224 | tf_op jit(solution)/shard_map/ppermute | solution.py:409

commit v5 on v4

--- a/solution.py
+++ b/solution.py
@@ -268,15 +268,17 @@
     pieces = len(weight_masks)
     kept_ref, got_ref = refs[:2]
     mine_refs, other_refs = refs[2 : 2 + pieces], refs[2 + pieces : 2 + 2 * pieces]
-    linear_ref, weight_ref = refs[2 + 2 * pieces :]
+    cot_ref, linear_ref, beside_ref = refs[2 + 2 * pieces :]
     features = features_in_order(row_masks, kept_ref, got_ref)
     side = lax.axis_index("dom") % 2
 
     def fill(self_refs, neighbour_refs):
         at = 0
         for ref in neighbour_refs:
-            weight_ref[at : at + ref.shape[0]] = ref[...]
-            at += ref.shape[0]
+            part = ref[...].reshape(-1, ref.shape[2])
+            beside_ref[at : at + part.shape[0]] = part
+            at += part.shape[0]
+        beside_ref[at:] = cot_ref[...]
         fill_linear(features, weight_masks, self_refs, linear_ref, linear_ref, False)
 
     @pl.when(side == 0)
@@ -304,45 +306,46 @@
         linear_ref[at : at + step] = total
 
 
-def forward_kernel(row_masks, masks, ready, *refs):
-    mean_ref, weight_ref, base_ref, cot_ref, kept_ref, got_ref = refs[:6]
-    hidden_ref, other_sums_ref, my_sums_ref, linear_ref, grad_ref = refs[6:]
+def forward_kernel(
+    row_masks, masks, mean_ref, beside_ref, base_ref, kept_ref, got_ref,
+    hidden_ref, grad_ref, other_sums_ref, my_sums_ref, linear_ref,
+):
     features, means = features_in_order(row_masks, kept_ref, got_ref), means_in_order(mean_ref)
-    ready(1, 2)
-    fill_linear(means, [masks], [weight_ref], base_ref, linear_ref, True)
-    ready(3)
-    step = min(128, linear_ref.shape[0])
-    for at in range(0, linear_ref.shape[0], step):
+    rows = linear_ref.shape[0]
+    depth = beside_ref.shape[0] - rows
+    fill_linear(means, [masks], [beside_ref.at[0:depth]], base_ref, linear_ref, True)
+    step = min(128, rows)
+    for at in range(0, rows, step):
         value, slope = gelu_pair(linear_ref[at : at + step])
         hidden_ref[at : at + step] = value.astype(bf16)
-        grad_ref[at : at + step] = (cot_ref[at : at + step].astype(f32) * slope).astype(bf16)
-    ready(4, 5)
-    fill_sums(1, features, means, grad_ref, other_sums_ref)
-    fill_sums(0, features, means, grad_ref, my_sums_ref)
-
-
-def fill_sums(core, features, means, grad_ref, sums_ref):
-    for i, source in enumerate((features, means)):
-        part = jnp.concatenate(
-            [source(mask) for mask in range(core, 2 * sums_ref.shape[0], 2)], axis=0
-        )
-        sums = jnp.dot(part, grad_ref[...], preferred_element_type=f32)
-        sums_ref[:, i] = sums.astype(sums_ref.dtype).reshape(sums_ref[:, i].shape)
-
-
-def first_kernel(kept_ref, got_ref, own_ref, own_sent_ref, neigh_ref, neigh_sent_ref):
+        cot = beside_ref[depth + at : depth + at + step].astype(f32)
+        grad_ref[at : at + step] = (cot * slope).astype(bf16)
+    fill_sums(1, features, grad_ref, other_sums_ref)
+    fill_sums(0, features, grad_ref, my_sums_ref)
+
+
+def neighbour_sums_kernel(mean_ref, grad_ref, other_sums_ref, my_sums_ref):
+    means = means_in_order(mean_ref)
+    fill_sums(1, means, grad_ref, other_sums_ref)
+    fill_sums(0, means, grad_ref, my_sums_ref)
+
+
+def fill_sums(core, source, grad_ref, sums_ref):
+    part = jnp.concatenate(
+        [source(mask) for mask in range(core, 2 * sums_ref.shape[0], 2)], axis=0
+    )
+    sums = jnp.dot(part, grad_ref[...], preferred_element_type=f32)
+    sums_ref[...] = sums.astype(sums_ref.dtype).reshape(sums_ref.shape)
+
+
+def first_kernel(place, kept_ref, got_ref, out_ref, sent_ref):
     for at in range(kept_ref.shape[0]):
-        far, a, b = at // 4, at // 2 % 2, at % 2
-        own = kept_ref[at, 0] + got_ref[at, 0].astype(f32)
-        neigh = kept_ref[at, 1] + got_ref[at, 1].astype(f32)
-        if b == 0:
-            own_ref[far, a] = own
+        far, rest = at // 4, (at // 2 % 2, at % 2)
+        total = kept_ref[at] + got_ref[at].astype(f32)
+        if rest[place] == 0:
+            out_ref[far, rest[1 - place]] = total
         else:
-            own_sent_ref[far, a] = own.astype(bf16)
-        if a == 0:
-            neigh_ref[far, b] = neigh
-        else:
-            neigh_sent_ref[far, b] = neigh.astype(bf16)
+            sent_ref[far, rest[1 - place]] = total.astype(bf16)
 
 
 def second_kernel(kept_ref, got_ref, out_ref, sent_ref):
@@ -377,22 +380,26 @@
     neigh_ref[...] = total[0, 1]
 
 
-def sum_gradients(kept, got):
+def sum_gradients(own_kept, own_got, neigh_kept, neigh_got):
     feat, dom = lax.axis_size("feat"), lax.axis_size("dom")
-    depth, hid = kept.shape[2:]
+    depth, hid = own_kept.shape[1:]
     far = feat // 8
 
     def pair(*lead):
         shape = (*lead, depth, hid)
         return [jax.ShapeDtypeStruct(shape, f32), jax.ShapeDtypeStruct(shape, bf16)]
 
-    own, own_sent, neigh, neigh_sent = local_call(
-        first_kernel, "first_sum", pair(far, 2) + pair(far, 2), (kept, got)
-    )
-    own_got, neigh_got = flip("feat", 2)(own_sent), flip("feat", 4)(neigh_sent)
-    own, own_sent = local_call(second_kernel, "own_sum", pair(far), (own, own_got))
+    own, own_sent = local_call(
+        functools.partial(first_kernel, 1), "own_first", pair(far, 2), (own_kept, own_got)
+    )
+    own_got = flip("feat", 2)(own_sent)
+    neigh, neigh_sent = local_call(
+        functools.partial(first_kernel, 0), "neigh_first", pair(far, 2), (neigh_kept, neigh_got)
+    )
+    neigh_got = flip("feat", 4)(neigh_sent)
+    own, own_sent = local_call(second_kernel, "own_second", pair(far), (own, own_got))
     own_got = flip("feat", 4)(own_sent)
-    neigh, neigh_sent = local_call(second_kernel, "neigh_sum", pair(far), (neigh, neigh_got))
+    neigh, neigh_sent = local_call(second_kernel, "neigh_second", pair(far), (neigh, neigh_got))
     neigh_got = flip("feat", 2)(neigh_sent)
     half = far // 2
     kept, sent = local_call(
@@ -460,33 +467,31 @@
     pieces = pieces + [flip("feat", 1)(p) for p in pieces]
     others = others + [flip("feat", 1)(p) for p in others]
     weight_masks = weight_masks + [flipped(m, 1) for m in weight_masks]
-    sums = (feat // 2, 2, depth, hid)
-    linear, weights = local_call(
+    linear, beside = local_call(
         functools.partial(own_linear_kernel, row_masks, weight_masks),
         "own_linear",
         [
             jax.ShapeDtypeStruct((rows, hid), f32),
-            jax.ShapeDtypeStruct((feat, depth, hid), bf16),
+            jax.ShapeDtypeStruct((feat * depth + rows, hid), bf16),
         ],
-        (*parts, *pieces, *others),
-
-    )
-    hidden, sent, kept = local_call(
+        (*parts, *pieces, *others, cotangent),
+    )
+    square = jax.ShapeDtypeStruct((rows, hid), bf16)
+    sums = (feat // 2, depth, hid)
+    sums = [jax.ShapeDtypeStruct(sums, bf16), jax.ShapeDtypeStruct(sums, f32)]
+    hidden, grad_linear, own_sent, own_kept = local_call(
         functools.partial(forward_kernel, row_masks, sum(weight_masks, [])),
         "forward",
-        [
-            jax.ShapeDtypeStruct((rows, hid), bf16),
-            jax.ShapeDtypeStruct(sums, bf16),
-            jax.ShapeDtypeStruct(sums, f32),
-        ],
-        (own_mean, weights, linear, cotangent, *parts),
-        scratch=[pltpu.VMEM((rows, hid), f32), pltpu.VMEM((rows, hid), bf16)],
-        lazy=True,
-        still=(0,),
-        limit=24 * 2**20,
-    )
-    got = flip("feat", 1)(sent)
-    grad_self, grad_neighbour = sum_gradients(kept, got)
+        [square, square, *sums],
+        (own_mean, beside, linear, *parts),
+        scratch=[pltpu.VMEM((rows, hid), f32)],
+    )
+    own_got = flip("feat", 1)(own_sent)
+    neigh_sent, neigh_kept = local_call(
+        neighbour_sums_kernel, "neighbour_sums", sums, (own_mean, grad_linear)
+    )
+    neigh_got = flip("feat", 1)(neigh_sent)
+    grad_self, grad_neighbour = sum_gradients(own_kept, own_got, neigh_kept, neigh_got)
     return (hidden, grad_self, grad_neighbour)
 
 

time: 108 us -> 107 us (level)
  waiting for transfers between devices: 48.2 us -> 46.7 us
    ppermute x1, starting transfers between devices: 3.21 us -> 1.8 us  [sum_gradients(): own_got = flip('feat', 4)(own_sent)]
    all_to_all x1, waiting for transfers between devices: 4.46 us -> 3.17 us  [on_device(): own_mean = lax.all_to_all(means, 'feat', 0, 0, tiled=True)]
    ppermute x3 -> x4, waiting for transfers between devices: 6.16 us -> 6.57 us  [the longest x1 5.11 us: sum_gradients(): neigh_got = flip('feat', 4)(neigh_sent)]
    pallas_call x12 -> x14, Pallas kernels: 18.5 us -> 18.4 us  [local_call(): pl.pallas_call(kernel, out_shape=outs, in_specs=in_specs, out_specs=[whol...]
    ppermute x3 -> x4, starting transfers between devices: 5.68 us -> 5.81 us  [the longest x1 3.45 us: sum_gradients(): neigh_got = flip('feat', 4)(neigh_sent)]
  transfers between devices with their start and end apart: 24 -> 25, of which waited for: 14 -> 14; matrix products, arithmetic and copies ran while one was open for 0% -> 0% of each run, Pallas kernels for 10% -> 11%
where the time goes in v5:
time: 107 us; the launch traced here: 106 us
  waiting for transfers between devices  46.7 us (44%)
  starting transfers between devices  35.1 us (33%)
  Pallas kernels  18.4 us (17%)
  local copies, waits for them, and re-layouts  5.22 us (5%)
    pallas_call x14, Pallas kernels, local_call(): pl.pallas_call(kernel, out_shape=outs, in_specs=in_specs, out_specs=[whol...  18.4 us
    ppermute x2, waiting for transfers between devices, on_device(): others = [flip('dom', 1)(p) for p in pieces]  11.4 us
    ppermute x3, waiting for transfers between devices, on_device(): flip('feat', i * below)(came[i:i + 1])  7.55 us
    ppermute x1, waiting for transfers between devices, sum_gradients(): got = flip('feat', half * 8)(sent)  5.67 us
    all_to_all x1, starting transfers between devices, on_device(): own_mean = lax.all_to_all(means, 'feat', 0, 0, tiled=True)  5.63 us
    unnamed x14, local copies, waits for them, and re-layouts  5.19 us
    ppermute x1, waiting for transfers between devices, sum_gradients(): neigh_got = flip('feat', 4)(neigh_sent)  5.11 us
    ppermute x3, starting transfers between devices, on_device(): flip('feat', i * below)(came[i:i + 1])  4.53 us
  transfers between devices with their start and end apart: 25, of which 14 were waited for; matrix products, arithmetic and copies ran while one was open for 0% of the time, Pallas kernels for 11%

profile of v5, /device:TPU:0, one launch (start us, length us, event | category | flops | bytes accessed | tf_op | source)
XLA Modules:
  0.0 106.2 jit_solution(7135285253859755208)
XLA Ops:
  0.6 3.2 %open_exchange.1 = (bf16[64,256]{1,0:T(8,128)(2,1)}, bf16[4,64,1024]{2,1,0:T(8,128)(2,1)}, bf16[1,64,1536]{2,1,0:T(8,128)(2,1)}, bf16[1,64,1536]{2,1,0:T(8,128)(...) custom-call(s32[2,2]{1,0:T(2,128)} %refs_2_.3, bf16[64,8192]{1,0:T(8,128)(2,1)} %bitcast.7, ...), custom_call_target="tpu_custom_call" | custom-call | tf_op jit(solution)/shard_map/open_exchange/pallas_call | solution.py:79
  3.8 3.0 %collective-permute-start = (bf16[4,64,1024]{2,1,0:T(8,128)(2,1)}, bf16[4,64,1024]{2,1,0:T(8,128)(2,1)S(1)}, u32[]{:S(2)}, u32[]{:S(2)}) collective-permute-start(bf16[4,64,1024]{2,1,0:T(8,128)(2,1)} %get-tuple-element.44), channel_id=1, source_target_pairs={{0,4},{2,6},{4,0},{6,2},{8,12},{10,14},{12,8},{14,10},{16,20},{18,... | collective-permute-start | bytes 1572872 | tf_op jit(solution)/shard_map/ppermute | solution.py:442
  6.8 1.6 %collective-permute-start.2 = (bf16[1,64,1536]{2,1,0:T(8,128)(2,1)}, bf16[1,64,1536]{2,1,0:T(8,128)(2,1)S(1)}, u32[]{:S(2)}, u32[]{:S(2)}) collective-permute-start(bf16[1,64,1536]{2,1,0:T(8,128)(2,1)} %get-tuple-element.48), channel_id=1, source_target_pairs={{0,8},{2,10},{4,12},{6,14},{8,0},{10,2},{12,4},{14,6},{16,24},{18,... | collective-permute-start | bytes 589832 | tf_op jit(solution)/shard_map/ppermute | solution.py:443
  8.4 2.6 %collective-permute-start.3 = (bf16[1,64,1536]{2,1,0:T(8,128)(2,1)}, bf16[1,64,1536]{2,1,0:T(8,128)(2,1)S(1)}, u32[]{:S(2)}, u32[]{:S(2)}) collective-permute-start(bf16[1,64,1536]{2,1,0:T(8,128)(2,1)} %get-tuple-element.49), channel_id=1, source_target_pairs={{0,16},{2,18},{4,20},{6,22},{8,24},{10,26},{12,28},{14,30},{16,0},... | collective-permute-start | bytes 589832 | tf_op jit(solution)/shard_map/ppermute | solution.py:443
  11.0 0.2 collective-permute-start.4
  11.2 1.5 %collective-permute-start.1 = (bf16[64,256]{1,0:T(8,128)(2,1)}, bf16[64,256]{1,0:T(8,128)(2,1)S(1)}, u32[]{:S(2)}, u32[]{:S(2)}) collective-permute-start(bf16[64,256]{1,0:T(8,128)(2,1)} %get-tuple-element.45), channel_id=1, source_target_pairs={{0,1},{1,0},{2,3},{3,2},{4,5},{5,4},{6,7},{7,6},{8,9},{9,8},{10,11... | collective-permute-start | bytes 98312 | tf_op jit(solution)/shard_map/ppermute | solution.py:445
  12.7 2.6 %collective-permute-done.1.refs_4_ = bf16[64,256]{1,0:T(8,128)(2,1)S(1)} collective-permute-done((bf16[64,256]{1,0:T(8,128)(2,1)}, bf16[64,256]{1,0:T(8,128)(2,1)S(1)}, u32[]{:S(2)}, u32[]{:S(2)}) %collective-permute-start.1) | collective-permute-done | bytes 32800 | tf_op jit(solution)/shard_map/ppermute | solution.py:445
  15.3 0.6 copy-done.6
  15.9 10.2 %neighbour_means.1 = bf16[16,64,512]{2,1,0:T(8,128)(2,1)} custom-call(s32[8,64]{1,0:T(8,128)} %bitcast.9, s32[8,64]{1,0:T(8,128)} %bitcast.10, s32[2,2]{1,0:T(2,128)} %refs_2_.3, bf16[64,8192]{1,0:T(8,128)(2,1)} %bitcast.8, bf16[64,256]{1,0:T(8,128)(2,1)} %copy-done.6, s32[2,2,256]{2,1,0:T(2,128)} %refs_5_.1, bf16[64,128,128]{2,1,0:T(8,128)(2,1)} %refs_6_.1), custom_call_target="tpu_custom_call" | custom-call | tf_op jit(solution)/shard_map/neighbour_means/pallas_call | solution.py:79
  26.2 0.4 collective-permute-start.8
  26.7 3.9 %collective-permute-start.7 = (bf16[1,64,1024]{2,1,0:T(8,128)(2,1)S(1)}, bf16[1,64,1024]{2,1,0:T(8,128)(2,1)S(1)}, u32[]{:S(2)}, u32[]{:S(2)}) collective-permute-start(bf16[1,64,1024]{2,1,0:T(8,128)(2,1)S(1)} %get-tuple-element.85), channel_id=1, source_target_pairs={{0,24},{2,26},{4,28},{6,30},{8,16},{10,18},{12,20},{14,22},{16,8},... | collective-permute-start | bytes 393224 | tf_op jit(solution)/shard_map/ppermute | solution.py:452
  30.6 0.5 collective-permute-start.6
  31.0 0.2 collective-permute-start.5
  31.2 1.5 %collective-permute-done.8.refs_3_ = bf16[4,64,512]{2,1,0:T(8,128)(2,1)S(1)} collective-permute-done((bf16[4,64,512]{2,1,0:T(8,128)(2,1)S(1)}, bf16[4,64,512]{2,1,0:T(8,128)(2,1)S(1)}, u32[]{:S(2)}, u32[]{:S(2)}) %collective-permute-start.8) | collective-permute-done | bytes 262176 | tf_op jit(solution)/shard_map/ppermute | solution.py:457
  32.7 2.3 %collective-permute-done.7.refs_7_ = bf16[1,64,1024]{2,1,0:T(8,128)(2,1)S(1)} collective-permute-done((bf16[1,64,1024]{2,1,0:T(8,128)(2,1)S(1)}, bf16[1,64,1024]{2,1,0:T(8,128)(2,1)S(1)}, u32[]{:S(2)}, u32[]{:S(2)}) %collective-permute-start.7) | collective-permute-done | bytes 131104 | tf_op jit(solution)/shard_map/ppermute | solution.py:452
  35.0 5.3 %collective-permute-done.6.refs_6_ = bf16[1,64,1024]{2,1,0:T(8,128)(2,1)S(1)} collective-permute-done((bf16[1,64,1024]{2,1,0:T(8,128)(2,1)S(1)}, bf16[1,64,1024]{2,1,0:T(8,128)(2,1)S(1)}, u32[]{:S(2)}, u32[]{:S(2)}) %collective-permute-start.6) | collective-permute-done | bytes 131104 | tf_op jit(solution)/shard_map/ppermute | solution.py:452
  40.2 5.6 %all-to-all-start = ((bf16[16,64,512]{2,1,0:T(8,128)(2,1)}), bf16[16,64,512]{2,1,0:T(8,128)(2,1)S(1)}, u32[]{:S(2)}, u32[]{:S(2)}) async-start(bf16[16,64,512]{2,1,0:T(8,128)(2,1)} %neighbour_means.1), calls=%async_computation | async-start | bytes 2097152 | tf_op jit(solution)/shard_map/all_to_all | solution.py:460
  45.9 1.6 %collective-permute-start.12 = (bf16[4,64,512]{2,1,0:T(8,128)(2,1)S(1)}, bf16[4,64,512]{2,1,0:T(8,128)(2,1)S(1)}, u32[]{:S(2)}, u32[]{:S(2)}) collective-permute-start(bf16[4,64,512]{2,1,0:T(8,128)(2,1)S(1)} %weight_pieces.1.refs_2_), channel_id=1, source_target_pairs={{0,1},{1,0},{2,3},{3,2},{4,5},{5,4},{6,7},{7,6},{8,9},{9,8},{10,11... | collective-permute-start | bytes 786440 | tf_op jit(solution)/shard_map/ppermute | solution.py:461
  47.5 0.1 collective-permute-start.9
  47.6 0.5 collective-permute-start.13
  48.2 0.2 collective-permute-start.10
  48.3 0.3 collective-permute-start.11
  48.7 6.4 %collective-permute-done.12.refs_6_ = bf16[4,64,512]{2,1,0:T(8,128)(2,1)S(1)} collective-permute-done((bf16[4,64,512]{2,1,0:T(8,128)(2,1)S(1)}, bf16[4,64,512]{2,1,0:T(8,128)(2,1)S(1)}, u32[]{:S(2)}, u32[]{:S(2)}) %collective-permute-start.12) | collective-permute-done | bytes 262176 | tf_op jit(solution)/shard_map/ppermute | solution.py:461
  55.0 5.0 %collective-permute-done.13.refs_7_ = bf16[4,64,512]{2,1,0:T(8,128)(2,1)S(1)} collective-permute-done((bf16[4,64,512]{2,1,0:T(8,128)(2,1)S(1)}, bf16[4,64,512]{2,1,0:T(8,128)(2,1)S(1)}, u32[]{:S(2)}, u32[]{:S(2)}) %collective-permute-start.13) | collective-permute-done | bytes 262176 | tf_op jit(solution)/shard_map/ppermute | solution.py:461
  60.1 1.5 %collective-permute-done.15.refs_9_ = bf16[4,64,512]{2,1,0:T(8,128)(2,1)S(1)} collective-permute-done((bf16[4,64,512]{2,1,0:T(8,128)(2,1)S(1)}, bf16[4,64,512]{2,1,0:T(8,128)(2,1)S(1)}, u32[]{:S(2)}, u32[]{:S(2)}) %collective-permute-start.15) | collective-permute-done | bytes 262176 | tf_op jit(solution)/shard_map/ppermute | solution.py:468
  61.6 1.0 copy-done.3
  62.7 0.9 copy-done.5
  63.6 0.8 own_linear.1
  64.5 1.2 %copy-done = bf16[1536,512]{1,0:T(8,128)(2,1)} copy-done((bf16[1536,512]{1,0:T(8,128)(2,1)}, bf16[1536,512]{1,0:T(8,128)(2,1)S(1)}, u32[]{:S(2)}) %copy-start) | copy-done | bytes 1572888
  65.6 3.2 %all-to-all-done.mean_ref = bf16[16,64,512]{2,1,0:T(8,128)(2,1)S(1)} async-done(((bf16[16,64,512]{2,1,0:T(8,128)(2,1)}), bf16[16,64,512]{2,1,0:T(8,128)(2,1)S(1)}, u32[]{:S(2)}, u32[]{:S(2)}) %all-to-all-start) | async-done | bytes 1048608 | tf_op jit(solution)/shard_map/all_to_all | solution.py:460
  68.8 1.4 %copy-done.1 = bf16[1536,512]{1,0:T(8,128)(2,1)S(1)} copy-done((bf16[1536,512]{1,0:T(8,128)(2,1)S(1)}, bf16[1536,512]{1,0:T(8,128)(2,1)}, u32[]{:S(2)}) %copy-start.1) | copy-done | bytes 1572888
  70.2 2.3 %forward.1 = (bf16[512,512]{1,0:T(8,128)(2,1)}, bf16[512,512]{1,0:T(8,128)(2,1)S(1)}, bf16[8,64,512]{2,1,0:T(8,128)(2,1)S(1)}, f32[8,64,512]{2,1,0:T(8,128)S(1)}) custom-call(bf16[16,64,512]{2,1,0:T(8,128)(2,1)S(1)} %all-to-all-done.mean_ref, bf16[1536,512]{1,0:T(8,128)(2,1)S(1)} %copy-done.1, f32[512,512]{1,0:T(8,128)S(1)} %get-tuple-element.66.base_ref, ...), custom_call_target="tpu_custom_call" | custom-call | tf_op jit(solution)/shard_map/forward/pallas_call | solution.py:79
  72.5 0.7 neighbour_sums.1
  73.3 0.7 collective-permute-start.19
  74.0 1.5 %collective-permute-done.19.got_ref = bf16[8,64,512]{2,1,0:T(8,128)(2,1)S(1)} collective-permute-done((bf16[8,64,512]{2,1,0:T(8,128)(2,1)S(1)}, bf16[8,64,512]{2,1,0:T(8,128)(2,1)S(1)}, u32[]{:S(2)}, u32[]{:S(2)}) %collective-permute-start.19) | collective-permute-done | bytes 524320 | tf_op jit(solution)/shard_map/ppermute | solution.py:493
  75.4 0.1 neigh_first.1
  75.5 3.5 %collective-permute-start.20 = (bf16[2,2,64,512]{3,2,1,0:T(8,128)(2,1)S(1)}, bf16[2,2,64,512]{3,2,1,0:T(8,128)(2,1)S(1)}, u32[]{:S(2)}, u32[]{:S(2)}) collective-permute-start(bf16[2,2,64,512]{3,2,1,0:T(8,128)(2,1)S(1)} %get-tuple-element.78), channel_id=1, source_target_pairs={{0,8},{2,10},{4,12},{6,14},{8,0},{10,2},{12,4},{14,6},{16,24},{18,... | collective-permute-start | bytes 786440 | tf_op jit(solution)/shard_map/ppermute | solution.py:399
  79.1 1.6 %collective-permute-start.17 = (bf16[2,2,64,512]{3,2,1,0:T(8,128)(2,1)S(1)}, bf16[2,2,64,512]{3,2,1,0:T(8,128)(2,1)S(1)}, u32[]{:S(2)}, u32[]{:S(2)}) collective-permute-start(bf16[2,2,64,512]{3,2,1,0:T(8,128)(2,1)S(1)} %get-tuple-element.71), channel_id=1, source_target_pairs={{0,4},{2,6},{4,0},{6,2},{8,12},{10,14},{12,8},{14,10},{16,20},{18,... | collective-permute-start | bytes 786440 | tf_op jit(solution)/shard_map/ppermute | solution.py:395
  80.7 5.1 %collective-permute-done.20.got_ref = bf16[2,2,64,512]{3,2,1,0:T(8,128)(2,1)S(1)} collective-permute-done((bf16[2,2,64,512]{3,2,1,0:T(8,128)(2,1)S(1)}, bf16[2,2,64,512]{3,2,1,0:T(8,128)(2,1)S(1)}, u32[]{:S(2)}, u32[]{:S(2)}) %collective-permute-start.20) | collective-permute-done | bytes 262176 | tf_op jit(solution)/shard_map/ppermute | solution.py:399
  85.9 1.6 %collective-permute-start.21 = (bf16[2,64,512]{2,1,0:T(8,128)(2,1)S(1)}, bf16[2,64,512]{2,1,0:T(8,128)(2,1)S(1)}, u32[]{:S(2)}, u32[]{:S(2)}) collective-permute-start(bf16[2,64,512]{2,1,0:T(8,128)(2,1)S(1)} %get-tuple-element.80), channel_id=1, source_target_pairs={{0,4},{2,6},{4,0},{6,2},{8,12},{10,14},{12,8},{14,10},{16,20},{18,... | collective-permute-start | bytes 393224 | tf_op jit(solution)/shard_map/ppermute | solution.py:403
  87.5 1.8 %collective-permute-start.18 = (bf16[2,64,512]{2,1,0:T(8,128)(2,1)S(1)}, bf16[2,64,512]{2,1,0:T(8,128)(2,1)S(1)}, u32[]{:S(2)}, u32[]{:S(2)}) collective-permute-start(bf16[2,64,512]{2,1,0:T(8,128)(2,1)S(1)} %get-tuple-element.73), channel_id=1, source_target_pairs={{0,8},{2,10},{4,12},{6,14},{8,0},{10,2},{12,4},{14,6},{16,24},{18,... | collective-permute-start | bytes 393224 | tf_op jit(solution)/shard_map/ppermute | solution.py:401
  89.3 1.8 %collective-permute-done.21.neigh_got_ref = bf16[2,64,512]{2,1,0:T(8,128)(2,1)S(1)} collective-permute-done((bf16[2,64,512]{2,1,0:T(8,128)(2,1)S(1)}, bf16[2,64,512]{2,1,0:T(8,128)(2,1)S(1)}, u32[]{:S(2)}, u32[]{:S(2)}) %collective-permute-start.21) | collective-permute-done | bytes 131104 | tf_op jit(solution)/shard_map/ppermute | solution.py:403
  91.1 1.4 %collective-permute-done.18.own_got_ref = bf16[2,64,512]{2,1,0:T(8,128)(2,1)S(1)} collective-permute-done((bf16[2,64,512]{2,1,0:T(8,128)(2,1)S(1)}, bf16[2,64,512]{2,1,0:T(8,128)(2,1)S(1)}, u32[]{:S(2)}, u32[]{:S(2)}) %collective-permute-start.18) | collective-permute-done | bytes 131104 | tf_op jit(solution)/shard_map/ppermute | solution.py:401
  92.6 2.2 %collective-permute-start.22 = (bf16[1,2,64,512]{3,2,1,0:T(8,128)(2,1)S(1)}, bf16[1,2,64,512]{3,2,1,0:T(8,128)(2,1)S(1)}, u32[]{:S(2)}, u32[]{:S(2)}) collective-permute-start(bf16[1,2,64,512]{3,2,1,0:T(8,128)(2,1)S(1)} %get-tuple-element.82), channel_id=1, source_target_pairs={{0,16},{2,18},{4,20},{6,22},{8,24},{10,26},{12,28},{14,30},{16,0},... | collective-permute-start | bytes 393224 | tf_op jit(solution)/shard_map/ppermute | solution.py:408
  94.7 5.7 %collective-permute-done.22.got_ref = bf16[1,2,64,512]{3,2,1,0:T(8,128)(2,1)S(1)} collective-permute-done((bf16[1,2,64,512]{3,2,1,0:T(8,128)(2,1)S(1)}, bf16[1,2,64,512]{3,2,1,0:T(8,128)(2,1)S(1)}, u32[]{:S(2)}, u32[]{:S(2)}) %collective-permute-start.22) | collective-permute-done | bytes 131104 | tf_op jit(solution)/shard_map/ppermute | solution.py:408
  100.4 1.6 %collective-permute-start.23 = (bf16[1,2,64,512]{3,2,1,0:T(8,128)(2,1)S(1)}, bf16[1,2,64,512]{3,2,1,0:T(8,128)(2,1)S(1)}, u32[]{:S(2)}, u32[]{:S(2)}) collective-permute-start(bf16[1,2,64,512]{3,2,1,0:T(8,128)(2,1)S(1)} %rounded_sum.1.kept_ref), channel_id=1, source_target_pairs={{0,1},{1,0},{2,3},{3,2},{4,5},{5,4},{6,7},{7,6},{8,9},{9,8},{10,11... | collective-permute-start | bytes 393224 | tf_op jit(solution)/shard_map/ppermute | solution.py:416
  102.0 3.5 %collective-permute-done.23.got_ref = bf16[1,2,64,512]{3,2,1,0:T(8,128)(2,1)S(1)} collective-permute-done((bf16[1,2,64,512]{3,2,1,0:T(8,128)(2,1)S(1)}, bf16[1,2,64,512]{3,2,1,0:T(8,128)(2,1)S(1)}, u32[]{:S(2)}, u32[]{:S(2)}) %collective-permute-start.23) | collective-permute-done | bytes 131104 | tf_op jit(solution)/shard_map/ppermute | solution.py:416
  105.5 0.7 last_sum.1
  (31 shorter events, 0.5 us)
Async XLA Ops:
  3.8 22.8 %collective-permute-start = (bf16[4,64,1024]{2,1,0:T(8,128)(2,1)}, bf16[4,64,1024]{2,1,0:T(8,128)(2,1)S(1)}, u32[]{:S(2)}, u32[]{:S(2)}) collective-permute-start(bf16[4,64,1024]{2,1,0:T(8,128)(2,1)} %get-tuple-element.44), channel_id=1, source_target_pairs={{0,4},{2,6},{4,0},{6,2},{8,12},{10,14},{12,8},{14,10},{16,20},{18,... | collective-permute-start | bytes 1572872 | tf_op jit(solution)/shard_map/ppermute | solution.py:442
  6.8 19.4 %collective-permute-start.2 = (bf16[1,64,1536]{2,1,0:T(8,128)(2,1)}, bf16[1,64,1536]{2,1,0:T(8,128)(2,1)S(1)}, u32[]{:S(2)}, u32[]{:S(2)}) collective-permute-start(bf16[1,64,1536]{2,1,0:T(8,128)(2,1)} %get-tuple-element.48), channel_id=1, source_target_pairs={{0,8},{2,10},{4,12},{6,14},{8,0},{10,2},{12,4},{14,6},{16,24},{18,... | collective-permute-start | bytes 589832 | tf_op jit(solution)/shard_map/ppermute | solution.py:443
  8.4 17.8 %collective-permute-start.3 = (bf16[1,64,1536]{2,1,0:T(8,128)(2,1)}, bf16[1,64,1536]{2,1,0:T(8,128)(2,1)S(1)}, u32[]{:S(2)}, u32[]{:S(2)}) collective-permute-start(bf16[1,64,1536]{2,1,0:T(8,128)(2,1)} %get-tuple-element.49), channel_id=1, source_target_pairs={{0,16},{2,18},{4,20},{6,22},{8,24},{10,26},{12,28},{14,30},{16,0},... | collective-permute-start | bytes 589832 | tf_op jit(solution)/shard_map/ppermute | solution.py:443
  11.0 15.2 %collective-permute-start.4 = (bf16[1,64,1536]{2,1,0:T(8,128)(2,1)}, bf16[1,64,1536]{2,1,0:T(8,128)(2,1)S(1)}, u32[]{:S(2)}, u32[]{:S(2)}) collective-permute-start(bf16[1,64,1536]{2,1,0:T(8,128)(2,1)} %get-tuple-element.50), channel_id=1, source_target_pairs={{0,24},{2,26},{4,28},{6,30},{8,16},{10,18},{12,20},{14,22},{16,8},... | collective-permute-start | bytes 589832 | tf_op jit(solution)/shard_map/ppermute | solution.py:443
  11.2 4.1 %collective-permute-start.1 = (bf16[64,256]{1,0:T(8,128)(2,1)}, bf16[64,256]{1,0:T(8,128)(2,1)S(1)}, u32[]{:S(2)}, u32[]{:S(2)}) collective-permute-start(bf16[64,256]{1,0:T(8,128)(2,1)} %get-tuple-element.45), channel_id=1, source_target_pairs={{0,1},{1,0},{2,3},{3,2},{4,5},{5,4},{6,7},{7,6},{8,9},{9,8},{10,11... | collective-permute-start | bytes 98312 | tf_op jit(solution)/shard_map/ppermute | solution.py:445
  15.3 0.6 copy-start.6
  15.9 10.3 %copy-start.2 = (bf16[1,64,1536]{2,1,0:T(8,128)(2,1)S(1)}, bf16[1,64,1536]{2,1,0:T(8,128)(2,1)}, u32[]{:S(2)}) copy-start(bf16[1,64,1536]{2,1,0:T(8,128)(2,1)} %get-tuple-element.53.refs_0_) | copy-start | bytes 589828
  26.2 6.4 %collective-permute-start.8 = (bf16[4,64,512]{2,1,0:T(8,128)(2,1)S(1)}, bf16[4,64,512]{2,1,0:T(8,128)(2,1)S(1)}, u32[]{:S(2)}, u32[]{:S(2)}) collective-permute-start(bf16[4,64,512]{2,1,0:T(8,128)(2,1)S(1)} %weight_pieces.1.refs_2_), channel_id=1, source_target_pairs={{0,4},{2,6},{4,0},{6,2},{8,12},{10,14},{12,8},{14,10},{16,20},{18,... | collective-permute-start | bytes 786440 | tf_op jit(solution)/shard_map/ppermute | solution.py:457
  26.7 8.3 %collective-permute-start.7 = (bf16[1,64,1024]{2,1,0:T(8,128)(2,1)S(1)}, bf16[1,64,1024]{2,1,0:T(8,128)(2,1)S(1)}, u32[]{:S(2)}, u32[]{:S(2)}) collective-permute-start(bf16[1,64,1024]{2,1,0:T(8,128)(2,1)S(1)} %get-tuple-element.85), channel_id=1, source_target_pairs={{0,24},{2,26},{4,28},{6,30},{8,16},{10,18},{12,20},{14,22},{16,8},... | collective-permute-start | bytes 393224 | tf_op jit(solution)/shard_map/ppermute | solution.py:452
  30.6 9.7 %collective-permute-start.6 = (bf16[1,64,1024]{2,1,0:T(8,128)(2,1)S(1)}, bf16[1,64,1024]{2,1,0:T(8,128)(2,1)S(1)}, u32[]{:S(2)}, u32[]{:S(2)}) collective-permute-start(bf16[1,64,1024]{2,1,0:T(8,128)(2,1)S(1)} %get-tuple-element.86), channel_id=1, source_target_pairs={{0,16},{2,18},{4,20},{6,22},{8,24},{10,26},{12,28},{14,30},{16,0},... | collective-permute-start | bytes 393224 | tf_op jit(solution)/shard_map/ppermute | solution.py:452
  31.0 9.2 %collective-permute-start.5 = (bf16[1,64,1024]{2,1,0:T(8,128)(2,1)S(1)}, bf16[1,64,1024]{2,1,0:T(8,128)(2,1)S(1)}, u32[]{:S(2)}, u32[]{:S(2)}) collective-permute-start(bf16[1,64,1024]{2,1,0:T(8,128)(2,1)S(1)} %get-tuple-element.87), channel_id=1, source_target_pairs={{0,8},{2,10},{4,12},{6,14},{8,0},{10,2},{12,4},{14,6},{16,24},{18,... | collective-permute-start | bytes 393224 | tf_op jit(solution)/shard_map/ppermute | solution.py:452
  32.7 29.0 %copy-start.4 = (bf16[4,64,512]{2,1,0:T(8,128)(2,1)}, bf16[4,64,512]{2,1,0:T(8,128)(2,1)S(1)}, u32[]{:S(2)}) copy-start(bf16[4,64,512]{2,1,0:T(8,128)(2,1)S(1)} %collective-permute-done.8.refs_3_) | copy-start | bytes 786436
  40.2 28.6 %all-to-all-start = ((bf16[16,64,512]{2,1,0:T(8,128)(2,1)}), bf16[16,64,512]{2,1,0:T(8,128)(2,1)S(1)}, u32[]{:S(2)}, u32[]{:S(2)}) async-start(bf16[16,64,512]{2,1,0:T(8,128)(2,1)} %neighbour_means.1), calls=%async_computation | async-start | bytes 2097152 | tf_op jit(solution)/shard_map/all_to_all | solution.py:460
  45.9 9.2 %collective-permute-start.12 = (bf16[4,64,512]{2,1,0:T(8,128)(2,1)S(1)}, bf16[4,64,512]{2,1,0:T(8,128)(2,1)S(1)}, u32[]{:S(2)}, u32[]{:S(2)}) collective-permute-start(bf16[4,64,512]{2,1,0:T(8,128)(2,1)S(1)} %weight_pieces.1.refs_2_), channel_id=1, source_target_pairs={{0,1},{1,0},{2,3},{3,2},{4,5},{5,4},{6,7},{7,6},{8,9},{9,8},{10,11... | collective-permute-start | bytes 786440 | tf_op jit(solution)/shard_map/ppermute | solution.py:461
  47.5 12.6 %collective-permute-start.9 = (bf16[8,64,512]{2,1,0:T(8,128)(2,1)S(1)}, bf16[8,64,512]{2,1,0:T(8,128)(2,1)S(1)}, u32[]{:S(2)}, u32[]{:S(2)}) collective-permute-start(bf16[8,64,512]{2,1,0:T(8,128)(2,1)S(1)} %get-tuple-element.62), channel_id=1, source_target_pairs={{0,2},{2,0},{4,6},{6,4},{8,10},{10,8},{12,14},{14,12},{16,18},{18,... | collective-permute-start | bytes 1572872 | tf_op jit(solution)/shard_map/ppermute | solution.py:465
  47.6 12.5 %collective-permute-start.13 = (bf16[4,64,512]{2,1,0:T(8,128)(2,1)S(1)}, bf16[4,64,512]{2,1,0:T(8,128)(2,1)S(1)}, u32[]{:S(2)}, u32[]{:S(2)}) collective-permute-start(bf16[4,64,512]{2,1,0:T(8,128)(2,1)S(1)} %collective-permute-done.8.refs_3_), channel_id=1, source_target_pairs={{0,1},{1,0},{2,3},{3,2},{4,5},{5,4},{6,7},{7,6},{8,9},{9,8},{10,11... | collective-permute-start | bytes 786440 | tf_op jit(solution)/shard_map/ppermute | solution.py:461
  48.2 11.9 %collective-permute-start.10 = (bf16[4,64,512]{2,1,0:T(8,128)(2,1)S(1)}, bf16[4,64,512]{2,1,0:T(8,128)(2,1)S(1)}, u32[]{:S(2)}, u32[]{:S(2)}) collective-permute-start(bf16[4,64,512]{2,1,0:T(8,128)(2,1)S(1)} %weight_pieces.1.refs_2_), channel_id=1, source_target_pairs={{0,2},{2,0},{4,6},{6,4},{8,10},{10,8},{12,14},{14,12},{16,18},{18,... | collective-permute-start | bytes 786440 | tf_op jit(solution)/shard_map/ppermute | solution.py:467
  48.3 11.8 %collective-permute-start.11 = (bf16[4,64,512]{2,1,0:T(8,128)(2,1)S(1)}, bf16[4,64,512]{2,1,0:T(8,128)(2,1)S(1)}, u32[]{:S(2)}, u32[]{:S(2)}) collective-permute-start(bf16[4,64,512]{2,1,0:T(8,128)(2,1)S(1)} %collective-permute-done.8.refs_3_), channel_id=1, source_target_pairs={{0,2},{2,0},{4,6},{6,4},{8,10},{10,8},{12,14},{14,12},{16,18},{18,... | collective-permute-start | bytes 786440 | tf_op jit(solution)/shard_map/ppermute | solution.py:467
  55.0 5.1 %collective-permute-start.14 = (bf16[4,64,512]{2,1,0:T(8,128)(2,1)S(1)}, bf16[4,64,512]{2,1,0:T(8,128)(2,1)S(1)}, u32[]{:S(2)}, u32[]{:S(2)}) collective-permute-start(bf16[4,64,512]{2,1,0:T(8,128)(2,1)S(1)} %collective-permute-done.12.refs_6_), channel_id=1, source_target_pairs={{0,2},{2,0},{4,6},{6,4},{8,10},{10,8},{12,14},{14,12},{16,18},{18,... | collective-permute-start | bytes 786440 | tf_op jit(solution)/shard_map/ppermute | solution.py:468
  60.1 1.5 %collective-permute-start.15 = (bf16[4,64,512]{2,1,0:T(8,128)(2,1)S(1)}, bf16[4,64,512]{2,1,0:T(8,128)(2,1)S(1)}, u32[]{:S(2)}, u32[]{:S(2)}) collective-permute-start(bf16[4,64,512]{2,1,0:T(8,128)(2,1)S(1)} %collective-permute-done.13.refs_7_), channel_id=1, source_target_pairs={{0,2},{2,0},{4,6},{6,4},{8,10},{10,8},{12,14},{14,12},{16,18},{18,... | collective-permute-start | bytes 786440 | tf_op jit(solution)/shard_map/ppermute | solution.py:468
  61.6 1.0 copy-start.3
  62.7 0.9 copy-start.5
  64.5 1.2 %copy-start = (bf16[1536,512]{1,0:T(8,128)(2,1)}, bf16[1536,512]{1,0:T(8,128)(2,1)S(1)}, u32[]{:S(2)}) copy-start(bf16[1536,512]{1,0:T(8,128)(2,1)S(1)} %get-tuple-element.65.beside_ref) | copy-start | bytes 4718596
  68.8 1.4 %copy-start.1 = (bf16[1536,512]{1,0:T(8,128)(2,1)S(1)}, bf16[1536,512]{1,0:T(8,128)(2,1)}, u32[]{:S(2)}) copy-start(bf16[1536,512]{1,0:T(8,128)(2,1)} %copy-done) | copy-start | bytes 4718596
  73.3 2.2 %collective-permute-start.19 = (bf16[8,64,512]{2,1,0:T(8,128)(2,1)S(1)}, bf16[8,64,512]{2,1,0:T(8,128)(2,1)S(1)}, u32[]{:S(2)}, u32[]{:S(2)}) collective-permute-start(bf16[8,64,512]{2,1,0:T(8,128)(2,1)S(1)} %get-tuple-element.76), channel_id=1, source_target_pairs={{0,2},{2,0},{4,6},{6,4},{8,10},{10,8},{12,14},{14,12},{16,18},{18,... | collective-permute-start | bytes 1572872 | tf_op jit(solution)/shard_map/ppermute | solution.py:493
  73.9 5.1 %collective-permute-start.16 = (bf16[8,64,512]{2,1,0:T(8,128)(2,1)S(1)}, bf16[8,64,512]{2,1,0:T(8,128)(2,1)S(1)}, u32[]{:S(2)}, u32[]{:S(2)}) collective-permute-start(bf16[8,64,512]{2,1,0:T(8,128)(2,1)S(1)} %get-tuple-element.69), channel_id=1, source_target_pairs={{0,2},{2,0},{4,6},{6,4},{8,10},{10,8},{12,14},{14,12},{16,18},{18,... | collective-permute-start | bytes 1572872 | tf_op jit(solution)/shard_map/ppermute | solution.py:489
  75.5 10.3 %collective-permute-start.20 = (bf16[2,2,64,512]{3,2,1,0:T(8,128)(2,1)S(1)}, bf16[2,2,64,512]{3,2,1,0:T(8,128)(2,1)S(1)}, u32[]{:S(2)}, u32[]{:S(2)}) collective-permute-start(bf16[2,2,64,512]{3,2,1,0:T(8,128)(2,1)S(1)} %get-tuple-element.78), channel_id=1, source_target_pairs={{0,8},{2,10},{4,12},{6,14},{8,0},{10,2},{12,4},{14,6},{16,24},{18,... | collective-permute-start | bytes 786440 | tf_op jit(solution)/shard_map/ppermute | solution.py:399
  79.1 8.4 %collective-permute-start.17 = (bf16[2,2,64,512]{3,2,1,0:T(8,128)(2,1)S(1)}, bf16[2,2,64,512]{3,2,1,0:T(8,128)(2,1)S(1)}, u32[]{:S(2)}, u32[]{:S(2)}) collective-permute-start(bf16[2,2,64,512]{3,2,1,0:T(8,128)(2,1)S(1)} %get-tuple-element.71), channel_id=1, source_target_pairs={{0,4},{2,6},{4,0},{6,2},{8,12},{10,14},{12,8},{14,10},{16,20},{18,... | collective-permute-start | bytes 786440 | tf_op jit(solution)/shard_map/ppermute | solution.py:395
  85.9 5.3 %collective-permute-start.21 = (bf16[2,64,512]{2,1,0:T(8,128)(2,1)S(1)}, bf16[2,64,512]{2,1,0:T(8,128)(2,1)S(1)}, u32[]{:S(2)}, u32[]{:S(2)}) collective-permute-start(bf16[2,64,512]{2,1,0:T(8,128)(2,1)S(1)} %get-tuple-element.80), channel_id=1, source_target_pairs={{0,4},{2,6},{4,0},{6,2},{8,12},{10,14},{12,8},{14,10},{16,20},{18,... | collective-permute-start | bytes 393224 | tf_op jit(solution)/shard_map/ppermute | solution.py:403
  87.5 5.0 %collective-permute-start.18 = (bf16[2,64,512]{2,1,0:T(8,128)(2,1)S(1)}, bf16[2,64,512]{2,1,0:T(8,128)(2,1)S(1)}, u32[]{:S(2)}, u32[]{:S(2)}) collective-permute-start(bf16[2,64,512]{2,1,0:T(8,128)(2,1)S(1)} %get-tuple-element.73), channel_id=1, source_target_pairs={{0,8},{2,10},{4,12},{6,14},{8,0},{10,2},{12,4},{14,6},{16,24},{18,... | collective-permute-start | bytes 393224 | tf_op jit(solution)/shard_map/ppermute | solution.py:401
  92.6 7.8 %collective-permute-start.22 = (bf16[1,2,64,512]{3,2,1,0:T(8,128)(2,1)S(1)}, bf16[1,2,64,512]{3,2,1,0:T(8,128)(2,1)S(1)}, u32[]{:S(2)}, u32[]{:S(2)}) collective-permute-start(bf16[1,2,64,512]{3,2,1,0:T(8,128)(2,1)S(1)} %get-tuple-element.82), channel_id=1, source_target_pairs={{0,16},{2,18},{4,20},{6,22},{8,24},{10,26},{12,28},{14,30},{16,0},... | collective-permute-start | bytes 393224 | tf_op jit(solution)/shard_map/ppermute | solution.py:408
  100.4 5.0 %collective-permute-start.23 = (bf16[1,2,64,512]{3,2,1,0:T(8,128)(2,1)S(1)}, bf16[1,2,64,512]{3,2,1,0:T(8,128)(2,1)S(1)}, u32[]{:S(2)}, u32[]{:S(2)}) collective-permute-start(bf16[1,2,64,512]{3,2,1,0:T(8,128)(2,1)S(1)} %rounded_sum.1.kept_ref), channel_id=1, source_target_pairs={{0,1},{1,0},{2,3},{3,2},{4,5},{5,4},{6,7},{7,6},{8,9},{9,8},{10,11... | collective-permute-start | bytes 393224 | tf_op jit(solution)/shard_map/ppermute | solution.py:416

commit v6 on v5

--- a/solution.py
+++ b/solution.py
@@ -150,7 +150,7 @@
 
 
 def mean_kernel(
-    unroll, ready, source_ref, kind_ref, count_ref, local_ref, halo_ref, ask_ref, pattern_ref, mean_ref, tiles
+    unroll, ready, source_ref, kind_ref, count_ref, local_ref, halo_ref, ask_ref, pattern_ref, mean_ref, tiles, turned
 ):
     depth = local_ref.shape[0]
     side = pattern_ref.shape[1]
@@ -171,14 +171,16 @@
     tiles[:, depth:, :] = jnp.ones((tiles.shape[0], tiles.shape[1] - depth, side), bf16)
     per_block = mean_ref.shape[2] // side
     ready(0, 1, 6)
+    for i in range(pattern_ref.shape[0]):
+        turned[i] = pattern_ref[i].T
 
     def one(t):
         rows = [tiles[source_ref[k, t]] for k in range(source_ref.shape[0])]
-        weights = [pattern_ref[kind_ref[k, t]] for k in range(source_ref.shape[0])]
+        weights = [turned[kind_ref[k, t]] for k in range(source_ref.shape[0])]
         summed = lax.dot_general(
             jnp.concatenate(rows, 1),
-            jnp.concatenate(weights, 1),
-            last_with_last,
+            jnp.concatenate(weights, 0),
+            (((1,), (0,)), ((), ())),
             preferred_element_type=f32,
         )
         mean = (summed[0:depth] / summed[depth : depth + 1]).astype(bf16)
@@ -196,12 +198,12 @@
     side = patterns.shape[1]
     tile_count = (count + asks.shape[1] * asks.shape[2]) // side
     return local_call(
-        functools.partial(mean_kernel, 8 if source.shape[1] % 8 == 0 else 1),
+        functools.partial(mean_kernel, 16 if source.shape[1] % 16 == 0 else 1),
         "neighbour_means",
         [jax.ShapeDtypeStruct((blocks, depth, count // blocks), bf16)],
         (source, kind, counts, local, halo, asks, patterns),
         scalars=3,
-        scratch=[pltpu.VMEM((tile_count, depth + 16, side), bf16)],
+        scratch=[pltpu.VMEM((tile_count, depth + 16, side), bf16), pltpu.VMEM(patterns.shape, bf16)],
         lazy=True,
     )[0]
 

time: 107 us -> 105 us (0.981)
  Pallas kernels: 18.4 us -> 16.1 us
    pallas_call x14, Pallas kernels: 18.4 us -> 16.1 us  [local_call(): pl.pallas_call(kernel, out_shape=outs, in_specs=in_specs, out_specs=[whol...]
    ppermute x3, waiting for transfers between devices: 0.01 us -> 1.89 us  [on_device(): flip('feat', i * below)(cuts[i])]
    ppermute x1, waiting for transfers between devices: 1.48 us -> 0.2 us  [on_device(): pieces = pieces + [flip('feat', bit)(p) for p in pieces]]
  transfers between devices with their start and end apart: 25 -> 25, of which waited for: 14 -> 15; matrix products, arithmetic and copies ran while one was open for 0% -> 0% of each run, Pallas kernels for 11% -> 9%
where the time goes in v6:
time: 105 us
  waiting for transfers between devices  47 us (45%)
  starting transfers between devices  35.7 us (34%)
  Pallas kernels  16.1 us (15%)
  local copies, waits for them, and re-layouts  5.22 us (5%)
    pallas_call x14, Pallas kernels, local_call(): pl.pallas_call(kernel, out_shape=outs, in_specs=in_specs, out_specs=[whol...  16.1 us
    ppermute x2, waiting for transfers between devices, on_device(): others = [flip('dom', 1)(p) for p in pieces]  11.4 us
    ppermute x3, waiting for transfers between devices, on_device(): flip('feat', i * below)(came[i:i + 1])  7.31 us
    ppermute x1, waiting for transfers between devices, sum_gradients(): got = flip('feat', half * 8)(sent)  5.68 us
    ppermute x3, starting transfers between devices, on_device(): flip('feat', i * below)(came[i:i + 1])  5.6 us
    unnamed x14, local copies, waits for them, and re-layouts  5.19 us
    ppermute x1, waiting for transfers between devices, sum_gradients(): neigh_got = flip('feat', 4)(neigh_sent)  5.12 us
    all_to_all x1, starting transfers between devices, on_device(): own_mean = lax.all_to_all(means, 'feat', 0, 0, tiled=True)  4.9 us
  transfers between devices with their start and end apart: 25, of which 15 were waited for; matrix products, arithmetic and copies ran while one was open for 0% of the time, Pallas kernels for 9%

profile of v6, /device:TPU:0, one launch (start us, length us, event | category | flops | bytes accessed | tf_op | source)
XLA Modules:
  0.0 104.8 jit_solution(2506105138864620008)
XLA Ops:
  0.6 3.2 %open_exchange.1 = (bf16[64,256]{1,0:T(8,128)(2,1)}, bf16[4,64,1024]{2,1,0:T(8,128)(2,1)}, bf16[1,64,1536]{2,1,0:T(8,128)(2,1)}, bf16[1,64,1536]{2,1,0:T(8,128)(...) custom-call(s32[2,2]{1,0:T(2,128)} %refs_2_.3, bf16[64,8192]{1,0:T(8,128)(2,1)} %bitcast.7, ...), custom_call_target="tpu_custom_call" | custom-call | tf_op jit(solution)/shard_map/open_exchange/pallas_call | solution.py:79
  3.8 3.0 %collective-permute-start = (bf16[4,64,1024]{2,1,0:T(8,128)(2,1)}, bf16[4,64,1024]{2,1,0:T(8,128)(2,1)S(1)}, u32[]{:S(2)}, u32[]{:S(2)}) collective-permute-start(bf16[4,64,1024]{2,1,0:T(8,128)(2,1)} %get-tuple-element.44), channel_id=1, source_target_pairs={{0,4},{2,6},{4,0},{6,2},{8,12},{10,14},{12,8},{14,10},{16,20},{18,... | collective-permute-start | bytes 1572872 | tf_op jit(solution)/shard_map/ppermute | solution.py:444
  6.8 1.6 %collective-permute-start.2 = (bf16[1,64,1536]{2,1,0:T(8,128)(2,1)}, bf16[1,64,1536]{2,1,0:T(8,128)(2,1)S(1)}, u32[]{:S(2)}, u32[]{:S(2)}) collective-permute-start(bf16[1,64,1536]{2,1,0:T(8,128)(2,1)} %get-tuple-element.48), channel_id=1, source_target_pairs={{0,8},{2,10},{4,12},{6,14},{8,0},{10,2},{12,4},{14,6},{16,24},{18,... | collective-permute-start | bytes 589832 | tf_op jit(solution)/shard_map/ppermute | solution.py:445
  8.4 2.6 %collective-permute-start.3 = (bf16[1,64,1536]{2,1,0:T(8,128)(2,1)}, bf16[1,64,1536]{2,1,0:T(8,128)(2,1)S(1)}, u32[]{:S(2)}, u32[]{:S(2)}) collective-permute-start(bf16[1,64,1536]{2,1,0:T(8,128)(2,1)} %get-tuple-element.49), channel_id=1, source_target_pairs={{0,16},{2,18},{4,20},{6,22},{8,24},{10,26},{12,28},{14,30},{16,0},... | collective-permute-start | bytes 589832 | tf_op jit(solution)/shard_map/ppermute | solution.py:445
  11.0 0.2 collective-permute-start.4
  11.2 1.5 %collective-permute-start.1 = (bf16[64,256]{1,0:T(8,128)(2,1)}, bf16[64,256]{1,0:T(8,128)(2,1)S(1)}, u32[]{:S(2)}, u32[]{:S(2)}) collective-permute-start(bf16[64,256]{1,0:T(8,128)(2,1)} %get-tuple-element.45), channel_id=1, source_target_pairs={{0,1},{1,0},{2,3},{3,2},{4,5},{5,4},{6,7},{7,6},{8,9},{9,8},{10,11... | collective-permute-start | bytes 98312 | tf_op jit(solution)/shard_map/ppermute | solution.py:447
  12.7 2.6 %collective-permute-done.1.refs_4_ = bf16[64,256]{1,0:T(8,128)(2,1)S(1)} collective-permute-done((bf16[64,256]{1,0:T(8,128)(2,1)}, bf16[64,256]{1,0:T(8,128)(2,1)S(1)}, u32[]{:S(2)}, u32[]{:S(2)}) %collective-permute-start.1) | collective-permute-done | bytes 32800 | tf_op jit(solution)/shard_map/ppermute | solution.py:447
  15.3 0.6 copy-done.6
  15.9 7.9 %neighbour_means.1 = bf16[16,64,512]{2,1,0:T(8,128)(2,1)} custom-call(s32[8,64]{1,0:T(8,128)} %bitcast.9, s32[8,64]{1,0:T(8,128)} %bitcast.10, s32[2,2]{1,0:T(2,128)} %refs_2_.3, bf16[64,8192]{1,0:T(8,128)(2,1)} %bitcast.8, bf16[64,256]{1,0:T(8,128)(2,1)} %copy-done.6, s32[2,2,256]{2,1,0:T(2,128)} %refs_5_.1, bf16[64,128,128]{2,1,0:T(8,128)(2,1)} %refs_6_.1), custom_call_target="tpu_custom_call" | custom-call | tf_op jit(solution)/shard_map/neighbour_means/pallas_call | solution.py:79
  23.9 1.9 %collective-permute-done.3.refs_2_ = bf16[1,64,1536]{2,1,0:T(8,128)(2,1)S(1)} collective-permute-done((bf16[1,64,1536]{2,1,0:T(8,128)(2,1)}, bf16[1,64,1536]{2,1,0:T(8,128)(2,1)S(1)}, u32[]{:S(2)}, u32[]{:S(2)}) %collective-permute-start.3) | collective-permute-done | bytes 196640 | tf_op jit(solution)/shard_map/ppermute | solution.py:445
  25.8 0.6 collective-permute-start.8
  26.4 2.4 %collective-permute-start.7 = (bf16[1,64,1024]{2,1,0:T(8,128)(2,1)S(1)}, bf16[1,64,1024]{2,1,0:T(8,128)(2,1)S(1)}, u32[]{:S(2)}, u32[]{:S(2)}) collective-permute-start(bf16[1,64,1024]{2,1,0:T(8,128)(2,1)S(1)} %get-tuple-element.85), channel_id=1, source_target_pairs={{0,24},{2,26},{4,28},{6,30},{8,16},{10,18},{12,20},{14,22},{16,8},... | collective-permute-start | bytes 393224 | tf_op jit(solution)/shard_map/ppermute | solution.py:454
  28.9 3.1 %collective-permute-start.6 = (bf16[1,64,1024]{2,1,0:T(8,128)(2,1)S(1)}, bf16[1,64,1024]{2,1,0:T(8,128)(2,1)S(1)}, u32[]{:S(2)}, u32[]{:S(2)}) collective-permute-start(bf16[1,64,1024]{2,1,0:T(8,128)(2,1)S(1)} %get-tuple-element.86), channel_id=1, source_target_pairs={{0,16},{2,18},{4,20},{6,22},{8,24},{10,26},{12,28},{14,30},{16,0},... | collective-permute-start | bytes 393224 | tf_op jit(solution)/shard_map/ppermute | solution.py:454
  31.9 0.1 collective-permute-start.5
  32.0 0.2 collective-permute-done.8.refs_3_
  32.2 2.4 %collective-permute-done.7.refs_7_ = bf16[1,64,1024]{2,1,0:T(8,128)(2,1)S(1)} collective-permute-done((bf16[1,64,1024]{2,1,0:T(8,128)(2,1)S(1)}, bf16[1,64,1024]{2,1,0:T(8,128)(2,1)S(1)}, u32[]{:S(2)}, u32[]{:S(2)}) %collective-permute-start.7) | collective-permute-done | bytes 131104 | tf_op jit(solution)/shard_map/ppermute | solution.py:454
  34.6 4.9 %collective-permute-done.6.refs_6_ = bf16[1,64,1024]{2,1,0:T(8,128)(2,1)S(1)} collective-permute-done((bf16[1,64,1024]{2,1,0:T(8,128)(2,1)S(1)}, bf16[1,64,1024]{2,1,0:T(8,128)(2,1)S(1)}, u32[]{:S(2)}, u32[]{:S(2)}) %collective-permute-start.6) | collective-permute-done | bytes 131104 | tf_op jit(solution)/shard_map/ppermute | solution.py:454
  39.5 4.9 %all-to-all-start = ((bf16[16,64,512]{2,1,0:T(8,128)(2,1)}), bf16[16,64,512]{2,1,0:T(8,128)(2,1)S(1)}, u32[]{:S(2)}, u32[]{:S(2)}) async-start(bf16[16,64,512]{2,1,0:T(8,128)(2,1)} %neighbour_means.1), calls=%async_computation | async-start | bytes 2097152 | tf_op jit(solution)/shard_map/all_to_all | solution.py:462
  44.5 1.6 %collective-permute-start.12 = (bf16[4,64,512]{2,1,0:T(8,128)(2,1)S(1)}, bf16[4,64,512]{2,1,0:T(8,128)(2,1)S(1)}, u32[]{:S(2)}, u32[]{:S(2)}) collective-permute-start(bf16[4,64,512]{2,1,0:T(8,128)(2,1)S(1)} %weight_pieces.1.refs_2_), channel_id=1, source_target_pairs={{0,1},{1,0},{2,3},{3,2},{4,5},{5,4},{6,7},{7,6},{8,9},{9,8},{10,11... | collective-permute-start | bytes 786440 | tf_op jit(solution)/shard_map/ppermute | solution.py:463
  46.1 0.1 collective-permute-start.9
  46.2 0.5 collective-permute-start.13
  46.8 0.2 collective-permute-start.10
  46.9 0.3 collective-permute-start.11
  47.3 6.4 %collective-permute-done.12.refs_6_ = bf16[4,64,512]{2,1,0:T(8,128)(2,1)S(1)} collective-permute-done((bf16[4,64,512]{2,1,0:T(8,128)(2,1)S(1)}, bf16[4,64,512]{2,1,0:T(8,128)(2,1)S(1)}, u32[]{:S(2)}, u32[]{:S(2)}) %collective-permute-start.12) | collective-permute-done | bytes 262176 | tf_op jit(solution)/shard_map/ppermute | solution.py:463
  53.6 5.0 %collective-permute-done.13.refs_7_ = bf16[4,64,512]{2,1,0:T(8,128)(2,1)S(1)} collective-permute-done((bf16[4,64,512]{2,1,0:T(8,128)(2,1)S(1)}, bf16[4,64,512]{2,1,0:T(8,128)(2,1)S(1)}, u32[]{:S(2)}, u32[]{:S(2)}) %collective-permute-start.13) | collective-permute-done | bytes 262176 | tf_op jit(solution)/shard_map/ppermute | solution.py:463
  58.7 1.5 %collective-permute-done.15.refs_9_ = bf16[4,64,512]{2,1,0:T(8,128)(2,1)S(1)} collective-permute-done((bf16[4,64,512]{2,1,0:T(8,128)(2,1)S(1)}, bf16[4,64,512]{2,1,0:T(8,128)(2,1)S(1)}, u32[]{:S(2)}, u32[]{:S(2)}) %collective-permute-start.15) | collective-permute-done | bytes 262176 | tf_op jit(solution)/shard_map/ppermute | solution.py:470
  60.2 1.0 copy-done.3
  61.3 0.9 copy-done.5
  62.2 0.8 own_linear.1
  63.1 1.2 %copy-done = bf16[1536,512]{1,0:T(8,128)(2,1)} copy-done((bf16[1536,512]{1,0:T(8,128)(2,1)}, bf16[1536,512]{1,0:T(8,128)(2,1)S(1)}, u32[]{:S(2)}) %copy-start) | copy-done | bytes 1572888
  64.2 3.2 %all-to-all-done.mean_ref = bf16[16,64,512]{2,1,0:T(8,128)(2,1)S(1)} async-done(((bf16[16,64,512]{2,1,0:T(8,128)(2,1)}), bf16[16,64,512]{2,1,0:T(8,128)(2,1)S(1)}, u32[]{:S(2)}, u32[]{:S(2)}) %all-to-all-start) | async-done | bytes 1048608 | tf_op jit(solution)/shard_map/all_to_all | solution.py:462
  67.4 1.4 %copy-done.1 = bf16[1536,512]{1,0:T(8,128)(2,1)S(1)} copy-done((bf16[1536,512]{1,0:T(8,128)(2,1)S(1)}, bf16[1536,512]{1,0:T(8,128)(2,1)}, u32[]{:S(2)}) %copy-start.1) | copy-done | bytes 1572888
  68.8 2.3 %forward.1 = (bf16[512,512]{1,0:T(8,128)(2,1)}, bf16[512,512]{1,0:T(8,128)(2,1)S(1)}, bf16[8,64,512]{2,1,0:T(8,128)(2,1)S(1)}, f32[8,64,512]{2,1,0:T(8,128)S(1)}) custom-call(bf16[16,64,512]{2,1,0:T(8,128)(2,1)S(1)} %all-to-all-done.mean_ref, bf16[1536,512]{1,0:T(8,128)(2,1)S(1)} %copy-done.1, f32[512,512]{1,0:T(8,128)S(1)} %get-tuple-element.66.base_ref, ...), custom_call_target="tpu_custom_call" | custom-call | tf_op jit(solution)/shard_map/forward/pallas_call | solution.py:79
  71.1 0.7 neighbour_sums.1
  71.8 0.7 collective-permute-start.19
  72.6 1.5 %collective-permute-done.19.got_ref = bf16[8,64,512]{2,1,0:T(8,128)(2,1)S(1)} collective-permute-done((bf16[8,64,512]{2,1,0:T(8,128)(2,1)S(1)}, bf16[8,64,512]{2,1,0:T(8,128)(2,1)S(1)}, u32[]{:S(2)}, u32[]{:S(2)}) %collective-permute-start.19) | collective-permute-done | bytes 524320 | tf_op jit(solution)/shard_map/ppermute | solution.py:495
  74.1 3.5 %collective-permute-start.20 = (bf16[2,2,64,512]{3,2,1,0:T(8,128)(2,1)S(1)}, bf16[2,2,64,512]{3,2,1,0:T(8,128)(2,1)S(1)}, u32[]{:S(2)}, u32[]{:S(2)}) collective-permute-start(bf16[2,2,64,512]{3,2,1,0:T(8,128)(2,1)S(1)} %get-tuple-element.78), channel_id=1, source_target_pairs={{0,8},{2,10},{4,12},{6,14},{8,0},{10,2},{12,4},{14,6},{16,24},{18,... | collective-permute-start | bytes 786440 | tf_op jit(solution)/shard_map/ppermute | solution.py:401
  77.7 1.6 %collective-permute-start.17 = (bf16[2,2,64,512]{3,2,1,0:T(8,128)(2,1)S(1)}, bf16[2,2,64,512]{3,2,1,0:T(8,128)(2,1)S(1)}, u32[]{:S(2)}, u32[]{:S(2)}) collective-permute-start(bf16[2,2,64,512]{3,2,1,0:T(8,128)(2,1)S(1)} %get-tuple-element.71), channel_id=1, source_target_pairs={{0,4},{2,6},{4,0},{6,2},{8,12},{10,14},{12,8},{14,10},{16,20},{18,... | collective-permute-start | bytes 786440 | tf_op jit(solution)/shard_map/ppermute | solution.py:397
  79.3 5.1 %collective-permute-done.20.got_ref = bf16[2,2,64,512]{3,2,1,0:T(8,128)(2,1)S(1)} collective-permute-done((bf16[2,2,64,512]{3,2,1,0:T(8,128)(2,1)S(1)}, bf16[2,2,64,512]{3,2,1,0:T(8,128)(2,1)S(1)}, u32[]{:S(2)}, u32[]{:S(2)}) %collective-permute-start.20) | collective-permute-done | bytes 262176 | tf_op jit(solution)/shard_map/ppermute | solution.py:401
  84.5 1.6 %collective-permute-start.21 = (bf16[2,64,512]{2,1,0:T(8,128)(2,1)S(1)}, bf16[2,64,512]{2,1,0:T(8,128)(2,1)S(1)}, u32[]{:S(2)}, u32[]{:S(2)}) collective-permute-start(bf16[2,64,512]{2,1,0:T(8,128)(2,1)S(1)} %get-tuple-element.80), channel_id=1, source_target_pairs={{0,4},{2,6},{4,0},{6,2},{8,12},{10,14},{12,8},{14,10},{16,20},{18,... | collective-permute-start | bytes 393224 | tf_op jit(solution)/shard_map/ppermute | solution.py:405
  86.1 1.8 %collective-permute-start.18 = (bf16[2,64,512]{2,1,0:T(8,128)(2,1)S(1)}, bf16[2,64,512]{2,1,0:T(8,128)(2,1)S(1)}, u32[]{:S(2)}, u32[]{:S(2)}) collective-permute-start(bf16[2,64,512]{2,1,0:T(8,128)(2,1)S(1)} %get-tuple-element.73), channel_id=1, source_target_pairs={{0,8},{2,10},{4,12},{6,14},{8,0},{10,2},{12,4},{14,6},{16,24},{18,... | collective-permute-start | bytes 393224 | tf_op jit(solution)/shard_map/ppermute | solution.py:403
  87.9 1.9 %collective-permute-done.21.neigh_got_ref = bf16[2,64,512]{2,1,0:T(8,128)(2,1)S(1)} collective-permute-done((bf16[2,64,512]{2,1,0:T(8,128)(2,1)S(1)}, bf16[2,64,512]{2,1,0:T(8,128)(2,1)S(1)}, u32[]{:S(2)}, u32[]{:S(2)}) %collective-permute-start.21) | collective-permute-done | bytes 131104 | tf_op jit(solution)/shard_map/ppermute | solution.py:405
  89.7 1.4 %collective-permute-done.18.own_got_ref = bf16[2,64,512]{2,1,0:T(8,128)(2,1)S(1)} collective-permute-done((bf16[2,64,512]{2,1,0:T(8,128)(2,1)S(1)}, bf16[2,64,512]{2,1,0:T(8,128)(2,1)S(1)}, u32[]{:S(2)}, u32[]{:S(2)}) %collective-permute-start.18) | collective-permute-done | bytes 131104 | tf_op jit(solution)/shard_map/ppermute | solution.py:403
  91.2 2.2 %collective-permute-start.22 = (bf16[1,2,64,512]{3,2,1,0:T(8,128)(2,1)S(1)}, bf16[1,2,64,512]{3,2,1,0:T(8,128)(2,1)S(1)}, u32[]{:S(2)}, u32[]{:S(2)}) collective-permute-start(bf16[1,2,64,512]{3,2,1,0:T(8,128)(2,1)S(1)} %get-tuple-element.82), channel_id=1, source_target_pairs={{0,16},{2,18},{4,20},{6,22},{8,24},{10,26},{12,28},{14,30},{16,0},... | collective-permute-start | bytes 393224 | tf_op jit(solution)/shard_map/ppermute | solution.py:410
  93.3 5.7 %collective-permute-done.22.got_ref = bf16[1,2,64,512]{3,2,1,0:T(8,128)(2,1)S(1)} collective-permute-done((bf16[1,2,64,512]{3,2,1,0:T(8,128)(2,1)S(1)}, bf16[1,2,64,512]{3,2,1,0:T(8,128)(2,1)S(1)}, u32[]{:S(2)}, u32[]{:S(2)}) %collective-permute-start.22) | collective-permute-done | bytes 131104 | tf_op jit(solution)/shard_map/ppermute | solution.py:410
  99.0 1.6 %collective-permute-start.23 = (bf16[1,2,64,512]{3,2,1,0:T(8,128)(2,1)S(1)}, bf16[1,2,64,512]{3,2,1,0:T(8,128)(2,1)S(1)}, u32[]{:S(2)}, u32[]{:S(2)}) collective-permute-start(bf16[1,2,64,512]{3,2,1,0:T(8,128)(2,1)S(1)} %rounded_sum.1.kept_ref), channel_id=1, source_target_pairs={{0,1},{1,0},{2,3},{3,2},{4,5},{5,4},{6,7},{7,6},{8,9},{9,8},{10,11... | collective-permute-start | bytes 393224 | tf_op jit(solution)/shard_map/ppermute | solution.py:418
  100.6 3.4 %collective-permute-done.23.got_ref = bf16[1,2,64,512]{3,2,1,0:T(8,128)(2,1)S(1)} collective-permute-done((bf16[1,2,64,512]{3,2,1,0:T(8,128)(2,1)S(1)}, bf16[1,2,64,512]{3,2,1,0:T(8,128)(2,1)S(1)}, u32[]{:S(2)}, u32[]{:S(2)}) %collective-permute-start.23) | collective-permute-done | bytes 131104 | tf_op jit(solution)/shard_map/ppermute | solution.py:418
  104.1 0.7 last_sum.1
  (31 shorter events, 0.6 us)
Async XLA Ops:
  3.8 22.6 %collective-permute-start = (bf16[4,64,1024]{2,1,0:T(8,128)(2,1)}, bf16[4,64,1024]{2,1,0:T(8,128)(2,1)S(1)}, u32[]{:S(2)}, u32[]{:S(2)}) collective-permute-start(bf16[4,64,1024]{2,1,0:T(8,128)(2,1)} %get-tuple-element.44), channel_id=1, source_target_pairs={{0,4},{2,6},{4,0},{6,2},{8,12},{10,14},{12,8},{14,10},{16,20},{18,... | collective-permute-start | bytes 1572872 | tf_op jit(solution)/shard_map/ppermute | solution.py:444
  6.8 17.1 %collective-permute-start.2 = (bf16[1,64,1536]{2,1,0:T(8,128)(2,1)}, bf16[1,64,1536]{2,1,0:T(8,128)(2,1)S(1)}, u32[]{:S(2)}, u32[]{:S(2)}) collective-permute-start(bf16[1,64,1536]{2,1,0:T(8,128)(2,1)} %get-tuple-element.48), channel_id=1, source_target_pairs={{0,8},{2,10},{4,12},{6,14},{8,0},{10,2},{12,4},{14,6},{16,24},{18,... | collective-permute-start | bytes 589832 | tf_op jit(solution)/shard_map/ppermute | solution.py:445
  8.4 17.4 %collective-permute-start.3 = (bf16[1,64,1536]{2,1,0:T(8,128)(2,1)}, bf16[1,64,1536]{2,1,0:T(8,128)(2,1)S(1)}, u32[]{:S(2)}, u32[]{:S(2)}) collective-permute-start(bf16[1,64,1536]{2,1,0:T(8,128)(2,1)} %get-tuple-element.49), channel_id=1, source_target_pairs={{0,16},{2,18},{4,20},{6,22},{8,24},{10,26},{12,28},{14,30},{16,0},... | collective-permute-start | bytes 589832 | tf_op jit(solution)/shard_map/ppermute | solution.py:445
  11.0 14.8 %collective-permute-start.4 = (bf16[1,64,1536]{2,1,0:T(8,128)(2,1)}, bf16[1,64,1536]{2,1,0:T(8,128)(2,1)S(1)}, u32[]{:S(2)}, u32[]{:S(2)}) collective-permute-start(bf16[1,64,1536]{2,1,0:T(8,128)(2,1)} %get-tuple-element.50), channel_id=1, source_target_pairs={{0,24},{2,26},{4,28},{6,30},{8,16},{10,18},{12,20},{14,22},{16,8},... | collective-permute-start | bytes 589832 | tf_op jit(solution)/shard_map/ppermute | solution.py:445
  11.2 4.1 %collective-permute-start.1 = (bf16[64,256]{1,0:T(8,128)(2,1)}, bf16[64,256]{1,0:T(8,128)(2,1)S(1)}, u32[]{:S(2)}, u32[]{:S(2)}) collective-permute-start(bf16[64,256]{1,0:T(8,128)(2,1)} %get-tuple-element.45), channel_id=1, source_target_pairs={{0,1},{1,0},{2,3},{3,2},{4,5},{5,4},{6,7},{7,6},{8,9},{9,8},{10,11... | collective-permute-start | bytes 98312 | tf_op jit(solution)/shard_map/ppermute | solution.py:447
  15.3 0.6 copy-start.6
  15.9 9.8 %copy-start.2 = (bf16[1,64,1536]{2,1,0:T(8,128)(2,1)S(1)}, bf16[1,64,1536]{2,1,0:T(8,128)(2,1)}, u32[]{:S(2)}) copy-start(bf16[1,64,1536]{2,1,0:T(8,128)(2,1)} %get-tuple-element.53.refs_0_) | copy-start | bytes 589828
  25.8 6.4 %collective-permute-start.8 = (bf16[4,64,512]{2,1,0:T(8,128)(2,1)S(1)}, bf16[4,64,512]{2,1,0:T(8,128)(2,1)S(1)}, u32[]{:S(2)}, u32[]{:S(2)}) collective-permute-start(bf16[4,64,512]{2,1,0:T(8,128)(2,1)S(1)} %weight_pieces.1.refs_2_), channel_id=1, source_target_pairs={{0,4},{2,6},{4,0},{6,2},{8,12},{10,14},{12,8},{14,10},{16,20},{18,... | collective-permute-start | bytes 786440 | tf_op jit(solution)/shard_map/ppermute | solution.py:459
  26.4 8.2 %collective-permute-start.7 = (bf16[1,64,1024]{2,1,0:T(8,128)(2,1)S(1)}, bf16[1,64,1024]{2,1,0:T(8,128)(2,1)S(1)}, u32[]{:S(2)}, u32[]{:S(2)}) collective-permute-start(bf16[1,64,1024]{2,1,0:T(8,128)(2,1)S(1)} %get-tuple-element.85), channel_id=1, source_target_pairs={{0,24},{2,26},{4,28},{6,30},{8,16},{10,18},{12,20},{14,22},{16,8},... | collective-permute-start | bytes 393224 | tf_op jit(solution)/shard_map/ppermute | solution.py:454
  28.9 10.7 %collective-permute-start.6 = (bf16[1,64,1024]{2,1,0:T(8,128)(2,1)S(1)}, bf16[1,64,1024]{2,1,0:T(8,128)(2,1)S(1)}, u32[]{:S(2)}, u32[]{:S(2)}) collective-permute-start(bf16[1,64,1024]{2,1,0:T(8,128)(2,1)S(1)} %get-tuple-element.86), channel_id=1, source_target_pairs={{0,16},{2,18},{4,20},{6,22},{8,24},{10,26},{12,28},{14,30},{16,0},... | collective-permute-start | bytes 393224 | tf_op jit(solution)/shard_map/ppermute | solution.py:454
  31.9 7.6 %collective-permute-start.5 = (bf16[1,64,1024]{2,1,0:T(8,128)(2,1)S(1)}, bf16[1,64,1024]{2,1,0:T(8,128)(2,1)S(1)}, u32[]{:S(2)}, u32[]{:S(2)}) collective-permute-start(bf16[1,64,1024]{2,1,0:T(8,128)(2,1)S(1)} %get-tuple-element.87), channel_id=1, source_target_pairs={{0,8},{2,10},{4,12},{6,14},{8,0},{10,2},{12,4},{14,6},{16,24},{18,... | collective-permute-start | bytes 393224 | tf_op jit(solution)/shard_map/ppermute | solution.py:454
  32.2 28.0 %copy-start.4 = (bf16[4,64,512]{2,1,0:T(8,128)(2,1)}, bf16[4,64,512]{2,1,0:T(8,128)(2,1)S(1)}, u32[]{:S(2)}) copy-start(bf16[4,64,512]{2,1,0:T(8,128)(2,1)S(1)} %collective-permute-done.8.refs_3_) | copy-start | bytes 786436
  39.5 27.9 %all-to-all-start = ((bf16[16,64,512]{2,1,0:T(8,128)(2,1)}), bf16[16,64,512]{2,1,0:T(8,128)(2,1)S(1)}, u32[]{:S(2)}, u32[]{:S(2)}) async-start(bf16[16,64,512]{2,1,0:T(8,128)(2,1)} %neighbour_means.1), calls=%async_computation | async-start | bytes 2097152 | tf_op jit(solution)/shard_map/all_to_all | solution.py:462
  44.5 9.2 %collective-permute-start.12 = (bf16[4,64,512]{2,1,0:T(8,128)(2,1)S(1)}, bf16[4,64,512]{2,1,0:T(8,128)(2,1)S(1)}, u32[]{:S(2)}, u32[]{:S(2)}) collective-permute-start(bf16[4,64,512]{2,1,0:T(8,128)(2,1)S(1)} %weight_pieces.1.refs_2_), channel_id=1, source_target_pairs={{0,1},{1,0},{2,3},{3,2},{4,5},{5,4},{6,7},{7,6},{8,9},{9,8},{10,11... | collective-permute-start | bytes 786440 | tf_op jit(solution)/shard_map/ppermute | solution.py:463
  46.1 12.6 %collective-permute-start.9 = (bf16[8,64,512]{2,1,0:T(8,128)(2,1)S(1)}, bf16[8,64,512]{2,1,0:T(8,128)(2,1)S(1)}, u32[]{:S(2)}, u32[]{:S(2)}) collective-permute-start(bf16[8,64,512]{2,1,0:T(8,128)(2,1)S(1)} %get-tuple-element.62), channel_id=1, source_target_pairs={{0,2},{2,0},{4,6},{6,4},{8,10},{10,8},{12,14},{14,12},{16,18},{18,... | collective-permute-start | bytes 1572872 | tf_op jit(solution)/shard_map/ppermute | solution.py:467
  46.2 12.5 %collective-permute-start.13 = (bf16[4,64,512]{2,1,0:T(8,128)(2,1)S(1)}, bf16[4,64,512]{2,1,0:T(8,128)(2,1)S(1)}, u32[]{:S(2)}, u32[]{:S(2)}) collective-permute-start(bf16[4,64,512]{2,1,0:T(8,128)(2,1)S(1)} %collective-permute-done.8.refs_3_), channel_id=1, source_target_pairs={{0,1},{1,0},{2,3},{3,2},{4,5},{5,4},{6,7},{7,6},{8,9},{9,8},{10,11... | collective-permute-start | bytes 786440 | tf_op jit(solution)/shard_map/ppermute | solution.py:463
  46.8 11.9 %collective-permute-start.10 = (bf16[4,64,512]{2,1,0:T(8,128)(2,1)S(1)}, bf16[4,64,512]{2,1,0:T(8,128)(2,1)S(1)}, u32[]{:S(2)}, u32[]{:S(2)}) collective-permute-start(bf16[4,64,512]{2,1,0:T(8,128)(2,1)S(1)} %weight_pieces.1.refs_2_), channel_id=1, source_target_pairs={{0,2},{2,0},{4,6},{6,4},{8,10},{10,8},{12,14},{14,12},{16,18},{18,... | collective-permute-start | bytes 786440 | tf_op jit(solution)/shard_map/ppermute | solution.py:469
  46.9 11.8 %collective-permute-start.11 = (bf16[4,64,512]{2,1,0:T(8,128)(2,1)S(1)}, bf16[4,64,512]{2,1,0:T(8,128)(2,1)S(1)}, u32[]{:S(2)}, u32[]{:S(2)}) collective-permute-start(bf16[4,64,512]{2,1,0:T(8,128)(2,1)S(1)} %collective-permute-done.8.refs_3_), channel_id=1, source_target_pairs={{0,2},{2,0},{4,6},{6,4},{8,10},{10,8},{12,14},{14,12},{16,18},{18,... | collective-permute-start | bytes 786440 | tf_op jit(solution)/shard_map/ppermute | solution.py:469
  53.6 5.1 %collective-permute-start.14 = (bf16[4,64,512]{2,1,0:T(8,128)(2,1)S(1)}, bf16[4,64,512]{2,1,0:T(8,128)(2,1)S(1)}, u32[]{:S(2)}, u32[]{:S(2)}) collective-permute-start(bf16[4,64,512]{2,1,0:T(8,128)(2,1)S(1)} %collective-permute-done.12.refs_6_), channel_id=1, source_target_pairs={{0,2},{2,0},{4,6},{6,4},{8,10},{10,8},{12,14},{14,12},{16,18},{18,... | collective-permute-start | bytes 786440 | tf_op jit(solution)/shard_map/ppermute | solution.py:470
  58.7 1.5 %collective-permute-start.15 = (bf16[4,64,512]{2,1,0:T(8,128)(2,1)S(1)}, bf16[4,64,512]{2,1,0:T(8,128)(2,1)S(1)}, u32[]{:S(2)}, u32[]{:S(2)}) collective-permute-start(bf16[4,64,512]{2,1,0:T(8,128)(2,1)S(1)} %collective-permute-done.13.refs_7_), channel_id=1, source_target_pairs={{0,2},{2,0},{4,6},{6,4},{8,10},{10,8},{12,14},{14,12},{16,18},{18,... | collective-permute-start | bytes 786440 | tf_op jit(solution)/shard_map/ppermute | solution.py:470
  60.2 1.0 copy-start.3
  61.3 0.9 copy-start.5
  63.1 1.2 %copy-start = (bf16[1536,512]{1,0:T(8,128)(2,1)}, bf16[1536,512]{1,0:T(8,128)(2,1)S(1)}, u32[]{:S(2)}) copy-start(bf16[1536,512]{1,0:T(8,128)(2,1)S(1)} %get-tuple-element.65.beside_ref) | copy-start | bytes 4718596
  67.4 1.4 %copy-start.1 = (bf16[1536,512]{1,0:T(8,128)(2,1)S(1)}, bf16[1536,512]{1,0:T(8,128)(2,1)}, u32[]{:S(2)}) copy-start(bf16[1536,512]{1,0:T(8,128)(2,1)} %copy-done) | copy-start | bytes 4718596
  71.8 2.2 %collective-permute-start.19 = (bf16[8,64,512]{2,1,0:T(8,128)(2,1)S(1)}, bf16[8,64,512]{2,1,0:T(8,128)(2,1)S(1)}, u32[]{:S(2)}, u32[]{:S(2)}) collective-permute-start(bf16[8,64,512]{2,1,0:T(8,128)(2,1)S(1)} %get-tuple-element.76), channel_id=1, source_target_pairs={{0,2},{2,0},{4,6},{6,4},{8,10},{10,8},{12,14},{14,12},{16,18},{18,... | collective-permute-start | bytes 1572872 | tf_op jit(solution)/shard_map/ppermute | solution.py:495
  72.5 5.1 %collective-permute-start.16 = (bf16[8,64,512]{2,1,0:T(8,128)(2,1)S(1)}, bf16[8,64,512]{2,1,0:T(8,128)(2,1)S(1)}, u32[]{:S(2)}, u32[]{:S(2)}) collective-permute-start(bf16[8,64,512]{2,1,0:T(8,128)(2,1)S(1)} %get-tuple-element.69), channel_id=1, source_target_pairs={{0,2},{2,0},{4,6},{6,4},{8,10},{10,8},{12,14},{14,12},{16,18},{18,... | collective-permute-start | bytes 1572872 | tf_op jit(solution)/shard_map/ppermute | solution.py:491
  74.1 10.3 %collective-permute-start.20 = (bf16[2,2,64,512]{3,2,1,0:T(8,128)(2,1)S(1)}, bf16[2,2,64,512]{3,2,1,0:T(8,128)(2,1)S(1)}, u32[]{:S(2)}, u32[]{:S(2)}) collective-permute-start(bf16[2,2,64,512]{3,2,1,0:T(8,128)(2,1)S(1)} %get-tuple-element.78), channel_id=1, source_target_pairs={{0,8},{2,10},{4,12},{6,14},{8,0},{10,2},{12,4},{14,6},{16,24},{18,... | collective-permute-start | bytes 786440 | tf_op jit(solution)/shard_map/ppermute | solution.py:401
  77.7 8.4 %collective-permute-start.17 = (bf16[2,2,64,512]{3,2,1,0:T(8,128)(2,1)S(1)}, bf16[2,2,64,512]{3,2,1,0:T(8,128)(2,1)S(1)}, u32[]{:S(2)}, u32[]{:S(2)}) collective-permute-start(bf16[2,2,64,512]{3,2,1,0:T(8,128)(2,1)S(1)} %get-tuple-element.71), channel_id=1, source_target_pairs={{0,4},{2,6},{4,0},{6,2},{8,12},{10,14},{12,8},{14,10},{16,20},{18,... | collective-permute-start | bytes 786440 | tf_op jit(solution)/shard_map/ppermute | solution.py:397
  84.5 5.3 %collective-permute-start.21 = (bf16[2,64,512]{2,1,0:T(8,128)(2,1)S(1)}, bf16[2,64,512]{2,1,0:T(8,128)(2,1)S(1)}, u32[]{:S(2)}, u32[]{:S(2)}) collective-permute-start(bf16[2,64,512]{2,1,0:T(8,128)(2,1)S(1)} %get-tuple-element.80), channel_id=1, source_target_pairs={{0,4},{2,6},{4,0},{6,2},{8,12},{10,14},{12,8},{14,10},{16,20},{18,... | collective-permute-start | bytes 393224 | tf_op jit(solution)/shard_map/ppermute | solution.py:405
  86.1 5.0 %collective-permute-start.18 = (bf16[2,64,512]{2,1,0:T(8,128)(2,1)S(1)}, bf16[2,64,512]{2,1,0:T(8,128)(2,1)S(1)}, u32[]{:S(2)}, u32[]{:S(2)}) collective-permute-start(bf16[2,64,512]{2,1,0:T(8,128)(2,1)S(1)} %get-tuple-element.73), channel_id=1, source_target_pairs={{0,8},{2,10},{4,12},{6,14},{8,0},{10,2},{12,4},{14,6},{16,24},{18,... | collective-permute-start | bytes 393224 | tf_op jit(solution)/shard_map/ppermute | solution.py:403
  91.2 7.8 %collective-permute-start.22 = (bf16[1,2,64,512]{3,2,1,0:T(8,128)(2,1)S(1)}, bf16[1,2,64,512]{3,2,1,0:T(8,128)(2,1)S(1)}, u32[]{:S(2)}, u32[]{:S(2)}) collective-permute-start(bf16[1,2,64,512]{3,2,1,0:T(8,128)(2,1)S(1)} %get-tuple-element.82), channel_id=1, source_target_pairs={{0,16},{2,18},{4,20},{6,22},{8,24},{10,26},{12,28},{14,30},{16,0},... | collective-permute-start | bytes 393224 | tf_op jit(solution)/shard_map/ppermute | solution.py:410
  99.0 5.0 %collective-permute-start.23 = (bf16[1,2,64,512]{3,2,1,0:T(8,128)(2,1)S(1)}, bf16[1,2,64,512]{3,2,1,0:T(8,128)(2,1)S(1)}, u32[]{:S(2)}, u32[]{:S(2)}) collective-permute-start(bf16[1,2,64,512]{3,2,1,0:T(8,128)(2,1)S(1)} %rounded_sum.1.kept_ref), channel_id=1, source_target_pairs={{0,1},{1,0},{2,3},{3,2},{4,5},{5,4},{6,7},{7,6},{8,9},{9,8},{10,11... | collective-permute-start | bytes 393224 | tf_op jit(solution)/shard_map/ppermute | solution.py:418

commit v7 on v6

--- a/solution.py
+++ b/solution.py
@@ -117,7 +117,8 @@
     for i, cut_ref in enumerate(cut_refs):
         at = (quarter ^ i) * 2 + half
         cut_ref[0, :, 0:width] = columns_ref[:, pl.ds(pl.multiple_of(at * width, width), width)]
-        cut_ref[0, :, width:] = weight
+        if cut_ref.shape[2] > width:
+            cut_ref[0, :, width:] = weight
         at = (quarter ^ i) * 2 + 1 - half
         across_ref[i] = columns_ref[:, pl.ds(pl.multiple_of(at * width, width), width)]
     parts = ask_ref.shape[1]
@@ -142,7 +143,8 @@
             jax.ShapeDtypeStruct((depth, asked), bf16),
             jax.ShapeDtypeStruct((quarters, depth, width), bf16),
         ]
-        + [jax.ShapeDtypeStruct((1, depth, width + self_weight.shape[1]), bf16)] * quarters,
+        + [jax.ShapeDtypeStruct((1, depth, width + self_weight.shape[1]), bf16)] * (quarters - 1)
+        + [jax.ShapeDtypeStruct((1, depth, width), bf16)],
         (counts, columns, self_weight, neighbour_weight, asks),
         scalars=1,
         fetch=True,
@@ -241,6 +243,30 @@
     return local_call(weight_kernel, "weight_pieces", [out], parts)[0]
 
 
+def relay_kernel(came_ref, near_ref, out_ref):
+    width = came_ref.shape[2]
+    out_ref[0, :, 0:width] = came_ref[1]
+    out_ref[0, :, width:] = near_ref[0, :, near_ref.shape[2] - (out_ref.shape[2] - width) :]
+
+
+def relayed(came, near):
+    out = jax.ShapeDtypeStruct((1, came.shape[1], near.shape[2]), bf16)
+    return local_call(relay_kernel, "relayed", [out], (came, near))[0]
+
+
+def gather_kernel(*refs):
+    *held_refs, out_ref = refs
+    at = 0
+    for ref in held_refs:
+        out_ref[at : at + ref.shape[0]] = ref[...]
+        at += ref.shape[0]
+
+
+def gathered(parts):
+    shape = (sum(p.shape[0] for p in parts), *parts[0].shape[1:])
+    return local_call(gather_kernel, "gathered", [jax.ShapeDtypeStruct(shape, bf16)], parts)[0]
+
+
 def flipped(masks, bit):
     return [m ^ bit for m in masks]
 
@@ -451,15 +477,18 @@
         tile_source[0].T, tile_kind[0].T, send_count, columns, halo, send_rows, tile_patterns, feat
     )
     came, means = lax.optimization_barrier((came, means))
-    far = [came[0:1]] + [flip("feat", i * below)(came[i : i + 1]) for i in range(1, quarters)]
+    leaving = [came[0:1], relayed(came, near[2]), came[2:3], came[3:4]]
+    far = leaving[:1] + [flip("feat", i * below)(leaving[i]) for i in range(1, quarters)]
     row_masks = [i * below for i in range(quarters)]
-    pieces, weight_masks = [weight_pieces(near, hid)], [list(row_masks)]
+    pieces = [weight_pieces(near[:3], hid), weight_pieces(far[1:2], hid)]
+    weight_masks = list(row_masks)
     row_masks = row_masks + flipped(row_masks, row_bits[0])
     for bit in row_bits[:-1]:
         pieces = pieces + [flip("feat", bit)(p) for p in pieces]
-        weight_masks = weight_masks + [flipped(m, bit) for m in weight_masks]
+        weight_masks = weight_masks + flipped(weight_masks, bit)
     means, near, far, pieces = lax.optimization_barrier((means, near, far, pieces))
     own_mean = lax.all_to_all(means, "feat", 0, 0, tiled=True)
+    pieces, weight_masks = [gathered(pieces)], [weight_masks]
     others = [flip("dom", 1)(p) for p in pieces]
     parts, width = [*near, *far], came.shape[2]
     for bit in row_bits[1:]:

time: 105 us -> 102 us (0.971)
  starting transfers between devices: 35.7 us -> 33.6 us
  local copies, waits for them, and re-layouts: 5.22 us -> 3.24 us
    ppermute x3, starting transfers between devices: 5.6 us -> 3.62 us  [on_device(): flip('feat', i * below)(leaving[i])]
    unnamed x14 -> x10, local copies, waits for them, and re-layouts: 5.19 us -> 3.21 us
    ppermute x3, waiting for transfers between devices: 1.89 us -> 0.35 us  [on_device(): flip('feat', i * below)(cuts[i])]
    ppermute x1 -> x2, starting transfers between devices: 0.6 us -> 2.08 us  [on_device(): pieces = pieces + [flip('feat', bit)(p) for p in pieces]]
    all_to_all x1, waiting for transfers between devices: 3.17 us -> 4.63 us  [on_device(): own_mean = lax.all_to_all(means, 'feat', 0, 0, tiled=True)]
    ppermute x2 -> x1, waiting for transfers between devices: 11.4 us -> 12.1 us  [on_device(): others = [flip('dom', 1)(p) for p in pieces]]
    ppermute x2 -> x1, starting transfers between devices: 2.1 us -> 1.56 us  [on_device(): others = [flip('dom', 1)(p) for p in pieces]]
    pallas_call x14 -> x17, Pallas kernels: 16.1 us -> 16.1 us  [local_call(): pl.pallas_call(kernel, out_shape=outs, in_specs=in_specs, out_specs=[whol...]
  transfers between devices with their start and end apart: 25 -> 23, of which waited for: 15 -> 14; matrix products, arithmetic and copies ran while one was open for 0% -> 0% of each run, Pallas kernels for 9% -> 9%
where the time goes in v7:
time: 102 us
  waiting for transfers between devices  48 us (47%)
  starting transfers between devices  33.6 us (33%)
  Pallas kernels  16.1 us (16%)
  local copies, waits for them, and re-layouts  3.24 us (3%)
    pallas_call x17, Pallas kernels, local_call(): pl.pallas_call(kernel, out_shape=outs, in_specs=in_specs, out_specs=[whol...  16.1 us
    ppermute x1, waiting for transfers between devices, on_device(): others = [flip('dom', 1)(p) for p in pieces]  12.1 us
    ppermute x3, waiting for transfers between devices, on_device(): flip('feat', i * below)(leaving[i])  7.57 us
    ppermute x1, waiting for transfers between devices, sum_gradients(): got = flip('feat', half * 8)(sent)  5.7 us
    ppermute x1, waiting for transfers between devices, sum_gradients(): neigh_got = flip('feat', 4)(neigh_sent)  5.13 us
    all_to_all x1, waiting for transfers between devices, on_device(): own_mean = lax.all_to_all(means, 'feat', 0, 0, tiled=True)  4.63 us
    ppermute x3, starting transfers between devices, on_device(): flip('feat', i * below)(cuts[i])  4.39 us
    all_to_all x1, starting transfers between devices, on_device(): own_mean = lax.all_to_all(means, 'feat', 0, 0, tiled=True)  3.98 us
  transfers between devices with their start and end apart: 23, of which 14 were waited for; matrix products, arithmetic and copies ran while one was open for 0% of the time, Pallas kernels for 9%

profile of v7, /device:TPU:0, one launch (start us, length us, event | category | flops | bytes accessed | tf_op | source)
XLA Modules:
  0.0 101.7 jit_solution(14053865476868677158)
XLA Ops:
  0.6 3.1 %open_exchange.1 = (bf16[64,256]{1,0:T(8,128)(2,1)}, bf16[4,64,1024]{2,1,0:T(8,128)(2,1)}, bf16[1,64,1536]{2,1,0:T(8,128)(2,1)}, bf16[1,64,1536]{2,1,0:T(8,128)(...) custom-call(s32[2,2]{1,0:T(2,128)} %refs_2_.3, bf16[64,8192]{1,0:T(8,128)(2,1)} %bitcast.7, ...), custom_call_target="tpu_custom_call" | custom-call | tf_op jit(solution)/shard_map/open_exchange/pallas_call | solution.py:79
  3.8 3.0 %collective-permute-start = (bf16[4,64,1024]{2,1,0:T(8,128)(2,1)}, bf16[4,64,1024]{2,1,0:T(8,128)(2,1)S(1)}, u32[]{:S(2)}, u32[]{:S(2)}) collective-permute-start(bf16[4,64,1024]{2,1,0:T(8,128)(2,1)} %get-tuple-element.46), channel_id=1, source_target_pairs={{0,4},{2,6},{4,0},{6,2},{8,12},{10,14},{12,8},{14,10},{16,20},{18,... | collective-permute-start | bytes 1572872 | tf_op jit(solution)/shard_map/ppermute | solution.py:470
  6.8 1.6 %collective-permute-start.2 = (bf16[1,64,1536]{2,1,0:T(8,128)(2,1)}, bf16[1,64,1536]{2,1,0:T(8,128)(2,1)S(1)}, u32[]{:S(2)}, u32[]{:S(2)}) collective-permute-start(bf16[1,64,1536]{2,1,0:T(8,128)(2,1)} %get-tuple-element.50), channel_id=1, source_target_pairs={{0,8},{2,10},{4,12},{6,14},{8,0},{10,2},{12,4},{14,6},{16,24},{18,... | collective-permute-start | bytes 589832 | tf_op jit(solution)/shard_map/ppermute | solution.py:471
  8.4 2.6 %collective-permute-start.3 = (bf16[1,64,1536]{2,1,0:T(8,128)(2,1)}, bf16[1,64,1536]{2,1,0:T(8,128)(2,1)S(1)}, u32[]{:S(2)}, u32[]{:S(2)}) collective-permute-start(bf16[1,64,1536]{2,1,0:T(8,128)(2,1)} %get-tuple-element.51), channel_id=1, source_target_pairs={{0,16},{2,18},{4,20},{6,22},{8,24},{10,26},{12,28},{14,30},{16,0},... | collective-permute-start | bytes 589832 | tf_op jit(solution)/shard_map/ppermute | solution.py:471
  10.9 1.5 %collective-permute-start.1 = (bf16[64,256]{1,0:T(8,128)(2,1)}, bf16[64,256]{1,0:T(8,128)(2,1)S(1)}, u32[]{:S(2)}, u32[]{:S(2)}) collective-permute-start(bf16[64,256]{1,0:T(8,128)(2,1)} %get-tuple-element.47), channel_id=1, source_target_pairs={{0,1},{1,0},{2,3},{3,2},{4,5},{5,4},{6,7},{7,6},{8,9},{9,8},{10,11... | collective-permute-start | bytes 98312 | tf_op jit(solution)/shard_map/ppermute | solution.py:473
  12.5 0.2 collective-permute-start.4
  12.7 2.4 %collective-permute-done.1.refs_4_ = bf16[64,256]{1,0:T(8,128)(2,1)S(1)} collective-permute-done((bf16[64,256]{1,0:T(8,128)(2,1)}, bf16[64,256]{1,0:T(8,128)(2,1)S(1)}, u32[]{:S(2)}, u32[]{:S(2)}) %collective-permute-start.1) | collective-permute-done | bytes 32800 | tf_op jit(solution)/shard_map/ppermute | solution.py:473
  15.1 0.6 copy-done.4
  15.7 8.0 %neighbour_means.1 = bf16[16,64,512]{2,1,0:T(8,128)(2,1)} custom-call(s32[8,64]{1,0:T(8,128)} %bitcast.9, s32[8,64]{1,0:T(8,128)} %bitcast.10, s32[2,2]{1,0:T(2,128)} %refs_2_.3, bf16[64,8192]{1,0:T(8,128)(2,1)} %bitcast.8, bf16[64,256]{1,0:T(8,128)(2,1)} %copy-done.4, s32[2,2,256]{2,1,0:T(2,128)} %refs_5_.1, bf16[64,128,128]{2,1,0:T(8,128)(2,1)} %refs_6_.2), custom_call_target="tpu_custom_call" | custom-call | tf_op jit(solution)/shard_map/neighbour_means/pallas_call | solution.py:79
  23.7 0.3 collective-permute-done.3.near_ref.refs_2_
  24.0 0.6 collective-permute-start.8
  24.7 0.2 collective-permute-start.5
  24.9 2.4 %collective-permute-start.7 = (bf16[1,64,1024]{2,1,0:T(8,128)(2,1)S(1)}, bf16[1,64,1024]{2,1,0:T(8,128)(2,1)S(1)}, u32[]{:S(2)}, u32[]{:S(2)}) collective-permute-start(bf16[1,64,1024]{2,1,0:T(8,128)(2,1)S(1)} %get-tuple-element.89), channel_id=1, source_target_pairs={{0,24},{2,26},{4,28},{6,30},{8,16},{10,18},{12,20},{14,22},{16,8},... | collective-permute-start | bytes 393224 | tf_op jit(solution)/shard_map/ppermute | solution.py:481
  27.3 1.0 collective-permute-start.6
  28.3 2.4 %collective-permute-done.5.refs_0_.refs_5_ = bf16[1,64,1536]{2,1,0:T(8,128)(2,1)S(1)} collective-permute-done((bf16[1,64,1536]{2,1,0:T(8,128)(2,1)S(1)}, bf16[1,64,1536]{2,1,0:T(8,128)(2,1)S(1)}, u32[]{:S(2)}, u32[]{:S(2)}) %collective-permute-start.5) | collective-permute-done | bytes 196640 | tf_op jit(solution)/shard_map/ppermute | solution.py:481
  30.7 1.5 %collective-permute-start.9 = (bf16[1,64,512]{2,1,0:T(8,128)(2,1)S(1)}, bf16[1,64,512]{2,1,0:T(8,128)(2,1)S(1)}, u32[]{:S(2)}, u32[]{:S(2)}) collective-permute-start(bf16[1,64,512]{2,1,0:T(8,128)(2,1)S(1)} %weight_pieces.3.refs_1_), channel_id=1, source_target_pairs={{0,4},{2,6},{4,0},{6,2},{8,12},{10,14},{12,8},{14,10},{16,20},{18,... | collective-permute-start | bytes 196616 | tf_op jit(solution)/shard_map/ppermute | solution.py:487
  32.2 1.2 %collective-permute-done.7.refs_7_ = bf16[1,64,1024]{2,1,0:T(8,128)(2,1)S(1)} collective-permute-done((bf16[1,64,1024]{2,1,0:T(8,128)(2,1)S(1)}, bf16[1,64,1024]{2,1,0:T(8,128)(2,1)S(1)}, u32[]{:S(2)}, u32[]{:S(2)}) %collective-permute-start.7) | collective-permute-done | bytes 131104 | tf_op jit(solution)/shard_map/ppermute | solution.py:481
  33.4 4.0 %collective-permute-done.6.refs_6_ = bf16[1,64,1024]{2,1,0:T(8,128)(2,1)S(1)} collective-permute-done((bf16[1,64,1024]{2,1,0:T(8,128)(2,1)S(1)}, bf16[1,64,1024]{2,1,0:T(8,128)(2,1)S(1)}, u32[]{:S(2)}, u32[]{:S(2)}) %collective-permute-start.6) | collective-permute-done | bytes 131104 | tf_op jit(solution)/shard_map/ppermute | solution.py:481
  37.4 4.0 %all-to-all-start = ((bf16[16,64,512]{2,1,0:T(8,128)(2,1)}), bf16[16,64,512]{2,1,0:T(8,128)(2,1)S(1)}, u32[]{:S(2)}, u32[]{:S(2)}) async-start(bf16[16,64,512]{2,1,0:T(8,128)(2,1)} %neighbour_means.1), calls=%async_computation | async-start | bytes 2097152 | tf_op jit(solution)/shard_map/all_to_all | solution.py:490
  41.4 1.6 %collective-permute-start.12 = (bf16[8,64,512]{2,1,0:T(8,128)(2,1)S(1)}, bf16[8,64,512]{2,1,0:T(8,128)(2,1)S(1)}, u32[]{:S(2)}, u32[]{:S(2)}) collective-permute-start(bf16[8,64,512]{2,1,0:T(8,128)(2,1)S(1)} %gathered.1.refs_2_), channel_id=1, source_target_pairs={{0,1},{1,0},{2,3},{3,2},{4,5},{5,4},{6,7},{7,6},{8,9},{9,8},{10,11... | collective-permute-start | bytes 1572872 | tf_op jit(solution)/shard_map/ppermute | solution.py:492
  43.0 0.1 collective-permute-start.11
  43.1 0.1 cut_rows.1
  43.2 0.4 collective-permute-start.10
  43.6 12.1 %collective-permute-done.12.refs_4_ = bf16[8,64,512]{2,1,0:T(8,128)(2,1)S(1)} collective-permute-done((bf16[8,64,512]{2,1,0:T(8,128)(2,1)S(1)}, bf16[8,64,512]{2,1,0:T(8,128)(2,1)S(1)}, u32[]{:S(2)}, u32[]{:S(2)}) %collective-permute-start.12) | collective-permute-done | bytes 524320 | tf_op jit(solution)/shard_map/ppermute | solution.py:492
  55.8 1.9 %collective-permute-done.13.refs_5_ = bf16[8,64,512]{2,1,0:T(8,128)(2,1)S(1)} collective-permute-done((bf16[8,64,512]{2,1,0:T(8,128)(2,1)S(1)}, bf16[8,64,512]{2,1,0:T(8,128)(2,1)S(1)}, u32[]{:S(2)}, u32[]{:S(2)}) %collective-permute-start.13) | collective-permute-done | bytes 524320 | tf_op jit(solution)/shard_map/ppermute | solution.py:499
  57.7 0.8 own_linear.1
  58.5 1.2 %copy-done = bf16[1536,512]{1,0:T(8,128)(2,1)} copy-done((bf16[1536,512]{1,0:T(8,128)(2,1)}, bf16[1536,512]{1,0:T(8,128)(2,1)S(1)}, u32[]{:S(2)}) %copy-start) | copy-done | bytes 1572888
  59.7 4.6 %all-to-all-done.mean_ref = bf16[16,64,512]{2,1,0:T(8,128)(2,1)S(1)} async-done(((bf16[16,64,512]{2,1,0:T(8,128)(2,1)}), bf16[16,64,512]{2,1,0:T(8,128)(2,1)S(1)}, u32[]{:S(2)}, u32[]{:S(2)}) %all-to-all-start) | async-done | bytes 1048608 | tf_op jit(solution)/shard_map/all_to_all | solution.py:490
  64.3 1.4 %copy-done.1 = bf16[1536,512]{1,0:T(8,128)(2,1)S(1)} copy-done((bf16[1536,512]{1,0:T(8,128)(2,1)S(1)}, bf16[1536,512]{1,0:T(8,128)(2,1)}, u32[]{:S(2)}) %copy-start.1) | copy-done | bytes 1572888
  65.7 2.3 %forward.1 = (bf16[512,512]{1,0:T(8,128)(2,1)}, bf16[512,512]{1,0:T(8,128)(2,1)S(1)}, bf16[8,64,512]{2,1,0:T(8,128)(2,1)S(1)}, f32[8,64,512]{2,1,0:T(8,128)S(1)}) custom-call(bf16[16,64,512]{2,1,0:T(8,128)(2,1)S(1)} %all-to-all-done.mean_ref, bf16[1536,512]{1,0:T(8,128)(2,1)S(1)} %copy-done.1, f32[512,512]{1,0:T(8,128)S(1)} %get-tuple-element.70.base_ref, ...), custom_call_target="tpu_custom_call" | custom-call | tf_op jit(solution)/shard_map/forward/pallas_call | solution.py:79
  68.0 0.7 neighbour_sums.1
  68.7 0.7 collective-permute-start.17
  69.4 0.1 collective-permute-start.14
  69.5 1.5 %collective-permute-done.17.got_ref = bf16[8,64,512]{2,1,0:T(8,128)(2,1)S(1)} collective-permute-done((bf16[8,64,512]{2,1,0:T(8,128)(2,1)S(1)}, bf16[8,64,512]{2,1,0:T(8,128)(2,1)S(1)}, u32[]{:S(2)}, u32[]{:S(2)}) %collective-permute-start.17) | collective-permute-done | bytes 524320 | tf_op jit(solution)/shard_map/ppermute | solution.py:524
  71.0 0.1 neigh_first.1
  71.0 3.5 %collective-permute-start.18 = (bf16[2,2,64,512]{3,2,1,0:T(8,128)(2,1)S(1)}, bf16[2,2,64,512]{3,2,1,0:T(8,128)(2,1)S(1)}, u32[]{:S(2)}, u32[]{:S(2)}) collective-permute-start(bf16[2,2,64,512]{3,2,1,0:T(8,128)(2,1)S(1)} %get-tuple-element.82), channel_id=1, source_target_pairs={{0,8},{2,10},{4,12},{6,14},{8,0},{10,2},{12,4},{14,6},{16,24},{18,... | collective-permute-start | bytes 786440 | tf_op jit(solution)/shard_map/ppermute | solution.py:427
  74.5 0.1 own_first.1
  74.6 1.6 %collective-permute-start.15 = (bf16[2,2,64,512]{3,2,1,0:T(8,128)(2,1)S(1)}, bf16[2,2,64,512]{3,2,1,0:T(8,128)(2,1)S(1)}, u32[]{:S(2)}, u32[]{:S(2)}) collective-permute-start(bf16[2,2,64,512]{3,2,1,0:T(8,128)(2,1)S(1)} %get-tuple-element.75), channel_id=1, source_target_pairs={{0,4},{2,6},{4,0},{6,2},{8,12},{10,14},{12,8},{14,10},{16,20},{18,... | collective-permute-start | bytes 786440 | tf_op jit(solution)/shard_map/ppermute | solution.py:423
  76.2 5.1 %collective-permute-done.18.got_ref = bf16[2,2,64,512]{3,2,1,0:T(8,128)(2,1)S(1)} collective-permute-done((bf16[2,2,64,512]{3,2,1,0:T(8,128)(2,1)S(1)}, bf16[2,2,64,512]{3,2,1,0:T(8,128)(2,1)S(1)}, u32[]{:S(2)}, u32[]{:S(2)}) %collective-permute-start.18) | collective-permute-done | bytes 262176 | tf_op jit(solution)/shard_map/ppermute | solution.py:427
  81.4 1.6 %collective-permute-start.19 = (bf16[2,64,512]{2,1,0:T(8,128)(2,1)S(1)}, bf16[2,64,512]{2,1,0:T(8,128)(2,1)S(1)}, u32[]{:S(2)}, u32[]{:S(2)}) collective-permute-start(bf16[2,64,512]{2,1,0:T(8,128)(2,1)S(1)} %get-tuple-element.84), channel_id=1, source_target_pairs={{0,4},{2,6},{4,0},{6,2},{8,12},{10,14},{12,8},{14,10},{16,20},{18,... | collective-permute-start | bytes 393224 | tf_op jit(solution)/shard_map/ppermute | solution.py:431
  83.0 1.8 %collective-permute-start.16 = (bf16[2,64,512]{2,1,0:T(8,128)(2,1)S(1)}, bf16[2,64,512]{2,1,0:T(8,128)(2,1)S(1)}, u32[]{:S(2)}, u32[]{:S(2)}) collective-permute-start(bf16[2,64,512]{2,1,0:T(8,128)(2,1)S(1)} %get-tuple-element.77), channel_id=1, source_target_pairs={{0,8},{2,10},{4,12},{6,14},{8,0},{10,2},{12,4},{14,6},{16,24},{18,... | collective-permute-start | bytes 393224 | tf_op jit(solution)/shard_map/ppermute | solution.py:429
  84.8 1.8 %collective-permute-done.19.neigh_got_ref = bf16[2,64,512]{2,1,0:T(8,128)(2,1)S(1)} collective-permute-done((bf16[2,64,512]{2,1,0:T(8,128)(2,1)S(1)}, bf16[2,64,512]{2,1,0:T(8,128)(2,1)S(1)}, u32[]{:S(2)}, u32[]{:S(2)}) %collective-permute-start.19) | collective-permute-done | bytes 131104 | tf_op jit(solution)/shard_map/ppermute | solution.py:431
  86.6 1.4 %collective-permute-done.16.own_got_ref = bf16[2,64,512]{2,1,0:T(8,128)(2,1)S(1)} collective-permute-done((bf16[2,64,512]{2,1,0:T(8,128)(2,1)S(1)}, bf16[2,64,512]{2,1,0:T(8,128)(2,1)S(1)}, u32[]{:S(2)}, u32[]{:S(2)}) %collective-permute-start.16) | collective-permute-done | bytes 131104 | tf_op jit(solution)/shard_map/ppermute | solution.py:429
  88.1 2.2 %collective-permute-start.20 = (bf16[1,2,64,512]{3,2,1,0:T(8,128)(2,1)S(1)}, bf16[1,2,64,512]{3,2,1,0:T(8,128)(2,1)S(1)}, u32[]{:S(2)}, u32[]{:S(2)}) collective-permute-start(bf16[1,2,64,512]{3,2,1,0:T(8,128)(2,1)S(1)} %get-tuple-element.86), channel_id=1, source_target_pairs={{0,16},{2,18},{4,20},{6,22},{8,24},{10,26},{12,28},{14,30},{16,0},... | collective-permute-start | bytes 393224 | tf_op jit(solution)/shard_map/ppermute | solution.py:436
  90.2 5.7 %collective-permute-done.20.got_ref = bf16[1,2,64,512]{3,2,1,0:T(8,128)(2,1)S(1)} collective-permute-done((bf16[1,2,64,512]{3,2,1,0:T(8,128)(2,1)S(1)}, bf16[1,2,64,512]{3,2,1,0:T(8,128)(2,1)S(1)}, u32[]{:S(2)}, u32[]{:S(2)}) %collective-permute-start.20) | collective-permute-done | bytes 131104 | tf_op jit(solution)/shard_map/ppermute | solution.py:436
  96.0 1.5 %collective-permute-start.21 = (bf16[1,2,64,512]{3,2,1,0:T(8,128)(2,1)S(1)}, bf16[1,2,64,512]{3,2,1,0:T(8,128)(2,1)S(1)}, u32[]{:S(2)}, u32[]{:S(2)}) collective-permute-start(bf16[1,2,64,512]{3,2,1,0:T(8,128)(2,1)S(1)} %rounded_sum.1.kept_ref), channel_id=1, source_target_pairs={{0,1},{1,0},{2,3},{3,2},{4,5},{5,4},{6,7},{7,6},{8,9},{9,8},{10,11... | collective-permute-start | bytes 393224 | tf_op jit(solution)/shard_map/ppermute | solution.py:444
  97.5 3.5 %collective-permute-done.21.got_ref = bf16[1,2,64,512]{3,2,1,0:T(8,128)(2,1)S(1)} collective-permute-done((bf16[1,2,64,512]{3,2,1,0:T(8,128)(2,1)S(1)}, bf16[1,2,64,512]{3,2,1,0:T(8,128)(2,1)S(1)}, u32[]{:S(2)}, u32[]{:S(2)}) %collective-permute-start.21) | collective-permute-done | bytes 131104 | tf_op jit(solution)/shard_map/ppermute | solution.py:444
  101.0 0.7 last_sum.1
  (26 shorter events, 0.3 us)
Async XLA Ops:
  3.8 20.9 %collective-permute-start = (bf16[4,64,1024]{2,1,0:T(8,128)(2,1)}, bf16[4,64,1024]{2,1,0:T(8,128)(2,1)S(1)}, u32[]{:S(2)}, u32[]{:S(2)}) collective-permute-start(bf16[4,64,1024]{2,1,0:T(8,128)(2,1)} %get-tuple-element.46), channel_id=1, source_target_pairs={{0,4},{2,6},{4,0},{6,2},{8,12},{10,14},{12,8},{14,10},{16,20},{18,... | collective-permute-start | bytes 1572872 | tf_op jit(solution)/shard_map/ppermute | solution.py:470
  6.8 16.9 %collective-permute-start.2 = (bf16[1,64,1536]{2,1,0:T(8,128)(2,1)}, bf16[1,64,1536]{2,1,0:T(8,128)(2,1)S(1)}, u32[]{:S(2)}, u32[]{:S(2)}) collective-permute-start(bf16[1,64,1536]{2,1,0:T(8,128)(2,1)} %get-tuple-element.50), channel_id=1, source_target_pairs={{0,8},{2,10},{4,12},{6,14},{8,0},{10,2},{12,4},{14,6},{16,24},{18,... | collective-permute-start | bytes 589832 | tf_op jit(solution)/shard_map/ppermute | solution.py:471
  8.4 15.7 %collective-permute-start.3 = (bf16[1,64,1536]{2,1,0:T(8,128)(2,1)}, bf16[1,64,1536]{2,1,0:T(8,128)(2,1)S(1)}, u32[]{:S(2)}, u32[]{:S(2)}) collective-permute-start(bf16[1,64,1536]{2,1,0:T(8,128)(2,1)} %get-tuple-element.51), channel_id=1, source_target_pairs={{0,16},{2,18},{4,20},{6,22},{8,24},{10,26},{12,28},{14,30},{16,0},... | collective-permute-start | bytes 589832 | tf_op jit(solution)/shard_map/ppermute | solution.py:471
  10.9 4.1 %collective-permute-start.1 = (bf16[64,256]{1,0:T(8,128)(2,1)}, bf16[64,256]{1,0:T(8,128)(2,1)S(1)}, u32[]{:S(2)}, u32[]{:S(2)}) collective-permute-start(bf16[64,256]{1,0:T(8,128)(2,1)} %get-tuple-element.47), channel_id=1, source_target_pairs={{0,1},{1,0},{2,3},{3,2},{4,5},{5,4},{6,7},{7,6},{8,9},{9,8},{10,11... | collective-permute-start | bytes 98312 | tf_op jit(solution)/shard_map/ppermute | solution.py:473
  12.5 19.8 %collective-permute-start.4 = (bf16[1,64,1024]{2,1,0:T(8,128)(2,1)}, bf16[1,64,1024]{2,1,0:T(8,128)(2,1)S(1)}, u32[]{:S(2)}, u32[]{:S(2)}) collective-permute-start(bf16[1,64,1024]{2,1,0:T(8,128)(2,1)} %get-tuple-element.52), channel_id=1, source_target_pairs={{0,24},{2,26},{4,28},{6,30},{8,16},{10,18},{12,20},{14,22},{16,8},... | collective-permute-start | bytes 393224 | tf_op jit(solution)/shard_map/ppermute | solution.py:471
  15.1 0.6 copy-start.4
  15.7 8.3 %copy-start.2 = (bf16[1,64,1536]{2,1,0:T(8,128)(2,1)S(1)}, bf16[1,64,1536]{2,1,0:T(8,128)(2,1)}, u32[]{:S(2)}) copy-start(bf16[1,64,1536]{2,1,0:T(8,128)(2,1)} %get-tuple-element.55.refs_0_) | copy-start | bytes 589828
  24.0 8.2 %collective-permute-start.8 = (bf16[3,64,512]{2,1,0:T(8,128)(2,1)S(1)}, bf16[3,64,512]{2,1,0:T(8,128)(2,1)S(1)}, u32[]{:S(2)}, u32[]{:S(2)}) collective-permute-start(bf16[3,64,512]{2,1,0:T(8,128)(2,1)S(1)} %weight_pieces.2.refs_0_), channel_id=1, source_target_pairs={{0,4},{2,6},{4,0},{6,2},{8,12},{10,14},{12,8},{14,10},{16,20},{18,... | collective-permute-start | bytes 589832 | tf_op jit(solution)/shard_map/ppermute | solution.py:487
  24.7 6.1 %collective-permute-start.5 = (bf16[1,64,1536]{2,1,0:T(8,128)(2,1)S(1)}, bf16[1,64,1536]{2,1,0:T(8,128)(2,1)S(1)}, u32[]{:S(2)}, u32[]{:S(2)}) collective-permute-start(bf16[1,64,1536]{2,1,0:T(8,128)(2,1)S(1)} %relayed.1), channel_id=1, source_target_pairs={{0,8},{2,10},{4,12},{6,14},{8,0},{10,2},{12,4},{14,6},{16,24},{18,... | collective-permute-start | bytes 589832 | tf_op jit(solution)/shard_map/ppermute | solution.py:481
  24.9 8.5 %collective-permute-start.7 = (bf16[1,64,1024]{2,1,0:T(8,128)(2,1)S(1)}, bf16[1,64,1024]{2,1,0:T(8,128)(2,1)S(1)}, u32[]{:S(2)}, u32[]{:S(2)}) collective-permute-start(bf16[1,64,1024]{2,1,0:T(8,128)(2,1)S(1)} %get-tuple-element.89), channel_id=1, source_target_pairs={{0,24},{2,26},{4,28},{6,30},{8,16},{10,18},{12,20},{14,22},{16,8},... | collective-permute-start | bytes 393224 | tf_op jit(solution)/shard_map/ppermute | solution.py:481
  27.3 10.1 %collective-permute-start.6 = (bf16[1,64,1024]{2,1,0:T(8,128)(2,1)S(1)}, bf16[1,64,1024]{2,1,0:T(8,128)(2,1)S(1)}, u32[]{:S(2)}, u32[]{:S(2)}) collective-permute-start(bf16[1,64,1024]{2,1,0:T(8,128)(2,1)S(1)} %get-tuple-element.90), channel_id=1, source_target_pairs={{0,16},{2,18},{4,20},{6,22},{8,24},{10,26},{12,28},{14,30},{16,0},... | collective-permute-start | bytes 393224 | tf_op jit(solution)/shard_map/ppermute | solution.py:481
  30.7 6.6 %collective-permute-start.9 = (bf16[1,64,512]{2,1,0:T(8,128)(2,1)S(1)}, bf16[1,64,512]{2,1,0:T(8,128)(2,1)S(1)}, u32[]{:S(2)}, u32[]{:S(2)}) collective-permute-start(bf16[1,64,512]{2,1,0:T(8,128)(2,1)S(1)} %weight_pieces.3.refs_1_), channel_id=1, source_target_pairs={{0,4},{2,6},{4,0},{6,2},{8,12},{10,14},{12,8},{14,10},{16,20},{18,... | collective-permute-start | bytes 196616 | tf_op jit(solution)/shard_map/ppermute | solution.py:487
  37.4 26.9 %all-to-all-start = ((bf16[16,64,512]{2,1,0:T(8,128)(2,1)}), bf16[16,64,512]{2,1,0:T(8,128)(2,1)S(1)}, u32[]{:S(2)}, u32[]{:S(2)}) async-start(bf16[16,64,512]{2,1,0:T(8,128)(2,1)} %neighbour_means.1), calls=%async_computation | async-start | bytes 2097152 | tf_op jit(solution)/shard_map/all_to_all | solution.py:490
  41.4 16.3 %copy-start.3 = (bf16[512,512]{1,0:T(8,128)(2,1)S(1)}, bf16[512,512]{1,0:T(8,128)(2,1)}, u32[]{:S(2)}) copy-start(bf16[512,512]{1,0:T(8,128)(2,1)} %refs_6_.3) | copy-start | bytes 1572868
  41.4 14.3 %collective-permute-start.12 = (bf16[8,64,512]{2,1,0:T(8,128)(2,1)S(1)}, bf16[8,64,512]{2,1,0:T(8,128)(2,1)S(1)}, u32[]{:S(2)}, u32[]{:S(2)}) collective-permute-start(bf16[8,64,512]{2,1,0:T(8,128)(2,1)S(1)} %gathered.1.refs_2_), channel_id=1, source_target_pairs={{0,1},{1,0},{2,3},{3,2},{4,5},{5,4},{6,7},{7,6},{8,9},{9,8},{10,11... | collective-permute-start | bytes 1572872 | tf_op jit(solution)/shard_map/ppermute | solution.py:492
  43.0 12.8 %collective-permute-start.11 = (bf16[8,64,512]{2,1,0:T(8,128)(2,1)S(1)}, bf16[8,64,512]{2,1,0:T(8,128)(2,1)S(1)}, u32[]{:S(2)}, u32[]{:S(2)}) collective-permute-start(bf16[8,64,512]{2,1,0:T(8,128)(2,1)S(1)} %gathered.1.refs_2_), channel_id=1, source_target_pairs={{0,2},{2,0},{4,6},{6,4},{8,10},{10,8},{12,14},{14,12},{16,18},{18,... | collective-permute-start | bytes 1572872 | tf_op jit(solution)/shard_map/ppermute | solution.py:498
  43.2 12.6 %collective-permute-start.10 = (bf16[8,64,512]{2,1,0:T(8,128)(2,1)S(1)}, bf16[8,64,512]{2,1,0:T(8,128)(2,1)S(1)}, u32[]{:S(2)}, u32[]{:S(2)}) collective-permute-start(bf16[8,64,512]{2,1,0:T(8,128)(2,1)S(1)} %get-tuple-element.64), channel_id=1, source_target_pairs={{0,2},{2,0},{4,6},{6,4},{8,10},{10,8},{12,14},{14,12},{16,18},{18,... | collective-permute-start | bytes 1572872 | tf_op jit(solution)/shard_map/ppermute | solution.py:496
  55.7 1.9 %collective-permute-start.13 = (bf16[8,64,512]{2,1,0:T(8,128)(2,1)S(1)}, bf16[8,64,512]{2,1,0:T(8,128)(2,1)S(1)}, u32[]{:S(2)}, u32[]{:S(2)}) collective-permute-start(bf16[8,64,512]{2,1,0:T(8,128)(2,1)S(1)} %collective-permute-done.12.refs_4_), channel_id=1, source_target_pairs={{0,2},{2,0},{4,6},{6,4},{8,10},{10,8},{12,14},{14,12},{16,18},{18,... | collective-permute-start | bytes 1572872 | tf_op jit(solution)/shard_map/ppermute | solution.py:499
  58.5 1.2 %copy-start = (bf16[1536,512]{1,0:T(8,128)(2,1)}, bf16[1536,512]{1,0:T(8,128)(2,1)S(1)}, u32[]{:S(2)}) copy-start(bf16[1536,512]{1,0:T(8,128)(2,1)S(1)} %get-tuple-element.69.beside_ref) | copy-start | bytes 4718596
  64.3 1.4 %copy-start.1 = (bf16[1536,512]{1,0:T(8,128)(2,1)S(1)}, bf16[1536,512]{1,0:T(8,128)(2,1)}, u32[]{:S(2)}) copy-start(bf16[1536,512]{1,0:T(8,128)(2,1)} %copy-done) | copy-start | bytes 4718596
  68.7 2.2 %collective-permute-start.17 = (bf16[8,64,512]{2,1,0:T(8,128)(2,1)S(1)}, bf16[8,64,512]{2,1,0:T(8,128)(2,1)S(1)}, u32[]{:S(2)}, u32[]{:S(2)}) collective-permute-start(bf16[8,64,512]{2,1,0:T(8,128)(2,1)S(1)} %get-tuple-element.80), channel_id=1, source_target_pairs={{0,2},{2,0},{4,6},{6,4},{8,10},{10,8},{12,14},{14,12},{16,18},{18,... | collective-permute-start | bytes 1572872 | tf_op jit(solution)/shard_map/ppermute | solution.py:524
  69.4 5.1 %collective-permute-start.14 = (bf16[8,64,512]{2,1,0:T(8,128)(2,1)S(1)}, bf16[8,64,512]{2,1,0:T(8,128)(2,1)S(1)}, u32[]{:S(2)}, u32[]{:S(2)}) collective-permute-start(bf16[8,64,512]{2,1,0:T(8,128)(2,1)S(1)} %get-tuple-element.73), channel_id=1, source_target_pairs={{0,2},{2,0},{4,6},{6,4},{8,10},{10,8},{12,14},{14,12},{16,18},{18,... | collective-permute-start | bytes 1572872 | tf_op jit(solution)/shard_map/ppermute | solution.py:520
  71.0 10.3 %collective-permute-start.18 = (bf16[2,2,64,512]{3,2,1,0:T(8,128)(2,1)S(1)}, bf16[2,2,64,512]{3,2,1,0:T(8,128)(2,1)S(1)}, u32[]{:S(2)}, u32[]{:S(2)}) collective-permute-start(bf16[2,2,64,512]{3,2,1,0:T(8,128)(2,1)S(1)} %get-tuple-element.82), channel_id=1, source_target_pairs={{0,8},{2,10},{4,12},{6,14},{8,0},{10,2},{12,4},{14,6},{16,24},{18,... | collective-permute-start | bytes 786440 | tf_op jit(solution)/shard_map/ppermute | solution.py:427
  74.6 8.4 %collective-permute-start.15 = (bf16[2,2,64,512]{3,2,1,0:T(8,128)(2,1)S(1)}, bf16[2,2,64,512]{3,2,1,0:T(8,128)(2,1)S(1)}, u32[]{:S(2)}, u32[]{:S(2)}) collective-permute-start(bf16[2,2,64,512]{3,2,1,0:T(8,128)(2,1)S(1)} %get-tuple-element.75), channel_id=1, source_target_pairs={{0,4},{2,6},{4,0},{6,2},{8,12},{10,14},{12,8},{14,10},{16,20},{18,... | collective-permute-start | bytes 786440 | tf_op jit(solution)/shard_map/ppermute | solution.py:423
  81.4 5.3 %collective-permute-start.19 = (bf16[2,64,512]{2,1,0:T(8,128)(2,1)S(1)}, bf16[2,64,512]{2,1,0:T(8,128)(2,1)S(1)}, u32[]{:S(2)}, u32[]{:S(2)}) collective-permute-start(bf16[2,64,512]{2,1,0:T(8,128)(2,1)S(1)} %get-tuple-element.84), channel_id=1, source_target_pairs={{0,4},{2,6},{4,0},{6,2},{8,12},{10,14},{12,8},{14,10},{16,20},{18,... | collective-permute-start | bytes 393224 | tf_op jit(solution)/shard_map/ppermute | solution.py:431
  83.0 5.0 %collective-permute-start.16 = (bf16[2,64,512]{2,1,0:T(8,128)(2,1)S(1)}, bf16[2,64,512]{2,1,0:T(8,128)(2,1)S(1)}, u32[]{:S(2)}, u32[]{:S(2)}) collective-permute-start(bf16[2,64,512]{2,1,0:T(8,128)(2,1)S(1)} %get-tuple-element.77), channel_id=1, source_target_pairs={{0,8},{2,10},{4,12},{6,14},{8,0},{10,2},{12,4},{14,6},{16,24},{18,... | collective-permute-start | bytes 393224 | tf_op jit(solution)/shard_map/ppermute | solution.py:429
  88.1 7.9 %collective-permute-start.20 = (bf16[1,2,64,512]{3,2,1,0:T(8,128)(2,1)S(1)}, bf16[1,2,64,512]{3,2,1,0:T(8,128)(2,1)S(1)}, u32[]{:S(2)}, u32[]{:S(2)}) collective-permute-start(bf16[1,2,64,512]{3,2,1,0:T(8,128)(2,1)S(1)} %get-tuple-element.86), channel_id=1, source_target_pairs={{0,16},{2,18},{4,20},{6,22},{8,24},{10,26},{12,28},{14,30},{16,0},... | collective-permute-start | bytes 393224 | tf_op jit(solution)/shard_map/ppermute | solution.py:436
  96.0 5.0 %collective-permute-start.21 = (bf16[1,2,64,512]{3,2,1,0:T(8,128)(2,1)S(1)}, bf16[1,2,64,512]{3,2,1,0:T(8,128)(2,1)S(1)}, u32[]{:S(2)}, u32[]{:S(2)}) collective-permute-start(bf16[1,2,64,512]{3,2,1,0:T(8,128)(2,1)S(1)} %rounded_sum.1.kept_ref), channel_id=1, source_target_pairs={{0,1},{1,0},{2,3},{3,2},{4,5},{5,4},{6,7},{7,6},{8,9},{9,8},{10,11... | collective-permute-start | bytes 393224 | tf_op jit(solution)/shard_map/ppermute | solution.py:444

commit v8 on v7

--- a/solution.py
+++ b/solution.py
@@ -383,14 +383,6 @@
         sent_ref[far] = total[1].astype(bf16)
 
 
-def third_kernel(own_ref, own_got_ref, neigh_ref, neigh_got_ref, out_ref, sent_ref):
-    half = out_ref.shape[0]
-    for i in range(half):
-        for at, ref in ((i, out_ref), (half + i, sent_ref)):
-            ref[i, 0] = (own_ref[at] + own_got_ref[at].astype(f32)).astype(ref.dtype)
-            ref[i, 1] = (neigh_ref[at] + neigh_got_ref[at].astype(f32)).astype(ref.dtype)
-
-
 def halving_kernel(kept_ref, got_ref, out_ref, sent_ref):
     half = out_ref.shape[0]
     for i in range(half):
@@ -402,16 +394,30 @@
     out_ref[...] = (kept_ref[...].astype(f32) + got_ref[...].astype(f32)).astype(out_ref.dtype)
 
 
-def last_sum_kernel(kept_ref, got_ref, own_ref, neigh_ref):
-    total = kept_ref[...].astype(f32) + got_ref[...].astype(f32)
-    own_ref[...] = total[0, 0]
-    neigh_ref[...] = total[0, 1]
+def last_sum_kernel(*refs):
+    for i, out_ref in enumerate(refs[4:]):
+        kept_ref, got_ref = refs[2 * i : 2 * i + 2]
+        out_ref[...] = (kept_ref[...].astype(f32) + got_ref[...].astype(f32))[0]
+
+
+def finish_sum(kept, got):
+    count, depth, hid = kept.shape
+    while count > 1:
+        count //= 2
+        shape = (count, depth, hid)
+        outs = [jax.ShapeDtypeStruct(shape, f32), jax.ShapeDtypeStruct(shape, bf16)]
+        kept, sent = local_call(halving_kernel, "halving", outs, (kept, got))
+        got = flip("feat", count * 8)(sent)
+    rounded = jax.ShapeDtypeStruct(kept.shape, bf16)
+    for bit in bits_of(lax.axis_size("dom")):
+        (kept,) = local_call(round_sum_kernel, "rounded_sum", [rounded], (kept, got))
+        got = flip("dom", bit)(kept)
+    return kept, got
 
 
 def sum_gradients(own_kept, own_got, neigh_kept, neigh_got):
-    feat, dom = lax.axis_size("feat"), lax.axis_size("dom")
     depth, hid = own_kept.shape[1:]
-    far = feat // 8
+    far = lax.axis_size("feat") // 8
 
     def pair(*lead):
         shape = (*lead, depth, hid)
@@ -429,21 +435,9 @@
     own_got = flip("feat", 4)(own_sent)
     neigh, neigh_sent = local_call(second_kernel, "neigh_second", pair(far), (neigh, neigh_got))
     neigh_got = flip("feat", 2)(neigh_sent)
-    half = far // 2
-    kept, sent = local_call(
-        third_kernel, "third_sum", pair(half, 2), (own, own_got, neigh, neigh_got)
-    )
-    got = flip("feat", half * 8)(sent)
-    while half > 1:
-        half //= 2
-        kept, sent = local_call(halving_kernel, "halving", pair(half, 2), (kept, got))
-        got = flip("feat", half * 8)(sent)
-    rounded = jax.ShapeDtypeStruct(kept.shape, bf16)
-    for bit in bits_of(dom):
-        (kept,) = local_call(round_sum_kernel, "rounded_sum", [rounded], (kept, got))
-        got = flip("dom", bit)(kept)
     out = jax.ShapeDtypeStruct((depth, hid), f32)
-    return local_call(last_sum_kernel, "last_sum", [out, out], (kept, got))
+    last = (*finish_sum(own, own_got), *finish_sum(neigh, neigh_got))
+    return local_call(last_sum_kernel, "last_sum", [out, out], last)
 
 
 def on_device(
@@ -468,7 +462,8 @@
         send_count, columns, self_weight, neighbour_weight, send_rows, quarters
     )
     came = flip("feat", row_bits[0])(across)
-    near = [cuts[0]] + [flip("feat", i * below)(cuts[i]) for i in range(1, quarters)]
+    near = {i: flip("feat", i * below)(cuts[i]) for i in (3, 2, 1)}
+    near = [cuts[0], near[1], near[2], near[3]]
     if dom == 2:
         halo = flip("dom", 1)(picked)
     else:

time: 102 us -> 101 us (level)
  waiting for transfers between devices: 48 us -> 43.8 us
  starting transfers between devices: 33.6 us -> 36.4 us
    ppermute x5 -> x7, starting transfers between devices: 8.09 us -> 10.9 us  [the longest x3 4.39 us: on_device(): near = {i: flip('feat', i * below)(cuts[i]) for i in (3, 2, 1)}]
    ppermute x5 -> x7, waiting for transfers between devices: 9.53 us -> 6.78 us  [the longest x2 3.53 us: finish_sum(): got = flip('feat', count * 8)(sent)]
    ppermute x1, waiting for transfers between devices: 1.38 us -> 0.01 us  [sum_gradients(): own_got = flip('feat', 4)(own_sent)]
    pallas_call x17 -> x19, Pallas kernels: 16.1 us -> 16.1 us  [local_call(): pl.pallas_call(kernel, out_shape=outs, in_specs=in_specs, out_specs=[whol...]
  transfers between devices with their start and end apart: 23 -> 25, of which waited for: 14 -> 14; matrix products, arithmetic and copies ran while one was open for 0% -> 0% of each run, Pallas kernels for 9% -> 9%
where the time goes in v8:
time: 101 us; the launch traced here: 100 us
  waiting for transfers between devices  43.8 us (43%)
  starting transfers between devices  36.4 us (36%)
  Pallas kernels  16.1 us (16%)
  local copies, waits for them, and re-layouts  3.22 us (3%)
    pallas_call x19, Pallas kernels, local_call(): pl.pallas_call(kernel, out_shape=outs, in_specs=in_specs, out_specs=[whol...  16.1 us
    ppermute x1, waiting for transfers between devices, on_device(): others = [flip('dom', 1)(p) for p in pieces]  12.1 us
    ppermute x3, waiting for transfers between devices, on_device(): flip('feat', i * below)(leaving[i])  7.56 us
    ppermute x1, waiting for transfers between devices, sum_gradients(): neigh_got = flip('feat', 4)(neigh_sent)  5.12 us
    all_to_all x1, waiting for transfers between devices, on_device(): own_mean = lax.all_to_all(means, 'feat', 0, 0, tiled=True)  4.64 us
    ppermute x3, starting transfers between devices, on_device(): near = {i: flip('feat', i * below)(cuts[i]) for i in (3, 2, 1)}  4.39 us
    all_to_all x1, starting transfers between devices, on_device(): own_mean = lax.all_to_all(means, 'feat', 0, 0, tiled=True)  3.98 us
    ppermute x3, starting transfers between devices, on_device(): flip('feat', i * below)(leaving[i])  3.62 us
  transfers between devices with their start and end apart: 25, of which 14 were waited for; matrix products, arithmetic and copies ran while one was open for 0% of the time, Pallas kernels for 9%

profile of v8, /device:TPU:0, one launch (start us, length us, event | category | flops | bytes accessed | tf_op | source)
XLA Modules:
  0.0 100.4 jit_solution(4679828889957231903)
XLA Ops:
  0.6 3.1 %open_exchange.1 = (bf16[64,256]{1,0:T(8,128)(2,1)}, bf16[4,64,1024]{2,1,0:T(8,128)(2,1)}, bf16[1,64,1536]{2,1,0:T(8,128)(2,1)}, bf16[1,64,1536]{2,1,0:T(8,128)(...) custom-call(s32[2,2]{1,0:T(2,128)} %refs_2_.3, bf16[64,8192]{1,0:T(8,128)(2,1)} %bitcast.7, ...), custom_call_target="tpu_custom_call" | custom-call | tf_op jit(solution)/shard_map/open_exchange/pallas_call | solution.py:79
  3.8 3.0 %collective-permute-start = (bf16[4,64,1024]{2,1,0:T(8,128)(2,1)}, bf16[4,64,1024]{2,1,0:T(8,128)(2,1)S(1)}, u32[]{:S(2)}, u32[]{:S(2)}) collective-permute-start(bf16[4,64,1024]{2,1,0:T(8,128)(2,1)} %get-tuple-element.48), channel_id=1, source_target_pairs={{0,4},{2,6},{4,0},{6,2},{8,12},{10,14},{12,8},{14,10},{16,20},{18,... | collective-permute-start | bytes 1572872 | tf_op jit(solution)/shard_map/ppermute | solution.py:464
  6.8 1.6 %collective-permute-start.2 = (bf16[1,64,1536]{2,1,0:T(8,128)(2,1)}, bf16[1,64,1536]{2,1,0:T(8,128)(2,1)S(1)}, u32[]{:S(2)}, u32[]{:S(2)}) collective-permute-start(bf16[1,64,1536]{2,1,0:T(8,128)(2,1)} %get-tuple-element.52), channel_id=1, source_target_pairs={{0,8},{2,10},{4,12},{6,14},{8,0},{10,2},{12,4},{14,6},{16,24},{18,... | collective-permute-start | bytes 589832 | tf_op jit(solution)/shard_map/ppermute | solution.py:465
  8.4 2.6 %collective-permute-start.3 = (bf16[1,64,1536]{2,1,0:T(8,128)(2,1)}, bf16[1,64,1536]{2,1,0:T(8,128)(2,1)S(1)}, u32[]{:S(2)}, u32[]{:S(2)}) collective-permute-start(bf16[1,64,1536]{2,1,0:T(8,128)(2,1)} %get-tuple-element.53), channel_id=1, source_target_pairs={{0,16},{2,18},{4,20},{6,22},{8,24},{10,26},{12,28},{14,30},{16,0},... | collective-permute-start | bytes 589832 | tf_op jit(solution)/shard_map/ppermute | solution.py:465
  10.9 1.5 %collective-permute-start.1 = (bf16[64,256]{1,0:T(8,128)(2,1)}, bf16[64,256]{1,0:T(8,128)(2,1)S(1)}, u32[]{:S(2)}, u32[]{:S(2)}) collective-permute-start(bf16[64,256]{1,0:T(8,128)(2,1)} %get-tuple-element.49), channel_id=1, source_target_pairs={{0,1},{1,0},{2,3},{3,2},{4,5},{5,4},{6,7},{7,6},{8,9},{9,8},{10,11... | collective-permute-start | bytes 98312 | tf_op jit(solution)/shard_map/ppermute | solution.py:468
  12.5 0.2 collective-permute-start.4
  12.7 2.4 %collective-permute-done.1.refs_4_ = bf16[64,256]{1,0:T(8,128)(2,1)S(1)} collective-permute-done((bf16[64,256]{1,0:T(8,128)(2,1)}, bf16[64,256]{1,0:T(8,128)(2,1)S(1)}, u32[]{:S(2)}, u32[]{:S(2)}) %collective-permute-start.1) | collective-permute-done | bytes 32800 | tf_op jit(solution)/shard_map/ppermute | solution.py:468
  15.1 0.6 copy-done.4
  15.7 8.0 %neighbour_means.1 = bf16[16,64,512]{2,1,0:T(8,128)(2,1)} custom-call(s32[8,64]{1,0:T(8,128)} %bitcast.9, s32[8,64]{1,0:T(8,128)} %bitcast.10, s32[2,2]{1,0:T(2,128)} %refs_2_.3, bf16[64,8192]{1,0:T(8,128)(2,1)} %bitcast.8, bf16[64,256]{1,0:T(8,128)(2,1)} %copy-done.4, s32[2,2,256]{2,1,0:T(2,128)} %refs_5_.1, bf16[64,128,128]{2,1,0:T(8,128)(2,1)} %refs_6_.2), custom_call_target="tpu_custom_call" | custom-call | tf_op jit(solution)/shard_map/neighbour_means/pallas_call | solution.py:79
  23.7 0.4 collective-permute-done.3.near_ref.refs_2_
  24.0 0.6 collective-permute-start.8
  24.7 0.2 collective-permute-start.5
  24.9 2.4 %collective-permute-start.7 = (bf16[1,64,1024]{2,1,0:T(8,128)(2,1)S(1)}, bf16[1,64,1024]{2,1,0:T(8,128)(2,1)S(1)}, u32[]{:S(2)}, u32[]{:S(2)}) collective-permute-start(bf16[1,64,1024]{2,1,0:T(8,128)(2,1)S(1)} %get-tuple-element.93), channel_id=1, source_target_pairs={{0,24},{2,26},{4,28},{6,30},{8,16},{10,18},{12,20},{14,22},{16,8},... | collective-permute-start | bytes 393224 | tf_op jit(solution)/shard_map/ppermute | solution.py:476
  27.3 1.0 collective-permute-start.6
  28.3 2.4 %collective-permute-done.5.refs_0_.refs_5_ = bf16[1,64,1536]{2,1,0:T(8,128)(2,1)S(1)} collective-permute-done((bf16[1,64,1536]{2,1,0:T(8,128)(2,1)S(1)}, bf16[1,64,1536]{2,1,0:T(8,128)(2,1)S(1)}, u32[]{:S(2)}, u32[]{:S(2)}) %collective-permute-start.5) | collective-permute-done | bytes 196640 | tf_op jit(solution)/shard_map/ppermute | solution.py:476
  30.7 1.5 %collective-permute-start.9 = (bf16[1,64,512]{2,1,0:T(8,128)(2,1)S(1)}, bf16[1,64,512]{2,1,0:T(8,128)(2,1)S(1)}, u32[]{:S(2)}, u32[]{:S(2)}) collective-permute-start(bf16[1,64,512]{2,1,0:T(8,128)(2,1)S(1)} %weight_pieces.3.refs_1_), channel_id=1, source_target_pairs={{0,4},{2,6},{4,0},{6,2},{8,12},{10,14},{12,8},{14,10},{16,20},{18,... | collective-permute-start | bytes 196616 | tf_op jit(solution)/shard_map/ppermute | solution.py:482
  32.2 1.2 %collective-permute-done.7.refs_7_ = bf16[1,64,1024]{2,1,0:T(8,128)(2,1)S(1)} collective-permute-done((bf16[1,64,1024]{2,1,0:T(8,128)(2,1)S(1)}, bf16[1,64,1024]{2,1,0:T(8,128)(2,1)S(1)}, u32[]{:S(2)}, u32[]{:S(2)}) %collective-permute-start.7) | collective-permute-done | bytes 131104 | tf_op jit(solution)/shard_map/ppermute | solution.py:476
  33.4 4.0 %collective-permute-done.6.refs_6_ = bf16[1,64,1024]{2,1,0:T(8,128)(2,1)S(1)} collective-permute-done((bf16[1,64,1024]{2,1,0:T(8,128)(2,1)S(1)}, bf16[1,64,1024]{2,1,0:T(8,128)(2,1)S(1)}, u32[]{:S(2)}, u32[]{:S(2)}) %collective-permute-start.6) | collective-permute-done | bytes 131104 | tf_op jit(solution)/shard_map/ppermute | solution.py:476
  37.4 4.0 %all-to-all-start = ((bf16[16,64,512]{2,1,0:T(8,128)(2,1)}), bf16[16,64,512]{2,1,0:T(8,128)(2,1)S(1)}, u32[]{:S(2)}, u32[]{:S(2)}) async-start(bf16[16,64,512]{2,1,0:T(8,128)(2,1)} %neighbour_means.1), calls=%async_computation | async-start | bytes 2097152 | tf_op jit(solution)/shard_map/all_to_all | solution.py:485
  41.4 1.6 %collective-permute-start.12 = (bf16[8,64,512]{2,1,0:T(8,128)(2,1)S(1)}, bf16[8,64,512]{2,1,0:T(8,128)(2,1)S(1)}, u32[]{:S(2)}, u32[]{:S(2)}) collective-permute-start(bf16[8,64,512]{2,1,0:T(8,128)(2,1)S(1)} %gathered.1.refs_2_), channel_id=1, source_target_pairs={{0,1},{1,0},{2,3},{3,2},{4,5},{5,4},{6,7},{7,6},{8,9},{9,8},{10,11... | collective-permute-start | bytes 1572872 | tf_op jit(solution)/shard_map/ppermute | solution.py:487
  43.0 0.1 collective-permute-start.11
  43.2 0.4 collective-permute-start.10
  43.6 12.1 %collective-permute-done.12.refs_4_ = bf16[8,64,512]{2,1,0:T(8,128)(2,1)S(1)} collective-permute-done((bf16[8,64,512]{2,1,0:T(8,128)(2,1)S(1)}, bf16[8,64,512]{2,1,0:T(8,128)(2,1)S(1)}, u32[]{:S(2)}, u32[]{:S(2)}) %collective-permute-start.12) | collective-permute-done | bytes 524320 | tf_op jit(solution)/shard_map/ppermute | solution.py:487
  55.7 1.9 %collective-permute-done.13.refs_5_ = bf16[8,64,512]{2,1,0:T(8,128)(2,1)S(1)} collective-permute-done((bf16[8,64,512]{2,1,0:T(8,128)(2,1)S(1)}, bf16[8,64,512]{2,1,0:T(8,128)(2,1)S(1)}, u32[]{:S(2)}, u32[]{:S(2)}) %collective-permute-start.13) | collective-permute-done | bytes 524320 | tf_op jit(solution)/shard_map/ppermute | solution.py:494
  57.6 0.8 own_linear.1
  58.5 1.2 %copy-done = bf16[1536,512]{1,0:T(8,128)(2,1)} copy-done((bf16[1536,512]{1,0:T(8,128)(2,1)}, bf16[1536,512]{1,0:T(8,128)(2,1)S(1)}, u32[]{:S(2)}) %copy-start) | copy-done | bytes 1572888
  59.6 4.6 %all-to-all-done.mean_ref = bf16[16,64,512]{2,1,0:T(8,128)(2,1)S(1)} async-done(((bf16[16,64,512]{2,1,0:T(8,128)(2,1)}), bf16[16,64,512]{2,1,0:T(8,128)(2,1)S(1)}, u32[]{:S(2)}, u32[]{:S(2)}) %all-to-all-start) | async-done | bytes 1048608 | tf_op jit(solution)/shard_map/all_to_all | solution.py:485
  64.3 1.4 %copy-done.1 = bf16[1536,512]{1,0:T(8,128)(2,1)S(1)} copy-done((bf16[1536,512]{1,0:T(8,128)(2,1)S(1)}, bf16[1536,512]{1,0:T(8,128)(2,1)}, u32[]{:S(2)}) %copy-start.1) | copy-done | bytes 1572888
  65.7 2.3 %forward.1 = (bf16[512,512]{1,0:T(8,128)(2,1)}, bf16[512,512]{1,0:T(8,128)(2,1)S(1)}, bf16[8,64,512]{2,1,0:T(8,128)(2,1)S(1)}, f32[8,64,512]{2,1,0:T(8,128)S(1)}) custom-call(bf16[16,64,512]{2,1,0:T(8,128)(2,1)S(1)} %all-to-all-done.mean_ref, bf16[1536,512]{1,0:T(8,128)(2,1)S(1)} %copy-done.1, f32[512,512]{1,0:T(8,128)S(1)} %get-tuple-element.72.base_ref, ...), custom_call_target="tpu_custom_call" | custom-call | tf_op jit(solution)/shard_map/forward/pallas_call | solution.py:79
  68.0 0.7 neighbour_sums.1
  68.7 0.7 collective-permute-start.19
  69.5 1.5 %collective-permute-done.19.got_ref = bf16[8,64,512]{2,1,0:T(8,128)(2,1)S(1)} collective-permute-done((bf16[8,64,512]{2,1,0:T(8,128)(2,1)S(1)}, bf16[8,64,512]{2,1,0:T(8,128)(2,1)S(1)}, u32[]{:S(2)}, u32[]{:S(2)}) %collective-permute-start.19) | collective-permute-done | bytes 524320 | tf_op jit(solution)/shard_map/ppermute | solution.py:519
  71.0 0.1 neigh_first.1
  71.0 3.5 %collective-permute-start.20 = (bf16[2,2,64,512]{3,2,1,0:T(8,128)(2,1)S(1)}, bf16[2,2,64,512]{3,2,1,0:T(8,128)(2,1)S(1)}, u32[]{:S(2)}, u32[]{:S(2)}) collective-permute-start(bf16[2,2,64,512]{3,2,1,0:T(8,128)(2,1)S(1)} %get-tuple-element.86), channel_id=1, source_target_pairs={{0,8},{2,10},{4,12},{6,14},{8,0},{10,2},{12,4},{14,6},{16,24},{18,... | collective-permute-start | bytes 786440 | tf_op jit(solution)/shard_map/ppermute | solution.py:433
  74.5 0.1 own_first.1
  74.6 1.6 %collective-permute-start.15 = (bf16[2,2,64,512]{3,2,1,0:T(8,128)(2,1)S(1)}, bf16[2,2,64,512]{3,2,1,0:T(8,128)(2,1)S(1)}, u32[]{:S(2)}, u32[]{:S(2)}) collective-permute-start(bf16[2,2,64,512]{3,2,1,0:T(8,128)(2,1)S(1)} %get-tuple-element.77), channel_id=1, source_target_pairs={{0,4},{2,6},{4,0},{6,2},{8,12},{10,14},{12,8},{14,10},{16,20},{18,... | collective-permute-start | bytes 786440 | tf_op jit(solution)/shard_map/ppermute | solution.py:429
  76.2 5.1 %collective-permute-done.20.got_ref = bf16[2,2,64,512]{3,2,1,0:T(8,128)(2,1)S(1)} collective-permute-done((bf16[2,2,64,512]{3,2,1,0:T(8,128)(2,1)S(1)}, bf16[2,2,64,512]{3,2,1,0:T(8,128)(2,1)S(1)}, u32[]{:S(2)}, u32[]{:S(2)}) %collective-permute-start.20) | collective-permute-done | bytes 262176 | tf_op jit(solution)/shard_map/ppermute | solution.py:433
  81.4 1.6 %collective-permute-start.21 = (bf16[2,64,512]{2,1,0:T(8,128)(2,1)S(1)}, bf16[2,64,512]{2,1,0:T(8,128)(2,1)S(1)}, u32[]{:S(2)}, u32[]{:S(2)}) collective-permute-start(bf16[2,64,512]{2,1,0:T(8,128)(2,1)S(1)} %get-tuple-element.88), channel_id=1, source_target_pairs={{0,4},{2,6},{4,0},{6,2},{8,12},{10,14},{12,8},{14,10},{16,20},{18,... | collective-permute-start | bytes 393224 | tf_op jit(solution)/shard_map/ppermute | solution.py:437
  83.0 1.8 %collective-permute-start.16 = (bf16[2,64,512]{2,1,0:T(8,128)(2,1)S(1)}, bf16[2,64,512]{2,1,0:T(8,128)(2,1)S(1)}, u32[]{:S(2)}, u32[]{:S(2)}) collective-permute-start(bf16[2,64,512]{2,1,0:T(8,128)(2,1)S(1)} %get-tuple-element.79), channel_id=1, source_target_pairs={{0,8},{2,10},{4,12},{6,14},{8,0},{10,2},{12,4},{14,6},{16,24},{18,... | collective-permute-start | bytes 393224 | tf_op jit(solution)/shard_map/ppermute | solution.py:435
  84.8 1.8 %collective-permute-done.21.got_ref = bf16[2,64,512]{2,1,0:T(8,128)(2,1)S(1)} collective-permute-done((bf16[2,64,512]{2,1,0:T(8,128)(2,1)S(1)}, bf16[2,64,512]{2,1,0:T(8,128)(2,1)S(1)}, u32[]{:S(2)}, u32[]{:S(2)}) %collective-permute-start.21) | collective-permute-done | bytes 131104 | tf_op jit(solution)/shard_map/ppermute | solution.py:437
  86.7 2.8 %collective-permute-start.22 = (bf16[1,64,512]{2,1,0:T(8,128)(2,1)S(1)}, bf16[1,64,512]{2,1,0:T(8,128)(2,1)S(1)}, u32[]{:S(2)}, u32[]{:S(2)}) collective-permute-start(bf16[1,64,512]{2,1,0:T(8,128)(2,1)S(1)} %get-tuple-element.90), channel_id=1, source_target_pairs={{0,16},{2,18},{4,20},{6,22},{8,24},{10,26},{12,28},{14,30},{16,0},... | collective-permute-start | bytes 196616 | tf_op jit(solution)/shard_map/ppermute | solution.py:410
  89.5 0.7 collective-permute-start.17
  90.2 3.5 %collective-permute-done.22.got_ref = bf16[1,64,512]{2,1,0:T(8,128)(2,1)S(1)} collective-permute-done((bf16[1,64,512]{2,1,0:T(8,128)(2,1)S(1)}, bf16[1,64,512]{2,1,0:T(8,128)(2,1)S(1)}, u32[]{:S(2)}, u32[]{:S(2)}) %collective-permute-start.22) | collective-permute-done | bytes 65568 | tf_op jit(solution)/shard_map/ppermute | solution.py:410
  93.8 1.5 %collective-permute-start.23 = (bf16[1,64,512]{2,1,0:T(8,128)(2,1)S(1)}, bf16[1,64,512]{2,1,0:T(8,128)(2,1)S(1)}, u32[]{:S(2)}, u32[]{:S(2)}) collective-permute-start(bf16[1,64,512]{2,1,0:T(8,128)(2,1)S(1)} %rounded_sum.3.refs_2_), channel_id=1, source_target_pairs={{0,1},{1,0},{2,3},{3,2},{4,5},{5,4},{6,7},{7,6},{8,9},{9,8},{10,11... | collective-permute-start | bytes 196616 | tf_op jit(solution)/shard_map/ppermute | solution.py:414
  95.3 1.4 %collective-permute-start.18 = (bf16[1,64,512]{2,1,0:T(8,128)(2,1)S(1)}, bf16[1,64,512]{2,1,0:T(8,128)(2,1)S(1)}, u32[]{:S(2)}, u32[]{:S(2)}) collective-permute-start(bf16[1,64,512]{2,1,0:T(8,128)(2,1)S(1)} %rounded_sum.2.refs_0_), channel_id=1, source_target_pairs={{0,1},{1,0},{2,3},{3,2},{4,5},{5,4},{6,7},{7,6},{8,9},{9,8},{10,11... | collective-permute-start | bytes 196616 | tf_op jit(solution)/shard_map/ppermute | solution.py:414
  96.8 1.3 %collective-permute-done.23.refs_3_ = bf16[1,64,512]{2,1,0:T(8,128)(2,1)S(1)} collective-permute-done((bf16[1,64,512]{2,1,0:T(8,128)(2,1)S(1)}, bf16[1,64,512]{2,1,0:T(8,128)(2,1)S(1)}, u32[]{:S(2)}, u32[]{:S(2)}) %collective-permute-start.23) | collective-permute-done | bytes 65568 | tf_op jit(solution)/shard_map/ppermute | solution.py:414
  98.1 1.6 %collective-permute-done.18.refs_1_ = bf16[1,64,512]{2,1,0:T(8,128)(2,1)S(1)} collective-permute-done((bf16[1,64,512]{2,1,0:T(8,128)(2,1)S(1)}, bf16[1,64,512]{2,1,0:T(8,128)(2,1)S(1)}, u32[]{:S(2)}, u32[]{:S(2)}) %collective-permute-start.18) | collective-permute-done | bytes 65568 | tf_op jit(solution)/shard_map/ppermute | solution.py:414
  99.7 0.7 last_sum.1
  (32 shorter events, 0.5 us)
Async XLA Ops:
  3.8 20.9 %collective-permute-start = (bf16[4,64,1024]{2,1,0:T(8,128)(2,1)}, bf16[4,64,1024]{2,1,0:T(8,128)(2,1)S(1)}, u32[]{:S(2)}, u32[]{:S(2)}) collective-permute-start(bf16[4,64,1024]{2,1,0:T(8,128)(2,1)} %get-tuple-element.48), channel_id=1, source_target_pairs={{0,4},{2,6},{4,0},{6,2},{8,12},{10,14},{12,8},{14,10},{16,20},{18,... | collective-permute-start | bytes 1572872 | tf_op jit(solution)/shard_map/ppermute | solution.py:464
  6.8 16.9 %collective-permute-start.2 = (bf16[1,64,1536]{2,1,0:T(8,128)(2,1)}, bf16[1,64,1536]{2,1,0:T(8,128)(2,1)S(1)}, u32[]{:S(2)}, u32[]{:S(2)}) collective-permute-start(bf16[1,64,1536]{2,1,0:T(8,128)(2,1)} %get-tuple-element.52), channel_id=1, source_target_pairs={{0,8},{2,10},{4,12},{6,14},{8,0},{10,2},{12,4},{14,6},{16,24},{18,... | collective-permute-start | bytes 589832 | tf_op jit(solution)/shard_map/ppermute | solution.py:465
  8.4 15.7 %collective-permute-start.3 = (bf16[1,64,1536]{2,1,0:T(8,128)(2,1)}, bf16[1,64,1536]{2,1,0:T(8,128)(2,1)S(1)}, u32[]{:S(2)}, u32[]{:S(2)}) collective-permute-start(bf16[1,64,1536]{2,1,0:T(8,128)(2,1)} %get-tuple-element.53), channel_id=1, source_target_pairs={{0,16},{2,18},{4,20},{6,22},{8,24},{10,26},{12,28},{14,30},{16,0},... | collective-permute-start | bytes 589832 | tf_op jit(solution)/shard_map/ppermute | solution.py:465
  10.9 4.1 %collective-permute-start.1 = (bf16[64,256]{1,0:T(8,128)(2,1)}, bf16[64,256]{1,0:T(8,128)(2,1)S(1)}, u32[]{:S(2)}, u32[]{:S(2)}) collective-permute-start(bf16[64,256]{1,0:T(8,128)(2,1)} %get-tuple-element.49), channel_id=1, source_target_pairs={{0,1},{1,0},{2,3},{3,2},{4,5},{5,4},{6,7},{7,6},{8,9},{9,8},{10,11... | collective-permute-start | bytes 98312 | tf_op jit(solution)/shard_map/ppermute | solution.py:468
  12.5 19.7 %collective-permute-start.4 = (bf16[1,64,1024]{2,1,0:T(8,128)(2,1)}, bf16[1,64,1024]{2,1,0:T(8,128)(2,1)S(1)}, u32[]{:S(2)}, u32[]{:S(2)}) collective-permute-start(bf16[1,64,1024]{2,1,0:T(8,128)(2,1)} %get-tuple-element.54), channel_id=1, source_target_pairs={{0,24},{2,26},{4,28},{6,30},{8,16},{10,18},{12,20},{14,22},{16,8},... | collective-permute-start | bytes 393224 | tf_op jit(solution)/shard_map/ppermute | solution.py:465
  15.1 0.6 copy-start.4
  15.7 8.3 %copy-start.2 = (bf16[1,64,1536]{2,1,0:T(8,128)(2,1)S(1)}, bf16[1,64,1536]{2,1,0:T(8,128)(2,1)}, u32[]{:S(2)}) copy-start(bf16[1,64,1536]{2,1,0:T(8,128)(2,1)} %get-tuple-element.57.refs_0_) | copy-start | bytes 589828
  24.0 8.2 %collective-permute-start.8 = (bf16[3,64,512]{2,1,0:T(8,128)(2,1)S(1)}, bf16[3,64,512]{2,1,0:T(8,128)(2,1)S(1)}, u32[]{:S(2)}, u32[]{:S(2)}) collective-permute-start(bf16[3,64,512]{2,1,0:T(8,128)(2,1)S(1)} %weight_pieces.2.refs_0_), channel_id=1, source_target_pairs={{0,4},{2,6},{4,0},{6,2},{8,12},{10,14},{12,8},{14,10},{16,20},{18,... | collective-permute-start | bytes 589832 | tf_op jit(solution)/shard_map/ppermute | solution.py:482
  24.7 6.1 %collective-permute-start.5 = (bf16[1,64,1536]{2,1,0:T(8,128)(2,1)S(1)}, bf16[1,64,1536]{2,1,0:T(8,128)(2,1)S(1)}, u32[]{:S(2)}, u32[]{:S(2)}) collective-permute-start(bf16[1,64,1536]{2,1,0:T(8,128)(2,1)S(1)} %relayed.1), channel_id=1, source_target_pairs={{0,8},{2,10},{4,12},{6,14},{8,0},{10,2},{12,4},{14,6},{16,24},{18,... | collective-permute-start | bytes 589832 | tf_op jit(solution)/shard_map/ppermute | solution.py:476
  24.9 8.5 %collective-permute-start.7 = (bf16[1,64,1024]{2,1,0:T(8,128)(2,1)S(1)}, bf16[1,64,1024]{2,1,0:T(8,128)(2,1)S(1)}, u32[]{:S(2)}, u32[]{:S(2)}) collective-permute-start(bf16[1,64,1024]{2,1,0:T(8,128)(2,1)S(1)} %get-tuple-element.93), channel_id=1, source_target_pairs={{0,24},{2,26},{4,28},{6,30},{8,16},{10,18},{12,20},{14,22},{16,8},... | collective-permute-start | bytes 393224 | tf_op jit(solution)/shard_map/ppermute | solution.py:476
  27.3 10.0 %collective-permute-start.6 = (bf16[1,64,1024]{2,1,0:T(8,128)(2,1)S(1)}, bf16[1,64,1024]{2,1,0:T(8,128)(2,1)S(1)}, u32[]{:S(2)}, u32[]{:S(2)}) collective-permute-start(bf16[1,64,1024]{2,1,0:T(8,128)(2,1)S(1)} %get-tuple-element.94), channel_id=1, source_target_pairs={{0,16},{2,18},{4,20},{6,22},{8,24},{10,26},{12,28},{14,30},{16,0},... | collective-permute-start | bytes 393224 | tf_op jit(solution)/shard_map/ppermute | solution.py:476
  30.7 6.6 %collective-permute-start.9 = (bf16[1,64,512]{2,1,0:T(8,128)(2,1)S(1)}, bf16[1,64,512]{2,1,0:T(8,128)(2,1)S(1)}, u32[]{:S(2)}, u32[]{:S(2)}) collective-permute-start(bf16[1,64,512]{2,1,0:T(8,128)(2,1)S(1)} %weight_pieces.3.refs_1_), channel_id=1, source_target_pairs={{0,4},{2,6},{4,0},{6,2},{8,12},{10,14},{12,8},{14,10},{16,20},{18,... | collective-permute-start | bytes 196616 | tf_op jit(solution)/shard_map/ppermute | solution.py:482
  37.4 26.9 %all-to-all-start = ((bf16[16,64,512]{2,1,0:T(8,128)(2,1)}), bf16[16,64,512]{2,1,0:T(8,128)(2,1)S(1)}, u32[]{:S(2)}, u32[]{:S(2)}) async-start(bf16[16,64,512]{2,1,0:T(8,128)(2,1)} %neighbour_means.1), calls=%async_computation | async-start | bytes 2097152 | tf_op jit(solution)/shard_map/all_to_all | solution.py:485
  41.4 16.3 %copy-start.3 = (bf16[512,512]{1,0:T(8,128)(2,1)S(1)}, bf16[512,512]{1,0:T(8,128)(2,1)}, u32[]{:S(2)}) copy-start(bf16[512,512]{1,0:T(8,128)(2,1)} %refs_6_.3) | copy-start | bytes 1572868
  41.4 14.3 %collective-permute-start.12 = (bf16[8,64,512]{2,1,0:T(8,128)(2,1)S(1)}, bf16[8,64,512]{2,1,0:T(8,128)(2,1)S(1)}, u32[]{:S(2)}, u32[]{:S(2)}) collective-permute-start(bf16[8,64,512]{2,1,0:T(8,128)(2,1)S(1)} %gathered.1.refs_2_), channel_id=1, source_target_pairs={{0,1},{1,0},{2,3},{3,2},{4,5},{5,4},{6,7},{7,6},{8,9},{9,8},{10,11... | collective-permute-start | bytes 1572872 | tf_op jit(solution)/shard_map/ppermute | solution.py:487
  43.0 12.8 %collective-permute-start.11 = (bf16[8,64,512]{2,1,0:T(8,128)(2,1)S(1)}, bf16[8,64,512]{2,1,0:T(8,128)(2,1)S(1)}, u32[]{:S(2)}, u32[]{:S(2)}) collective-permute-start(bf16[8,64,512]{2,1,0:T(8,128)(2,1)S(1)} %gathered.1.refs_2_), channel_id=1, source_target_pairs={{0,2},{2,0},{4,6},{6,4},{8,10},{10,8},{12,14},{14,12},{16,18},{18,... | collective-permute-start | bytes 1572872 | tf_op jit(solution)/shard_map/ppermute | solution.py:493
  43.2 12.6 %collective-permute-start.10 = (bf16[8,64,512]{2,1,0:T(8,128)(2,1)S(1)}, bf16[8,64,512]{2,1,0:T(8,128)(2,1)S(1)}, u32[]{:S(2)}, u32[]{:S(2)}) collective-permute-start(bf16[8,64,512]{2,1,0:T(8,128)(2,1)S(1)} %get-tuple-element.66), channel_id=1, source_target_pairs={{0,2},{2,0},{4,6},{6,4},{8,10},{10,8},{12,14},{14,12},{16,18},{18,... | collective-permute-start | bytes 1572872 | tf_op jit(solution)/shard_map/ppermute | solution.py:491
  55.7 1.9 %collective-permute-start.13 = (bf16[8,64,512]{2,1,0:T(8,128)(2,1)S(1)}, bf16[8,64,512]{2,1,0:T(8,128)(2,1)S(1)}, u32[]{:S(2)}, u32[]{:S(2)}) collective-permute-start(bf16[8,64,512]{2,1,0:T(8,128)(2,1)S(1)} %collective-permute-done.12.refs_4_), channel_id=1, source_target_pairs={{0,2},{2,0},{4,6},{6,4},{8,10},{10,8},{12,14},{14,12},{16,18},{18,... | collective-permute-start | bytes 1572872 | tf_op jit(solution)/shard_map/ppermute | solution.py:494
  58.5 1.2 %copy-start = (bf16[1536,512]{1,0:T(8,128)(2,1)}, bf16[1536,512]{1,0:T(8,128)(2,1)S(1)}, u32[]{:S(2)}) copy-start(bf16[1536,512]{1,0:T(8,128)(2,1)S(1)} %get-tuple-element.71.beside_ref) | copy-start | bytes 4718596
  64.3 1.4 %copy-start.1 = (bf16[1536,512]{1,0:T(8,128)(2,1)S(1)}, bf16[1536,512]{1,0:T(8,128)(2,1)}, u32[]{:S(2)}) copy-start(bf16[1536,512]{1,0:T(8,128)(2,1)} %copy-done) | copy-start | bytes 4718596
  68.7 2.2 %collective-permute-start.19 = (bf16[8,64,512]{2,1,0:T(8,128)(2,1)S(1)}, bf16[8,64,512]{2,1,0:T(8,128)(2,1)S(1)}, u32[]{:S(2)}, u32[]{:S(2)}) collective-permute-start(bf16[8,64,512]{2,1,0:T(8,128)(2,1)S(1)} %get-tuple-element.84), channel_id=1, source_target_pairs={{0,2},{2,0},{4,6},{6,4},{8,10},{10,8},{12,14},{14,12},{16,18},{18,... | collective-permute-start | bytes 1572872 | tf_op jit(solution)/shard_map/ppermute | solution.py:519
  69.4 5.1 %collective-permute-start.14 = (bf16[8,64,512]{2,1,0:T(8,128)(2,1)S(1)}, bf16[8,64,512]{2,1,0:T(8,128)(2,1)S(1)}, u32[]{:S(2)}, u32[]{:S(2)}) collective-permute-start(bf16[8,64,512]{2,1,0:T(8,128)(2,1)S(1)} %get-tuple-element.75), channel_id=1, source_target_pairs={{0,2},{2,0},{4,6},{6,4},{8,10},{10,8},{12,14},{14,12},{16,18},{18,... | collective-permute-start | bytes 1572872 | tf_op jit(solution)/shard_map/ppermute | solution.py:515
  71.0 10.3 %collective-permute-start.20 = (bf16[2,2,64,512]{3,2,1,0:T(8,128)(2,1)S(1)}, bf16[2,2,64,512]{3,2,1,0:T(8,128)(2,1)S(1)}, u32[]{:S(2)}, u32[]{:S(2)}) collective-permute-start(bf16[2,2,64,512]{3,2,1,0:T(8,128)(2,1)S(1)} %get-tuple-element.86), channel_id=1, source_target_pairs={{0,8},{2,10},{4,12},{6,14},{8,0},{10,2},{12,4},{14,6},{16,24},{18,... | collective-permute-start | bytes 786440 | tf_op jit(solution)/shard_map/ppermute | solution.py:433
  74.6 8.4 %collective-permute-start.15 = (bf16[2,2,64,512]{3,2,1,0:T(8,128)(2,1)S(1)}, bf16[2,2,64,512]{3,2,1,0:T(8,128)(2,1)S(1)}, u32[]{:S(2)}, u32[]{:S(2)}) collective-permute-start(bf16[2,2,64,512]{3,2,1,0:T(8,128)(2,1)S(1)} %get-tuple-element.77), channel_id=1, source_target_pairs={{0,4},{2,6},{4,0},{6,2},{8,12},{10,14},{12,8},{14,10},{16,20},{18,... | collective-permute-start | bytes 786440 | tf_op jit(solution)/shard_map/ppermute | solution.py:429
  81.4 5.3 %collective-permute-start.21 = (bf16[2,64,512]{2,1,0:T(8,128)(2,1)S(1)}, bf16[2,64,512]{2,1,0:T(8,128)(2,1)S(1)}, u32[]{:S(2)}, u32[]{:S(2)}) collective-permute-start(bf16[2,64,512]{2,1,0:T(8,128)(2,1)S(1)} %get-tuple-element.88), channel_id=1, source_target_pairs={{0,4},{2,6},{4,0},{6,2},{8,12},{10,14},{12,8},{14,10},{16,20},{18,... | collective-permute-start | bytes 393224 | tf_op jit(solution)/shard_map/ppermute | solution.py:437
  83.0 6.5 %collective-permute-start.16 = (bf16[2,64,512]{2,1,0:T(8,128)(2,1)S(1)}, bf16[2,64,512]{2,1,0:T(8,128)(2,1)S(1)}, u32[]{:S(2)}, u32[]{:S(2)}) collective-permute-start(bf16[2,64,512]{2,1,0:T(8,128)(2,1)S(1)} %get-tuple-element.79), channel_id=1, source_target_pairs={{0,8},{2,10},{4,12},{6,14},{8,0},{10,2},{12,4},{14,6},{16,24},{18,... | collective-permute-start | bytes 393224 | tf_op jit(solution)/shard_map/ppermute | solution.py:435
  86.7 7.1 %collective-permute-start.22 = (bf16[1,64,512]{2,1,0:T(8,128)(2,1)S(1)}, bf16[1,64,512]{2,1,0:T(8,128)(2,1)S(1)}, u32[]{:S(2)}, u32[]{:S(2)}) collective-permute-start(bf16[1,64,512]{2,1,0:T(8,128)(2,1)S(1)} %get-tuple-element.90), channel_id=1, source_target_pairs={{0,16},{2,18},{4,20},{6,22},{8,24},{10,26},{12,28},{14,30},{16,0},... | collective-permute-start | bytes 196616 | tf_op jit(solution)/shard_map/ppermute | solution.py:410
  89.5 5.8 %collective-permute-start.17 = (bf16[1,64,512]{2,1,0:T(8,128)(2,1)S(1)}, bf16[1,64,512]{2,1,0:T(8,128)(2,1)S(1)}, u32[]{:S(2)}, u32[]{:S(2)}) collective-permute-start(bf16[1,64,512]{2,1,0:T(8,128)(2,1)S(1)} %get-tuple-element.81), channel_id=1, source_target_pairs={{0,16},{2,18},{4,20},{6,22},{8,24},{10,26},{12,28},{14,30},{16,0},... | collective-permute-start | bytes 196616 | tf_op jit(solution)/shard_map/ppermute | solution.py:410
  93.8 4.3 %collective-permute-start.23 = (bf16[1,64,512]{2,1,0:T(8,128)(2,1)S(1)}, bf16[1,64,512]{2,1,0:T(8,128)(2,1)S(1)}, u32[]{:S(2)}, u32[]{:S(2)}) collective-permute-start(bf16[1,64,512]{2,1,0:T(8,128)(2,1)S(1)} %rounded_sum.3.refs_2_), channel_id=1, source_target_pairs={{0,1},{1,0},{2,3},{3,2},{4,5},{5,4},{6,7},{7,6},{8,9},{9,8},{10,11... | collective-permute-start | bytes 196616 | tf_op jit(solution)/shard_map/ppermute | solution.py:414
  95.3 4.3 %collective-permute-start.18 = (bf16[1,64,512]{2,1,0:T(8,128)(2,1)S(1)}, bf16[1,64,512]{2,1,0:T(8,128)(2,1)S(1)}, u32[]{:S(2)}, u32[]{:S(2)}) collective-permute-start(bf16[1,64,512]{2,1,0:T(8,128)(2,1)S(1)} %rounded_sum.2.refs_0_), channel_id=1, source_target_pairs={{0,1},{1,0},{2,3},{3,2},{4,5},{5,4},{6,7},{7,6},{8,9},{9,8},{10,11... | collective-permute-start | bytes 196616 | tf_op jit(solution)/shard_map/ppermute | solution.py:414

commit v9 on v8

--- a/solution.py
+++ b/solution.py
@@ -336,7 +336,7 @@
 
 def forward_kernel(
     row_masks, masks, mean_ref, beside_ref, base_ref, kept_ref, got_ref,
-    hidden_ref, grad_ref, other_sums_ref, my_sums_ref, linear_ref,
+    hidden_ref, other_own_ref, my_own_ref, other_neigh_ref, my_neigh_ref, linear_ref, grad_ref,
 ):
     features, means = features_in_order(row_masks, kept_ref, got_ref), means_in_order(mean_ref)
     rows = linear_ref.shape[0]
@@ -348,14 +348,10 @@
         hidden_ref[at : at + step] = value.astype(bf16)
         cot = beside_ref[depth + at : depth + at + step].astype(f32)
         grad_ref[at : at + step] = (cot * slope).astype(bf16)
-    fill_sums(1, features, grad_ref, other_sums_ref)
-    fill_sums(0, features, grad_ref, my_sums_ref)
-
-
-def neighbour_sums_kernel(mean_ref, grad_ref, other_sums_ref, my_sums_ref):
-    means = means_in_order(mean_ref)
-    fill_sums(1, means, grad_ref, other_sums_ref)
-    fill_sums(0, means, grad_ref, my_sums_ref)
+    fill_sums(1, features, grad_ref, other_own_ref)
+    fill_sums(1, means, grad_ref, other_neigh_ref)
+    fill_sums(0, features, grad_ref, my_own_ref)
+    fill_sums(0, means, grad_ref, my_neigh_ref)
 
 
 def fill_sums(core, source, grad_ref, sums_ref):
@@ -505,18 +501,14 @@
     square = jax.ShapeDtypeStruct((rows, hid), bf16)
     sums = (feat // 2, depth, hid)
     sums = [jax.ShapeDtypeStruct(sums, bf16), jax.ShapeDtypeStruct(sums, f32)]
-    hidden, grad_linear, own_sent, own_kept = local_call(
+    hidden, own_sent, own_kept, neigh_sent, neigh_kept = local_call(
         functools.partial(forward_kernel, row_masks, sum(weight_masks, [])),
         "forward",
-        [square, square, *sums],
+        [square, *sums, *sums],
         (own_mean, beside, linear, *parts),
-        scratch=[pltpu.VMEM((rows, hid), f32)],
-    )
-    own_got = flip("feat", 1)(own_sent)
-    neigh_sent, neigh_kept = local_call(
-        neighbour_sums_kernel, "neighbour_sums", sums, (own_mean, grad_linear)
-    )
-    neigh_got = flip("feat", 1)(neigh_sent)
+        scratch=[pltpu.VMEM((rows, hid), f32), pltpu.VMEM((rows, hid), bf16)],
+    )
+    own_got, neigh_got = flip("feat", 1)(own_sent), flip("feat", 1)(neigh_sent)
     grad_self, grad_neighbour = sum_gradients(own_kept, own_got, neigh_kept, neigh_got)
     return (hidden, grad_self, grad_neighbour)
 

time: 101 us -> 100 us (0.990)
  starting transfers between devices: 36.4 us -> 37.9 us
  waiting for transfers between devices: 43.8 us -> 42.3 us
    ppermute x1, waiting for transfers between devices: 5.12 us -> 0.01 us  [sum_gradients(): neigh_got = flip('feat', 4)(neigh_sent)]
    ppermute x1, waiting for transfers between devices: 0.01 us -> 3.71 us  [sum_gradients(): own_got = flip('feat', 2)(own_sent)]
    ppermute x1, waiting for transfers between devices: 1.85 us -> 0.01 us  [sum_gradients(): neigh_got = flip('feat', 2)(neigh_sent)]
    ppermute x1, waiting for transfers between devices: 0.01 us -> 1.6 us  [sum_gradients(): own_got = flip('feat', 4)(own_sent)]
    ppermute x1, starting transfers between devices: 1.8 us -> 3.2 us  [sum_gradients(): own_got = flip('feat', 4)(own_sent)]
    pallas_call x19 -> x18, Pallas kernels: 16.1 us -> 15.8 us  [local_call(): pl.pallas_call(kernel, out_shape=outs, in_specs=in_specs, out_specs=[whol...]
where the time goes in v9:
time: 100 us
  waiting for transfers between devices  42.3 us (42%)
  starting transfers between devices  37.9 us (38%)
  Pallas kernels  15.8 us (16%)
  local copies, waits for them, and re-layouts  3.23 us (3%)
    pallas_call x18, Pallas kernels, local_call(): pl.pallas_call(kernel, out_shape=outs, in_specs=in_specs, out_specs=[whol...  15.8 us
    ppermute x1, waiting for transfers between devices, on_device(): others = [flip('dom', 1)(p) for p in pieces]  12.1 us
    ppermute x3, waiting for transfers between devices, on_device(): flip('feat', i * below)(leaving[i])  7.53 us
    all_to_all x1, waiting for transfers between devices, on_device(): own_mean = lax.all_to_all(means, 'feat', 0, 0, tiled=True)  4.64 us
    ppermute x3, starting transfers between devices, on_device(): near = {i: flip('feat', i * below)(cuts[i]) for i in (3, 2, 1)}  4.39 us
    all_to_all x1, starting transfers between devices, on_device(): own_mean = lax.all_to_all(means, 'feat', 0, 0, tiled=True)  3.98 us
    ppermute x2, starting transfers between devices, finish_sum(): got = flip('feat', count * 8)(sent)  3.76 us
    ppermute x1, waiting for transfers between devices, sum_gradients(): own_got = flip('feat', 2)(own_sent)  3.71 us
  transfers between devices with their start and end apart: 25, of which 14 were waited for; matrix products, arithmetic and copies ran while one was open for 0% of the time, Pallas kernels for 9%

profile of v9, /device:TPU:0, one launch (start us, length us, event | category | flops | bytes accessed | tf_op | source)
XLA Modules:
  0.0 100.0 jit_solution(11213784299914427115)
XLA Ops:
  0.6 3.1 %open_exchange.1 = (bf16[64,256]{1,0:T(8,128)(2,1)}, bf16[4,64,1024]{2,1,0:T(8,128)(2,1)}, bf16[1,64,1536]{2,1,0:T(8,128)(2,1)}, bf16[1,64,1536]{2,1,0:T(8,128)(...) custom-call(s32[2,2]{1,0:T(2,128)} %refs_2_.3, bf16[64,8192]{1,0:T(8,128)(2,1)} %bitcast.7, ...), custom_call_target="tpu_custom_call" | custom-call | tf_op jit(solution)/shard_map/open_exchange/pallas_call | solution.py:79
  3.8 3.0 %collective-permute-start = (bf16[4,64,1024]{2,1,0:T(8,128)(2,1)}, bf16[4,64,1024]{2,1,0:T(8,128)(2,1)S(1)}, u32[]{:S(2)}, u32[]{:S(2)}) collective-permute-start(bf16[4,64,1024]{2,1,0:T(8,128)(2,1)} %get-tuple-element.47), channel_id=1, source_target_pairs={{0,4},{2,6},{4,0},{6,2},{8,12},{10,14},{12,8},{14,10},{16,20},{18,... | collective-permute-start | bytes 1572872 | tf_op jit(solution)/shard_map/ppermute | solution.py:460
  6.8 1.6 %collective-permute-start.2 = (bf16[1,64,1536]{2,1,0:T(8,128)(2,1)}, bf16[1,64,1536]{2,1,0:T(8,128)(2,1)S(1)}, u32[]{:S(2)}, u32[]{:S(2)}) collective-permute-start(bf16[1,64,1536]{2,1,0:T(8,128)(2,1)} %get-tuple-element.51), channel_id=1, source_target_pairs={{0,8},{2,10},{4,12},{6,14},{8,0},{10,2},{12,4},{14,6},{16,24},{18,... | collective-permute-start | bytes 589832 | tf_op jit(solution)/shard_map/ppermute | solution.py:461
  8.4 2.6 %collective-permute-start.3 = (bf16[1,64,1536]{2,1,0:T(8,128)(2,1)}, bf16[1,64,1536]{2,1,0:T(8,128)(2,1)S(1)}, u32[]{:S(2)}, u32[]{:S(2)}) collective-permute-start(bf16[1,64,1536]{2,1,0:T(8,128)(2,1)} %get-tuple-element.52), channel_id=1, source_target_pairs={{0,16},{2,18},{4,20},{6,22},{8,24},{10,26},{12,28},{14,30},{16,0},... | collective-permute-start | bytes 589832 | tf_op jit(solution)/shard_map/ppermute | solution.py:461
  10.9 1.5 %collective-permute-start.1 = (bf16[64,256]{1,0:T(8,128)(2,1)}, bf16[64,256]{1,0:T(8,128)(2,1)S(1)}, u32[]{:S(2)}, u32[]{:S(2)}) collective-permute-start(bf16[64,256]{1,0:T(8,128)(2,1)} %get-tuple-element.48), channel_id=1, source_target_pairs={{0,1},{1,0},{2,3},{3,2},{4,5},{5,4},{6,7},{7,6},{8,9},{9,8},{10,11... | collective-permute-start | bytes 98312 | tf_op jit(solution)/shard_map/ppermute | solution.py:464
  12.5 0.2 collective-permute-start.4
  12.7 2.4 %collective-permute-done.1.refs_4_ = bf16[64,256]{1,0:T(8,128)(2,1)S(1)} collective-permute-done((bf16[64,256]{1,0:T(8,128)(2,1)}, bf16[64,256]{1,0:T(8,128)(2,1)S(1)}, u32[]{:S(2)}, u32[]{:S(2)}) %collective-permute-start.1) | collective-permute-done | bytes 32800 | tf_op jit(solution)/shard_map/ppermute | solution.py:464
  15.1 0.6 copy-done.4
  15.7 8.0 %neighbour_means.1 = bf16[16,64,512]{2,1,0:T(8,128)(2,1)} custom-call(s32[8,64]{1,0:T(8,128)} %bitcast.9, s32[8,64]{1,0:T(8,128)} %bitcast.10, s32[2,2]{1,0:T(2,128)} %refs_2_.3, bf16[64,8192]{1,0:T(8,128)(2,1)} %bitcast.8, bf16[64,256]{1,0:T(8,128)(2,1)} %copy-done.4, s32[2,2,256]{2,1,0:T(2,128)} %refs_5_.1, bf16[64,128,128]{2,1,0:T(8,128)(2,1)} %refs_6_.2), custom_call_target="tpu_custom_call" | custom-call | tf_op jit(solution)/shard_map/neighbour_means/pallas_call | solution.py:79
  23.7 0.4 collective-permute-done.3.near_ref.refs_2_
  24.0 0.6 collective-permute-start.8
  24.7 0.2 collective-permute-start.5
  24.9 2.4 %collective-permute-start.7 = (bf16[1,64,1024]{2,1,0:T(8,128)(2,1)S(1)}, bf16[1,64,1024]{2,1,0:T(8,128)(2,1)S(1)}, u32[]{:S(2)}, u32[]{:S(2)}) collective-permute-start(bf16[1,64,1024]{2,1,0:T(8,128)(2,1)S(1)} %get-tuple-element.91), channel_id=1, source_target_pairs={{0,24},{2,26},{4,28},{6,30},{8,16},{10,18},{12,20},{14,22},{16,8},... | collective-permute-start | bytes 393224 | tf_op jit(solution)/shard_map/ppermute | solution.py:472
  27.3 1.0 collective-permute-start.6
  28.3 2.4 %collective-permute-done.5.refs_0_.refs_5_ = bf16[1,64,1536]{2,1,0:T(8,128)(2,1)S(1)} collective-permute-done((bf16[1,64,1536]{2,1,0:T(8,128)(2,1)S(1)}, bf16[1,64,1536]{2,1,0:T(8,128)(2,1)S(1)}, u32[]{:S(2)}, u32[]{:S(2)}) %collective-permute-start.5) | collective-permute-done | bytes 196640 | tf_op jit(solution)/shard_map/ppermute | solution.py:472
  30.7 1.5 %collective-permute-start.9 = (bf16[1,64,512]{2,1,0:T(8,128)(2,1)S(1)}, bf16[1,64,512]{2,1,0:T(8,128)(2,1)S(1)}, u32[]{:S(2)}, u32[]{:S(2)}) collective-permute-start(bf16[1,64,512]{2,1,0:T(8,128)(2,1)S(1)} %weight_pieces.3.refs_1_), channel_id=1, source_target_pairs={{0,4},{2,6},{4,0},{6,2},{8,12},{10,14},{12,8},{14,10},{16,20},{18,... | collective-permute-start | bytes 196616 | tf_op jit(solution)/shard_map/ppermute | solution.py:478
  32.2 1.1 %collective-permute-done.7.refs_7_ = bf16[1,64,1024]{2,1,0:T(8,128)(2,1)S(1)} collective-permute-done((bf16[1,64,1024]{2,1,0:T(8,128)(2,1)S(1)}, bf16[1,64,1024]{2,1,0:T(8,128)(2,1)S(1)}, u32[]{:S(2)}, u32[]{:S(2)}) %collective-permute-start.7) | collective-permute-done | bytes 131104 | tf_op jit(solution)/shard_map/ppermute | solution.py:472
  33.4 4.0 %collective-permute-done.6.refs_6_ = bf16[1,64,1024]{2,1,0:T(8,128)(2,1)S(1)} collective-permute-done((bf16[1,64,1024]{2,1,0:T(8,128)(2,1)S(1)}, bf16[1,64,1024]{2,1,0:T(8,128)(2,1)S(1)}, u32[]{:S(2)}, u32[]{:S(2)}) %collective-permute-start.6) | collective-permute-done | bytes 131104 | tf_op jit(solution)/shard_map/ppermute | solution.py:472
  37.4 4.0 %all-to-all-start = ((bf16[16,64,512]{2,1,0:T(8,128)(2,1)}), bf16[16,64,512]{2,1,0:T(8,128)(2,1)S(1)}, u32[]{:S(2)}, u32[]{:S(2)}) async-start(bf16[16,64,512]{2,1,0:T(8,128)(2,1)} %neighbour_means.1), calls=%async_computation | async-start | bytes 2097152 | tf_op jit(solution)/shard_map/all_to_all | solution.py:481
  41.4 1.6 %collective-permute-start.12 = (bf16[8,64,512]{2,1,0:T(8,128)(2,1)S(1)}, bf16[8,64,512]{2,1,0:T(8,128)(2,1)S(1)}, u32[]{:S(2)}, u32[]{:S(2)}) collective-permute-start(bf16[8,64,512]{2,1,0:T(8,128)(2,1)S(1)} %gathered.1.refs_2_), channel_id=1, source_target_pairs={{0,1},{1,0},{2,3},{3,2},{4,5},{5,4},{6,7},{7,6},{8,9},{9,8},{10,11... | collective-permute-start | bytes 1572872 | tf_op jit(solution)/shard_map/ppermute | solution.py:483
  43.0 0.1 collective-permute-start.11
  43.1 0.1 cut_rows.1
  43.2 0.4 collective-permute-start.10
  43.6 12.1 %collective-permute-done.12.refs_4_ = bf16[8,64,512]{2,1,0:T(8,128)(2,1)S(1)} collective-permute-done((bf16[8,64,512]{2,1,0:T(8,128)(2,1)S(1)}, bf16[8,64,512]{2,1,0:T(8,128)(2,1)S(1)}, u32[]{:S(2)}, u32[]{:S(2)}) %collective-permute-start.12) | collective-permute-done | bytes 524320 | tf_op jit(solution)/shard_map/ppermute | solution.py:483
  55.7 1.9 %collective-permute-done.13.refs_5_ = bf16[8,64,512]{2,1,0:T(8,128)(2,1)S(1)} collective-permute-done((bf16[8,64,512]{2,1,0:T(8,128)(2,1)S(1)}, bf16[8,64,512]{2,1,0:T(8,128)(2,1)S(1)}, u32[]{:S(2)}, u32[]{:S(2)}) %collective-permute-start.13) | collective-permute-done | bytes 524320 | tf_op jit(solution)/shard_map/ppermute | solution.py:490
  57.6 0.8 own_linear.1
  58.5 1.2 %copy-done = bf16[1536,512]{1,0:T(8,128)(2,1)} copy-done((bf16[1536,512]{1,0:T(8,128)(2,1)}, bf16[1536,512]{1,0:T(8,128)(2,1)S(1)}, u32[]{:S(2)}) %copy-start) | copy-done | bytes 1572888
  59.6 4.6 %all-to-all-done.mean_ref = bf16[16,64,512]{2,1,0:T(8,128)(2,1)S(1)} async-done(((bf16[16,64,512]{2,1,0:T(8,128)(2,1)}), bf16[16,64,512]{2,1,0:T(8,128)(2,1)S(1)}, u32[]{:S(2)}, u32[]{:S(2)}) %all-to-all-start) | async-done | bytes 1048608 | tf_op jit(solution)/shard_map/all_to_all | solution.py:481
  64.3 1.4 %copy-done.1 = bf16[1536,512]{1,0:T(8,128)(2,1)S(1)} copy-done((bf16[1536,512]{1,0:T(8,128)(2,1)S(1)}, bf16[1536,512]{1,0:T(8,128)(2,1)}, u32[]{:S(2)}) %copy-start.1) | copy-done | bytes 1572888
  65.7 2.7 %forward.1 = (bf16[512,512]{1,0:T(8,128)(2,1)}, bf16[8,64,512]{2,1,0:T(8,128)(2,1)S(1)}, f32[8,64,512]{2,1,0:T(8,128)S(1)}, bf16[8,64,512]{2,1,0:T(8,128)(2,1)S(1)}, f32[8,64,512]{2,1,0:T(8,128)S(1)}) custom-call(bf16[16,64,512]{2,1,0:T(8,128)(2,1)S(1)} %all-to-all-done.mean_ref, bf16[1536,512]{1,0:T(8,128)(2,1)S(1)} %copy-done.1, ...), custom_call_target="tpu_custom_call" | custom-call | tf_op jit(solution)/shard_map/forward/pallas_call | solution.py:79
  68.4 0.6 collective-permute-start.14
  69.0 1.5 %collective-permute-done.14.got_ref = bf16[8,64,512]{2,1,0:T(8,128)(2,1)S(1)} collective-permute-done((bf16[8,64,512]{2,1,0:T(8,128)(2,1)S(1)}, bf16[8,64,512]{2,1,0:T(8,128)(2,1)S(1)}, u32[]{:S(2)}, u32[]{:S(2)}) %collective-permute-start.14) | collective-permute-done | bytes 524320 | tf_op jit(solution)/shard_map/ppermute | solution.py:511
  70.5 0.1 own_first.1
  70.6 2.1 %collective-permute-start.15 = (bf16[2,2,64,512]{3,2,1,0:T(8,128)(2,1)S(1)}, bf16[2,2,64,512]{3,2,1,0:T(8,128)(2,1)S(1)}, u32[]{:S(2)}, u32[]{:S(2)}) collective-permute-start(bf16[2,2,64,512]{3,2,1,0:T(8,128)(2,1)S(1)} %get-tuple-element.76), channel_id=1, source_target_pairs={{0,4},{2,6},{4,0},{6,2},{8,12},{10,14},{12,8},{14,10},{16,20},{18,... | collective-permute-start | bytes 786440 | tf_op jit(solution)/shard_map/ppermute | solution.py:425
  72.6 0.1 neigh_first.1
  72.7 3.0 %collective-permute-start.20 = (bf16[2,2,64,512]{3,2,1,0:T(8,128)(2,1)S(1)}, bf16[2,2,64,512]{3,2,1,0:T(8,128)(2,1)S(1)}, u32[]{:S(2)}, u32[]{:S(2)}) collective-permute-start(bf16[2,2,64,512]{3,2,1,0:T(8,128)(2,1)S(1)} %get-tuple-element.84), channel_id=1, source_target_pairs={{0,8},{2,10},{4,12},{6,14},{8,0},{10,2},{12,4},{14,6},{16,24},{18,... | collective-permute-start | bytes 786440 | tf_op jit(solution)/shard_map/ppermute | solution.py:429
  75.8 3.7 %collective-permute-done.15.got_ref = bf16[2,2,64,512]{3,2,1,0:T(8,128)(2,1)S(1)} collective-permute-done((bf16[2,2,64,512]{3,2,1,0:T(8,128)(2,1)S(1)}, bf16[2,2,64,512]{3,2,1,0:T(8,128)(2,1)S(1)}, u32[]{:S(2)}, u32[]{:S(2)}) %collective-permute-start.15) | collective-permute-done | bytes 262176 | tf_op jit(solution)/shard_map/ppermute | solution.py:425
  79.5 3.2 %collective-permute-start.16 = (bf16[2,64,512]{2,1,0:T(8,128)(2,1)S(1)}, bf16[2,64,512]{2,1,0:T(8,128)(2,1)S(1)}, u32[]{:S(2)}, u32[]{:S(2)}) collective-permute-start(bf16[2,64,512]{2,1,0:T(8,128)(2,1)S(1)} %get-tuple-element.78), channel_id=1, source_target_pairs={{0,8},{2,10},{4,12},{6,14},{8,0},{10,2},{12,4},{14,6},{16,24},{18,... | collective-permute-start | bytes 393224 | tf_op jit(solution)/shard_map/ppermute | solution.py:431
  82.8 1.6 %collective-permute-start.21 = (bf16[2,64,512]{2,1,0:T(8,128)(2,1)S(1)}, bf16[2,64,512]{2,1,0:T(8,128)(2,1)S(1)}, u32[]{:S(2)}, u32[]{:S(2)}) collective-permute-start(bf16[2,64,512]{2,1,0:T(8,128)(2,1)S(1)} %get-tuple-element.86), channel_id=1, source_target_pairs={{0,4},{2,6},{4,0},{6,2},{8,12},{10,14},{12,8},{14,10},{16,20},{18,... | collective-permute-start | bytes 393224 | tf_op jit(solution)/shard_map/ppermute | solution.py:433
  84.3 1.6 %collective-permute-done.16.got_ref = bf16[2,64,512]{2,1,0:T(8,128)(2,1)S(1)} collective-permute-done((bf16[2,64,512]{2,1,0:T(8,128)(2,1)S(1)}, bf16[2,64,512]{2,1,0:T(8,128)(2,1)S(1)}, u32[]{:S(2)}, u32[]{:S(2)}) %collective-permute-start.16) | collective-permute-done | bytes 131104 | tf_op jit(solution)/shard_map/ppermute | solution.py:431
  86.0 3.0 %collective-permute-start.17 = (bf16[1,64,512]{2,1,0:T(8,128)(2,1)S(1)}, bf16[1,64,512]{2,1,0:T(8,128)(2,1)S(1)}, u32[]{:S(2)}, u32[]{:S(2)}) collective-permute-start(bf16[1,64,512]{2,1,0:T(8,128)(2,1)S(1)} %get-tuple-element.80), channel_id=1, source_target_pairs={{0,16},{2,18},{4,20},{6,22},{8,24},{10,26},{12,28},{14,30},{16,0},... | collective-permute-start | bytes 196616 | tf_op jit(solution)/shard_map/ppermute | solution.py:406
  89.0 0.7 collective-permute-start.22
  89.8 3.5 %collective-permute-done.17.got_ref = bf16[1,64,512]{2,1,0:T(8,128)(2,1)S(1)} collective-permute-done((bf16[1,64,512]{2,1,0:T(8,128)(2,1)S(1)}, bf16[1,64,512]{2,1,0:T(8,128)(2,1)S(1)}, u32[]{:S(2)}, u32[]{:S(2)}) %collective-permute-start.17) | collective-permute-done | bytes 65568 | tf_op jit(solution)/shard_map/ppermute | solution.py:406
  93.3 1.6 %collective-permute-start.18 = (bf16[1,64,512]{2,1,0:T(8,128)(2,1)S(1)}, bf16[1,64,512]{2,1,0:T(8,128)(2,1)S(1)}, u32[]{:S(2)}, u32[]{:S(2)}) collective-permute-start(bf16[1,64,512]{2,1,0:T(8,128)(2,1)S(1)} %rounded_sum.2.refs_0_), channel_id=1, source_target_pairs={{0,1},{1,0},{2,3},{3,2},{4,5},{5,4},{6,7},{7,6},{8,9},{9,8},{10,11... | collective-permute-start | bytes 196616 | tf_op jit(solution)/shard_map/ppermute | solution.py:410
  94.9 1.4 %collective-permute-start.23 = (bf16[1,64,512]{2,1,0:T(8,128)(2,1)S(1)}, bf16[1,64,512]{2,1,0:T(8,128)(2,1)S(1)}, u32[]{:S(2)}, u32[]{:S(2)}) collective-permute-start(bf16[1,64,512]{2,1,0:T(8,128)(2,1)S(1)} %rounded_sum.3.refs_2_), channel_id=1, source_target_pairs={{0,1},{1,0},{2,3},{3,2},{4,5},{5,4},{6,7},{7,6},{8,9},{9,8},{10,11... | collective-permute-start | bytes 196616 | tf_op jit(solution)/shard_map/ppermute | solution.py:410
  96.3 1.4 %collective-permute-done.18.refs_1_ = bf16[1,64,512]{2,1,0:T(8,128)(2,1)S(1)} collective-permute-done((bf16[1,64,512]{2,1,0:T(8,128)(2,1)S(1)}, bf16[1,64,512]{2,1,0:T(8,128)(2,1)S(1)}, u32[]{:S(2)}, u32[]{:S(2)}) %collective-permute-start.18) | collective-permute-done | bytes 65568 | tf_op jit(solution)/shard_map/ppermute | solution.py:410
  97.6 1.6 %collective-permute-done.23.refs_3_ = bf16[1,64,512]{2,1,0:T(8,128)(2,1)S(1)} collective-permute-done((bf16[1,64,512]{2,1,0:T(8,128)(2,1)S(1)}, bf16[1,64,512]{2,1,0:T(8,128)(2,1)S(1)}, u32[]{:S(2)}, u32[]{:S(2)}) %collective-permute-start.23) | collective-permute-done | bytes 65568 | tf_op jit(solution)/shard_map/ppermute | solution.py:410
  99.3 0.7 last_sum.1
  (31 shorter events, 0.3 us)
Async XLA Ops:
  3.8 20.9 %collective-permute-start = (bf16[4,64,1024]{2,1,0:T(8,128)(2,1)}, bf16[4,64,1024]{2,1,0:T(8,128)(2,1)S(1)}, u32[]{:S(2)}, u32[]{:S(2)}) collective-permute-start(bf16[4,64,1024]{2,1,0:T(8,128)(2,1)} %get-tuple-element.47), channel_id=1, source_target_pairs={{0,4},{2,6},{4,0},{6,2},{8,12},{10,14},{12,8},{14,10},{16,20},{18,... | collective-permute-start | bytes 1572872 | tf_op jit(solution)/shard_map/ppermute | solution.py:460
  6.8 16.9 %collective-permute-start.2 = (bf16[1,64,1536]{2,1,0:T(8,128)(2,1)}, bf16[1,64,1536]{2,1,0:T(8,128)(2,1)S(1)}, u32[]{:S(2)}, u32[]{:S(2)}) collective-permute-start(bf16[1,64,1536]{2,1,0:T(8,128)(2,1)} %get-tuple-element.51), channel_id=1, source_target_pairs={{0,8},{2,10},{4,12},{6,14},{8,0},{10,2},{12,4},{14,6},{16,24},{18,... | collective-permute-start | bytes 589832 | tf_op jit(solution)/shard_map/ppermute | solution.py:461
  8.4 15.7 %collective-permute-start.3 = (bf16[1,64,1536]{2,1,0:T(8,128)(2,1)}, bf16[1,64,1536]{2,1,0:T(8,128)(2,1)S(1)}, u32[]{:S(2)}, u32[]{:S(2)}) collective-permute-start(bf16[1,64,1536]{2,1,0:T(8,128)(2,1)} %get-tuple-element.52), channel_id=1, source_target_pairs={{0,16},{2,18},{4,20},{6,22},{8,24},{10,26},{12,28},{14,30},{16,0},... | collective-permute-start | bytes 589832 | tf_op jit(solution)/shard_map/ppermute | solution.py:461
  10.9 4.1 %collective-permute-start.1 = (bf16[64,256]{1,0:T(8,128)(2,1)}, bf16[64,256]{1,0:T(8,128)(2,1)S(1)}, u32[]{:S(2)}, u32[]{:S(2)}) collective-permute-start(bf16[64,256]{1,0:T(8,128)(2,1)} %get-tuple-element.48), channel_id=1, source_target_pairs={{0,1},{1,0},{2,3},{3,2},{4,5},{5,4},{6,7},{7,6},{8,9},{9,8},{10,11... | collective-permute-start | bytes 98312 | tf_op jit(solution)/shard_map/ppermute | solution.py:464
  12.5 19.8 %collective-permute-start.4 = (bf16[1,64,1024]{2,1,0:T(8,128)(2,1)}, bf16[1,64,1024]{2,1,0:T(8,128)(2,1)S(1)}, u32[]{:S(2)}, u32[]{:S(2)}) collective-permute-start(bf16[1,64,1024]{2,1,0:T(8,128)(2,1)} %get-tuple-element.53), channel_id=1, source_target_pairs={{0,24},{2,26},{4,28},{6,30},{8,16},{10,18},{12,20},{14,22},{16,8},... | collective-permute-start | bytes 393224 | tf_op jit(solution)/shard_map/ppermute | solution.py:461
  15.1 0.6 copy-start.4
  15.7 8.3 %copy-start.2 = (bf16[1,64,1536]{2,1,0:T(8,128)(2,1)S(1)}, bf16[1,64,1536]{2,1,0:T(8,128)(2,1)}, u32[]{:S(2)}) copy-start(bf16[1,64,1536]{2,1,0:T(8,128)(2,1)} %get-tuple-element.56.refs_0_) | copy-start | bytes 589828
  24.0 8.2 %collective-permute-start.8 = (bf16[3,64,512]{2,1,0:T(8,128)(2,1)S(1)}, bf16[3,64,512]{2,1,0:T(8,128)(2,1)S(1)}, u32[]{:S(2)}, u32[]{:S(2)}) collective-permute-start(bf16[3,64,512]{2,1,0:T(8,128)(2,1)S(1)} %weight_pieces.2.refs_0_), channel_id=1, source_target_pairs={{0,4},{2,6},{4,0},{6,2},{8,12},{10,14},{12,8},{14,10},{16,20},{18,... | collective-permute-start | bytes 589832 | tf_op jit(solution)/shard_map/ppermute | solution.py:478
  24.7 6.0 %collective-permute-start.5 = (bf16[1,64,1536]{2,1,0:T(8,128)(2,1)S(1)}, bf16[1,64,1536]{2,1,0:T(8,128)(2,1)S(1)}, u32[]{:S(2)}, u32[]{:S(2)}) collective-permute-start(bf16[1,64,1536]{2,1,0:T(8,128)(2,1)S(1)} %relayed.1), channel_id=1, source_target_pairs={{0,8},{2,10},{4,12},{6,14},{8,0},{10,2},{12,4},{14,6},{16,24},{18,... | collective-permute-start | bytes 589832 | tf_op jit(solution)/shard_map/ppermute | solution.py:472
  24.9 8.5 %collective-permute-start.7 = (bf16[1,64,1024]{2,1,0:T(8,128)(2,1)S(1)}, bf16[1,64,1024]{2,1,0:T(8,128)(2,1)S(1)}, u32[]{:S(2)}, u32[]{:S(2)}) collective-permute-start(bf16[1,64,1024]{2,1,0:T(8,128)(2,1)S(1)} %get-tuple-element.91), channel_id=1, source_target_pairs={{0,24},{2,26},{4,28},{6,30},{8,16},{10,18},{12,20},{14,22},{16,8},... | collective-permute-start | bytes 393224 | tf_op jit(solution)/shard_map/ppermute | solution.py:472
  27.3 10.0 %collective-permute-start.6 = (bf16[1,64,1024]{2,1,0:T(8,128)(2,1)S(1)}, bf16[1,64,1024]{2,1,0:T(8,128)(2,1)S(1)}, u32[]{:S(2)}, u32[]{:S(2)}) collective-permute-start(bf16[1,64,1024]{2,1,0:T(8,128)(2,1)S(1)} %get-tuple-element.92), channel_id=1, source_target_pairs={{0,16},{2,18},{4,20},{6,22},{8,24},{10,26},{12,28},{14,30},{16,0},... | collective-permute-start | bytes 393224 | tf_op jit(solution)/shard_map/ppermute | solution.py:472
  30.7 6.7 %collective-permute-start.9 = (bf16[1,64,512]{2,1,0:T(8,128)(2,1)S(1)}, bf16[1,64,512]{2,1,0:T(8,128)(2,1)S(1)}, u32[]{:S(2)}, u32[]{:S(2)}) collective-permute-start(bf16[1,64,512]{2,1,0:T(8,128)(2,1)S(1)} %weight_pieces.3.refs_1_), channel_id=1, source_target_pairs={{0,4},{2,6},{4,0},{6,2},{8,12},{10,14},{12,8},{14,10},{16,20},{18,... | collective-permute-start | bytes 196616 | tf_op jit(solution)/shard_map/ppermute | solution.py:478
  37.4 26.9 %all-to-all-start = ((bf16[16,64,512]{2,1,0:T(8,128)(2,1)}), bf16[16,64,512]{2,1,0:T(8,128)(2,1)S(1)}, u32[]{:S(2)}, u32[]{:S(2)}) async-start(bf16[16,64,512]{2,1,0:T(8,128)(2,1)} %neighbour_means.1), calls=%async_computation | async-start | bytes 2097152 | tf_op jit(solution)/shard_map/all_to_all | solution.py:481
  41.3 16.3 %copy-start.3 = (bf16[512,512]{1,0:T(8,128)(2,1)S(1)}, bf16[512,512]{1,0:T(8,128)(2,1)}, u32[]{:S(2)}) copy-start(bf16[512,512]{1,0:T(8,128)(2,1)} %refs_6_.3) | copy-start | bytes 1572868
  41.4 14.3 %collective-permute-start.12 = (bf16[8,64,512]{2,1,0:T(8,128)(2,1)S(1)}, bf16[8,64,512]{2,1,0:T(8,128)(2,1)S(1)}, u32[]{:S(2)}, u32[]{:S(2)}) collective-permute-start(bf16[8,64,512]{2,1,0:T(8,128)(2,1)S(1)} %gathered.1.refs_2_), channel_id=1, source_target_pairs={{0,1},{1,0},{2,3},{3,2},{4,5},{5,4},{6,7},{7,6},{8,9},{9,8},{10,11... | collective-permute-start | bytes 1572872 | tf_op jit(solution)/shard_map/ppermute | solution.py:483
  43.0 12.7 %collective-permute-start.11 = (bf16[8,64,512]{2,1,0:T(8,128)(2,1)S(1)}, bf16[8,64,512]{2,1,0:T(8,128)(2,1)S(1)}, u32[]{:S(2)}, u32[]{:S(2)}) collective-permute-start(bf16[8,64,512]{2,1,0:T(8,128)(2,1)S(1)} %gathered.1.refs_2_), channel_id=1, source_target_pairs={{0,2},{2,0},{4,6},{6,4},{8,10},{10,8},{12,14},{14,12},{16,18},{18,... | collective-permute-start | bytes 1572872 | tf_op jit(solution)/shard_map/ppermute | solution.py:489
  43.2 12.5 %collective-permute-start.10 = (bf16[8,64,512]{2,1,0:T(8,128)(2,1)S(1)}, bf16[8,64,512]{2,1,0:T(8,128)(2,1)S(1)}, u32[]{:S(2)}, u32[]{:S(2)}) collective-permute-start(bf16[8,64,512]{2,1,0:T(8,128)(2,1)S(1)} %get-tuple-element.65), channel_id=1, source_target_pairs={{0,2},{2,0},{4,6},{6,4},{8,10},{10,8},{12,14},{14,12},{16,18},{18,... | collective-permute-start | bytes 1572872 | tf_op jit(solution)/shard_map/ppermute | solution.py:487
  55.7 1.9 %collective-permute-start.13 = (bf16[8,64,512]{2,1,0:T(8,128)(2,1)S(1)}, bf16[8,64,512]{2,1,0:T(8,128)(2,1)S(1)}, u32[]{:S(2)}, u32[]{:S(2)}) collective-permute-start(bf16[8,64,512]{2,1,0:T(8,128)(2,1)S(1)} %collective-permute-done.12.refs_4_), channel_id=1, source_target_pairs={{0,2},{2,0},{4,6},{6,4},{8,10},{10,8},{12,14},{14,12},{16,18},{18,... | collective-permute-start | bytes 1572872 | tf_op jit(solution)/shard_map/ppermute | solution.py:490
  58.5 1.2 %copy-start = (bf16[1536,512]{1,0:T(8,128)(2,1)}, bf16[1536,512]{1,0:T(8,128)(2,1)S(1)}, u32[]{:S(2)}) copy-start(bf16[1536,512]{1,0:T(8,128)(2,1)S(1)} %get-tuple-element.70.beside_ref) | copy-start | bytes 4718596
  64.3 1.4 %copy-start.1 = (bf16[1536,512]{1,0:T(8,128)(2,1)S(1)}, bf16[1536,512]{1,0:T(8,128)(2,1)}, u32[]{:S(2)}) copy-start(bf16[1536,512]{1,0:T(8,128)(2,1)} %copy-done) | copy-start | bytes 4718596
  68.4 2.1 %collective-permute-start.14 = (bf16[8,64,512]{2,1,0:T(8,128)(2,1)S(1)}, bf16[8,64,512]{2,1,0:T(8,128)(2,1)S(1)}, u32[]{:S(2)}, u32[]{:S(2)}) collective-permute-start(bf16[8,64,512]{2,1,0:T(8,128)(2,1)S(1)} %get-tuple-element.74), channel_id=1, source_target_pairs={{0,2},{2,0},{4,6},{6,4},{8,10},{10,8},{12,14},{14,12},{16,18},{18,... | collective-permute-start | bytes 1572872 | tf_op jit(solution)/shard_map/ppermute | solution.py:511
  69.0 3.7 %collective-permute-start.19 = (bf16[8,64,512]{2,1,0:T(8,128)(2,1)S(1)}, bf16[8,64,512]{2,1,0:T(8,128)(2,1)S(1)}, u32[]{:S(2)}, u32[]{:S(2)}) collective-permute-start(bf16[8,64,512]{2,1,0:T(8,128)(2,1)S(1)} %get-tuple-element.82), channel_id=1, source_target_pairs={{0,2},{2,0},{4,6},{6,4},{8,10},{10,8},{12,14},{14,12},{16,18},{18,... | collective-permute-start | bytes 1572872 | tf_op jit(solution)/shard_map/ppermute | solution.py:511
  70.6 8.9 %collective-permute-start.15 = (bf16[2,2,64,512]{3,2,1,0:T(8,128)(2,1)S(1)}, bf16[2,2,64,512]{3,2,1,0:T(8,128)(2,1)S(1)}, u32[]{:S(2)}, u32[]{:S(2)}) collective-permute-start(bf16[2,2,64,512]{3,2,1,0:T(8,128)(2,1)S(1)} %get-tuple-element.76), channel_id=1, source_target_pairs={{0,4},{2,6},{4,0},{6,2},{8,12},{10,14},{12,8},{14,10},{16,20},{18,... | collective-permute-start | bytes 786440 | tf_op jit(solution)/shard_map/ppermute | solution.py:425
  72.7 10.0 %collective-permute-start.20 = (bf16[2,2,64,512]{3,2,1,0:T(8,128)(2,1)S(1)}, bf16[2,2,64,512]{3,2,1,0:T(8,128)(2,1)S(1)}, u32[]{:S(2)}, u32[]{:S(2)}) collective-permute-start(bf16[2,2,64,512]{3,2,1,0:T(8,128)(2,1)S(1)} %get-tuple-element.84), channel_id=1, source_target_pairs={{0,8},{2,10},{4,12},{6,14},{8,0},{10,2},{12,4},{14,6},{16,24},{18,... | collective-permute-start | bytes 786440 | tf_op jit(solution)/shard_map/ppermute | solution.py:429
  79.5 6.4 %collective-permute-start.16 = (bf16[2,64,512]{2,1,0:T(8,128)(2,1)S(1)}, bf16[2,64,512]{2,1,0:T(8,128)(2,1)S(1)}, u32[]{:S(2)}, u32[]{:S(2)}) collective-permute-start(bf16[2,64,512]{2,1,0:T(8,128)(2,1)S(1)} %get-tuple-element.78), channel_id=1, source_target_pairs={{0,8},{2,10},{4,12},{6,14},{8,0},{10,2},{12,4},{14,6},{16,24},{18,... | collective-permute-start | bytes 393224 | tf_op jit(solution)/shard_map/ppermute | solution.py:431
  82.8 6.2 %collective-permute-start.21 = (bf16[2,64,512]{2,1,0:T(8,128)(2,1)S(1)}, bf16[2,64,512]{2,1,0:T(8,128)(2,1)S(1)}, u32[]{:S(2)}, u32[]{:S(2)}) collective-permute-start(bf16[2,64,512]{2,1,0:T(8,128)(2,1)S(1)} %get-tuple-element.86), channel_id=1, source_target_pairs={{0,4},{2,6},{4,0},{6,2},{8,12},{10,14},{12,8},{14,10},{16,20},{18,... | collective-permute-start | bytes 393224 | tf_op jit(solution)/shard_map/ppermute | solution.py:433
  86.0 7.3 %collective-permute-start.17 = (bf16[1,64,512]{2,1,0:T(8,128)(2,1)S(1)}, bf16[1,64,512]{2,1,0:T(8,128)(2,1)S(1)}, u32[]{:S(2)}, u32[]{:S(2)}) collective-permute-start(bf16[1,64,512]{2,1,0:T(8,128)(2,1)S(1)} %get-tuple-element.80), channel_id=1, source_target_pairs={{0,16},{2,18},{4,20},{6,22},{8,24},{10,26},{12,28},{14,30},{16,0},... | collective-permute-start | bytes 196616 | tf_op jit(solution)/shard_map/ppermute | solution.py:406
  89.0 5.9 %collective-permute-start.22 = (bf16[1,64,512]{2,1,0:T(8,128)(2,1)S(1)}, bf16[1,64,512]{2,1,0:T(8,128)(2,1)S(1)}, u32[]{:S(2)}, u32[]{:S(2)}) collective-permute-start(bf16[1,64,512]{2,1,0:T(8,128)(2,1)S(1)} %get-tuple-element.88), channel_id=1, source_target_pairs={{0,16},{2,18},{4,20},{6,22},{8,24},{10,26},{12,28},{14,30},{16,0},... | collective-permute-start | bytes 196616 | tf_op jit(solution)/shard_map/ppermute | solution.py:406
  93.3 4.3 %collective-permute-start.18 = (bf16[1,64,512]{2,1,0:T(8,128)(2,1)S(1)}, bf16[1,64,512]{2,1,0:T(8,128)(2,1)S(1)}, u32[]{:S(2)}, u32[]{:S(2)}) collective-permute-start(bf16[1,64,512]{2,1,0:T(8,128)(2,1)S(1)} %rounded_sum.2.refs_0_), channel_id=1, source_target_pairs={{0,1},{1,0},{2,3},{3,2},{4,5},{5,4},{6,7},{7,6},{8,9},{9,8},{10,11... | collective-permute-start | bytes 196616 | tf_op jit(solution)/shard_map/ppermute | solution.py:410
  94.9 4.3 %collective-permute-start.23 = (bf16[1,64,512]{2,1,0:T(8,128)(2,1)S(1)}, bf16[1,64,512]{2,1,0:T(8,128)(2,1)S(1)}, u32[]{:S(2)}, u32[]{:S(2)}) collective-permute-start(bf16[1,64,512]{2,1,0:T(8,128)(2,1)S(1)} %rounded_sum.3.refs_2_), channel_id=1, source_target_pairs={{0,1},{1,0},{2,3},{3,2},{4,5},{5,4},{6,7},{7,6},{8,9},{9,8},{10,11... | collective-permute-start | bytes 196616 | tf_op jit(solution)/shard_map/ppermute | solution.py:410

commit v10 on v8

--- a/solution.py
+++ b/solution.py
@@ -12,7 +12,7 @@
 bf16 = jnp.bfloat16
 f32 = jnp.float32
 vmem_bytes = 16 * 2**20
-most_vmem = 60 * 2**20
+most_vmem = 54 * 2**20
 whole_vmem = pl.BlockSpec(memory_space=pltpu.VMEM)
 whole_smem = pl.BlockSpec(memory_space=pltpu.SMEM)
 anywhere = pl.BlockSpec(memory_space=pl.ANY)
@@ -89,15 +89,20 @@
 
 
 def pick(columns_ref, asked):
-    count = columns_ref.shape[1]
-    step = min(256, count)
-    total = jnp.zeros((columns_ref.shape[0], asked.shape[1]), f32)
-    for at in range(0, count, step):
-        ids = lax.broadcasted_iota(jnp.int32, (step, asked.shape[1]), 0) + at
-        one_hot = jnp.where(ids == asked, 1.0, 0.0).astype(bf16)
-        total = total + jnp.dot(
-            columns_ref[:, at : at + step], one_hot, preferred_element_type=f32
-        )
+    depth, count = columns_ref.shape
+    span = 256 if count % 256 == 0 else count
+    spans = count // span
+    low = lax.rem(asked + span, span)
+    high = lax.div(asked + span, span) - 1
+    ids = lax.broadcasted_iota(jnp.int32, (span, asked.shape[1]), 0)
+    one_hot = jnp.where(ids == low, 1.0, 0.0).astype(bf16)
+    total = jnp.zeros((depth, asked.shape[1]), f32)
+    group = 8 if spans % 8 == 0 else 1
+    for first in range(0, spans, group):
+        rows = [columns_ref[:, i * span : (i + 1) * span] for i in range(first, first + group)]
+        found = jnp.dot(jnp.concatenate(rows, 0), one_hot, preferred_element_type=f32)
+        for i in range(group):
+            total = total + jnp.where(high == first + i, found[i * depth : (i + 1) * depth], 0.0)
     return total.astype(bf16)
 
 
@@ -320,7 +325,7 @@
 
 def fill_linear(source, weight_masks, weight_refs, base_ref, linear_ref, more):
     rows, hid = linear_ref.shape
-    step = min(256, rows)
+    step = min(512, rows)
     for at in range(0, rows, step):
         total = base_ref[at : at + step] if more else jnp.zeros((step, hid), f32)
         for masks, weight_ref in zip(weight_masks, weight_refs):

time: 101 us -> 101 us (level)
  starting transfers between devices: 36.4 us -> 37.5 us
    all_to_all x1, starting transfers between devices: 3.98 us -> 5.02 us  [on_device(): own_mean = lax.all_to_all(means, 'feat', 0, 0, tiled=True)]
where the time goes in v10:
time: 101 us; the launch traced here: 100 us
  waiting for transfers between devices  43.8 us (43%)
  starting transfers between devices  37.5 us (37%)
  Pallas kernels  15.1 us (15%)
  local copies, waits for them, and re-layouts  3.23 us (3%)
    pallas_call x19, Pallas kernels, local_call(): pl.pallas_call(kernel, out_shape=outs, in_specs=in_specs, out_specs=[whol...  15.1 us
    ppermute x1, waiting for transfers between devices, on_device(): others = [flip('dom', 1)(p) for p in pieces]  12.1 us
    ppermute x3, waiting for transfers between devices, on_device(): flip('feat', i * below)(leaving[i])  7.21 us
    ppermute x1, waiting for transfers between devices, sum_gradients(): neigh_got = flip('feat', 4)(neigh_sent)  5.1 us
    all_to_all x1, starting transfers between devices, on_device(): own_mean = lax.all_to_all(means, 'feat', 0, 0, tiled=True)  5.02 us
    all_to_all x1, waiting for transfers between devices, on_device(): own_mean = lax.all_to_all(means, 'feat', 0, 0, tiled=True)  4.65 us
    ppermute x3, starting transfers between devices, on_device(): near = {i: flip('feat', i * below)(cuts[i]) for i in (3, 2, 1)}  4.39 us
    ppermute x3, starting transfers between devices, on_device(): flip('feat', i * below)(leaving[i])  3.6 us
  transfers between devices with their start and end apart: 25, of which 14 were waited for; matrix products, arithmetic and copies ran while one was open for 0% of the time, Pallas kernels for 9%

profile of v10, /device:TPU:0, one launch (start us, length us, event | category | flops | bytes accessed | tf_op | source)
XLA Modules:
  0.0 100.5 jit_solution(9055673730522734659)
XLA Ops:
  0.6 2.8 %open_exchange.1 = (bf16[64,256]{1,0:T(8,128)(2,1)}, bf16[4,64,1024]{2,1,0:T(8,128)(2,1)}, bf16[1,64,1536]{2,1,0:T(8,128)(2,1)}, bf16[1,64,1536]{2,1,0:T(8,128)(...) custom-call(s32[2,2]{1,0:T(2,128)} %refs_2_.3, bf16[64,8192]{1,0:T(8,128)(2,1)} %bitcast.7, ...), custom_call_target="tpu_custom_call" | custom-call | tf_op jit(solution)/shard_map/open_exchange/pallas_call | solution.py:79
  3.5 3.0 %collective-permute-start = (bf16[4,64,1024]{2,1,0:T(8,128)(2,1)}, bf16[4,64,1024]{2,1,0:T(8,128)(2,1)S(1)}, u32[]{:S(2)}, u32[]{:S(2)}) collective-permute-start(bf16[4,64,1024]{2,1,0:T(8,128)(2,1)} %get-tuple-element.48), channel_id=1, source_target_pairs={{0,4},{2,6},{4,0},{6,2},{8,12},{10,14},{12,8},{14,10},{16,20},{18,... | collective-permute-start | bytes 1572872 | tf_op jit(solution)/shard_map/ppermute | solution.py:469
  6.5 1.6 %collective-permute-start.2 = (bf16[1,64,1536]{2,1,0:T(8,128)(2,1)}, bf16[1,64,1536]{2,1,0:T(8,128)(2,1)S(1)}, u32[]{:S(2)}, u32[]{:S(2)}) collective-permute-start(bf16[1,64,1536]{2,1,0:T(8,128)(2,1)} %get-tuple-element.52), channel_id=1, source_target_pairs={{0,8},{2,10},{4,12},{6,14},{8,0},{10,2},{12,4},{14,6},{16,24},{18,... | collective-permute-start | bytes 589832 | tf_op jit(solution)/shard_map/ppermute | solution.py:470
  8.0 2.6 %collective-permute-start.3 = (bf16[1,64,1536]{2,1,0:T(8,128)(2,1)}, bf16[1,64,1536]{2,1,0:T(8,128)(2,1)S(1)}, u32[]{:S(2)}, u32[]{:S(2)}) collective-permute-start(bf16[1,64,1536]{2,1,0:T(8,128)(2,1)} %get-tuple-element.53), channel_id=1, source_target_pairs={{0,16},{2,18},{4,20},{6,22},{8,24},{10,26},{12,28},{14,30},{16,0},... | collective-permute-start | bytes 589832 | tf_op jit(solution)/shard_map/ppermute | solution.py:470
  10.6 1.5 %collective-permute-start.1 = (bf16[64,256]{1,0:T(8,128)(2,1)}, bf16[64,256]{1,0:T(8,128)(2,1)S(1)}, u32[]{:S(2)}, u32[]{:S(2)}) collective-permute-start(bf16[64,256]{1,0:T(8,128)(2,1)} %get-tuple-element.49), channel_id=1, source_target_pairs={{0,1},{1,0},{2,3},{3,2},{4,5},{5,4},{6,7},{7,6},{8,9},{9,8},{10,11... | collective-permute-start | bytes 98312 | tf_op jit(solution)/shard_map/ppermute | solution.py:473
  12.1 0.2 collective-permute-start.4
  12.4 2.4 %collective-permute-done.1.refs_4_ = bf16[64,256]{1,0:T(8,128)(2,1)S(1)} collective-permute-done((bf16[64,256]{1,0:T(8,128)(2,1)}, bf16[64,256]{1,0:T(8,128)(2,1)S(1)}, u32[]{:S(2)}, u32[]{:S(2)}) %collective-permute-start.1) | collective-permute-done | bytes 32800 | tf_op jit(solution)/shard_map/ppermute | solution.py:473
  14.8 0.6 copy-done.4
  15.4 7.6 %neighbour_means.1 = bf16[16,64,512]{2,1,0:T(8,128)(2,1)} custom-call(s32[8,64]{1,0:T(8,128)} %bitcast.9, s32[8,64]{1,0:T(8,128)} %bitcast.10, s32[2,2]{1,0:T(2,128)} %refs_2_.3, bf16[64,8192]{1,0:T(8,128)(2,1)} %bitcast.8, bf16[64,256]{1,0:T(8,128)(2,1)} %copy-done.4, s32[2,2,256]{2,1,0:T(2,128)} %refs_5_.1, bf16[64,128,128]{2,1,0:T(8,128)(2,1)} %refs_6_.2), custom_call_target="tpu_custom_call" | custom-call | tf_op jit(solution)/shard_map/neighbour_means/pallas_call | solution.py:79
  23.0 0.7 collective-permute-done.3.near_ref.refs_2_
  23.7 0.6 collective-permute-start.8
  24.5 2.5 %collective-permute-start.7 = (bf16[1,64,1024]{2,1,0:T(8,128)(2,1)S(1)}, bf16[1,64,1024]{2,1,0:T(8,128)(2,1)S(1)}, u32[]{:S(2)}, u32[]{:S(2)}) collective-permute-start(bf16[1,64,1024]{2,1,0:T(8,128)(2,1)S(1)} %get-tuple-element.93), channel_id=1, source_target_pairs={{0,24},{2,26},{4,28},{6,30},{8,16},{10,18},{12,20},{14,22},{16,8},... | collective-permute-start | bytes 393224 | tf_op jit(solution)/shard_map/ppermute | solution.py:481
  27.0 1.0 collective-permute-start.6
  28.0 2.5 %collective-permute-done.5.refs_0_.refs_5_ = bf16[1,64,1536]{2,1,0:T(8,128)(2,1)S(1)} collective-permute-done((bf16[1,64,1536]{2,1,0:T(8,128)(2,1)S(1)}, bf16[1,64,1536]{2,1,0:T(8,128)(2,1)S(1)}, u32[]{:S(2)}, u32[]{:S(2)}) %collective-permute-start.5) | collective-permute-done | bytes 196640 | tf_op jit(solution)/shard_map/ppermute | solution.py:481
  30.5 1.5 %collective-permute-start.9 = (bf16[1,64,512]{2,1,0:T(8,128)(2,1)S(1)}, bf16[1,64,512]{2,1,0:T(8,128)(2,1)S(1)}, u32[]{:S(2)}, u32[]{:S(2)}) collective-permute-start(bf16[1,64,512]{2,1,0:T(8,128)(2,1)S(1)} %weight_pieces.3.refs_1_), channel_id=1, source_target_pairs={{0,4},{2,6},{4,0},{6,2},{8,12},{10,14},{12,8},{14,10},{16,20},{18,... | collective-permute-start | bytes 196616 | tf_op jit(solution)/shard_map/ppermute | solution.py:487
  32.0 0.7 collective-permute-done.7.refs_7_
  32.7 4.0 %collective-permute-done.6.refs_6_ = bf16[1,64,1024]{2,1,0:T(8,128)(2,1)S(1)} collective-permute-done((bf16[1,64,1024]{2,1,0:T(8,128)(2,1)S(1)}, bf16[1,64,1024]{2,1,0:T(8,128)(2,1)S(1)}, u32[]{:S(2)}, u32[]{:S(2)}) %collective-permute-start.6) | collective-permute-done | bytes 131104 | tf_op jit(solution)/shard_map/ppermute | solution.py:481
  36.7 5.0 %all-to-all-start = ((bf16[16,64,512]{2,1,0:T(8,128)(2,1)}), bf16[16,64,512]{2,1,0:T(8,128)(2,1)S(1)}, u32[]{:S(2)}, u32[]{:S(2)}) async-start(bf16[16,64,512]{2,1,0:T(8,128)(2,1)} %neighbour_means.1), calls=%async_computation | async-start | bytes 2097152 | tf_op jit(solution)/shard_map/all_to_all | solution.py:490
  41.8 1.6 %collective-permute-start.12 = (bf16[8,64,512]{2,1,0:T(8,128)(2,1)S(1)}, bf16[8,64,512]{2,1,0:T(8,128)(2,1)S(1)}, u32[]{:S(2)}, u32[]{:S(2)}) collective-permute-start(bf16[8,64,512]{2,1,0:T(8,128)(2,1)S(1)} %gathered.1.refs_2_), channel_id=1, source_target_pairs={{0,1},{1,0},{2,3},{3,2},{4,5},{5,4},{6,7},{7,6},{8,9},{9,8},{10,11... | collective-permute-start | bytes 1572872 | tf_op jit(solution)/shard_map/ppermute | solution.py:492
  43.3 0.1 collective-permute-start.11
  43.6 0.4 collective-permute-start.10
  44.0 12.1 %collective-permute-done.12.refs_4_ = bf16[8,64,512]{2,1,0:T(8,128)(2,1)S(1)} collective-permute-done((bf16[8,64,512]{2,1,0:T(8,128)(2,1)S(1)}, bf16[8,64,512]{2,1,0:T(8,128)(2,1)S(1)}, u32[]{:S(2)}, u32[]{:S(2)}) %collective-permute-start.12) | collective-permute-done | bytes 524320 | tf_op jit(solution)/shard_map/ppermute | solution.py:492
  56.1 1.9 %collective-permute-done.13.refs_5_ = bf16[8,64,512]{2,1,0:T(8,128)(2,1)S(1)} collective-permute-done((bf16[8,64,512]{2,1,0:T(8,128)(2,1)S(1)}, bf16[8,64,512]{2,1,0:T(8,128)(2,1)S(1)}, u32[]{:S(2)}, u32[]{:S(2)}) %collective-permute-start.13) | collective-permute-done | bytes 524320 | tf_op jit(solution)/shard_map/ppermute | solution.py:499
  58.0 0.8 own_linear.1
  58.8 1.2 %copy-done = bf16[1536,512]{1,0:T(8,128)(2,1)} copy-done((bf16[1536,512]{1,0:T(8,128)(2,1)}, bf16[1536,512]{1,0:T(8,128)(2,1)S(1)}, u32[]{:S(2)}) %copy-start) | copy-done | bytes 1572888
  60.0 4.6 %all-to-all-done.mean_ref = bf16[16,64,512]{2,1,0:T(8,128)(2,1)S(1)} async-done(((bf16[16,64,512]{2,1,0:T(8,128)(2,1)}), bf16[16,64,512]{2,1,0:T(8,128)(2,1)S(1)}, u32[]{:S(2)}, u32[]{:S(2)}) %all-to-all-start) | async-done | bytes 1048608 | tf_op jit(solution)/shard_map/all_to_all | solution.py:490
  64.6 1.4 %copy-done.1 = bf16[1536,512]{1,0:T(8,128)(2,1)S(1)} copy-done((bf16[1536,512]{1,0:T(8,128)(2,1)S(1)}, bf16[1536,512]{1,0:T(8,128)(2,1)}, u32[]{:S(2)}) %copy-start.1) | copy-done | bytes 1572888
  66.1 2.0 %forward.1 = (bf16[512,512]{1,0:T(8,128)(2,1)}, bf16[512,512]{1,0:T(8,128)(2,1)S(1)}, bf16[8,64,512]{2,1,0:T(8,128)(2,1)S(1)}, f32[8,64,512]{2,1,0:T(8,128)S(1)}) custom-call(bf16[16,64,512]{2,1,0:T(8,128)(2,1)S(1)} %all-to-all-done.mean_ref, bf16[1536,512]{1,0:T(8,128)(2,1)S(1)} %copy-done.1, f32[512,512]{1,0:T(8,128)S(1)} %get-tuple-element.72.base_ref, ...), custom_call_target="tpu_custom_call" | custom-call | tf_op jit(solution)/shard_map/forward/pallas_call | solution.py:79
  68.1 0.7 neighbour_sums.1
  68.8 0.7 collective-permute-start.19
  69.5 0.1 collective-permute-start.14
  69.5 1.5 %collective-permute-done.19.got_ref = bf16[8,64,512]{2,1,0:T(8,128)(2,1)S(1)} collective-permute-done((bf16[8,64,512]{2,1,0:T(8,128)(2,1)S(1)}, bf16[8,64,512]{2,1,0:T(8,128)(2,1)S(1)}, u32[]{:S(2)}, u32[]{:S(2)}) %collective-permute-start.19) | collective-permute-done | bytes 524320 | tf_op jit(solution)/shard_map/ppermute | solution.py:524
  71.0 0.1 neigh_first.1
  71.1 3.4 %collective-permute-start.20 = (bf16[2,2,64,512]{3,2,1,0:T(8,128)(2,1)S(1)}, bf16[2,2,64,512]{3,2,1,0:T(8,128)(2,1)S(1)}, u32[]{:S(2)}, u32[]{:S(2)}) collective-permute-start(bf16[2,2,64,512]{3,2,1,0:T(8,128)(2,1)S(1)} %get-tuple-element.86), channel_id=1, source_target_pairs={{0,8},{2,10},{4,12},{6,14},{8,0},{10,2},{12,4},{14,6},{16,24},{18,... | collective-permute-start | bytes 786440 | tf_op jit(solution)/shard_map/ppermute | solution.py:438
  74.5 0.1 own_first.1
  74.6 1.6 %collective-permute-start.15 = (bf16[2,2,64,512]{3,2,1,0:T(8,128)(2,1)S(1)}, bf16[2,2,64,512]{3,2,1,0:T(8,128)(2,1)S(1)}, u32[]{:S(2)}, u32[]{:S(2)}) collective-permute-start(bf16[2,2,64,512]{3,2,1,0:T(8,128)(2,1)S(1)} %get-tuple-element.77), channel_id=1, source_target_pairs={{0,4},{2,6},{4,0},{6,2},{8,12},{10,14},{12,8},{14,10},{16,20},{18,... | collective-permute-start | bytes 786440 | tf_op jit(solution)/shard_map/ppermute | solution.py:434
  76.3 5.1 %collective-permute-done.20.got_ref = bf16[2,2,64,512]{3,2,1,0:T(8,128)(2,1)S(1)} collective-permute-done((bf16[2,2,64,512]{3,2,1,0:T(8,128)(2,1)S(1)}, bf16[2,2,64,512]{3,2,1,0:T(8,128)(2,1)S(1)}, u32[]{:S(2)}, u32[]{:S(2)}) %collective-permute-start.20) | collective-permute-done | bytes 262176 | tf_op jit(solution)/shard_map/ppermute | solution.py:438
  81.4 1.6 %collective-permute-start.21 = (bf16[2,64,512]{2,1,0:T(8,128)(2,1)S(1)}, bf16[2,64,512]{2,1,0:T(8,128)(2,1)S(1)}, u32[]{:S(2)}, u32[]{:S(2)}) collective-permute-start(bf16[2,64,512]{2,1,0:T(8,128)(2,1)S(1)} %get-tuple-element.88), channel_id=1, source_target_pairs={{0,4},{2,6},{4,0},{6,2},{8,12},{10,14},{12,8},{14,10},{16,20},{18,... | collective-permute-start | bytes 393224 | tf_op jit(solution)/shard_map/ppermute | solution.py:442
  83.0 1.8 %collective-permute-start.16 = (bf16[2,64,512]{2,1,0:T(8,128)(2,1)S(1)}, bf16[2,64,512]{2,1,0:T(8,128)(2,1)S(1)}, u32[]{:S(2)}, u32[]{:S(2)}) collective-permute-start(bf16[2,64,512]{2,1,0:T(8,128)(2,1)S(1)} %get-tuple-element.79), channel_id=1, source_target_pairs={{0,8},{2,10},{4,12},{6,14},{8,0},{10,2},{12,4},{14,6},{16,24},{18,... | collective-permute-start | bytes 393224 | tf_op jit(solution)/shard_map/ppermute | solution.py:440
  84.8 1.8 %collective-permute-done.21.got_ref = bf16[2,64,512]{2,1,0:T(8,128)(2,1)S(1)} collective-permute-done((bf16[2,64,512]{2,1,0:T(8,128)(2,1)S(1)}, bf16[2,64,512]{2,1,0:T(8,128)(2,1)S(1)}, u32[]{:S(2)}, u32[]{:S(2)}) %collective-permute-start.21) | collective-permute-done | bytes 131104 | tf_op jit(solution)/shard_map/ppermute | solution.py:442
  86.7 2.8 %collective-permute-start.22 = (bf16[1,64,512]{2,1,0:T(8,128)(2,1)S(1)}, bf16[1,64,512]{2,1,0:T(8,128)(2,1)S(1)}, u32[]{:S(2)}, u32[]{:S(2)}) collective-permute-start(bf16[1,64,512]{2,1,0:T(8,128)(2,1)S(1)} %get-tuple-element.90), channel_id=1, source_target_pairs={{0,16},{2,18},{4,20},{6,22},{8,24},{10,26},{12,28},{14,30},{16,0},... | collective-permute-start | bytes 196616 | tf_op jit(solution)/shard_map/ppermute | solution.py:415
  89.5 0.7 collective-permute-start.17
  90.2 3.5 %collective-permute-done.22.got_ref = bf16[1,64,512]{2,1,0:T(8,128)(2,1)S(1)} collective-permute-done((bf16[1,64,512]{2,1,0:T(8,128)(2,1)S(1)}, bf16[1,64,512]{2,1,0:T(8,128)(2,1)S(1)}, u32[]{:S(2)}, u32[]{:S(2)}) %collective-permute-start.22) | collective-permute-done | bytes 65568 | tf_op jit(solution)/shard_map/ppermute | solution.py:415
  93.8 1.6 %collective-permute-start.23 = (bf16[1,64,512]{2,1,0:T(8,128)(2,1)S(1)}, bf16[1,64,512]{2,1,0:T(8,128)(2,1)S(1)}, u32[]{:S(2)}, u32[]{:S(2)}) collective-permute-start(bf16[1,64,512]{2,1,0:T(8,128)(2,1)S(1)} %rounded_sum.3.refs_2_), channel_id=1, source_target_pairs={{0,1},{1,0},{2,3},{3,2},{4,5},{5,4},{6,7},{7,6},{8,9},{9,8},{10,11... | collective-permute-start | bytes 196616 | tf_op jit(solution)/shard_map/ppermute | solution.py:419
  95.4 1.4 %collective-permute-start.18 = (bf16[1,64,512]{2,1,0:T(8,128)(2,1)S(1)}, bf16[1,64,512]{2,1,0:T(8,128)(2,1)S(1)}, u32[]{:S(2)}, u32[]{:S(2)}) collective-permute-start(bf16[1,64,512]{2,1,0:T(8,128)(2,1)S(1)} %rounded_sum.2.refs_0_), channel_id=1, source_target_pairs={{0,1},{1,0},{2,3},{3,2},{4,5},{5,4},{6,7},{7,6},{8,9},{9,8},{10,11... | collective-permute-start | bytes 196616 | tf_op jit(solution)/shard_map/ppermute | solution.py:419
  96.9 1.3 %collective-permute-done.23.refs_3_ = bf16[1,64,512]{2,1,0:T(8,128)(2,1)S(1)} collective-permute-done((bf16[1,64,512]{2,1,0:T(8,128)(2,1)S(1)}, bf16[1,64,512]{2,1,0:T(8,128)(2,1)S(1)}, u32[]{:S(2)}, u32[]{:S(2)}) %collective-permute-start.23) | collective-permute-done | bytes 65568 | tf_op jit(solution)/shard_map/ppermute | solution.py:419
  98.1 1.6 %collective-permute-done.18.refs_1_ = bf16[1,64,512]{2,1,0:T(8,128)(2,1)S(1)} collective-permute-done((bf16[1,64,512]{2,1,0:T(8,128)(2,1)S(1)}, bf16[1,64,512]{2,1,0:T(8,128)(2,1)S(1)}, u32[]{:S(2)}, u32[]{:S(2)}) %collective-permute-start.18) | collective-permute-done | bytes 65568 | tf_op jit(solution)/shard_map/ppermute | solution.py:419
  99.7 0.7 last_sum.1
  (32 shorter events, 0.5 us)
Async XLA Ops:
  3.5 20.9 %collective-permute-start = (bf16[4,64,1024]{2,1,0:T(8,128)(2,1)}, bf16[4,64,1024]{2,1,0:T(8,128)(2,1)S(1)}, u32[]{:S(2)}, u32[]{:S(2)}) collective-permute-start(bf16[4,64,1024]{2,1,0:T(8,128)(2,1)} %get-tuple-element.48), channel_id=1, source_target_pairs={{0,4},{2,6},{4,0},{6,2},{8,12},{10,14},{12,8},{14,10},{16,20},{18,... | collective-permute-start | bytes 1572872 | tf_op jit(solution)/shard_map/ppermute | solution.py:469
  6.5 16.5 %collective-permute-start.2 = (bf16[1,64,1536]{2,1,0:T(8,128)(2,1)}, bf16[1,64,1536]{2,1,0:T(8,128)(2,1)S(1)}, u32[]{:S(2)}, u32[]{:S(2)}) collective-permute-start(bf16[1,64,1536]{2,1,0:T(8,128)(2,1)} %get-tuple-element.52), channel_id=1, source_target_pairs={{0,8},{2,10},{4,12},{6,14},{8,0},{10,2},{12,4},{14,6},{16,24},{18,... | collective-permute-start | bytes 589832 | tf_op jit(solution)/shard_map/ppermute | solution.py:470
  8.0 15.7 %collective-permute-start.3 = (bf16[1,64,1536]{2,1,0:T(8,128)(2,1)}, bf16[1,64,1536]{2,1,0:T(8,128)(2,1)S(1)}, u32[]{:S(2)}, u32[]{:S(2)}) collective-permute-start(bf16[1,64,1536]{2,1,0:T(8,128)(2,1)} %get-tuple-element.53), channel_id=1, source_target_pairs={{0,16},{2,18},{4,20},{6,22},{8,24},{10,26},{12,28},{14,30},{16,0},... | collective-permute-start | bytes 589832 | tf_op jit(solution)/shard_map/ppermute | solution.py:470
  10.6 4.1 %collective-permute-start.1 = (bf16[64,256]{1,0:T(8,128)(2,1)}, bf16[64,256]{1,0:T(8,128)(2,1)S(1)}, u32[]{:S(2)}, u32[]{:S(2)}) collective-permute-start(bf16[64,256]{1,0:T(8,128)(2,1)} %get-tuple-element.49), channel_id=1, source_target_pairs={{0,1},{1,0},{2,3},{3,2},{4,5},{5,4},{6,7},{7,6},{8,9},{9,8},{10,11... | collective-permute-start | bytes 98312 | tf_op jit(solution)/shard_map/ppermute | solution.py:473
  12.1 19.8 %collective-permute-start.4 = (bf16[1,64,1024]{2,1,0:T(8,128)(2,1)}, bf16[1,64,1024]{2,1,0:T(8,128)(2,1)S(1)}, u32[]{:S(2)}, u32[]{:S(2)}) collective-permute-start(bf16[1,64,1024]{2,1,0:T(8,128)(2,1)} %get-tuple-element.54), channel_id=1, source_target_pairs={{0,24},{2,26},{4,28},{6,30},{8,16},{10,18},{12,20},{14,22},{16,8},... | collective-permute-start | bytes 393224 | tf_op jit(solution)/shard_map/ppermute | solution.py:470
  14.8 0.6 copy-start.4
  15.4 8.3 %copy-start.2 = (bf16[1,64,1536]{2,1,0:T(8,128)(2,1)S(1)}, bf16[1,64,1536]{2,1,0:T(8,128)(2,1)}, u32[]{:S(2)}) copy-start(bf16[1,64,1536]{2,1,0:T(8,128)(2,1)} %get-tuple-element.57.refs_0_) | copy-start | bytes 589828
  23.7 8.2 %collective-permute-start.8 = (bf16[3,64,512]{2,1,0:T(8,128)(2,1)S(1)}, bf16[3,64,512]{2,1,0:T(8,128)(2,1)S(1)}, u32[]{:S(2)}, u32[]{:S(2)}) collective-permute-start(bf16[3,64,512]{2,1,0:T(8,128)(2,1)S(1)} %weight_pieces.2.refs_0_), channel_id=1, source_target_pairs={{0,4},{2,6},{4,0},{6,2},{8,12},{10,14},{12,8},{14,10},{16,20},{18,... | collective-permute-start | bytes 589832 | tf_op jit(solution)/shard_map/ppermute | solution.py:487
  24.3 6.2 %collective-permute-start.5 = (bf16[1,64,1536]{2,1,0:T(8,128)(2,1)S(1)}, bf16[1,64,1536]{2,1,0:T(8,128)(2,1)S(1)}, u32[]{:S(2)}, u32[]{:S(2)}) collective-permute-start(bf16[1,64,1536]{2,1,0:T(8,128)(2,1)S(1)} %relayed.1), channel_id=1, source_target_pairs={{0,8},{2,10},{4,12},{6,14},{8,0},{10,2},{12,4},{14,6},{16,24},{18,... | collective-permute-start | bytes 589832 | tf_op jit(solution)/shard_map/ppermute | solution.py:481
  24.5 8.2 %collective-permute-start.7 = (bf16[1,64,1024]{2,1,0:T(8,128)(2,1)S(1)}, bf16[1,64,1024]{2,1,0:T(8,128)(2,1)S(1)}, u32[]{:S(2)}, u32[]{:S(2)}) collective-permute-start(bf16[1,64,1024]{2,1,0:T(8,128)(2,1)S(1)} %get-tuple-element.93), channel_id=1, source_target_pairs={{0,24},{2,26},{4,28},{6,30},{8,16},{10,18},{12,20},{14,22},{16,8},... | collective-permute-start | bytes 393224 | tf_op jit(solution)/shard_map/ppermute | solution.py:481
  27.0 9.7 %collective-permute-start.6 = (bf16[1,64,1024]{2,1,0:T(8,128)(2,1)S(1)}, bf16[1,64,1024]{2,1,0:T(8,128)(2,1)S(1)}, u32[]{:S(2)}, u32[]{:S(2)}) collective-permute-start(bf16[1,64,1024]{2,1,0:T(8,128)(2,1)S(1)} %get-tuple-element.94), channel_id=1, source_target_pairs={{0,16},{2,18},{4,20},{6,22},{8,24},{10,26},{12,28},{14,30},{16,0},... | collective-permute-start | bytes 393224 | tf_op jit(solution)/shard_map/ppermute | solution.py:481
  30.5 6.2 %collective-permute-start.9 = (bf16[1,64,512]{2,1,0:T(8,128)(2,1)S(1)}, bf16[1,64,512]{2,1,0:T(8,128)(2,1)S(1)}, u32[]{:S(2)}, u32[]{:S(2)}) collective-permute-start(bf16[1,64,512]{2,1,0:T(8,128)(2,1)S(1)} %weight_pieces.3.refs_1_), channel_id=1, source_target_pairs={{0,4},{2,6},{4,0},{6,2},{8,12},{10,14},{12,8},{14,10},{16,20},{18,... | collective-permute-start | bytes 196616 | tf_op jit(solution)/shard_map/ppermute | solution.py:487
  36.7 28.0 %all-to-all-start = ((bf16[16,64,512]{2,1,0:T(8,128)(2,1)}), bf16[16,64,512]{2,1,0:T(8,128)(2,1)S(1)}, u32[]{:S(2)}, u32[]{:S(2)}) async-start(bf16[16,64,512]{2,1,0:T(8,128)(2,1)} %neighbour_means.1), calls=%async_computation | async-start | bytes 2097152 | tf_op jit(solution)/shard_map/all_to_all | solution.py:490
  41.7 16.3 %copy-start.3 = (bf16[512,512]{1,0:T(8,128)(2,1)S(1)}, bf16[512,512]{1,0:T(8,128)(2,1)}, u32[]{:S(2)}) copy-start(bf16[512,512]{1,0:T(8,128)(2,1)} %refs_6_.3) | copy-start | bytes 1572868
  41.8 14.3 %collective-permute-start.12 = (bf16[8,64,512]{2,1,0:T(8,128)(2,1)S(1)}, bf16[8,64,512]{2,1,0:T(8,128)(2,1)S(1)}, u32[]{:S(2)}, u32[]{:S(2)}) collective-permute-start(bf16[8,64,512]{2,1,0:T(8,128)(2,1)S(1)} %gathered.1.refs_2_), channel_id=1, source_target_pairs={{0,1},{1,0},{2,3},{3,2},{4,5},{5,4},{6,7},{7,6},{8,9},{9,8},{10,11... | collective-permute-start | bytes 1572872 | tf_op jit(solution)/shard_map/ppermute | solution.py:492
  43.3 12.7 %collective-permute-start.11 = (bf16[8,64,512]{2,1,0:T(8,128)(2,1)S(1)}, bf16[8,64,512]{2,1,0:T(8,128)(2,1)S(1)}, u32[]{:S(2)}, u32[]{:S(2)}) collective-permute-start(bf16[8,64,512]{2,1,0:T(8,128)(2,1)S(1)} %gathered.1.refs_2_), channel_id=1, source_target_pairs={{0,2},{2,0},{4,6},{6,4},{8,10},{10,8},{12,14},{14,12},{16,18},{18,... | collective-permute-start | bytes 1572872 | tf_op jit(solution)/shard_map/ppermute | solution.py:498
  43.6 12.5 %collective-permute-start.10 = (bf16[8,64,512]{2,1,0:T(8,128)(2,1)S(1)}, bf16[8,64,512]{2,1,0:T(8,128)(2,1)S(1)}, u32[]{:S(2)}, u32[]{:S(2)}) collective-permute-start(bf16[8,64,512]{2,1,0:T(8,128)(2,1)S(1)} %get-tuple-element.66), channel_id=1, source_target_pairs={{0,2},{2,0},{4,6},{6,4},{8,10},{10,8},{12,14},{14,12},{16,18},{18,... | collective-permute-start | bytes 1572872 | tf_op jit(solution)/shard_map/ppermute | solution.py:496
  56.1 1.9 %collective-permute-start.13 = (bf16[8,64,512]{2,1,0:T(8,128)(2,1)S(1)}, bf16[8,64,512]{2,1,0:T(8,128)(2,1)S(1)}, u32[]{:S(2)}, u32[]{:S(2)}) collective-permute-start(bf16[8,64,512]{2,1,0:T(8,128)(2,1)S(1)} %collective-permute-done.12.refs_4_), channel_id=1, source_target_pairs={{0,2},{2,0},{4,6},{6,4},{8,10},{10,8},{12,14},{14,12},{16,18},{18,... | collective-permute-start | bytes 1572872 | tf_op jit(solution)/shard_map/ppermute | solution.py:499
  58.8 1.2 %copy-start = (bf16[1536,512]{1,0:T(8,128)(2,1)}, bf16[1536,512]{1,0:T(8,128)(2,1)S(1)}, u32[]{:S(2)}) copy-start(bf16[1536,512]{1,0:T(8,128)(2,1)S(1)} %get-tuple-element.71.beside_ref) | copy-start | bytes 4718596
  64.6 1.4 %copy-start.1 = (bf16[1536,512]{1,0:T(8,128)(2,1)S(1)}, bf16[1536,512]{1,0:T(8,128)(2,1)}, u32[]{:S(2)}) copy-start(bf16[1536,512]{1,0:T(8,128)(2,1)} %copy-done) | copy-start | bytes 4718596
  68.8 2.2 %collective-permute-start.19 = (bf16[8,64,512]{2,1,0:T(8,128)(2,1)S(1)}, bf16[8,64,512]{2,1,0:T(8,128)(2,1)S(1)}, u32[]{:S(2)}, u32[]{:S(2)}) collective-permute-start(bf16[8,64,512]{2,1,0:T(8,128)(2,1)S(1)} %get-tuple-element.84), channel_id=1, source_target_pairs={{0,2},{2,0},{4,6},{6,4},{8,10},{10,8},{12,14},{14,12},{16,18},{18,... | collective-permute-start | bytes 1572872 | tf_op jit(solution)/shard_map/ppermute | solution.py:524
  69.5 5.1 %collective-permute-start.14 = (bf16[8,64,512]{2,1,0:T(8,128)(2,1)S(1)}, bf16[8,64,512]{2,1,0:T(8,128)(2,1)S(1)}, u32[]{:S(2)}, u32[]{:S(2)}) collective-permute-start(bf16[8,64,512]{2,1,0:T(8,128)(2,1)S(1)} %get-tuple-element.75), channel_id=1, source_target_pairs={{0,2},{2,0},{4,6},{6,4},{8,10},{10,8},{12,14},{14,12},{16,18},{18,... | collective-permute-start | bytes 1572872 | tf_op jit(solution)/shard_map/ppermute | solution.py:520
  71.1 10.3 %collective-permute-start.20 = (bf16[2,2,64,512]{3,2,1,0:T(8,128)(2,1)S(1)}, bf16[2,2,64,512]{3,2,1,0:T(8,128)(2,1)S(1)}, u32[]{:S(2)}, u32[]{:S(2)}) collective-permute-start(bf16[2,2,64,512]{3,2,1,0:T(8,128)(2,1)S(1)} %get-tuple-element.86), channel_id=1, source_target_pairs={{0,8},{2,10},{4,12},{6,14},{8,0},{10,2},{12,4},{14,6},{16,24},{18,... | collective-permute-start | bytes 786440 | tf_op jit(solution)/shard_map/ppermute | solution.py:438
  74.6 8.4 %collective-permute-start.15 = (bf16[2,2,64,512]{3,2,1,0:T(8,128)(2,1)S(1)}, bf16[2,2,64,512]{3,2,1,0:T(8,128)(2,1)S(1)}, u32[]{:S(2)}, u32[]{:S(2)}) collective-permute-start(bf16[2,2,64,512]{3,2,1,0:T(8,128)(2,1)S(1)} %get-tuple-element.77), channel_id=1, source_target_pairs={{0,4},{2,6},{4,0},{6,2},{8,12},{10,14},{12,8},{14,10},{16,20},{18,... | collective-permute-start | bytes 786440 | tf_op jit(solution)/shard_map/ppermute | solution.py:434
  81.4 5.3 %collective-permute-start.21 = (bf16[2,64,512]{2,1,0:T(8,128)(2,1)S(1)}, bf16[2,64,512]{2,1,0:T(8,128)(2,1)S(1)}, u32[]{:S(2)}, u32[]{:S(2)}) collective-permute-start(bf16[2,64,512]{2,1,0:T(8,128)(2,1)S(1)} %get-tuple-element.88), channel_id=1, source_target_pairs={{0,4},{2,6},{4,0},{6,2},{8,12},{10,14},{12,8},{14,10},{16,20},{18,... | collective-permute-start | bytes 393224 | tf_op jit(solution)/shard_map/ppermute | solution.py:442
  83.0 6.5 %collective-permute-start.16 = (bf16[2,64,512]{2,1,0:T(8,128)(2,1)S(1)}, bf16[2,64,512]{2,1,0:T(8,128)(2,1)S(1)}, u32[]{:S(2)}, u32[]{:S(2)}) collective-permute-start(bf16[2,64,512]{2,1,0:T(8,128)(2,1)S(1)} %get-tuple-element.79), channel_id=1, source_target_pairs={{0,8},{2,10},{4,12},{6,14},{8,0},{10,2},{12,4},{14,6},{16,24},{18,... | collective-permute-start | bytes 393224 | tf_op jit(solution)/shard_map/ppermute | solution.py:440
  86.7 7.1 %collective-permute-start.22 = (bf16[1,64,512]{2,1,0:T(8,128)(2,1)S(1)}, bf16[1,64,512]{2,1,0:T(8,128)(2,1)S(1)}, u32[]{:S(2)}, u32[]{:S(2)}) collective-permute-start(bf16[1,64,512]{2,1,0:T(8,128)(2,1)S(1)} %get-tuple-element.90), channel_id=1, source_target_pairs={{0,16},{2,18},{4,20},{6,22},{8,24},{10,26},{12,28},{14,30},{16,0},... | collective-permute-start | bytes 196616 | tf_op jit(solution)/shard_map/ppermute | solution.py:415
  89.5 5.9 %collective-permute-start.17 = (bf16[1,64,512]{2,1,0:T(8,128)(2,1)S(1)}, bf16[1,64,512]{2,1,0:T(8,128)(2,1)S(1)}, u32[]{:S(2)}, u32[]{:S(2)}) collective-permute-start(bf16[1,64,512]{2,1,0:T(8,128)(2,1)S(1)} %get-tuple-element.81), channel_id=1, source_target_pairs={{0,16},{2,18},{4,20},{6,22},{8,24},{10,26},{12,28},{14,30},{16,0},... | collective-permute-start | bytes 196616 | tf_op jit(solution)/shard_map/ppermute | solution.py:415
  93.8 4.3 %collective-permute-start.23 = (bf16[1,64,512]{2,1,0:T(8,128)(2,1)S(1)}, bf16[1,64,512]{2,1,0:T(8,128)(2,1)S(1)}, u32[]{:S(2)}, u32[]{:S(2)}) collective-permute-start(bf16[1,64,512]{2,1,0:T(8,128)(2,1)S(1)} %rounded_sum.3.refs_2_), channel_id=1, source_target_pairs={{0,1},{1,0},{2,3},{3,2},{4,5},{5,4},{6,7},{7,6},{8,9},{9,8},{10,11... | collective-permute-start | bytes 196616 | tf_op jit(solution)/shard_map/ppermute | solution.py:419
  95.4 4.3 %collective-permute-start.18 = (bf16[1,64,512]{2,1,0:T(8,128)(2,1)S(1)}, bf16[1,64,512]{2,1,0:T(8,128)(2,1)S(1)}, u32[]{:S(2)}, u32[]{:S(2)}) collective-permute-start(bf16[1,64,512]{2,1,0:T(8,128)(2,1)S(1)} %rounded_sum.2.refs_0_), channel_id=1, source_target_pairs={{0,1},{1,0},{2,3},{3,2},{4,5},{5,4},{6,7},{7,6},{8,9},{9,8},{10,11... | collective-permute-start | bytes 196616 | tf_op jit(solution)/shard_map/ppermute | solution.py:419
